TPU v7x, 512 devices: a whole 4x4x16 slice. The times are simulated.
512 devices in a mesh: row: 8 (over x, y_hi), col: 16 (over z), pipe: 4 (over y_lo, core).
Axes of the slice: x: 4, y: 4 (y_hi: 2, y_lo: 2; y = y_hi * 2 + y_lo), z: 16, core: 2. Of those that a mesh axis runs over, the one named last changes fastest.
Arguments:
- inputs: bfloat16 [1024, 12288], P('col', ('row', 'pipe')), may hold values from -6 to 6
- weight: bfloat16 [12288, 49152], P(('row', 'pipe'), 'col'), may hold values from -0.0546875 to 0.0546875
- upstream: bfloat16 [1024, 49152], P(('row', 'pipe'), 'col'), may hold values from -1.5 to 1.5
- preactivation: bfloat16 [1024, 49152], P(('row', 'pipe'), 'col'), may hold values from -6 to 6
Outputs:
- input_gradient: bfloat16 [1024, 12288], P('col', ('row', 'pipe'))
- weight_gradient: bfloat16 [12288, 49152], P(('row', 'pipe'), 'col')
All inputs are finite; a program needn't handle non-finite values.
Results may differ from a plain program's by a relative error of at most 0.0049.
Values may be sent and summed in bfloat16 or wider, within the bound.
No kernel may reach another device: no remote copies, remote signals or barrier semaphores. Data moves between devices by JAX's collectives and lax.ppermute only.
A program may use at most 64 MiB of HBM per device.

v0:
```python
import math

import jax
import jax.numpy as jnp
from jax import lax
from jax.sharding import PartitionSpec as P

gelu_scale = math.sqrt(2.0 / math.pi)
cubic_term = 0.044715


def gelu_slope(values):
    inner = gelu_scale * (values + cubic_term * values * values * values)
    tangent = jnp.tanh(inner)
    return 0.5 * (1.0 + tangent) + 0.5 * values * (1.0 - tangent * tangent) * gelu_scale * (
        1.0 + 3.0 * cubic_term * values * values
    )


def over_tokens(left, right):
    return lax.dot_general(
        left, right, (((0,), (0,)), ((), ())), preferred_element_type=jnp.float32
    )


def over_hidden(left, right):
    return lax.dot_general(
        left, right, (((1,), (1,)), ((), ())), preferred_element_type=jnp.float32
    )


def per_device(inputs, weight, upstream, preactivation):
    slope = gelu_slope(preactivation.astype(jnp.float32))
    local_gradient = (upstream.astype(jnp.float32) * slope).astype(jnp.bfloat16)
    gathered = lax.all_gather(inputs, "col", axis=0, tiled=True)
    gathered_gradient = lax.all_gather(local_gradient, ("row", "pipe"), axis=0, tiled=True)
    weight_total = over_tokens(gathered, gathered_gradient)
    input_partial = over_hidden(gathered_gradient, weight)
    input_gradient = lax.psum_scatter(input_partial, "col", scatter_dimension=0, tiled=True).astype(
        jnp.bfloat16
    )
    return (input_gradient, weight_total.astype(jnp.bfloat16))


def solution(mesh):
    in_specs = (
        P("col", ("row", "pipe")),
        P(("row", "pipe"), "col"),
        P(("row", "pipe"), "col"),
        P(("row", "pipe"), "col"),
    )
    out_specs = (P("col", ("row", "pipe")), P(("row", "pipe"), "col"))
    return jax.shard_map(
        per_device, mesh=mesh, in_specs=in_specs, out_specs=out_specs, check_vma=False
    )
```

profile of v0, /device:TPU:16, one launch (start us, length us, event | category | flops | bytes accessed | tf_op | source)
XLA Modules:
  0.0 167.5 jit_solution(11210258130066500009)
XLA Ops:
  7.2 0.0 copy-start
  7.2 0.0 all-gather.2.cloned.1.call-start
  7.2 2.1 %fusion.8 = bf16[32,3072]{1,0:T(8,128)(2,1)} fusion(bf16[32,3072]{1,0:T(8,128)(2,1)} %param.7, bf16[32,3072]{1,0:T(8,128)(2,1)} %param.6), kind=kLoop, calls=%fused_computation.16 | loop fusion | flops 2064384 | bytes 589824 | tf_op jit(solution)/shard_map/convert_element_type | solution.py:34
  9.4 0.0 all-gather.2.cloned.1.call-update
  9.4 0.0 copy-start.1
  9.4 0.0 reduce-scatter.2.cloned.1.call-start
  9.4 69.9 %all-gather.2.cloned.1.call-done = bf16[1024,3072]{1,0:T(8,128)(2,1)} async-done(((bf16[32,3072]{1,0:T(8,128)(2,1)}), bf16[1024,3072]{1,0:T(8,128)(2,1)}) %all-gather.2.cloned.1.call-update) | async-done | bytes 6291472 | tf_op jit(solution)/shard_map/all_gather | solution.py:36
  79.3 0.0 copy-done
  79.3 6.7 %fusion.10 = f32[1024,384]{1,0:T(8,128)} fusion(bf16[1024,3072]{1,0:T(8,128)(2,1)} %all-gather.2.cloned.1.call-done, bf16[384,3072]{1,0:T(8,128)(2,1)S(1)} %copy-done), kind=kOutput, calls=%fused_computation.18 | convolution fusion | flops 2415919104 | bytes 10223616 | tf_op jit(solution)/shard_map/dot_general | solution.py:27
  86.0 0.0 reduce-scatter.2.cloned.1.call-update
  86.1 0.0 copy-done.1
  86.1 35.5 %all_gather.7 = bf16[1024,384]{1,0:T(8,128)(2,1)S(1)} all-gather(bf16[64,384]{1,0:T(8,128)(2,1)S(1)} %copy-done.1), channel_id=1, replica_groups=mesh['row'=8,'col'=16,'pipe'=4] {'col'}, dimensions={0}, use_global_device_ids=true | all-gather | bytes 835584 | tf_op jit(solution)/shard_map/all_gather | solution.py:35
  121.6 7.7 %fusion = bf16[384,3072]{0,1:T(8,128)(2,1)} fusion(bf16[1024,3072]{1,0:T(8,128)(2,1)} %all-gather.2.cloned.1.call-done, bf16[1024,384]{1,0:T(8,128)(2,1)S(1)} %all_gather.7), kind=kOutput, calls=%fused_computation.1 | convolution fusion | flops 2417098752 | bytes 9437184 | tf_op jit(solution)/shard_map/dot_general | solution.py:21
  129.3 4.3 %copy.6 = bf16[384,3072]{1,0:T(8,128)(2,1)} copy(bf16[384,3072]{0,1:T(8,128)(2,1)} %fusion) | data formatting | bytes 4718592
  133.6 25.5 %reduce-scatter.2.cloned.1.call-done = f32[64,384]{1,0:T(8,128)} async-done(((f32[1024,384]{1,0:T(8,128)}), f32[64,384]{1,0:T(8,128)}) %reduce-scatter.2.cloned.1.call-update) | async-done | bytes 98320 | tf_op jit(solution)/shard_map/reduce_scatter | solution.py:39
  159.1 1.5 convert_element_type.21
Async XLA Ops:
  7.2 72.1 %copy-start = (bf16[384,3072]{1,0:T(8,128)(2,1)S(1)}, bf16[384,3072]{1,0:T(8,128)(2,1)}, u32[]{:S(2)}) copy-start(bf16[384,3072]{1,0:T(8,128)(2,1)} %param.5) | copy-start | bytes 7077892
  7.2 72.1 %all-gather.2.cloned.1.call-start = ((), (), s32[]{:S(2)}) async-start(), calls=%async_computation.1 | async-start | bytes 6488064 | tf_op jit(solution)/shard_map/all_gather | solution.py:36
  9.4 76.7 %copy-start.1 = (bf16[64,384]{1,0:T(8,128)(2,1)S(1)}, bf16[64,384]{1,0:T(8,128)(2,1)}, u32[]{:S(2)}) copy-start(bf16[64,384]{1,0:T(8,128)(2,1)} %param.4) | copy-start | bytes 147460
  9.4 149.7 %reduce-scatter.2.cloned.1.call-start = ((), (), s32[]{:S(2)}) async-start(), calls=%async_computation.2 | async-start | bytes 1671168 | tf_op jit(solution)/shard_map/reduce_scatter | solution.py:39
Sparse Core Ops, SparseCore 0:
  11.7 67.5 all-gather.1
  86.2 72.8 reduce-scatter.1
where the time goes:
time: 168 us; the launch traced here: 167 us
  waiting for transfers between devices  95.4 us (57%)
  blocking collectives  35.5 us (21%)
  matrix products  14.5 us (9%)
  between operations  14.1 us (8%)
  local copies, waits for them, and re-layouts  4.29 us (3%)
  other arithmetic  3.64 us (2%)
    all_gather x1, waiting for transfers between devices, per_device(): lax.all_gather(local_gradient, ('row', 'pipe'), axis=0, tiled=True)  69.9 us
    all_gather x1, blocking collectives, per_device(): gathered = lax.all_gather(inputs, 'col', axis=0, tiled=True)  35.5 us
    reduce_scatter x1, waiting for transfers between devices, per_device(): lax.psum_scatter(input_partial, 'col', scatter_dimension=0, tiled=True)  25.5 us
    dot_general x1, matrix products, over_tokens(): lax.dot_general(left, right, (((0,), (0,)), ((), ())), preferred_element_...  7.73 us
    dot_general x1, matrix products, over_hidden(): lax.dot_general(left, right, (((1,), (1,)), ((), ())), preferred_element_...  6.74 us
    unnamed x5, local copies, waits for them, and re-layouts  4.29 us
  transfers between devices with their start and end apart: 2, of which 2 were waited for; matrix products, arithmetic and copies ran while one was open for 7% of the time, Pallas kernels for 0%

commit v1 on v0

v1 whole, which is shorter than its diff:
```python
import math

import jax
import jax.numpy as jnp
from jax import lax
from jax.experimental import pallas as pl
from jax.experimental.pallas import tpu as pltpu
from jax.sharding import Mesh
from jax.sharding import PartitionSpec as P

gelu_scale = math.sqrt(2.0 / math.pi)
cubic_term = 0.044715

MIB = 1024 * 1024
PLANE = ("x", "yh", "yl", "core")
Z = ("zh", "zl")
ROWS_BY_ROWS = (((1,), (1,)), ((), ()))


def gelu_slope(values):
    inner = gelu_scale * (values + cubic_term * values * values * values)
    tangent = jnp.tanh(inner)
    return 0.5 * (1.0 + tangent) + 0.5 * values * (1.0 - tangent * tangent) * gelu_scale * (
        1.0 + 3.0 * cubic_term * values * values
    )


def vmem():
    return pl.BlockSpec(memory_space=pltpu.VMEM)


def smem():
    return pl.BlockSpec(memory_space=pltpu.SMEM)


def chip_number(info_ref, first, second):
    core = info_ref[3]
    return first * (4 - 3 * core) + second * (1 + 3 * core)


def block_rows(k):
    return pl.ds(pl.multiple_of(k * 32, 32), 32)


def early_kernel(l0_ref, l1_ref, l3_ref, w_own_ref, w_sib_ref, out_ref, left):
    for j, ref in enumerate((l0_ref, l1_ref, l3_ref)):
        for i in range(4):
            left[pl.ds(j * 128 + i * 32, 32), :] = ref[i]
    for n, w_ref in enumerate((w_own_ref, w_sib_ref)):
        out_ref[:, n * 384 : (n + 1) * 384] = lax.dot_general(
            left[...], w_ref[...], ROWS_BY_ROWS, preferred_element_type=jnp.float32
        )


def early_sums(lines, w_own, w_sib):
    return pl.pallas_call(
        early_kernel,
        out_shape=jax.ShapeDtypeStruct((384, 768), jnp.float32),
        in_specs=[vmem()] * 5,
        out_specs=vmem(),
        scratch_shapes=[pltpu.VMEM((384, 3072), jnp.bfloat16)],
        compiler_params=pltpu.CompilerParams(vmem_limit_bytes=24 * MIB),
        cost_estimate=pl.CostEstimate(
            flops=2 * 384 * 3072 * 768, bytes_accessed=8 * MIB, transcendentals=0
        ),
        name="early_sums",
    )(*lines, w_own, w_sib)


def late_kernel(info_ref, l0_ref, l1_ref, l3_ref, l2_ref, early_ref, w_own_ref, w_sib_ref, own_ref, s1_ref, s2_ref, s3_ref, plane_ref, left, acc):
    for i in range(4):
        left[pl.ds(i * 32, 32), :] = l2_ref[i]
    second = info_ref[2]
    for n, w_ref in enumerate((w_own_ref, w_sib_ref)):
        total = lax.dot_general(
            left[...], w_ref[...], ROWS_BY_ROWS, preferred_element_type=jnp.float32
        )
        for i in range(4):
            k = chip_number(info_ref, i, lax.rem(second + 2, 4))
            acc[block_rows(k), n * 384 : (n + 1) * 384] = total[i * 32 : (i + 1) * 32]
    for i in range(4):
        k = chip_number(info_ref, i, lax.rem(second + 2, 4))
        plane_ref[block_rows(k), :] = l2_ref[i]
        for j, (d, ref) in enumerate(((0, l0_ref), (1, l1_ref), (3, l3_ref))):
            k = chip_number(info_ref, i, lax.rem(second + d, 4))
            acc[block_rows(k), :] = early_ref[j * 128 + i * 32 : j * 128 + (i + 1) * 32, :]
            plane_ref[block_rows(k), :] = ref[i]
    for d, out in enumerate((own_ref, s1_ref, s2_ref, s3_ref)):
        residue = lax.rem(info_ref[0] + d, 4)
        for x in range(4):
            out[x] = acc[block_rows(x * 4 + residue), :].astype(out.dtype)


def late_sums(info, lines, far, early, w_own, w_sib):
    shape = (4, 32, 768)
    return pl.pallas_call(
        late_kernel,
        out_shape=[jax.ShapeDtypeStruct(shape, jnp.float32)]
        + [jax.ShapeDtypeStruct(shape, jnp.bfloat16)] * 3
        + [jax.ShapeDtypeStruct((512, 3072), jnp.bfloat16)],
        in_specs=[smem()] + [vmem()] * 7,
        out_specs=[vmem()] * 5,
        scratch_shapes=[
            pltpu.VMEM((128, 3072), jnp.bfloat16),
            pltpu.VMEM((512, 768), jnp.float32),
        ],
        compiler_params=pltpu.CompilerParams(vmem_limit_bytes=28 * MIB),
        cost_estimate=pl.CostEstimate(
            flops=2 * 128 * 3072 * 768, bytes_accessed=8 * MIB, transcendentals=0
        ),
        name="late_sums",
    )(info, *lines, far, early, w_own, w_sib)


def stage_kernel(info_ref, own_ref, r1_ref, r2_ref, r3_ref, o_ref, s1_ref, s2_ref, s3_ref):
    zh = info_ref[0] // 4
    for d, out in enumerate((o_ref, s1_ref, s2_ref, s3_ref)):
        i = lax.rem(zh + d, 4)
        total = own_ref[i]
        for r in (r1_ref, r2_ref, r3_ref):
            total = total + r[i].astype(jnp.float32)
        out[...] = total.astype(out.dtype)


def stage_sums(info, own, received):
    shape = (32, 768)
    return pl.pallas_call(
        stage_kernel,
        out_shape=[jax.ShapeDtypeStruct(shape, jnp.float32)]
        + [jax.ShapeDtypeStruct(shape, jnp.bfloat16)] * 3,
        in_specs=[smem()] + [vmem()] * 4,
        out_specs=[vmem()] * 4,
        compiler_params=pltpu.CompilerParams(vmem_limit_bytes=16 * MIB),
        cost_estimate=pl.CostEstimate(flops=400000, bytes_accessed=2 * MIB, transcendentals=0),
        name="stage_sums",
    )(info, own, *received)


def final_kernel(own_ref, r1_ref, r2_ref, r3_ref, o_ref, s_ref):
    total = own_ref[...]
    for r in (r1_ref, r2_ref, r3_ref):
        total = total + r[...].astype(jnp.float32)
    o_ref[...] = total[:, :384].astype(jnp.bfloat16)
    s_ref[...] = total[:, 384:].astype(jnp.bfloat16)


def final_sums(own, received):
    shape = jax.ShapeDtypeStruct((32, 384), jnp.bfloat16)
    return pl.pallas_call(
        final_kernel,
        out_shape=[shape, shape],
        in_specs=[vmem()] * 4,
        out_specs=[vmem()] * 2,
        compiler_params=pltpu.CompilerParams(vmem_limit_bytes=4 * MIB),
        cost_estimate=pl.CostEstimate(flops=100000, bytes_accessed=MIB // 4, transcendentals=0),
        name="final_sums",
    )(own, *received)


def weight_kernel(info_ref, in_ref, own_ref, sib_ref, out_ref, left):

    @pl.when(pl.program_id(0) == 0)
    def _():
        core = info_ref[3]
        for which in range(2):
            half = core if which == 0 else 1 - core
            rows = [
                in_ref[pl.ds(pl.multiple_of(k * 64 + half * 32, 32), 32), :] for k in range(16)
            ]
            block = jnp.concatenate(rows, axis=0)
            left[:, which * 512 : (which + 1) * 512] = block.T

    total = jnp.dot(left[:, :512], own_ref[...], preferred_element_type=jnp.float32)
    total += jnp.dot(left[:, 512:], sib_ref[...], preferred_element_type=jnp.float32)
    out_ref[...] = total.astype(jnp.bfloat16)


def weight_sums(info, gathered, hg_own, hg_sib):
    tile = 512
    return pl.pallas_call(
        weight_kernel,
        out_shape=jax.ShapeDtypeStruct((384, 3072), jnp.bfloat16),
        grid_spec=pltpu.PrefetchScalarGridSpec(
            num_scalar_prefetch=1,
            grid=(3072 // tile,),
            in_specs=[
                pl.BlockSpec((1024, 384), lambda j, info: (0, 0)),
                pl.BlockSpec((512, tile), lambda j, info: (0, j)),
                pl.BlockSpec((512, tile), lambda j, info: (0, j)),
            ],
            out_specs=pl.BlockSpec((384, tile), lambda j, info: (0, j)),
            scratch_shapes=[pltpu.VMEM((384, 1024), jnp.bfloat16)],
        ),
        compiler_params=pltpu.CompilerParams(vmem_limit_bytes=24 * MIB),
        cost_estimate=pl.CostEstimate(
            flops=2 * 1024 * 3072 * 384, bytes_accessed=10 * MIB, transcendentals=0
        ),
        name="weight_sums",
    )(info, gathered, hg_own, hg_sib)


def plane_shift(first, by):
    pairs = []
    for x in range(4):
        for y in range(4):
            for core in range(2):
                along_x = (core == 0) == first
                to = ((x + by) % 4, y) if along_x else (x, (y + by) % 4)
                pairs.append(((x * 4 + y) * 2 + core, (to[0] * 4 + to[1]) * 2 + core))
    return pairs


def column_shift(by):
    return [(z * 2 + c, (z + by[c]) % 16 * 2 + c) for z in range(16) for c in range(2)]


def first_axis_groups():
    place = [[[(x * 4 + y) * 2 + c for c in range(2)] for y in range(4)] for x in range(4)]
    along_x = [[place[i][j][0] for i in range(4)] for j in range(4)]
    along_y = [[place[j][i][1] for i in range(4)] for j in range(4)]
    return along_x + along_y


def per_device(inputs, weight, upstream, preactivation):
    core = lax.axis_index("core")
    x, y, z = lax.axis_index("x"), lax.axis_index(("yh", "yl")), lax.axis_index(Z)
    first, second = jnp.where(core == 0, x, y), jnp.where(core == 0, y, x)
    info = jnp.stack([z, first, second, core]).astype(jnp.int32)
    swap = [(0, 1), (1, 0)]

    slope = gelu_slope(preactivation.astype(jnp.float32))
    local = (upstream.astype(jnp.float32) * slope).astype(jnp.bfloat16)
    line = lax.all_gather(
        local, PLANE, axis=0, tiled=True, axis_index_groups=first_axis_groups()
    ).reshape(4, 32, 3072)
    weight_then, inputs, line = lax.optimization_barrier((weight, inputs, line))
    w_sib = lax.ppermute(weight_then, "core", swap)
    far = lax.ppermute(line, PLANE, plane_shift(False, -2))
    line1 = lax.ppermute(line, PLANE, plane_shift(False, -1))
    line3 = lax.ppermute(line, PLANE, plane_shift(False, 1))
    gathered = lax.all_gather(inputs, Z, axis=0, tiled=True)
    far, line1, line3, gathered = lax.optimization_barrier((far, line1, line3, gathered))
    lines = (line, line1, line3)
    early = early_sums(lines, weight, w_sib)

    own, *sends, hg_own = late_sums(info, lines, far, early, weight, w_sib)
    received = [
        lax.ppermute(s, Z + ("core",), column_shift(by))
        for s, by in zip(sends, ((1, 1), (2, -2), (-1, -1)))
    ]
    *received, hg_own = lax.optimization_barrier((*received, hg_own))
    hg_sib = lax.ppermute(hg_own, "core", swap)
    own, *sends = stage_sums(info, own, received)
    received = [
        lax.ppermute(s, Z, [(i, (i + 4 * (d + 1)) % 16) for i in range(16)])
        for d, s in enumerate(sends)
    ]
    weight_total = weight_sums(info, gathered, hg_own, hg_sib)
    weight_total, *received = lax.optimization_barrier((weight_total, *received))
    mine, other = final_sums(own, received)
    other = lax.ppermute(other, "core", swap)
    input_gradient = jnp.concatenate(
        [jnp.where(core == 0, mine, other), jnp.where(core == 0, other, mine)], axis=0
    )
    return (input_gradient, weight_total)


def solution(mesh):
    fine = Mesh(
        mesh.devices.reshape(4, 2, 4, 4, 2, 2), ("x", "yh", "zh", "zl", "yl", "core")
    )
    in_specs = (P(Z, PLANE), P(PLANE, Z), P(PLANE, Z), P(PLANE, Z))
    out_specs = (P(Z, PLANE), P(PLANE, Z))
    return jax.shard_map(
        per_device, mesh=fine, in_specs=in_specs, out_specs=out_specs, check_vma=False
    )
```

time: 168 us -> 126 us (0.75)
  the two profiles are of different devices: /device:TPU:16 before, /device:TPU:1 now
where the time goes in v1:
time: 126 us; the launch traced here: 125 us
  starting transfers between devices  54.2 us (43%)
  blocking collectives  43 us (34%)
  Pallas kernels  15.4 us (12%)
  waiting for transfers between devices  9.7 us (8%)
  other arithmetic  2.17 us (2%)
    all_gather x1, blocking collectives, per_device(): gathered = lax.all_gather(inputs, Z, axis=0, tiled=True)  30.7 us
    ppermute x3, starting transfers between devices, per_device(): lax.ppermute(s, Z, [(i, (i + 4 * (d + 1)) % 16) for i in range(16)])  16.4 us
    all_gather x1, blocking collectives, per_device(): lax.all_gather(local, PLANE, axis=0, tiled=True, axis_index_groups=first_...  12.4 us
    ppermute x1, starting transfers between devices, per_device(): w_sib = lax.ppermute(weight_then, 'core', swap)  9.73 us
    ppermute x1, starting transfers between devices, per_device(): hg_sib = lax.ppermute(hg_own, 'core', swap)  8.66 us
    ppermute x3, starting transfers between devices, per_device(): lax.ppermute(s, Z + ('core',), column_shift(by))  8.41 us
    ppermute x3, waiting for transfers between devices, per_device(): lax.ppermute(s, Z + ('core',), column_shift(by))  6.31 us
    pallas_call x1, Pallas kernels, weight_sums(): pl.pallas_call(weight_kernel, out_shape=jax.ShapeDtypeStruct((384, 3072),...  5.71 us
  transfers between devices with their start and end apart: 12, of which 4 were waited for; matrix products, arithmetic and copies ran while one was open for 0% of the time, Pallas kernels for 5%

profile of v1, /device:TPU:1, one launch (start us, length us, event | category | flops | bytes accessed | tf_op | source)
XLA Modules:
  0.0 125.2 jit_solution(8620941152026630075)
XLA Ops:
  0.6 0.0 copy-start
  0.6 1.5 %fusion.7 = bf16[32,3072]{1,0:T(8,128)(2,1)S(1)} fusion(bf16[32,3072]{1,0:T(8,128)(2,1)} %param.7, bf16[32,3072]{1,0:T(8,128)(2,1)} %param.6), kind=kLoop, calls=%fused_computation.14 | loop fusion | flops 2064384 | bytes 589824 | tf_op jit(solution)/shard_map/convert_element_type | solution.py:232
  2.1 12.4 %all_gather.6 = bf16[128,3072]{1,0:T(8,128)(2,1)S(1)} all-gather(bf16[32,3072]{1,0:T(8,128)(2,1)S(1)} %fusion.7), channel_id=1, replica_groups={{0,128,256,384},{2,130,258,386},{64,192,320,448},{66,194,322,450},{1,3,..., dimensions={0}, use_global_device_ids=true | all-gather | bytes 983040 | tf_op jit(solution)/shard_map/all_gather | solution.py:233
  14.5 9.7 %collective-permute-start.3 = (bf16[384,3072]{1,0:T(8,128)(2,1)}, bf16[384,3072]{1,0:T(8,128)(2,1)}, u32[]{:S(2)}, u32[]{:S(2)}) collective-permute-start(bf16[384,3072]{1,0:T(8,128)(2,1)} %w_own_ref.3), channel_id=1, source_target_pairs={{0,1},{1,0},{2,3},{3,2},{4,5},{5,4},{6,7},{7,6},{8,9},{9,8},{10,11... | collective-permute-start | bytes 7077896 | tf_op jit(solution)/shard_map/ppermute | solution.py:237
  24.2 1.9 %collective-permute-start.2 = (bf16[4,32,3072]{2,1,0:T(8,128)(2,1)S(1)}, bf16[4,32,3072]{2,1,0:T(8,128)(2,1)}, u32[]{:S(2)}, u32[]{:S(2)}) collective-permute-start(bf16[4,32,3072]{2,1,0:T(8,128)(2,1)S(1)} %bitcast.5), channel_id=1, source_target_pairs={{0,2},{1,129},{2,64},{3,131},{64,66},{65,193},{66,0},{67,195},{128... | collective-permute-start | bytes 2359304 | tf_op jit(solution)/shard_map/ppermute | solution.py:240
  26.1 4.6 %collective-permute-start.1 = (bf16[4,32,3072]{2,1,0:T(8,128)(2,1)S(1)}, bf16[4,32,3072]{2,1,0:T(8,128)(2,1)}, u32[]{:S(2)}, u32[]{:S(2)}) collective-permute-start(bf16[4,32,3072]{2,1,0:T(8,128)(2,1)S(1)} %bitcast.6), channel_id=1, source_target_pairs={{0,66},{1,385},{2,0},{3,387},{64,2},{65,449},{66,64},{67,451},{128... | collective-permute-start | bytes 2359304 | tf_op jit(solution)/shard_map/ppermute | solution.py:239
  30.7 1.9 %collective-permute-start = (bf16[4,32,3072]{2,1,0:T(8,128)(2,1)S(1)}, bf16[4,32,3072]{2,1,0:T(8,128)(2,1)}, u32[]{:S(2)}, u32[]{:S(2)}) collective-permute-start(bf16[4,32,3072]{2,1,0:T(8,128)(2,1)S(1)} %bitcast.7), channel_id=1, source_target_pairs={{0,64},{1,257},{2,66},{3,259},{64,0},{65,321},{66,2},{67,323},{128... | collective-permute-start | bytes 2359304 | tf_op jit(solution)/shard_map/ppermute | solution.py:238
  32.7 0.1 pad_add_fusion.info_ref
  32.7 30.7 %all_gather.7.in_ref = bf16[1024,384]{1,0:T(8,128)(2,1)S(1)} all-gather(bf16[64,384]{1,0:T(8,128)(2,1)} %param.4), channel_id=1, replica_groups=mesh['x'=4,'yh'=2,'zh'=4,'zl'=4,'yl'=2,'core'=2] {'zh','zl'}, dimensions={0}, use_global_device_ids=true | all-gather | bytes 835584 | tf_op jit(solution)/shard_map/all_gather | solution.py:241
  63.4 0.0 collective-permute-done.2.l3_ref
  63.4 0.0 collective-permute-done.1.l1_ref
  63.4 0.0 collective-permute-done.l2_ref
  63.4 0.0 collective-permute-done.3.w_sib_ref
  63.4 0.0 copy-done
  63.4 4.8 %early_sums.1.early_ref = f32[384,768]{1,0:T(8,128)S(1)} custom-call(bf16[4,32,3072]{2,1,0:T(8,128)(2,1)S(1)} %bitcast.8, bf16[4,32,3072]{2,1,0:T(8,128)(2,1)} %collective-permute-done.1.l1_ref, bf16[4,32,3072]{2,1,0:T(8,128)(2,1)} %collective-permute-done.2.l3_ref, bf16[384,3072]{1,0:T(8,128)(2,1)S(1)} %copy-done, ...), custom_call_target="tpu_custom_call" | custom-call | flops 1811939328 | bytes 8388608 | tf_op jit(solution)/shard_map/early_sums/pallas_call | solution.py:56
  68.2 4.2 %late_sums.1 = (f32[4,32,768]{2,1,0:T(8,128)S(1)}, bf16[4,32,768]{2,1,0:T(8,128)(2,1)S(1)}, bf16[4,32,768]{2,1,0:T(8,128)(2,1)S(1)}, bf16[4,32,768]{2,1,0:T(8,128)(2,1)S(1)}, bf16[512,3072]{1,0:T(8,128)(2,1)S(1)}) custom-call(s32[4]{0:T(128)S(1)} %pad_add_fusion.info_ref, bf16[4,32,3072]{2,1,0:T(8,128)(2,1)S(1)} %bitcast.9, ...), custom_call_target="tpu_custom_call" | custom-call | flops 603979776 | bytes 8388608 | tf_op jit(solution)/shard_map/late_sums/pallas_call | solution.py:96
  72.4 1.9 %collective-permute-start.4 = (bf16[4,32,768]{2,1,0:T(8,128)(2,1)S(1)}, bf16[4,32,768]{2,1,0:T(8,128)(2,1)S(1)}, u32[]{:S(2)}, u32[]{:S(2)}) collective-permute-start(bf16[4,32,768]{2,1,0:T(8,128)(2,1)S(1)} %get-tuple-element.35), channel_id=1, source_target_pairs={{0,4},{1,5},{4,8},{5,9},{8,12},{9,13},{12,16},{13,17},{16,20},{17,... | collective-permute-start | bytes 589832 | tf_op jit(solution)/shard_map/ppermute | solution.py:248
  74.4 2.8 %collective-permute-start.5 = (bf16[4,32,768]{2,1,0:T(8,128)(2,1)S(1)}, bf16[4,32,768]{2,1,0:T(8,128)(2,1)S(1)}, u32[]{:S(2)}, u32[]{:S(2)}) collective-permute-start(bf16[4,32,768]{2,1,0:T(8,128)(2,1)S(1)} %get-tuple-element.36), channel_id=1, source_target_pairs={{0,8},{1,57},{4,12},{5,61},{8,16},{9,1},{12,20},{13,5},{16,24},{17... | collective-permute-start | bytes 589832 | tf_op jit(solution)/shard_map/ppermute | solution.py:248
  77.2 3.7 %collective-permute-start.6 = (bf16[4,32,768]{2,1,0:T(8,128)(2,1)S(1)}, bf16[4,32,768]{2,1,0:T(8,128)(2,1)S(1)}, u32[]{:S(2)}, u32[]{:S(2)}) collective-permute-start(bf16[4,32,768]{2,1,0:T(8,128)(2,1)S(1)} %get-tuple-element.37), channel_id=1, source_target_pairs={{0,60},{1,61},{4,0},{5,1},{8,4},{9,5},{12,8},{13,9},{16,12},{17,13... | collective-permute-start | bytes 589832 | tf_op jit(solution)/shard_map/ppermute | solution.py:248
  80.9 0.0 collective-permute-done.4.r1_ref
  80.9 3.0 %collective-permute-done.5.r2_ref = bf16[4,32,768]{2,1,0:T(8,128)(2,1)S(1)} collective-permute-done((bf16[4,32,768]{2,1,0:T(8,128)(2,1)S(1)}, bf16[4,32,768]{2,1,0:T(8,128)(2,1)S(1)}, u32[]{:S(2)}, u32[]{:S(2)}) %collective-permute-start.5) | collective-permute-done | bytes 196640 | tf_op jit(solution)/shard_map/ppermute | solution.py:248
  83.8 3.3 %collective-permute-done.6.r3_ref = bf16[4,32,768]{2,1,0:T(8,128)(2,1)S(1)} collective-permute-done((bf16[4,32,768]{2,1,0:T(8,128)(2,1)S(1)}, bf16[4,32,768]{2,1,0:T(8,128)(2,1)S(1)}, u32[]{:S(2)}, u32[]{:S(2)}) %collective-permute-start.6) | collective-permute-done | bytes 196640 | tf_op jit(solution)/shard_map/ppermute | solution.py:248
  87.2 8.7 %collective-permute-start.7 = (bf16[512,3072]{1,0:T(8,128)(2,1)S(1)}, bf16[512,3072]{1,0:T(8,128)(2,1)S(1)}, u32[]{:S(2)}, u32[]{:S(2)}) collective-permute-start(bf16[512,3072]{1,0:T(8,128)(2,1)S(1)} %get-tuple-element.44.own_ref), channel_id=1, source_target_pairs={{0,1},{1,0},{2,3},{3,2},{4,5},{5,4},{6,7},{7,6},{8,9},{9,8},{10,11... | collective-permute-start | bytes 9437192 | tf_op jit(solution)/shard_map/ppermute | solution.py:252
  95.9 0.6 stage_sums.1
  96.5 3.6 %collective-permute-start.8 = (bf16[32,768]{1,0:T(8,128)(2,1)S(1)}, bf16[32,768]{1,0:T(8,128)(2,1)S(1)}, u32[]{:S(2)}, u32[]{:S(2)}) collective-permute-start(bf16[32,768]{1,0:T(8,128)(2,1)S(1)} %get-tuple-element.45), channel_id=1, source_target_pairs={{0,16},{4,20},{8,24},{12,28},{16,32},{20,36},{24,40},{28,44},{32,4... | collective-permute-start | bytes 147464 | tf_op jit(solution)/shard_map/ppermute | solution.py:255
  100.1 8.5 %collective-permute-start.9 = (bf16[32,768]{1,0:T(8,128)(2,1)S(1)}, bf16[32,768]{1,0:T(8,128)(2,1)S(1)}, u32[]{:S(2)}, u32[]{:S(2)}) collective-permute-start(bf16[32,768]{1,0:T(8,128)(2,1)S(1)} %get-tuple-element.46), channel_id=1, source_target_pairs={{0,32},{4,36},{8,40},{12,44},{16,48},{20,52},{24,56},{28,60},{32,0... | collective-permute-start | bytes 147464 | tf_op jit(solution)/shard_map/ppermute | solution.py:255
  108.6 4.3 %collective-permute-start.10 = (bf16[32,768]{1,0:T(8,128)(2,1)S(1)}, bf16[32,768]{1,0:T(8,128)(2,1)S(1)}, u32[]{:S(2)}, u32[]{:S(2)}) collective-permute-start(bf16[32,768]{1,0:T(8,128)(2,1)S(1)} %get-tuple-element.47), channel_id=1, source_target_pairs={{0,48},{4,52},{8,56},{12,60},{16,0},{20,4},{24,8},{28,12},{32,16},... | collective-permute-start | bytes 147464 | tf_op jit(solution)/shard_map/ppermute | solution.py:255
  112.9 0.0 collective-permute-done.7.sib_ref
  112.9 5.7 %weight_sums.1 = bf16[384,3072]{1,0:T(8,128)(2,1)} custom-call(s32[4]{0:T(128)S(1)} %pad_add_fusion.info_ref, bf16[1024,384]{1,0:T(8,128)(2,1)S(1)} %all_gather.7.in_ref, bf16[512,3072]{1,0:T(8,128)(2,1)S(1)} %get-tuple-element.44.own_ref, bf16[512,3072]{1,0:T(8,128)(2,1)S(1)} %collective-permute-done.7.sib_ref), custom_call_target="tpu_custom_call" | custom-call | flops 2415919104 | bytes 10485760 | tf_op jit(solution)/shard_map/weight_sums/pallas_call | solution.py:180
  118.7 0.0 collective-permute-done.8.r1_ref
  118.7 0.0 collective-permute-done.9.r2_ref
  118.7 2.5 %collective-permute-done.10.r3_ref = bf16[32,768]{1,0:T(8,128)(2,1)S(1)} collective-permute-done((bf16[32,768]{1,0:T(8,128)(2,1)S(1)}, bf16[32,768]{1,0:T(8,128)(2,1)S(1)}, u32[]{:S(2)}, u32[]{:S(2)}) %collective-permute-start.10) | collective-permute-done | bytes 49184 | tf_op jit(solution)/shard_map/ppermute | solution.py:255
  121.2 2.5 %collective-permute-start.11 = (bf16[32,384]{1,0:T(8,128)(2,1)S(1)}, bf16[32,384]{1,0:T(8,128)(2,1)S(1)}, u32[]{:S(2)}, u32[]{:S(2)}) collective-permute-start(bf16[32,384]{1,0:T(8,128)(2,1)S(1)} %get-tuple-element.52), channel_id=1, source_target_pairs={{0,1},{1,0},{2,3},{3,2},{4,5},{5,4},{6,7},{7,6},{8,9},{9,8},{10,11... | collective-permute-start | bytes 73736 | tf_op jit(solution)/shard_map/ppermute | solution.py:261
  123.8 0.8 collective-permute-done.11
  124.6 0.6 pad_maximum_fusion
  (2 shorter events, 0.0 us)
Async XLA Ops:
  0.6 62.8 %copy-start = (bf16[384,3072]{1,0:T(8,128)(2,1)S(1)}, bf16[384,3072]{1,0:T(8,128)(2,1)}, u32[]{:S(2)}) copy-start(bf16[384,3072]{1,0:T(8,128)(2,1)} %w_own_ref.3) | copy-start | bytes 7077892
  14.5 49.0 %collective-permute-start.3 = (bf16[384,3072]{1,0:T(8,128)(2,1)}, bf16[384,3072]{1,0:T(8,128)(2,1)}, u32[]{:S(2)}, u32[]{:S(2)}) collective-permute-start(bf16[384,3072]{1,0:T(8,128)(2,1)} %w_own_ref.3), channel_id=1, source_target_pairs={{0,1},{1,0},{2,3},{3,2},{4,5},{5,4},{6,7},{7,6},{8,9},{9,8},{10,11... | collective-permute-start | bytes 7077896 | tf_op jit(solution)/shard_map/ppermute | solution.py:237
  24.2 39.2 %collective-permute-start.2 = (bf16[4,32,3072]{2,1,0:T(8,128)(2,1)S(1)}, bf16[4,32,3072]{2,1,0:T(8,128)(2,1)}, u32[]{:S(2)}, u32[]{:S(2)}) collective-permute-start(bf16[4,32,3072]{2,1,0:T(8,128)(2,1)S(1)} %bitcast.5), channel_id=1, source_target_pairs={{0,2},{1,129},{2,64},{3,131},{64,66},{65,193},{66,0},{67,195},{128... | collective-permute-start | bytes 2359304 | tf_op jit(solution)/shard_map/ppermute | solution.py:240
  26.1 37.3 %collective-permute-start.1 = (bf16[4,32,3072]{2,1,0:T(8,128)(2,1)S(1)}, bf16[4,32,3072]{2,1,0:T(8,128)(2,1)}, u32[]{:S(2)}, u32[]{:S(2)}) collective-permute-start(bf16[4,32,3072]{2,1,0:T(8,128)(2,1)S(1)} %bitcast.6), channel_id=1, source_target_pairs={{0,66},{1,385},{2,0},{3,387},{64,2},{65,449},{66,64},{67,451},{128... | collective-permute-start | bytes 2359304 | tf_op jit(solution)/shard_map/ppermute | solution.py:239
  30.7 32.7 %collective-permute-start = (bf16[4,32,3072]{2,1,0:T(8,128)(2,1)S(1)}, bf16[4,32,3072]{2,1,0:T(8,128)(2,1)}, u32[]{:S(2)}, u32[]{:S(2)}) collective-permute-start(bf16[4,32,3072]{2,1,0:T(8,128)(2,1)S(1)} %bitcast.7), channel_id=1, source_target_pairs={{0,64},{1,257},{2,66},{3,259},{64,0},{65,321},{66,2},{67,323},{128... | collective-permute-start | bytes 2359304 | tf_op jit(solution)/shard_map/ppermute | solution.py:238
  72.4 8.4 %collective-permute-start.4 = (bf16[4,32,768]{2,1,0:T(8,128)(2,1)S(1)}, bf16[4,32,768]{2,1,0:T(8,128)(2,1)S(1)}, u32[]{:S(2)}, u32[]{:S(2)}) collective-permute-start(bf16[4,32,768]{2,1,0:T(8,128)(2,1)S(1)} %get-tuple-element.35), channel_id=1, source_target_pairs={{0,4},{1,5},{4,8},{5,9},{8,12},{9,13},{12,16},{13,17},{16,20},{17,... | collective-permute-start | bytes 589832 | tf_op jit(solution)/shard_map/ppermute | solution.py:248
  74.4 9.5 %collective-permute-start.5 = (bf16[4,32,768]{2,1,0:T(8,128)(2,1)S(1)}, bf16[4,32,768]{2,1,0:T(8,128)(2,1)S(1)}, u32[]{:S(2)}, u32[]{:S(2)}) collective-permute-start(bf16[4,32,768]{2,1,0:T(8,128)(2,1)S(1)} %get-tuple-element.36), channel_id=1, source_target_pairs={{0,8},{1,57},{4,12},{5,61},{8,16},{9,1},{12,20},{13,5},{16,24},{17... | collective-permute-start | bytes 589832 | tf_op jit(solution)/shard_map/ppermute | solution.py:248
  77.2 10.0 %collective-permute-start.6 = (bf16[4,32,768]{2,1,0:T(8,128)(2,1)S(1)}, bf16[4,32,768]{2,1,0:T(8,128)(2,1)S(1)}, u32[]{:S(2)}, u32[]{:S(2)}) collective-permute-start(bf16[4,32,768]{2,1,0:T(8,128)(2,1)S(1)} %get-tuple-element.37), channel_id=1, source_target_pairs={{0,60},{1,61},{4,0},{5,1},{8,4},{9,5},{12,8},{13,9},{16,12},{17,13... | collective-permute-start | bytes 589832 | tf_op jit(solution)/shard_map/ppermute | solution.py:248
  87.2 25.8 %collective-permute-start.7 = (bf16[512,3072]{1,0:T(8,128)(2,1)S(1)}, bf16[512,3072]{1,0:T(8,128)(2,1)S(1)}, u32[]{:S(2)}, u32[]{:S(2)}) collective-permute-start(bf16[512,3072]{1,0:T(8,128)(2,1)S(1)} %get-tuple-element.44.own_ref), channel_id=1, source_target_pairs={{0,1},{1,0},{2,3},{3,2},{4,5},{5,4},{6,7},{7,6},{8,9},{9,8},{10,11... | collective-permute-start | bytes 9437192 | tf_op jit(solution)/shard_map/ppermute | solution.py:252
  96.5 22.2 %collective-permute-start.8 = (bf16[32,768]{1,0:T(8,128)(2,1)S(1)}, bf16[32,768]{1,0:T(8,128)(2,1)S(1)}, u32[]{:S(2)}, u32[]{:S(2)}) collective-permute-start(bf16[32,768]{1,0:T(8,128)(2,1)S(1)} %get-tuple-element.45), channel_id=1, source_target_pairs={{0,16},{4,20},{8,24},{12,28},{16,32},{20,36},{24,40},{28,44},{32,4... | collective-permute-start | bytes 147464 | tf_op jit(solution)/shard_map/ppermute | solution.py:255
  100.1 18.6 %collective-permute-start.9 = (bf16[32,768]{1,0:T(8,128)(2,1)S(1)}, bf16[32,768]{1,0:T(8,128)(2,1)S(1)}, u32[]{:S(2)}, u32[]{:S(2)}) collective-permute-start(bf16[32,768]{1,0:T(8,128)(2,1)S(1)} %get-tuple-element.46), channel_id=1, source_target_pairs={{0,32},{4,36},{8,40},{12,44},{16,48},{20,52},{24,56},{28,60},{32,0... | collective-permute-start | bytes 147464 | tf_op jit(solution)/shard_map/ppermute | solution.py:255
  108.6 12.6 %collective-permute-start.10 = (bf16[32,768]{1,0:T(8,128)(2,1)S(1)}, bf16[32,768]{1,0:T(8,128)(2,1)S(1)}, u32[]{:S(2)}, u32[]{:S(2)}) collective-permute-start(bf16[32,768]{1,0:T(8,128)(2,1)S(1)} %get-tuple-element.47), channel_id=1, source_target_pairs={{0,48},{4,52},{8,56},{12,60},{16,0},{20,4},{24,8},{28,12},{32,16},... | collective-permute-start | bytes 147464 | tf_op jit(solution)/shard_map/ppermute | solution.py:255
  121.2 3.4 %collective-permute-start.11 = (bf16[32,384]{1,0:T(8,128)(2,1)S(1)}, bf16[32,384]{1,0:T(8,128)(2,1)S(1)}, u32[]{:S(2)}, u32[]{:S(2)}) collective-permute-start(bf16[32,384]{1,0:T(8,128)(2,1)S(1)} %get-tuple-element.52), channel_id=1, source_target_pairs={{0,1},{1,0},{2,3},{3,2},{4,5},{5,4},{6,7},{7,6},{8,9},{9,8},{10,11... | collective-permute-start | bytes 73736 | tf_op jit(solution)/shard_map/ppermute | solution.py:261

commit v2 on v1

v2 whole, which is shorter than its diff:
```python
import math

import jax
import jax.numpy as jnp
from jax import lax
from jax.experimental import pallas as pl
from jax.experimental.pallas import tpu as pltpu
from jax.sharding import Mesh
from jax.sharding import PartitionSpec as P

gelu_scale = math.sqrt(2.0 / math.pi)
cubic_term = 0.044715

MIB = 1024 * 1024
PLANE = ("x", "yh", "yl", "core")
Z = ("zh", "zl")
ROWS_BY_ROWS = (((1,), (1,)), ((), ()))


def gelu_slope(values):
    inner = gelu_scale * (values + cubic_term * values * values * values)
    tangent = jnp.tanh(inner)
    return 0.5 * (1.0 + tangent) + 0.5 * values * (1.0 - tangent * tangent) * gelu_scale * (
        1.0 + 3.0 * cubic_term * values * values
    )


def vmem():
    return pl.BlockSpec(memory_space=pltpu.VMEM)


def smem():
    return pl.BlockSpec(memory_space=pltpu.SMEM)


def chip_number(info_ref, first, second):
    core = info_ref[3]
    return first * (4 - 3 * core) + second * (1 + 3 * core)


def block_rows(k):
    return pl.ds(pl.multiple_of(k * 32, 32), 32)


def partial_kernel(info_ref, l0_ref, l1_ref, l2_ref, l3_ref, w_own_ref, w_sib_ref, own_ref, s1_ref, s2_ref, s3_ref, plane_ref, plane, w, acc, sems):
    second = info_ref[2]
    copies = []
    for d, ref in enumerate((l0_ref, l1_ref, l2_ref, l3_ref)):
        for i in range(4):
            k = chip_number(info_ref, i, lax.rem(second + d, 4))
            copies.append(
                pltpu.make_async_copy(ref.at[i], plane.at[block_rows(k), :], sems.at[d * 4 + i])
            )
    weights = [
        pltpu.make_async_copy(ref, w.at[n], sems.at[16 + n])
        for n, ref in enumerate((w_own_ref, w_sib_ref))
    ]
    for copy in copies + weights:
        copy.start()
    for copy in copies:
        copy.wait()
    result = pltpu.make_async_copy(plane, plane_ref, sems.at[18])
    result.start()
    for n, copy in enumerate(weights):
        copy.wait()
        acc[:, n * 384 : (n + 1) * 384] = lax.dot_general(
            plane[...], w[n], ROWS_BY_ROWS, preferred_element_type=jnp.float32
        )
    result.wait()
    for d, out in enumerate((own_ref, s1_ref, s2_ref, s3_ref)):
        residue = lax.rem(info_ref[0] + d, 4)
        for x in range(4):
            out[x] = acc[block_rows(x * 4 + residue), :].astype(out.dtype)


def partial_sums(info, lines, w_own, w_sib):
    shape = (4, 32, 768)
    return pl.pallas_call(
        partial_kernel,
        out_shape=[jax.ShapeDtypeStruct(shape, jnp.float32)]
        + [jax.ShapeDtypeStruct(shape, jnp.bfloat16)] * 3
        + [jax.ShapeDtypeStruct((512, 3072), jnp.bfloat16)],
        in_specs=[smem()] + [pl.BlockSpec(memory_space=pl.ANY)] * 6,
        out_specs=[vmem()] * 4 + [pl.BlockSpec(memory_space=pl.ANY)],
        scratch_shapes=[
            pltpu.VMEM((512, 3072), jnp.bfloat16),
            pltpu.VMEM((2, 384, 3072), jnp.bfloat16),
            pltpu.VMEM((512, 768), jnp.float32),
            pltpu.SemaphoreType.DMA((19,)),
        ],
        compiler_params=pltpu.CompilerParams(vmem_limit_bytes=52 * MIB),
        cost_estimate=pl.CostEstimate(
            flops=2 * 512 * 3072 * 768, bytes_accessed=8 * MIB, transcendentals=0
        ),
        name="partial_sums",
    )(info, *lines, w_own, w_sib)


def stage_kernel(info_ref, own_ref, r1_ref, r2_ref, r3_ref, o_ref, s1_ref, s2_ref, s3_ref):
    zh = info_ref[0] // 4
    for d, out in enumerate((o_ref, s1_ref, s2_ref, s3_ref)):
        i = lax.rem(zh + d, 4)
        total = own_ref[i]
        for r in (r1_ref, r2_ref, r3_ref):
            total = total + r[i].astype(jnp.float32)
        out[...] = total.astype(out.dtype)


def stage_sums(info, own, received):
    shape = (32, 768)
    return pl.pallas_call(
        stage_kernel,
        out_shape=[jax.ShapeDtypeStruct(shape, jnp.float32)]
        + [jax.ShapeDtypeStruct(shape, jnp.bfloat16)] * 3,
        in_specs=[smem()] + [vmem()] * 4,
        out_specs=[vmem()] * 4,
        compiler_params=pltpu.CompilerParams(vmem_limit_bytes=16 * MIB),
        cost_estimate=pl.CostEstimate(flops=400000, bytes_accessed=2 * MIB, transcendentals=0),
        name="stage_sums",
    )(info, own, *received)


def final_kernel(own_ref, r1_ref, r2_ref, r3_ref, o_ref, s_ref):
    total = own_ref[...]
    for r in (r1_ref, r2_ref, r3_ref):
        total = total + r[...].astype(jnp.float32)
    o_ref[...] = total[:, :384].astype(jnp.bfloat16)
    s_ref[...] = total[:, 384:].astype(jnp.bfloat16)


def final_sums(own, received):
    shape = jax.ShapeDtypeStruct((32, 384), jnp.bfloat16)
    return pl.pallas_call(
        final_kernel,
        out_shape=[shape, shape],
        in_specs=[vmem()] * 4,
        out_specs=[vmem()] * 2,
        compiler_params=pltpu.CompilerParams(vmem_limit_bytes=4 * MIB),
        cost_estimate=pl.CostEstimate(flops=100000, bytes_accessed=MIB // 4, transcendentals=0),
        name="final_sums",
    )(own, *received)


def weight_kernel(info_ref, n0_ref, n1_ref, n2_ref, n3_ref, own_ref, sib_ref, out_ref, tokens, left):

    @pl.when(pl.program_id(0) == 0)
    def _():
        z, core = info_ref[0], info_ref[3]
        for ref, far in ((n0_ref, 0), (n1_ref, -1), (n2_ref, 4 * core - 2), (n3_ref, 1)):
            for e in range(4):
                k = lax.rem(z + far + 4 * e + 16, 16)
                for which in range(2):
                    half = core if which == 0 else 1 - core
                    rows = pl.ds(pl.multiple_of(which * 512 + k * 32, 32), 32)
                    tokens[rows, :] = ref[e, pl.ds(pl.multiple_of(half * 32, 32), 32), :]
        left[...] = tokens[...].T

    total = jnp.dot(left[:, :512], own_ref[...], preferred_element_type=jnp.float32)
    total += jnp.dot(left[:, 512:], sib_ref[...], preferred_element_type=jnp.float32)
    out_ref[...] = total.astype(jnp.bfloat16)


def weight_sums(info, near, hg_own, hg_sib):
    tile = 512
    return pl.pallas_call(
        weight_kernel,
        out_shape=jax.ShapeDtypeStruct((384, 3072), jnp.bfloat16),
        grid_spec=pltpu.PrefetchScalarGridSpec(
            num_scalar_prefetch=1,
            grid=(3072 // tile,),
            in_specs=[pl.BlockSpec((4, 64, 384), lambda j, info: (0, 0, 0))] * 4
            + [pl.BlockSpec((512, tile), lambda j, info: (0, j))] * 2,
            out_specs=pl.BlockSpec((384, tile), lambda j, info: (0, j)),
            scratch_shapes=[
                pltpu.VMEM((1024, 384), jnp.bfloat16),
                pltpu.VMEM((384, 1024), jnp.bfloat16),
            ],
        ),
        compiler_params=pltpu.CompilerParams(vmem_limit_bytes=24 * MIB),
        cost_estimate=pl.CostEstimate(
            flops=2 * 1024 * 3072 * 384, bytes_accessed=10 * MIB, transcendentals=0
        ),
        name="weight_sums",
    )(info, *near, hg_own, hg_sib)


def plane_shift(first, by):
    pairs = []
    for x in range(4):
        for y in range(4):
            for core in range(2):
                along_x = (core == 0) == first
                to = ((x + by) % 4, y) if along_x else (x, (y + by) % 4)
                pairs.append(((x * 4 + y) * 2 + core, (to[0] * 4 + to[1]) * 2 + core))
    return pairs


def far_shift(by):
    return [(z, (z + 4 * by) % 16) for z in range(16)]


def column_shift(by):
    return [(z * 2 + c, (z + by[c]) % 16 * 2 + c) for z in range(16) for c in range(2)]


def first_axis_groups():
    place = [[[(x * 4 + y) * 2 + c for c in range(2)] for y in range(4)] for x in range(4)]
    along_x = [[place[i][j][0] for i in range(4)] for j in range(4)]
    along_y = [[place[j][i][1] for i in range(4)] for j in range(4)]
    return along_x + along_y


NEAR = ((1, 1), (2, -2), (-1, -1))


def per_device(inputs, weight, upstream, preactivation):
    core = lax.axis_index("core")
    x, y, z = lax.axis_index("x"), lax.axis_index(("yh", "yl")), lax.axis_index(Z)
    first, second = jnp.where(core == 0, x, y), jnp.where(core == 0, y, x)
    info = jnp.stack([z, first, second, core]).astype(jnp.int32)
    swap = [(0, 1), (1, 0)]

    slope = gelu_slope(preactivation.astype(jnp.float32))
    local = (upstream.astype(jnp.float32) * slope).astype(jnp.bfloat16)
    line = lax.all_gather(
        local, PLANE, axis=0, tiled=True, axis_index_groups=first_axis_groups()
    ).reshape(4, 32, 3072)
    weight_then, line = lax.optimization_barrier((weight, line))
    w_sib = lax.ppermute(weight_then, "core", swap)
    inputs, w_sib = lax.optimization_barrier((inputs, w_sib))
    lines = [line] + [lax.ppermute(line, PLANE, plane_shift(False, -d)) for d in (1, 2, 3)]
    near = [inputs] + [lax.ppermute(inputs, Z, far_shift(-d)) for d in (1, 2)]
    inputs, near[1] = lax.optimization_barrier((inputs, near[1]))
    last = lax.ppermute(inputs, Z, far_shift(-3))
    lines, near = lax.optimization_barrier((lines, near))
    near = near + [last]

    own, *sends, hg_own = partial_sums(info, lines, weight, w_sib)
    own, near = lax.optimization_barrier((own, near))
    near, hg_own = lax.optimization_barrier((jnp.stack(near), hg_own))
    nears = [near] + [lax.ppermute(near, Z + ("core",), column_shift(by)) for by in NEAR]
    received = [
        lax.ppermute(s, Z + ("core",), column_shift(by)) for s, by in zip(sends, NEAR)
    ]
    hg_sib = lax.ppermute(hg_own, "core", swap)
    own, *sends = stage_sums(info, own, received)
    received = [
        lax.ppermute(s, Z, far_shift(d + 1))
        for d, s in enumerate(sends)
    ]
    weight_total = weight_sums(info, nears, hg_own, hg_sib)
    weight_total, *received = lax.optimization_barrier((weight_total, *received))
    mine, other = final_sums(own, received)
    other = lax.ppermute(other, "core", swap)
    input_gradient = jnp.concatenate(
        [jnp.where(core == 0, mine, other), jnp.where(core == 0, other, mine)], axis=0
    )
    return (input_gradient, weight_total)


def solution(mesh):
    fine = Mesh(
        mesh.devices.reshape(4, 2, 4, 4, 2, 2), ("x", "yh", "zh", "zl", "yl", "core")
    )
    in_specs = (P(Z, PLANE), P(PLANE, Z), P(PLANE, Z), P(PLANE, Z))
    out_specs = (P(Z, PLANE), P(PLANE, Z))
    return jax.shard_map(
        per_device, mesh=fine, in_specs=in_specs, out_specs=out_specs, check_vma=False
    )
```

time: 126 us -> 122 us (0.968)
  blocking collectives: 43 us -> 12.4 us
  starting transfers between devices: 54.2 us -> 79.3 us
  local copies, waits for them, and re-layouts: 0.01 us -> 1.89 us
    all_gather x1 -> x0, blocking collectives: 30.7 us -> none  [per_device(): gathered = lax.all_gather(inputs, Z, axis=0, tiled=True)]
    ppermute x6 -> x12, starting transfers between devices: 24.8 us -> 51.6 us  [the longest x3 13.9 us: per_device(): lax.ppermute(s, Z, far_shift(d + 1))]
    ppermute x6 -> x12, waiting for transfers between devices: 2.56 us -> 9.3 us  [the longest x2 6.96 us: per_device(): near = [inputs] + [lax.ppermute(inputs, Z, far_shift(-d)) for d in (1, 2)]]
    ppermute x3, waiting for transfers between devices: 6.31 us -> 0.01 us  [per_device(): lax.ppermute(s, Z + ('core',), column_shift(by))]
    ppermute x1, starting transfers between devices: 8.66 us -> 5.56 us  [per_device(): hg_sib = lax.ppermute(hg_own, 'core', swap)]
    unnamed x2 -> x6, local copies, waits for them, and re-layouts: 0.01 us -> 1.89 us
    pallas_call x2 -> x1, Pallas kernels: 8.97 us -> 8.03 us  [partial_sums(): pl.pallas_call(partial_kernel, out_shape=[jax.ShapeDtypeStruct(shape, jnp...]
  transfers between devices with their start and end apart: 12 -> 18, of which waited for: 4 -> 3; matrix products, arithmetic and copies ran while one was open for 0% -> 0% of each run, Pallas kernels for 5% -> 12%
where the time goes in v2:
time: 122 us; the launch traced here: 121 us
  starting transfers between devices  79.3 us (65%)
  Pallas kernels  14.5 us (12%)
  blocking collectives  12.4 us (10%)
  waiting for transfers between devices  10.1 us (8%)
  other arithmetic  2.05 us (2%)
  local copies, waits for them, and re-layouts  1.89 us (2%)
    ppermute x3, starting transfers between devices, per_device(): lax.ppermute(s, Z, far_shift(d + 1))  13.9 us
    ppermute x2, starting transfers between devices, per_device(): near = [inputs] + [lax.ppermute(inputs, Z, far_shift(-d)) for d in (1, 2)]  12.4 us
    all_gather x1, blocking collectives, per_device(): lax.all_gather(local, PLANE, axis=0, tiled=True, axis_index_groups=first_...  12.4 us
    ppermute x3, starting transfers between devices, per_device(): lax.ppermute(near, Z + ('core',), column_shift(by))  11.3 us
    ppermute x1, starting transfers between devices, per_device(): w_sib = lax.ppermute(weight_then, 'core', swap)  9.73 us
    ppermute x3, starting transfers between devices, per_device(): lax.ppermute(s, Z + ('core',), column_shift(by))  9.31 us
    ppermute x3, starting transfers between devices, per_device(): lax.ppermute(line, PLANE, plane_shift(False, -d))  8.98 us
    pallas_call x1, Pallas kernels, partial_sums(): pl.pallas_call(partial_kernel, out_shape=[jax.ShapeDtypeStruct(shape, jnp...  8.03 us
  transfers between devices with their start and end apart: 18, of which 3 were waited for; matrix products, arithmetic and copies ran while one was open for 0% of the time, Pallas kernels for 12%

profile of v2, /device:TPU:1, one launch (start us, length us, event | category | flops | bytes accessed | tf_op | source)
XLA Modules:
  0.0 121.2 jit_solution(6727099436110239318)
XLA Ops:
  0.6 1.3 %fusion.7 = bf16[32,3072]{1,0:T(8,128)(2,1)S(1)} fusion(bf16[32,3072]{1,0:T(8,128)(2,1)} %param.7, bf16[32,3072]{1,0:T(8,128)(2,1)} %param.6), kind=kLoop, calls=%fused_computation.14 | loop fusion | flops 2064384 | bytes 589824 | tf_op jit(solution)/shard_map/convert_element_type | solution.py:224
  1.9 12.4 %all_gather.3 = bf16[128,3072]{1,0:T(8,128)(2,1)S(1)} all-gather(bf16[32,3072]{1,0:T(8,128)(2,1)S(1)} %fusion.7), channel_id=1, replica_groups={{0,128,256,384},{2,130,258,386},{64,192,320,448},{66,194,322,450},{1,3,..., dimensions={0}, use_global_device_ids=true | all-gather | bytes 983040 | tf_op jit(solution)/shard_map/all_gather | solution.py:225
  14.3 9.7 %collective-permute-start.3 = (bf16[384,3072]{1,0:T(8,128)(2,1)}, bf16[384,3072]{1,0:T(8,128)(2,1)S(1)}, u32[]{:S(2)}, u32[]{:S(2)}) collective-permute-start(bf16[384,3072]{1,0:T(8,128)(2,1)} %w_own_ref.1), channel_id=1, source_target_pairs={{0,1},{1,0},{2,3},{3,2},{4,5},{5,4},{6,7},{7,6},{8,9},{9,8},{10,11... | collective-permute-start | bytes 7077896 | tf_op jit(solution)/shard_map/ppermute | solution.py:229
  24.0 1.9 %collective-permute-start.2 = (bf16[4,32,3072]{2,1,0:T(8,128)(2,1)S(1)}, bf16[4,32,3072]{2,1,0:T(8,128)(2,1)}, u32[]{:S(2)}, u32[]{:S(2)}) collective-permute-start(bf16[4,32,3072]{2,1,0:T(8,128)(2,1)S(1)} %bitcast.9), channel_id=1, source_target_pairs={{0,2},{1,129},{2,64},{3,131},{64,66},{65,193},{66,0},{67,195},{128... | collective-permute-start | bytes 2359304 | tf_op jit(solution)/shard_map/ppermute | solution.py:231
  26.0 3.1 %collective-permute-start.1 = (bf16[4,32,3072]{2,1,0:T(8,128)(2,1)S(1)}, bf16[4,32,3072]{2,1,0:T(8,128)(2,1)}, u32[]{:S(2)}, u32[]{:S(2)}) collective-permute-start(bf16[4,32,3072]{2,1,0:T(8,128)(2,1)S(1)} %bitcast.10), channel_id=1, source_target_pairs={{0,64},{1,257},{2,66},{3,259},{64,0},{65,321},{66,2},{67,323},{128... | collective-permute-start | bytes 2359304 | tf_op jit(solution)/shard_map/ppermute | solution.py:231
  29.1 4.0 %collective-permute-start = (bf16[4,32,3072]{2,1,0:T(8,128)(2,1)S(1)}, bf16[4,32,3072]{2,1,0:T(8,128)(2,1)}, u32[]{:S(2)}, u32[]{:S(2)}) collective-permute-start(bf16[4,32,3072]{2,1,0:T(8,128)(2,1)S(1)} %bitcast.11), channel_id=1, source_target_pairs={{0,66},{1,385},{2,0},{3,387},{64,2},{65,449},{66,64},{67,451},{128... | collective-permute-start | bytes 2359304 | tf_op jit(solution)/shard_map/ppermute | solution.py:231
  33.1 0.0 collective-permute-done.3.w_sib_ref
  33.1 0.0 copy-start.2
  33.1 10.5 %collective-permute-start.5 = (bf16[64,384]{1,0:T(8,128)(2,1)}, bf16[64,384]{1,0:T(8,128)(2,1)S(1)}, u32[]{:S(2)}, u32[]{:S(2)}) collective-permute-start(bf16[64,384]{1,0:T(8,128)(2,1)} %param.4), channel_id=1, source_target_pairs={{0,32},{4,36},{8,40},{12,44},{16,48},{20,52},{24,56},{28,60},{32,0... | collective-permute-start | bytes 147464 | tf_op jit(solution)/shard_map/ppermute | solution.py:232
  43.6 1.9 %collective-permute-start.4 = (bf16[64,384]{1,0:T(8,128)(2,1)}, bf16[64,384]{1,0:T(8,128)(2,1)S(1)}, u32[]{:S(2)}, u32[]{:S(2)}) collective-permute-start(bf16[64,384]{1,0:T(8,128)(2,1)} %param.4), channel_id=1, source_target_pairs={{0,48},{4,52},{8,56},{12,60},{16,0},{20,4},{24,8},{28,12},{32,16},... | collective-permute-start | bytes 147464 | tf_op jit(solution)/shard_map/ppermute | solution.py:232
  45.5 0.1 pad_add_fusion.info_ref
  45.6 7.0 %collective-permute-done.4 = bf16[64,384]{1,0:T(8,128)(2,1)S(1)} collective-permute-done((bf16[64,384]{1,0:T(8,128)(2,1)}, bf16[64,384]{1,0:T(8,128)(2,1)S(1)}, u32[]{:S(2)}, u32[]{:S(2)}) %collective-permute-start.4) | collective-permute-done | bytes 49184 | tf_op jit(solution)/shard_map/ppermute | solution.py:232
  52.5 0.0 collective-permute-done.2.l3_ref
  52.5 0.0 collective-permute-done.1.l2_ref
  52.5 0.0 collective-permute-done.l1_ref
  52.6 0.0 collective-permute-done.5
  52.6 4.9 %collective-permute-start.6 = (bf16[64,384]{1,0:T(8,128)(2,1)}, bf16[64,384]{1,0:T(8,128)(2,1)S(1)}, u32[]{:S(2)}, u32[]{:S(2)}) collective-permute-start(bf16[64,384]{1,0:T(8,128)(2,1)} %param.4), channel_id=1, source_target_pairs={{0,16},{4,20},{8,24},{12,28},{16,32},{20,36},{24,40},{28,44},{32,4... | collective-permute-start | bytes 147464 | tf_op jit(solution)/shard_map/ppermute | solution.py:234
  57.5 0.0 copy-done.2
  57.5 8.0 %partial_sums.1 = (f32[4,32,768]{2,1,0:T(8,128)S(1)}, bf16[4,32,768]{2,1,0:T(8,128)(2,1)S(1)}, bf16[4,32,768]{2,1,0:T(8,128)(2,1)S(1)}, bf16[4,32,768]{2,1,0:T(8,128)(2,1)S(1)}, bf16[512,3072]{1,0:T(8,128)(2,1)}) custom-call(s32[4]{0:T(128)S(1)} %pad_add_fusion.info_ref, bf16[4,32,3072]{2,1,0:T(8,128)(2,1)S(1)} %bitcast.12, ...), custom_call_target="tpu_custom_call" | custom-call | flops 2415919104 | bytes 8388608 | tf_op jit(solution)/shard_map/partial_sums/pallas_call | solution.py:78
  65.5 0.0 collective-permute-done.6
  65.6 0.0 copy-done.1
  65.6 5.6 %collective-permute-start.13 = (bf16[512,3072]{1,0:T(8,128)(2,1)}, bf16[512,3072]{1,0:T(8,128)(2,1)S(1)}, u32[]{:S(2)}, u32[]{:S(2)}) collective-permute-start(bf16[512,3072]{1,0:T(8,128)(2,1)} %get-tuple-element.62.own_ref), channel_id=1, source_target_pairs={{0,1},{1,0},{2,3},{3,2},{4,5},{5,4},{6,7},{7,6},{8,9},{9,8},{10,11... | collective-permute-start | bytes 9437192 | tf_op jit(solution)/shard_map/ppermute | solution.py:245
  71.2 4.1 %collective-permute-start.7 = (bf16[4,32,768]{2,1,0:T(8,128)(2,1)S(1)}, bf16[4,32,768]{2,1,0:T(8,128)(2,1)S(1)}, u32[]{:S(2)}, u32[]{:S(2)}) collective-permute-start(bf16[4,32,768]{2,1,0:T(8,128)(2,1)S(1)} %get-tuple-element.52), channel_id=1, source_target_pairs={{0,4},{1,5},{4,8},{5,9},{8,12},{9,13},{12,16},{13,17},{16,20},{17,... | collective-permute-start | bytes 589832 | tf_op jit(solution)/shard_map/ppermute | solution.py:243
  75.3 2.6 %collective-permute-start.8 = (bf16[4,32,768]{2,1,0:T(8,128)(2,1)S(1)}, bf16[4,32,768]{2,1,0:T(8,128)(2,1)S(1)}, u32[]{:S(2)}, u32[]{:S(2)}) collective-permute-start(bf16[4,32,768]{2,1,0:T(8,128)(2,1)S(1)} %get-tuple-element.53), channel_id=1, source_target_pairs={{0,8},{1,57},{4,12},{5,61},{8,16},{9,1},{12,20},{13,5},{16,24},{17... | collective-permute-start | bytes 589832 | tf_op jit(solution)/shard_map/ppermute | solution.py:243
  77.9 2.6 %collective-permute-start.9 = (bf16[4,32,768]{2,1,0:T(8,128)(2,1)S(1)}, bf16[4,32,768]{2,1,0:T(8,128)(2,1)S(1)}, u32[]{:S(2)}, u32[]{:S(2)}) collective-permute-start(bf16[4,32,768]{2,1,0:T(8,128)(2,1)S(1)} %get-tuple-element.54), channel_id=1, source_target_pairs={{0,60},{1,61},{4,0},{5,1},{8,4},{9,5},{12,8},{13,9},{16,12},{17,13... | collective-permute-start | bytes 589832 | tf_op jit(solution)/shard_map/ppermute | solution.py:243
  80.5 3.6 %collective-permute-start.12 = (bf16[4,64,384]{2,1,0:T(8,128)(2,1)S(1)}, bf16[4,64,384]{2,1,0:T(8,128)(2,1)S(1)}, u32[]{:S(2)}, u32[]{:S(2)}) collective-permute-start(bf16[4,64,384]{2,1,0:T(8,128)(2,1)S(1)} %pad_maximum_fusion.n0_ref), channel_id=1, source_target_pairs={{0,60},{1,61},{4,0},{5,1},{8,4},{9,5},{12,8},{13,9},{16,12},{17,13... | collective-permute-start | bytes 589832 | tf_op jit(solution)/shard_map/ppermute | solution.py:241
  84.2 0.0 collective-permute-done.7.r1_ref
  84.2 4.3 %collective-permute-start.11 = (bf16[4,64,384]{2,1,0:T(8,128)(2,1)S(1)}, bf16[4,64,384]{2,1,0:T(8,128)(2,1)S(1)}, u32[]{:S(2)}, u32[]{:S(2)}) collective-permute-start(bf16[4,64,384]{2,1,0:T(8,128)(2,1)S(1)} %pad_maximum_fusion.n0_ref), channel_id=1, source_target_pairs={{0,8},{1,57},{4,12},{5,61},{8,16},{9,1},{12,20},{13,5},{16,24},{17... | collective-permute-start | bytes 589832 | tf_op jit(solution)/shard_map/ppermute | solution.py:241
  88.5 0.0 collective-permute-done.8.r2_ref
  88.5 3.4 %collective-permute-start.10 = (bf16[4,64,384]{2,1,0:T(8,128)(2,1)S(1)}, bf16[4,64,384]{2,1,0:T(8,128)(2,1)S(1)}, u32[]{:S(2)}, u32[]{:S(2)}) collective-permute-start(bf16[4,64,384]{2,1,0:T(8,128)(2,1)S(1)} %pad_maximum_fusion.n0_ref), channel_id=1, source_target_pairs={{0,4},{1,5},{4,8},{5,9},{8,12},{9,13},{12,16},{13,17},{16,20},{17,... | collective-permute-start | bytes 589832 | tf_op jit(solution)/shard_map/ppermute | solution.py:241
  91.9 0.0 collective-permute-done.9.r3_ref
  91.9 0.6 stage_sums.1
  92.5 2.5 %collective-permute-start.14 = (bf16[32,768]{1,0:T(8,128)(2,1)S(1)}, bf16[32,768]{1,0:T(8,128)(2,1)S(1)}, u32[]{:S(2)}, u32[]{:S(2)}) collective-permute-start(bf16[32,768]{1,0:T(8,128)(2,1)S(1)} %get-tuple-element.63), channel_id=1, source_target_pairs={{0,16},{4,20},{8,24},{12,28},{16,32},{20,36},{24,40},{28,44},{32,4... | collective-permute-start | bytes 147464 | tf_op jit(solution)/shard_map/ppermute | solution.py:248
  95.1 0.0 collective-permute-done.12.n3_ref
  95.1 9.5 %collective-permute-start.15 = (bf16[32,768]{1,0:T(8,128)(2,1)S(1)}, bf16[32,768]{1,0:T(8,128)(2,1)S(1)}, u32[]{:S(2)}, u32[]{:S(2)}) collective-permute-start(bf16[32,768]{1,0:T(8,128)(2,1)S(1)} %get-tuple-element.64), channel_id=1, source_target_pairs={{0,32},{4,36},{8,40},{12,44},{16,48},{20,52},{24,56},{28,60},{32,0... | collective-permute-start | bytes 147464 | tf_op jit(solution)/shard_map/ppermute | solution.py:248
  104.6 0.0 collective-permute-done.11.n2_ref
  104.6 1.9 %collective-permute-start.16 = (bf16[32,768]{1,0:T(8,128)(2,1)S(1)}, bf16[32,768]{1,0:T(8,128)(2,1)S(1)}, u32[]{:S(2)}, u32[]{:S(2)}) collective-permute-start(bf16[32,768]{1,0:T(8,128)(2,1)S(1)} %get-tuple-element.65), channel_id=1, source_target_pairs={{0,48},{4,52},{8,56},{12,60},{16,0},{20,4},{24,8},{28,12},{32,16},... | collective-permute-start | bytes 147464 | tf_op jit(solution)/shard_map/ppermute | solution.py:248
  106.5 0.0 collective-permute-done.10.n1_ref
  106.5 0.0 collective-permute-done.13.sib_ref
  106.5 0.0 copy-start
  106.5 1.9 %copy-done = bf16[512,3072]{1,0:T(8,128)(2,1)S(1)} copy-done((bf16[512,3072]{1,0:T(8,128)(2,1)S(1)}, bf16[512,3072]{1,0:T(8,128)(2,1)}, u32[]{:S(2)}) %copy-start) | copy-done | bytes 3145752
  108.4 5.8 %weight_sums.1 = bf16[384,3072]{1,0:T(8,128)(2,1)} custom-call(s32[4]{0:T(128)S(1)} %pad_add_fusion.info_ref, bf16[4,64,384]{2,1,0:T(8,128)(2,1)S(1)} %pad_maximum_fusion.n0_ref, bf16[4,64,384]{2,1,0:T(8,128)(2,1)S(1)} %collective-permute-done.10.n1_ref, bf16[4,64,384]{2,1,0:T(8,128)(2,1)S(1)} %collective-permute-done.11.n2_ref, ...), custom_call_target="tpu_custom_call" | custom-call | flops 2415919104 | bytes 10485760 | tf_op jit(solution)/shard_map/weight_sums/pallas_call | solution.py:165
  114.2 0.0 collective-permute-done.14.r1_ref
  114.2 0.0 collective-permute-done.15.r2_ref
  114.2 2.3 %collective-permute-done.16.r3_ref = bf16[32,768]{1,0:T(8,128)(2,1)S(1)} collective-permute-done((bf16[32,768]{1,0:T(8,128)(2,1)S(1)}, bf16[32,768]{1,0:T(8,128)(2,1)S(1)}, u32[]{:S(2)}, u32[]{:S(2)}) %collective-permute-start.16) | collective-permute-done | bytes 49184 | tf_op jit(solution)/shard_map/ppermute | solution.py:248
  116.6 3.2 %collective-permute-start.17 = (bf16[32,384]{1,0:T(8,128)(2,1)S(1)}, bf16[32,384]{1,0:T(8,128)(2,1)S(1)}, u32[]{:S(2)}, u32[]{:S(2)}) collective-permute-start(bf16[32,384]{1,0:T(8,128)(2,1)S(1)} %get-tuple-element.70), channel_id=1, source_target_pairs={{0,1},{1,0},{2,3},{3,2},{4,5},{5,4},{6,7},{7,6},{8,9},{9,8},{10,11... | collective-permute-start | bytes 73736 | tf_op jit(solution)/shard_map/ppermute | solution.py:254
  119.7 0.8 collective-permute-done.17
  120.6 0.6 pad_maximum_fusion.1
  (4 shorter events, 0.1 us)
Async XLA Ops:
  14.3 18.8 %collective-permute-start.3 = (bf16[384,3072]{1,0:T(8,128)(2,1)}, bf16[384,3072]{1,0:T(8,128)(2,1)S(1)}, u32[]{:S(2)}, u32[]{:S(2)}) collective-permute-start(bf16[384,3072]{1,0:T(8,128)(2,1)} %w_own_ref.1), channel_id=1, source_target_pairs={{0,1},{1,0},{2,3},{3,2},{4,5},{5,4},{6,7},{7,6},{8,9},{9,8},{10,11... | collective-permute-start | bytes 7077896 | tf_op jit(solution)/shard_map/ppermute | solution.py:229
  24.0 28.5 %collective-permute-start.2 = (bf16[4,32,3072]{2,1,0:T(8,128)(2,1)S(1)}, bf16[4,32,3072]{2,1,0:T(8,128)(2,1)}, u32[]{:S(2)}, u32[]{:S(2)}) collective-permute-start(bf16[4,32,3072]{2,1,0:T(8,128)(2,1)S(1)} %bitcast.9), channel_id=1, source_target_pairs={{0,2},{1,129},{2,64},{3,131},{64,66},{65,193},{66,0},{67,195},{128... | collective-permute-start | bytes 2359304 | tf_op jit(solution)/shard_map/ppermute | solution.py:231
  26.0 26.6 %collective-permute-start.1 = (bf16[4,32,3072]{2,1,0:T(8,128)(2,1)S(1)}, bf16[4,32,3072]{2,1,0:T(8,128)(2,1)}, u32[]{:S(2)}, u32[]{:S(2)}) collective-permute-start(bf16[4,32,3072]{2,1,0:T(8,128)(2,1)S(1)} %bitcast.10), channel_id=1, source_target_pairs={{0,64},{1,257},{2,66},{3,259},{64,0},{65,321},{66,2},{67,323},{128... | collective-permute-start | bytes 2359304 | tf_op jit(solution)/shard_map/ppermute | solution.py:231
  29.1 23.5 %collective-permute-start = (bf16[4,32,3072]{2,1,0:T(8,128)(2,1)S(1)}, bf16[4,32,3072]{2,1,0:T(8,128)(2,1)}, u32[]{:S(2)}, u32[]{:S(2)}) collective-permute-start(bf16[4,32,3072]{2,1,0:T(8,128)(2,1)S(1)} %bitcast.11), channel_id=1, source_target_pairs={{0,66},{1,385},{2,0},{3,387},{64,2},{65,449},{66,64},{67,451},{128... | collective-permute-start | bytes 2359304 | tf_op jit(solution)/shard_map/ppermute | solution.py:231
  33.1 24.4 %copy-start.2 = (bf16[384,3072]{1,0:T(8,128)(2,1)}, bf16[384,3072]{1,0:T(8,128)(2,1)S(1)}, u32[]{:S(2)}) copy-start(bf16[384,3072]{1,0:T(8,128)(2,1)S(1)} %collective-permute-done.3.w_sib_ref) | copy-start | bytes 7077892
  33.1 19.5 %collective-permute-start.5 = (bf16[64,384]{1,0:T(8,128)(2,1)}, bf16[64,384]{1,0:T(8,128)(2,1)S(1)}, u32[]{:S(2)}, u32[]{:S(2)}) collective-permute-start(bf16[64,384]{1,0:T(8,128)(2,1)} %param.4), channel_id=1, source_target_pairs={{0,32},{4,36},{8,40},{12,44},{16,48},{20,52},{24,56},{28,60},{32,0... | collective-permute-start | bytes 147464 | tf_op jit(solution)/shard_map/ppermute | solution.py:232
  43.6 9.0 %collective-permute-start.4 = (bf16[64,384]{1,0:T(8,128)(2,1)}, bf16[64,384]{1,0:T(8,128)(2,1)S(1)}, u32[]{:S(2)}, u32[]{:S(2)}) collective-permute-start(bf16[64,384]{1,0:T(8,128)(2,1)} %param.4), channel_id=1, source_target_pairs={{0,48},{4,52},{8,56},{12,60},{16,0},{20,4},{24,8},{28,12},{32,16},... | collective-permute-start | bytes 147464 | tf_op jit(solution)/shard_map/ppermute | solution.py:232
  45.6 20.0 %copy-start.1 = (bf16[64,384]{1,0:T(8,128)(2,1)S(1)}, bf16[64,384]{1,0:T(8,128)(2,1)}, u32[]{:S(2)}) copy-start(bf16[64,384]{1,0:T(8,128)(2,1)} %param.4) | copy-start | bytes 147460
  52.6 13.0 %collective-permute-start.6 = (bf16[64,384]{1,0:T(8,128)(2,1)}, bf16[64,384]{1,0:T(8,128)(2,1)S(1)}, u32[]{:S(2)}, u32[]{:S(2)}) collective-permute-start(bf16[64,384]{1,0:T(8,128)(2,1)} %param.4), channel_id=1, source_target_pairs={{0,16},{4,20},{8,24},{12,28},{16,32},{20,36},{24,40},{28,44},{32,4... | collective-permute-start | bytes 147464 | tf_op jit(solution)/shard_map/ppermute | solution.py:234
  65.6 40.9 %collective-permute-start.13 = (bf16[512,3072]{1,0:T(8,128)(2,1)}, bf16[512,3072]{1,0:T(8,128)(2,1)S(1)}, u32[]{:S(2)}, u32[]{:S(2)}) collective-permute-start(bf16[512,3072]{1,0:T(8,128)(2,1)} %get-tuple-element.62.own_ref), channel_id=1, source_target_pairs={{0,1},{1,0},{2,3},{3,2},{4,5},{5,4},{6,7},{7,6},{8,9},{9,8},{10,11... | collective-permute-start | bytes 9437192 | tf_op jit(solution)/shard_map/ppermute | solution.py:245
  71.2 13.0 %collective-permute-start.7 = (bf16[4,32,768]{2,1,0:T(8,128)(2,1)S(1)}, bf16[4,32,768]{2,1,0:T(8,128)(2,1)S(1)}, u32[]{:S(2)}, u32[]{:S(2)}) collective-permute-start(bf16[4,32,768]{2,1,0:T(8,128)(2,1)S(1)} %get-tuple-element.52), channel_id=1, source_target_pairs={{0,4},{1,5},{4,8},{5,9},{8,12},{9,13},{12,16},{13,17},{16,20},{17,... | collective-permute-start | bytes 589832 | tf_op jit(solution)/shard_map/ppermute | solution.py:243
  75.3 13.2 %collective-permute-start.8 = (bf16[4,32,768]{2,1,0:T(8,128)(2,1)S(1)}, bf16[4,32,768]{2,1,0:T(8,128)(2,1)S(1)}, u32[]{:S(2)}, u32[]{:S(2)}) collective-permute-start(bf16[4,32,768]{2,1,0:T(8,128)(2,1)S(1)} %get-tuple-element.53), channel_id=1, source_target_pairs={{0,8},{1,57},{4,12},{5,61},{8,16},{9,1},{12,20},{13,5},{16,24},{17... | collective-permute-start | bytes 589832 | tf_op jit(solution)/shard_map/ppermute | solution.py:243
  77.9 13.9 %collective-permute-start.9 = (bf16[4,32,768]{2,1,0:T(8,128)(2,1)S(1)}, bf16[4,32,768]{2,1,0:T(8,128)(2,1)S(1)}, u32[]{:S(2)}, u32[]{:S(2)}) collective-permute-start(bf16[4,32,768]{2,1,0:T(8,128)(2,1)S(1)} %get-tuple-element.54), channel_id=1, source_target_pairs={{0,60},{1,61},{4,0},{5,1},{8,4},{9,5},{12,8},{13,9},{16,12},{17,13... | collective-permute-start | bytes 589832 | tf_op jit(solution)/shard_map/ppermute | solution.py:243
  80.5 14.6 %collective-permute-start.12 = (bf16[4,64,384]{2,1,0:T(8,128)(2,1)S(1)}, bf16[4,64,384]{2,1,0:T(8,128)(2,1)S(1)}, u32[]{:S(2)}, u32[]{:S(2)}) collective-permute-start(bf16[4,64,384]{2,1,0:T(8,128)(2,1)S(1)} %pad_maximum_fusion.n0_ref), channel_id=1, source_target_pairs={{0,60},{1,61},{4,0},{5,1},{8,4},{9,5},{12,8},{13,9},{16,12},{17,13... | collective-permute-start | bytes 589832 | tf_op jit(solution)/shard_map/ppermute | solution.py:241
  84.2 20.4 %collective-permute-start.11 = (bf16[4,64,384]{2,1,0:T(8,128)(2,1)S(1)}, bf16[4,64,384]{2,1,0:T(8,128)(2,1)S(1)}, u32[]{:S(2)}, u32[]{:S(2)}) collective-permute-start(bf16[4,64,384]{2,1,0:T(8,128)(2,1)S(1)} %pad_maximum_fusion.n0_ref), channel_id=1, source_target_pairs={{0,8},{1,57},{4,12},{5,61},{8,16},{9,1},{12,20},{13,5},{16,24},{17... | collective-permute-start | bytes 589832 | tf_op jit(solution)/shard_map/ppermute | solution.py:241
  88.5 18.0 %collective-permute-start.10 = (bf16[4,64,384]{2,1,0:T(8,128)(2,1)S(1)}, bf16[4,64,384]{2,1,0:T(8,128)(2,1)S(1)}, u32[]{:S(2)}, u32[]{:S(2)}) collective-permute-start(bf16[4,64,384]{2,1,0:T(8,128)(2,1)S(1)} %pad_maximum_fusion.n0_ref), channel_id=1, source_target_pairs={{0,4},{1,5},{4,8},{5,9},{8,12},{9,13},{12,16},{13,17},{16,20},{17,... | collective-permute-start | bytes 589832 | tf_op jit(solution)/shard_map/ppermute | solution.py:241
  92.5 21.7 %collective-permute-start.14 = (bf16[32,768]{1,0:T(8,128)(2,1)S(1)}, bf16[32,768]{1,0:T(8,128)(2,1)S(1)}, u32[]{:S(2)}, u32[]{:S(2)}) collective-permute-start(bf16[32,768]{1,0:T(8,128)(2,1)S(1)} %get-tuple-element.63), channel_id=1, source_target_pairs={{0,16},{4,20},{8,24},{12,28},{16,32},{20,36},{24,40},{28,44},{32,4... | collective-permute-start | bytes 147464 | tf_op jit(solution)/shard_map/ppermute | solution.py:248
  95.1 19.1 %collective-permute-start.15 = (bf16[32,768]{1,0:T(8,128)(2,1)S(1)}, bf16[32,768]{1,0:T(8,128)(2,1)S(1)}, u32[]{:S(2)}, u32[]{:S(2)}) collective-permute-start(bf16[32,768]{1,0:T(8,128)(2,1)S(1)} %get-tuple-element.64), channel_id=1, source_target_pairs={{0,32},{4,36},{8,40},{12,44},{16,48},{20,52},{24,56},{28,60},{32,0... | collective-permute-start | bytes 147464 | tf_op jit(solution)/shard_map/ppermute | solution.py:248
  104.6 12.0 %collective-permute-start.16 = (bf16[32,768]{1,0:T(8,128)(2,1)S(1)}, bf16[32,768]{1,0:T(8,128)(2,1)S(1)}, u32[]{:S(2)}, u32[]{:S(2)}) collective-permute-start(bf16[32,768]{1,0:T(8,128)(2,1)S(1)} %get-tuple-element.65), channel_id=1, source_target_pairs={{0,48},{4,52},{8,56},{12,60},{16,0},{20,4},{24,8},{28,12},{32,16},... | collective-permute-start | bytes 147464 | tf_op jit(solution)/shard_map/ppermute | solution.py:248
  106.5 1.9 %copy-start = (bf16[512,3072]{1,0:T(8,128)(2,1)S(1)}, bf16[512,3072]{1,0:T(8,128)(2,1)}, u32[]{:S(2)}) copy-start(bf16[512,3072]{1,0:T(8,128)(2,1)} %get-tuple-element.62.own_ref) | copy-start | bytes 9437188
  116.6 4.0 %collective-permute-start.17 = (bf16[32,384]{1,0:T(8,128)(2,1)S(1)}, bf16[32,384]{1,0:T(8,128)(2,1)S(1)}, u32[]{:S(2)}, u32[]{:S(2)}) collective-permute-start(bf16[32,384]{1,0:T(8,128)(2,1)S(1)} %get-tuple-element.70), channel_id=1, source_target_pairs={{0,1},{1,0},{2,3},{3,2},{4,5},{5,4},{6,7},{7,6},{8,9},{9,8},{10,11... | collective-permute-start | bytes 73736 | tf_op jit(solution)/shard_map/ppermute | solution.py:254

commit v3 on v2

--- a/solution.py
+++ b/solution.py
@@ -96,49 +96,27 @@
     )(info, *lines, w_own, w_sib)
 
 
-def stage_kernel(info_ref, own_ref, r1_ref, r2_ref, r3_ref, o_ref, s1_ref, s2_ref, s3_ref):
-    zh = info_ref[0] // 4
-    for d, out in enumerate((o_ref, s1_ref, s2_ref, s3_ref)):
-        i = lax.rem(zh + d, 4)
+def stage_kernel(info_ref, own_ref, r1_ref, r2_ref, r3_ref, out_ref):
+    core = info_ref[3]
+    for i in range(4):
         total = own_ref[i]
         for r in (r1_ref, r2_ref, r3_ref):
             total = total + r[i].astype(jnp.float32)
-        out[...] = total.astype(out.dtype)
+        total = total.astype(jnp.bfloat16)
+        out_ref[i, core] = total[:, :384]
+        out_ref[i, 1 - core] = total[:, 384:]
 
 
 def stage_sums(info, own, received):
-    shape = (32, 768)
     return pl.pallas_call(
         stage_kernel,
-        out_shape=[jax.ShapeDtypeStruct(shape, jnp.float32)]
-        + [jax.ShapeDtypeStruct(shape, jnp.bfloat16)] * 3,
+        out_shape=jax.ShapeDtypeStruct((4, 2, 32, 384), jnp.bfloat16),
         in_specs=[smem()] + [vmem()] * 4,
-        out_specs=[vmem()] * 4,
-        compiler_params=pltpu.CompilerParams(vmem_limit_bytes=16 * MIB),
-        cost_estimate=pl.CostEstimate(flops=400000, bytes_accessed=2 * MIB, transcendentals=0),
+        out_specs=vmem(),
+        compiler_params=pltpu.CompilerParams(vmem_limit_bytes=8 * MIB),
+        cost_estimate=pl.CostEstimate(flops=400000, bytes_accessed=MIB, transcendentals=0),
         name="stage_sums",
     )(info, own, *received)
-
-
-def final_kernel(own_ref, r1_ref, r2_ref, r3_ref, o_ref, s_ref):
-    total = own_ref[...]
-    for r in (r1_ref, r2_ref, r3_ref):
-        total = total + r[...].astype(jnp.float32)
-    o_ref[...] = total[:, :384].astype(jnp.bfloat16)
-    s_ref[...] = total[:, 384:].astype(jnp.bfloat16)
-
-
-def final_sums(own, received):
-    shape = jax.ShapeDtypeStruct((32, 384), jnp.bfloat16)
-    return pl.pallas_call(
-        final_kernel,
-        out_shape=[shape, shape],
-        in_specs=[vmem()] * 4,
-        out_specs=[vmem()] * 2,
-        compiler_params=pltpu.CompilerParams(vmem_limit_bytes=4 * MIB),
-        cost_estimate=pl.CostEstimate(flops=100000, bytes_accessed=MIB // 4, transcendentals=0),
-        name="final_sums",
-    )(own, *received)
 
 
 def weight_kernel(info_ref, n0_ref, n1_ref, n2_ref, n3_ref, own_ref, sib_ref, out_ref, tokens, left):
@@ -146,9 +124,9 @@
     @pl.when(pl.program_id(0) == 0)
     def _():
         z, core = info_ref[0], info_ref[3]
-        for ref, far in ((n0_ref, 0), (n1_ref, -1), (n2_ref, 4 * core - 2), (n3_ref, 1)):
+        for d, ref in enumerate((n0_ref, n1_ref, n2_ref, n3_ref)):
             for e in range(4):
-                k = lax.rem(z + far + 4 * e + 16, 16)
+                k = 4 * e + lax.rem(z + 4 - d, 4)
                 for which in range(2):
                     half = core if which == 0 else 1 - core
                     rows = pl.ds(pl.multiple_of(which * 512 + k * 32, 32), 32)
@@ -176,7 +154,7 @@
                 pltpu.VMEM((384, 1024), jnp.bfloat16),
             ],
         ),
-        compiler_params=pltpu.CompilerParams(vmem_limit_bytes=24 * MIB),
+        compiler_params=pltpu.CompilerParams(vmem_limit_bytes=53 * MIB),
         cost_estimate=pl.CostEstimate(
             flops=2 * 1024 * 3072 * 384, bytes_accessed=10 * MIB, transcendentals=0
         ),
@@ -195,10 +173,6 @@
     return pairs
 
 
-def far_shift(by):
-    return [(z, (z + 4 * by) % 16) for z in range(16)]
-
-
 def column_shift(by):
     return [(z * 2 + c, (z + by[c]) % 16 * 2 + c) for z in range(16) for c in range(2)]
 
@@ -229,32 +203,24 @@
     w_sib = lax.ppermute(weight_then, "core", swap)
     inputs, w_sib = lax.optimization_barrier((inputs, w_sib))
     lines = [line] + [lax.ppermute(line, PLANE, plane_shift(False, -d)) for d in (1, 2, 3)]
-    near = [inputs] + [lax.ppermute(inputs, Z, far_shift(-d)) for d in (1, 2)]
-    inputs, near[1] = lax.optimization_barrier((inputs, near[1]))
-    last = lax.ppermute(inputs, Z, far_shift(-3))
+    near = lax.all_to_all(
+        jnp.broadcast_to(inputs[None], (4, 64, 384)), "zh", split_axis=0, concat_axis=0, tiled=True
+    )
     lines, near = lax.optimization_barrier((lines, near))
-    near = near + [last]
 
     own, *sends, hg_own = partial_sums(info, lines, weight, w_sib)
     own, near = lax.optimization_barrier((own, near))
-    near, hg_own = lax.optimization_barrier((jnp.stack(near), hg_own))
-    nears = [near] + [lax.ppermute(near, Z + ("core",), column_shift(by)) for by in NEAR]
     received = [
         lax.ppermute(s, Z + ("core",), column_shift(by)) for s, by in zip(sends, NEAR)
     ]
+    nears = [near] + [lax.ppermute(near, Z + ("core",), column_shift(by)) for by in NEAR]
     hg_sib = lax.ppermute(hg_own, "core", swap)
-    own, *sends = stage_sums(info, own, received)
-    received = [
-        lax.ppermute(s, Z, far_shift(d + 1))
-        for d, s in enumerate(sends)
-    ]
+    summed = stage_sums(info, own, received).reshape(8, 32, 384)
+    summed = lax.all_to_all(summed, ("zh", "core"), split_axis=0, concat_axis=0, tiled=True)
     weight_total = weight_sums(info, nears, hg_own, hg_sib)
-    weight_total, *received = lax.optimization_barrier((weight_total, *received))
-    mine, other = final_sums(own, received)
-    other = lax.ppermute(other, "core", swap)
-    input_gradient = jnp.concatenate(
-        [jnp.where(core == 0, mine, other), jnp.where(core == 0, other, mine)], axis=0
-    )
+    weight_total, summed = lax.optimization_barrier((weight_total, summed))
+    summed = summed.reshape(4, 64, 384).astype(jnp.float32)
+    input_gradient = (summed[0] + summed[1] + summed[2] + summed[3]).astype(jnp.bfloat16)
     return (input_gradient, weight_total)
 
 

time: 122 us -> 126 us (1.033)
  waiting for transfers between devices: 10.1 us -> 30.9 us
  starting transfers between devices: 79.3 us -> 60.5 us
  Pallas kernels: 14.5 us -> 17.4 us
    ppermute x7 -> x0, starting transfers between devices: 34.4 us -> none  [the longest x3 13.9 us: per_device(): lax.ppermute(s, Z, far_shift(d + 1))]
    all_to_all x0 -> x2, starting transfers between devices: none -> 14.1 us  [the longest x1 9.85 us: per_device(): lax.all_to_all(jnp.broadcast_to(inputs[None], (4, 64, 384)), 'zh', split_...]
    ppermute x7 -> x0, waiting for transfers between devices: 10.1 us -> none  [the longest x2 6.96 us: per_device(): near = [inputs] + [lax.ppermute(inputs, Z, far_shift(-d)) for d in (1, 2)]]
    ppermute x3, waiting for transfers between devices: 0.01 us -> 10 us  [per_device(): lax.ppermute(near, Z + ('core',), column_shift(by))]
    ppermute x3, waiting for transfers between devices: 0.01 us -> 8.31 us  [per_device(): lax.ppermute(s, Z + ('core',), column_shift(by))]
    all_to_all x0 -> x2, waiting for transfers between devices: none -> 7.75 us  [the longest x1 7.75 us: per_device(): lax.all_to_all(jnp.broadcast_to(inputs[None], (4, 64, 384)), 'zh', split_...]
    ppermute x3, waiting for transfers between devices: 0.01 us -> 4.82 us  [per_device(): lax.ppermute(line, PLANE, plane_shift(False, -d))]
    pallas_call x1, Pallas kernels: 5.79 us -> 8.05 us  [weight_sums(): pl.pallas_call(weight_kernel, out_shape=jax.ShapeDtypeStruct((384, 3072),...]
  transfers between devices with their start and end apart: 18 -> 13, of which waited for: 3 -> 9; matrix products, arithmetic and copies ran while one was open for 0% -> 1% of each run, Pallas kernels for 12% -> 7%
where the time goes in v3:
time: 126 us; the launch traced here: 125 us
  starting transfers between devices  60.5 us (48%)
  waiting for transfers between devices  30.9 us (25%)
  Pallas kernels  17.4 us (14%)
  blocking collectives  12.4 us (10%)
  other arithmetic  2.05 us (2%)
  local copies, waits for them, and re-layouts  1.55 us (1%)
    all_gather x1, blocking collectives, per_device(): lax.all_gather(local, PLANE, axis=0, tiled=True, axis_index_groups=first_...  12.4 us
    ppermute x3, starting transfers between devices, per_device(): lax.ppermute(near, Z + ('core',), column_shift(by))  11.9 us
    ppermute x3, waiting for transfers between devices, per_device(): lax.ppermute(near, Z + ('core',), column_shift(by))  10 us
    all_to_all x1, starting transfers between devices, per_device(): lax.all_to_all(jnp.broadcast_to(inputs[None], (4, 64, 384)), 'zh', split_...  9.85 us
    ppermute x1, starting transfers between devices, per_device(): w_sib = lax.ppermute(weight_then, 'core', swap)  9.73 us
    ppermute x3, starting transfers between devices, per_device(): lax.ppermute(line, PLANE, plane_shift(False, -d))  8.98 us
    ppermute x3, starting transfers between devices, per_device(): lax.ppermute(s, Z + ('core',), column_shift(by))  8.91 us
    ppermute x3, waiting for transfers between devices, per_device(): lax.ppermute(s, Z + ('core',), column_shift(by))  8.31 us
  transfers between devices with their start and end apart: 13, of which 9 were waited for; matrix products, arithmetic and copies ran while one was open for 1% of the time, Pallas kernels for 7%

profile of v3, /device:TPU:1, one launch (start us, length us, event | category | flops | bytes accessed | tf_op | source)
XLA Modules:
  0.0 125.5 jit_solution(16139779648270407964)
XLA Ops:
  0.6 1.3 %fusion.7 = bf16[32,3072]{1,0:T(8,128)(2,1)S(1)} fusion(bf16[32,3072]{1,0:T(8,128)(2,1)} %param.7, bf16[32,3072]{1,0:T(8,128)(2,1)} %param.6), kind=kLoop, calls=%fused_computation.14 | loop fusion | flops 2064384 | bytes 589824 | tf_op jit(solution)/shard_map/convert_element_type | solution.py:198
  1.9 12.4 %all_gather.3 = bf16[128,3072]{1,0:T(8,128)(2,1)S(1)} all-gather(bf16[32,3072]{1,0:T(8,128)(2,1)S(1)} %fusion.7), channel_id=1, replica_groups={{0,128,256,384},{2,130,258,386},{64,192,320,448},{66,194,322,450},{1,3,..., dimensions={0}, use_global_device_ids=true | all-gather | bytes 983040 | tf_op jit(solution)/shard_map/all_gather | solution.py:199
  14.3 9.7 %collective-permute-start.3 = (bf16[384,3072]{1,0:T(8,128)(2,1)}, bf16[384,3072]{1,0:T(8,128)(2,1)S(1)}, u32[]{:S(2)}, u32[]{:S(2)}) collective-permute-start(bf16[384,3072]{1,0:T(8,128)(2,1)} %w_own_ref.1), channel_id=1, source_target_pairs={{0,1},{1,0},{2,3},{3,2},{4,5},{5,4},{6,7},{7,6},{8,9},{9,8},{10,11... | collective-permute-start | bytes 7077896 | tf_op jit(solution)/shard_map/ppermute | solution.py:203
  24.0 1.9 %collective-permute-start.2 = (bf16[4,32,3072]{2,1,0:T(8,128)(2,1)S(1)}, bf16[4,32,3072]{2,1,0:T(8,128)(2,1)}, u32[]{:S(2)}, u32[]{:S(2)}) collective-permute-start(bf16[4,32,3072]{2,1,0:T(8,128)(2,1)S(1)} %bitcast.7), channel_id=1, source_target_pairs={{0,2},{1,129},{2,64},{3,131},{64,66},{65,193},{66,0},{67,195},{128... | collective-permute-start | bytes 2359304 | tf_op jit(solution)/shard_map/ppermute | solution.py:205
  26.0 3.1 %collective-permute-start.1 = (bf16[4,32,3072]{2,1,0:T(8,128)(2,1)S(1)}, bf16[4,32,3072]{2,1,0:T(8,128)(2,1)}, u32[]{:S(2)}, u32[]{:S(2)}) collective-permute-start(bf16[4,32,3072]{2,1,0:T(8,128)(2,1)S(1)} %bitcast.8), channel_id=1, source_target_pairs={{0,64},{1,257},{2,66},{3,259},{64,0},{65,321},{66,2},{67,323},{128... | collective-permute-start | bytes 2359304 | tf_op jit(solution)/shard_map/ppermute | solution.py:205
  29.1 4.0 %collective-permute-start = (bf16[4,32,3072]{2,1,0:T(8,128)(2,1)S(1)}, bf16[4,32,3072]{2,1,0:T(8,128)(2,1)}, u32[]{:S(2)}, u32[]{:S(2)}) collective-permute-start(bf16[4,32,3072]{2,1,0:T(8,128)(2,1)S(1)} %bitcast.9), channel_id=1, source_target_pairs={{0,66},{1,385},{2,0},{3,387},{64,2},{65,449},{66,64},{67,451},{128... | collective-permute-start | bytes 2359304 | tf_op jit(solution)/shard_map/ppermute | solution.py:205
  33.0 0.0 collective-permute-done.3.w_sib_ref
  33.0 0.0 copy-start
  33.1 1.5 %broadcast_in_dim.2 = bf16[4,64,384]{2,1,0:T(8,128)(2,1)} broadcast(bf16[64,384]{1,0:T(8,128)(2,1)} %param.4), dimensions={1,2} | broadcast | bytes 245760 | tf_op jit(solution)/shard_map/broadcast_in_dim | solution.py:207
  34.6 9.8 %all-to-all-start = ((bf16[4,64,384]{2,1,0:T(8,128)(2,1)}), bf16[4,64,384]{2,1,0:T(8,128)(2,1)S(1)}, u32[]{:S(2)}, u32[]{:S(2)}) async-start(bf16[4,64,384]{2,1,0:T(8,128)(2,1)} %broadcast_in_dim.2), calls=%async_computation | async-start | bytes 393216 | tf_op jit(solution)/shard_map/all_to_all | solution.py:206
  44.4 0.1 pad_add_fusion.info_ref
  44.5 2.3 %collective-permute-done.2.l3_ref = bf16[4,32,3072]{2,1,0:T(8,128)(2,1)} collective-permute-done((bf16[4,32,3072]{2,1,0:T(8,128)(2,1)S(1)}, bf16[4,32,3072]{2,1,0:T(8,128)(2,1)}, u32[]{:S(2)}, u32[]{:S(2)}) %collective-permute-start.2) | collective-permute-done | bytes 786464 | tf_op jit(solution)/shard_map/ppermute | solution.py:205
  46.8 0.0 collective-permute-done.1.l2_ref
  46.8 2.5 %collective-permute-done.l1_ref = bf16[4,32,3072]{2,1,0:T(8,128)(2,1)} collective-permute-done((bf16[4,32,3072]{2,1,0:T(8,128)(2,1)S(1)}, bf16[4,32,3072]{2,1,0:T(8,128)(2,1)}, u32[]{:S(2)}, u32[]{:S(2)}) %collective-permute-start) | collective-permute-done | bytes 786464 | tf_op jit(solution)/shard_map/ppermute | solution.py:205
  49.3 7.8 %all-to-all-done.n0_ref = bf16[4,64,384]{2,1,0:T(8,128)(2,1)S(1)} async-done(((bf16[4,64,384]{2,1,0:T(8,128)(2,1)}), bf16[4,64,384]{2,1,0:T(8,128)(2,1)S(1)}, u32[]{:S(2)}, u32[]{:S(2)}) %all-to-all-start) | async-done | bytes 196640 | tf_op jit(solution)/shard_map/all_to_all | solution.py:206
  57.1 0.0 copy-done
  57.1 8.0 %partial_sums.1 = (f32[4,32,768]{2,1,0:T(8,128)S(1)}, bf16[4,32,768]{2,1,0:T(8,128)(2,1)S(1)}, bf16[4,32,768]{2,1,0:T(8,128)(2,1)S(1)}, bf16[4,32,768]{2,1,0:T(8,128)(2,1)S(1)}, bf16[512,3072]{1,0:T(8,128)(2,1)}) custom-call(s32[4]{0:T(128)S(1)} %pad_add_fusion.info_ref, bf16[4,32,3072]{2,1,0:T(8,128)(2,1)S(1)} %bitcast.10, ...), custom_call_target="tpu_custom_call" | custom-call | flops 2415919104 | bytes 8388608 | tf_op jit(solution)/shard_map/partial_sums/pallas_call | solution.py:78
  65.1 6.9 %collective-permute-start.7 = (bf16[512,3072]{1,0:T(8,128)(2,1)}, bf16[512,3072]{1,0:T(8,128)(2,1)}, u32[]{:S(2)}, u32[]{:S(2)}) collective-permute-start(bf16[512,3072]{1,0:T(8,128)(2,1)} %get-tuple-element.31.own_ref), channel_id=1, source_target_pairs={{0,1},{1,0},{2,3},{3,2},{4,5},{5,4},{6,7},{7,6},{8,9},{9,8},{10,11... | collective-permute-start | bytes 9437192 | tf_op jit(solution)/shard_map/ppermute | solution.py:217
  72.0 4.4 %collective-permute-start.8 = (bf16[4,32,768]{2,1,0:T(8,128)(2,1)S(1)}, bf16[4,32,768]{2,1,0:T(8,128)(2,1)S(1)}, u32[]{:S(2)}, u32[]{:S(2)}) collective-permute-start(bf16[4,32,768]{2,1,0:T(8,128)(2,1)S(1)} %get-tuple-element.33), channel_id=1, source_target_pairs={{0,4},{1,5},{4,8},{5,9},{8,12},{9,13},{12,16},{13,17},{16,20},{17,... | collective-permute-start | bytes 589832 | tf_op jit(solution)/shard_map/ppermute | solution.py:214
  76.4 2.4 %collective-permute-start.9 = (bf16[4,32,768]{2,1,0:T(8,128)(2,1)S(1)}, bf16[4,32,768]{2,1,0:T(8,128)(2,1)S(1)}, u32[]{:S(2)}, u32[]{:S(2)}) collective-permute-start(bf16[4,32,768]{2,1,0:T(8,128)(2,1)S(1)} %get-tuple-element.34), channel_id=1, source_target_pairs={{0,8},{1,57},{4,12},{5,61},{8,16},{9,1},{12,20},{13,5},{16,24},{17... | collective-permute-start | bytes 589832 | tf_op jit(solution)/shard_map/ppermute | solution.py:214
  78.8 2.1 %collective-permute-start.10 = (bf16[4,32,768]{2,1,0:T(8,128)(2,1)S(1)}, bf16[4,32,768]{2,1,0:T(8,128)(2,1)S(1)}, u32[]{:S(2)}, u32[]{:S(2)}) collective-permute-start(bf16[4,32,768]{2,1,0:T(8,128)(2,1)S(1)} %get-tuple-element.35), channel_id=1, source_target_pairs={{0,60},{1,61},{4,0},{5,1},{8,4},{9,5},{12,8},{13,9},{16,12},{17,13... | collective-permute-start | bytes 589832 | tf_op jit(solution)/shard_map/ppermute | solution.py:214
  81.0 0.7 collective-permute-done.8.r1_ref
  81.7 4.7 %collective-permute-done.9.r2_ref = bf16[4,32,768]{2,1,0:T(8,128)(2,1)S(1)} collective-permute-done((bf16[4,32,768]{2,1,0:T(8,128)(2,1)S(1)}, bf16[4,32,768]{2,1,0:T(8,128)(2,1)S(1)}, u32[]{:S(2)}, u32[]{:S(2)}) %collective-permute-start.9) | collective-permute-done | bytes 196640 | tf_op jit(solution)/shard_map/ppermute | solution.py:214
  86.4 2.9 %collective-permute-done.10.r3_ref = bf16[4,32,768]{2,1,0:T(8,128)(2,1)S(1)} collective-permute-done((bf16[4,32,768]{2,1,0:T(8,128)(2,1)S(1)}, bf16[4,32,768]{2,1,0:T(8,128)(2,1)S(1)}, u32[]{:S(2)}, u32[]{:S(2)}) %collective-permute-start.10) | collective-permute-done | bytes 196640 | tf_op jit(solution)/shard_map/ppermute | solution.py:214
  89.3 1.3 %stage_sums.1 = bf16[4,2,32,384]{3,2,1,0:T(8,128)(2,1)} custom-call(s32[4]{0:T(128)S(1)} %pad_add_fusion.info_ref, f32[4,32,768]{2,1,0:T(8,128)S(1)} %get-tuple-element.32.own_ref, bf16[4,32,768]{2,1,0:T(8,128)(2,1)S(1)} %collective-permute-done.8.r1_ref, bf16[4,32,768]{2,1,0:T(8,128)(2,1)S(1)} %collective-permute-done.9.r2_ref, ...), custom_call_target="tpu_custom_call" | custom-call | flops 400000 | bytes 1048576 | tf_op jit(solution)/shard_map/stage_sums/pallas_call | solution.py:111
  90.6 4.2 %all-to-all-start.1 = ((bf16[8,32,384]{2,1,0:T(8,128)(2,1)}), bf16[8,32,384]{2,1,0:T(8,128)(2,1)S(1)}, u32[]{:S(2)}, u32[]{:S(2)}) async-start(bf16[8,32,384]{2,1,0:T(8,128)(2,1)} %bitcast.5), calls=%async_computation.1 | async-start | bytes 393216 | tf_op jit(solution)/shard_map/all_to_all | solution.py:219
  94.8 6.9 %collective-permute-start.6 = (bf16[4,64,384]{2,1,0:T(8,128)(2,1)S(1)}, bf16[4,64,384]{2,1,0:T(8,128)(2,1)S(1)}, u32[]{:S(2)}, u32[]{:S(2)}) collective-permute-start(bf16[4,64,384]{2,1,0:T(8,128)(2,1)S(1)} %all-to-all-done.n0_ref), channel_id=1, source_target_pairs={{0,60},{1,61},{4,0},{5,1},{8,4},{9,5},{12,8},{13,9},{16,12},{17,13... | collective-permute-start | bytes 589832 | tf_op jit(solution)/shard_map/ppermute | solution.py:216
  101.7 1.9 %collective-permute-start.5 = (bf16[4,64,384]{2,1,0:T(8,128)(2,1)S(1)}, bf16[4,64,384]{2,1,0:T(8,128)(2,1)S(1)}, u32[]{:S(2)}, u32[]{:S(2)}) collective-permute-start(bf16[4,64,384]{2,1,0:T(8,128)(2,1)S(1)} %all-to-all-done.n0_ref), channel_id=1, source_target_pairs={{0,8},{1,57},{4,12},{5,61},{8,16},{9,1},{12,20},{13,5},{16,24},{17... | collective-permute-start | bytes 589832 | tf_op jit(solution)/shard_map/ppermute | solution.py:216
  103.6 3.1 %collective-permute-start.4 = (bf16[4,64,384]{2,1,0:T(8,128)(2,1)S(1)}, bf16[4,64,384]{2,1,0:T(8,128)(2,1)S(1)}, u32[]{:S(2)}, u32[]{:S(2)}) collective-permute-start(bf16[4,64,384]{2,1,0:T(8,128)(2,1)S(1)} %all-to-all-done.n0_ref), channel_id=1, source_target_pairs={{0,4},{1,5},{4,8},{5,9},{8,12},{9,13},{12,16},{13,17},{16,20},{17,... | collective-permute-start | bytes 589832 | tf_op jit(solution)/shard_map/ppermute | solution.py:216
  106.7 2.2 %collective-permute-done.6.n3_ref = bf16[4,64,384]{2,1,0:T(8,128)(2,1)S(1)} collective-permute-done((bf16[4,64,384]{2,1,0:T(8,128)(2,1)S(1)}, bf16[4,64,384]{2,1,0:T(8,128)(2,1)S(1)}, u32[]{:S(2)}, u32[]{:S(2)}) %collective-permute-start.6) | collective-permute-done | bytes 196640 | tf_op jit(solution)/shard_map/ppermute | solution.py:216
  108.9 5.7 %collective-permute-done.5.n2_ref = bf16[4,64,384]{2,1,0:T(8,128)(2,1)S(1)} collective-permute-done((bf16[4,64,384]{2,1,0:T(8,128)(2,1)S(1)}, bf16[4,64,384]{2,1,0:T(8,128)(2,1)S(1)}, u32[]{:S(2)}, u32[]{:S(2)}) %collective-permute-start.5) | collective-permute-done | bytes 196640 | tf_op jit(solution)/shard_map/ppermute | solution.py:216
  114.6 2.1 %collective-permute-done.4.n1_ref = bf16[4,64,384]{2,1,0:T(8,128)(2,1)S(1)} collective-permute-done((bf16[4,64,384]{2,1,0:T(8,128)(2,1)S(1)}, bf16[4,64,384]{2,1,0:T(8,128)(2,1)S(1)}, u32[]{:S(2)}, u32[]{:S(2)}) %collective-permute-start.4) | collective-permute-done | bytes 196640 | tf_op jit(solution)/shard_map/ppermute | solution.py:216
  116.7 0.0 collective-permute-done.7.sib_ref
  116.7 8.0 %weight_sums.1 = bf16[384,3072]{1,0:T(8,128)(2,1)} custom-call(s32[4]{0:T(128)S(1)} %pad_add_fusion.info_ref, bf16[4,64,384]{2,1,0:T(8,128)(2,1)S(1)} %all-to-all-done.n0_ref, bf16[4,64,384]{2,1,0:T(8,128)(2,1)S(1)} %collective-permute-done.4.n1_ref, bf16[4,64,384]{2,1,0:T(8,128)(2,1)S(1)} %collective-permute-done.5.n2_ref, ...), custom_call_target="tpu_custom_call" | custom-call | flops 2415919104 | bytes 10485760 | tf_op jit(solution)/shard_map/weight_sums/pallas_call | solution.py:143
  124.8 0.0 all-to-all-done.1
  124.8 0.6 fusion.9
  (1 shorter events, 0.0 us)
Async XLA Ops:
  14.3 18.7 %collective-permute-start.3 = (bf16[384,3072]{1,0:T(8,128)(2,1)}, bf16[384,3072]{1,0:T(8,128)(2,1)S(1)}, u32[]{:S(2)}, u32[]{:S(2)}) collective-permute-start(bf16[384,3072]{1,0:T(8,128)(2,1)} %w_own_ref.1), channel_id=1, source_target_pairs={{0,1},{1,0},{2,3},{3,2},{4,5},{5,4},{6,7},{7,6},{8,9},{9,8},{10,11... | collective-permute-start | bytes 7077896 | tf_op jit(solution)/shard_map/ppermute | solution.py:203
  24.0 22.8 %collective-permute-start.2 = (bf16[4,32,3072]{2,1,0:T(8,128)(2,1)S(1)}, bf16[4,32,3072]{2,1,0:T(8,128)(2,1)}, u32[]{:S(2)}, u32[]{:S(2)}) collective-permute-start(bf16[4,32,3072]{2,1,0:T(8,128)(2,1)S(1)} %bitcast.7), channel_id=1, source_target_pairs={{0,2},{1,129},{2,64},{3,131},{64,66},{65,193},{66,0},{67,195},{128... | collective-permute-start | bytes 2359304 | tf_op jit(solution)/shard_map/ppermute | solution.py:205
  26.0 20.8 %collective-permute-start.1 = (bf16[4,32,3072]{2,1,0:T(8,128)(2,1)S(1)}, bf16[4,32,3072]{2,1,0:T(8,128)(2,1)}, u32[]{:S(2)}, u32[]{:S(2)}) collective-permute-start(bf16[4,32,3072]{2,1,0:T(8,128)(2,1)S(1)} %bitcast.8), channel_id=1, source_target_pairs={{0,64},{1,257},{2,66},{3,259},{64,0},{65,321},{66,2},{67,323},{128... | collective-permute-start | bytes 2359304 | tf_op jit(solution)/shard_map/ppermute | solution.py:205
  29.1 20.3 %collective-permute-start = (bf16[4,32,3072]{2,1,0:T(8,128)(2,1)S(1)}, bf16[4,32,3072]{2,1,0:T(8,128)(2,1)}, u32[]{:S(2)}, u32[]{:S(2)}) collective-permute-start(bf16[4,32,3072]{2,1,0:T(8,128)(2,1)S(1)} %bitcast.9), channel_id=1, source_target_pairs={{0,66},{1,385},{2,0},{3,387},{64,2},{65,449},{66,64},{67,451},{128... | collective-permute-start | bytes 2359304 | tf_op jit(solution)/shard_map/ppermute | solution.py:205
  33.0 24.1 %copy-start = (bf16[384,3072]{1,0:T(8,128)(2,1)}, bf16[384,3072]{1,0:T(8,128)(2,1)S(1)}, u32[]{:S(2)}) copy-start(bf16[384,3072]{1,0:T(8,128)(2,1)S(1)} %collective-permute-done.3.w_sib_ref) | copy-start | bytes 7077892
  34.6 22.5 %all-to-all-start = ((bf16[4,64,384]{2,1,0:T(8,128)(2,1)}), bf16[4,64,384]{2,1,0:T(8,128)(2,1)S(1)}, u32[]{:S(2)}, u32[]{:S(2)}) async-start(bf16[4,64,384]{2,1,0:T(8,128)(2,1)} %broadcast_in_dim.2), calls=%async_computation | async-start | bytes 393216 | tf_op jit(solution)/shard_map/all_to_all | solution.py:206
  65.1 51.6 %collective-permute-start.7 = (bf16[512,3072]{1,0:T(8,128)(2,1)}, bf16[512,3072]{1,0:T(8,128)(2,1)}, u32[]{:S(2)}, u32[]{:S(2)}) collective-permute-start(bf16[512,3072]{1,0:T(8,128)(2,1)} %get-tuple-element.31.own_ref), channel_id=1, source_target_pairs={{0,1},{1,0},{2,3},{3,2},{4,5},{5,4},{6,7},{7,6},{8,9},{9,8},{10,11... | collective-permute-start | bytes 9437192 | tf_op jit(solution)/shard_map/ppermute | solution.py:217
  72.0 9.6 %collective-permute-start.8 = (bf16[4,32,768]{2,1,0:T(8,128)(2,1)S(1)}, bf16[4,32,768]{2,1,0:T(8,128)(2,1)S(1)}, u32[]{:S(2)}, u32[]{:S(2)}) collective-permute-start(bf16[4,32,768]{2,1,0:T(8,128)(2,1)S(1)} %get-tuple-element.33), channel_id=1, source_target_pairs={{0,4},{1,5},{4,8},{5,9},{8,12},{9,13},{12,16},{13,17},{16,20},{17,... | collective-permute-start | bytes 589832 | tf_op jit(solution)/shard_map/ppermute | solution.py:214
  76.4 10.0 %collective-permute-start.9 = (bf16[4,32,768]{2,1,0:T(8,128)(2,1)S(1)}, bf16[4,32,768]{2,1,0:T(8,128)(2,1)S(1)}, u32[]{:S(2)}, u32[]{:S(2)}) collective-permute-start(bf16[4,32,768]{2,1,0:T(8,128)(2,1)S(1)} %get-tuple-element.34), channel_id=1, source_target_pairs={{0,8},{1,57},{4,12},{5,61},{8,16},{9,1},{12,20},{13,5},{16,24},{17... | collective-permute-start | bytes 589832 | tf_op jit(solution)/shard_map/ppermute | solution.py:214
  78.8 10.4 %collective-permute-start.10 = (bf16[4,32,768]{2,1,0:T(8,128)(2,1)S(1)}, bf16[4,32,768]{2,1,0:T(8,128)(2,1)S(1)}, u32[]{:S(2)}, u32[]{:S(2)}) collective-permute-start(bf16[4,32,768]{2,1,0:T(8,128)(2,1)S(1)} %get-tuple-element.35), channel_id=1, source_target_pairs={{0,60},{1,61},{4,0},{5,1},{8,4},{9,5},{12,8},{13,9},{16,12},{17,13... | collective-permute-start | bytes 589832 | tf_op jit(solution)/shard_map/ppermute | solution.py:214
  90.6 34.2 %all-to-all-start.1 = ((bf16[8,32,384]{2,1,0:T(8,128)(2,1)}), bf16[8,32,384]{2,1,0:T(8,128)(2,1)S(1)}, u32[]{:S(2)}, u32[]{:S(2)}) async-start(bf16[8,32,384]{2,1,0:T(8,128)(2,1)} %bitcast.5), calls=%async_computation.1 | async-start | bytes 393216 | tf_op jit(solution)/shard_map/all_to_all | solution.py:219
  94.8 14.1 %collective-permute-start.6 = (bf16[4,64,384]{2,1,0:T(8,128)(2,1)S(1)}, bf16[4,64,384]{2,1,0:T(8,128)(2,1)S(1)}, u32[]{:S(2)}, u32[]{:S(2)}) collective-permute-start(bf16[4,64,384]{2,1,0:T(8,128)(2,1)S(1)} %all-to-all-done.n0_ref), channel_id=1, source_target_pairs={{0,60},{1,61},{4,0},{5,1},{8,4},{9,5},{12,8},{13,9},{16,12},{17,13... | collective-permute-start | bytes 589832 | tf_op jit(solution)/shard_map/ppermute | solution.py:216
  101.7 12.9 %collective-permute-start.5 = (bf16[4,64,384]{2,1,0:T(8,128)(2,1)S(1)}, bf16[4,64,384]{2,1,0:T(8,128)(2,1)S(1)}, u32[]{:S(2)}, u32[]{:S(2)}) collective-permute-start(bf16[4,64,384]{2,1,0:T(8,128)(2,1)S(1)} %all-to-all-done.n0_ref), channel_id=1, source_target_pairs={{0,8},{1,57},{4,12},{5,61},{8,16},{9,1},{12,20},{13,5},{16,24},{17... | collective-permute-start | bytes 589832 | tf_op jit(solution)/shard_map/ppermute | solution.py:216
  103.6 13.1 %collective-permute-start.4 = (bf16[4,64,384]{2,1,0:T(8,128)(2,1)S(1)}, bf16[4,64,384]{2,1,0:T(8,128)(2,1)S(1)}, u32[]{:S(2)}, u32[]{:S(2)}) collective-permute-start(bf16[4,64,384]{2,1,0:T(8,128)(2,1)S(1)} %all-to-all-done.n0_ref), channel_id=1, source_target_pairs={{0,4},{1,5},{4,8},{5,9},{8,12},{9,13},{12,16},{13,17},{16,20},{17,... | collective-permute-start | bytes 589832 | tf_op jit(solution)/shard_map/ppermute | solution.py:216

commit v4 on v2

--- a/solution.py
+++ b/solution.py
@@ -42,31 +42,27 @@
     return pl.ds(pl.multiple_of(k * 32, 32), 32)
 
 
-def partial_kernel(info_ref, l0_ref, l1_ref, l2_ref, l3_ref, w_own_ref, w_sib_ref, own_ref, s1_ref, s2_ref, s3_ref, plane_ref, plane, w, acc, sems):
-    second = info_ref[2]
+def partial_kernel(info_ref, lines_ref, w_own_ref, w_sib_ref, own_ref, s1_ref, s2_ref, s3_ref, plane_ref, w_sib, acc, sems):
     copies = []
-    for d, ref in enumerate((l0_ref, l1_ref, l2_ref, l3_ref)):
+    for j in range(4):
         for i in range(4):
-            k = chip_number(info_ref, i, lax.rem(second + d, 4))
+            rows = block_rows(chip_number(info_ref, i, j))
             copies.append(
-                pltpu.make_async_copy(ref.at[i], plane.at[block_rows(k), :], sems.at[d * 4 + i])
+                pltpu.make_async_copy(lines_ref.at[j, i], plane_ref.at[rows, :], sems.at[j * 4 + i])
             )
-    weights = [
-        pltpu.make_async_copy(ref, w.at[n], sems.at[16 + n])
-        for n, ref in enumerate((w_own_ref, w_sib_ref))
-    ]
-    for copy in copies + weights:
+    weights = pltpu.make_async_copy(w_sib_ref, w_sib, sems.at[16])
+    for copy in copies:
         copy.start()
+    weights.start()
     for copy in copies:
         copy.wait()
-    result = pltpu.make_async_copy(plane, plane_ref, sems.at[18])
-    result.start()
-    for n, copy in enumerate(weights):
-        copy.wait()
-        acc[:, n * 384 : (n + 1) * 384] = lax.dot_general(
-            plane[...], w[n], ROWS_BY_ROWS, preferred_element_type=jnp.float32
-        )
-    result.wait()
+    acc[:, :384] = lax.dot_general(
+        plane_ref[...], w_own_ref[...], ROWS_BY_ROWS, preferred_element_type=jnp.float32
+    )
+    weights.wait()
+    acc[:, 384:] = lax.dot_general(
+        plane_ref[...], w_sib[...], ROWS_BY_ROWS, preferred_element_type=jnp.float32
+    )
     for d, out in enumerate((own_ref, s1_ref, s2_ref, s3_ref)):
         residue = lax.rem(info_ref[0] + d, 4)
         for x in range(4):
@@ -80,15 +76,14 @@
         out_shape=[jax.ShapeDtypeStruct(shape, jnp.float32)]
         + [jax.ShapeDtypeStruct(shape, jnp.bfloat16)] * 3
         + [jax.ShapeDtypeStruct((512, 3072), jnp.bfloat16)],
-        in_specs=[smem()] + [pl.BlockSpec(memory_space=pl.ANY)] * 6,
-        out_specs=[vmem()] * 4 + [pl.BlockSpec(memory_space=pl.ANY)],
+        in_specs=[smem(), pl.BlockSpec(memory_space=pl.ANY), vmem(), pl.BlockSpec(memory_space=pl.ANY)],
+        out_specs=[vmem()] * 5,
         scratch_shapes=[
-            pltpu.VMEM((512, 3072), jnp.bfloat16),
-            pltpu.VMEM((2, 384, 3072), jnp.bfloat16),
+            pltpu.VMEM((384, 3072), jnp.bfloat16),
             pltpu.VMEM((512, 768), jnp.float32),
-            pltpu.SemaphoreType.DMA((19,)),
+            pltpu.SemaphoreType.DMA((17,)),
         ],
-        compiler_params=pltpu.CompilerParams(vmem_limit_bytes=52 * MIB),
+        compiler_params=pltpu.CompilerParams(vmem_limit_bytes=44 * MIB),
         cost_estimate=pl.CostEstimate(
             flops=2 * 512 * 3072 * 768, bytes_accessed=8 * MIB, transcendentals=0
         ),
@@ -203,6 +198,13 @@
     return [(z * 2 + c, (z + by[c]) % 16 * 2 + c) for z in range(16) for c in range(2)]
 
 
+def second_axis_groups():
+    place = [[[(x * 4 + y) * 2 + c for c in range(2)] for y in range(4)] for x in range(4)]
+    along_y = [[place[j][i][0] for i in range(4)] for j in range(4)]
+    along_x = [[place[i][j][1] for i in range(4)] for j in range(4)]
+    return along_y + along_x
+
+
 def first_axis_groups():
     place = [[[(x * 4 + y) * 2 + c for c in range(2)] for y in range(4)] for x in range(4)]
     along_x = [[place[i][j][0] for i in range(4)] for j in range(4)]
@@ -225,14 +227,21 @@
     line = lax.all_gather(
         local, PLANE, axis=0, tiled=True, axis_index_groups=first_axis_groups()
     ).reshape(4, 32, 3072)
-    weight_then, line = lax.optimization_barrier((weight, line))
+    weight_then, inputs, line = lax.optimization_barrier((weight, inputs, line))
     w_sib = lax.ppermute(weight_then, "core", swap)
-    inputs, w_sib = lax.optimization_barrier((inputs, w_sib))
-    lines = [line] + [lax.ppermute(line, PLANE, plane_shift(False, -d)) for d in (1, 2, 3)]
+    lines = lax.all_to_all(
+        jnp.broadcast_to(line[None], (4, 4, 32, 3072)),
+        PLANE,
+        split_axis=0,
+        concat_axis=0,
+        tiled=True,
+        axis_index_groups=second_axis_groups(),
+    )
     near = [inputs] + [lax.ppermute(inputs, Z, far_shift(-d)) for d in (1, 2)]
     inputs, near[1] = lax.optimization_barrier((inputs, near[1]))
     last = lax.ppermute(inputs, Z, far_shift(-3))
     lines, near = lax.optimization_barrier((lines, near))
+    lines = [lines]
     near = near + [last]
 
     own, *sends, hg_own = partial_sums(info, lines, weight, w_sib)

time: 122 us -> 113 us (0.926)
  waiting for transfers between devices: 10.1 us -> 3.97 us
  starting transfers between devices: 79.3 us -> 77.6 us
  Pallas kernels: 14.5 us -> 12.8 us
    ppermute x3 -> x0, starting transfers between devices: 8.98 us -> none  [per_device(): lax.ppermute(line, PLANE, plane_shift(False, -d))]
    ppermute x2, waiting for transfers between devices: 6.96 us -> 1.6 us  [per_device(): near = [inputs] + [lax.ppermute(inputs, Z, far_shift(-d)) for d in (1, 2)]]
    all_to_all x0 -> x1, starting transfers between devices: none -> 4.78 us  [per_device(): lax.all_to_all(jnp.broadcast_to(line[None], (4, 4, 32, 3072)), PLANE, spl...]
    ppermute x3, starting transfers between devices: 9.31 us -> 12.9 us  [per_device(): lax.ppermute(s, Z + ('core',), column_shift(by))]
    ppermute x3, starting transfers between devices: 11.3 us -> 8.41 us  [per_device(): lax.ppermute(near, Z + ('core',), column_shift(by))]
    ppermute x1, starting transfers between devices: 4.92 us -> 7.26 us  [per_device(): last = lax.ppermute(inputs, Z, far_shift(-3))]
    ppermute x1, starting transfers between devices: 5.56 us -> 3.32 us  [per_device(): hg_sib = lax.ppermute(hg_own, 'core', swap)]
    broadcast_in_dim x0 -> x1, local copies, waits for them, and re-layouts: none -> 2.06 us  [per_device(): jnp.broadcast_to(line[None], (4, 4, 32, 3072))]
  transfers between devices with their start and end apart: 18 -> 16, of which waited for: 3 -> 3; matrix products, arithmetic and copies ran while one was open for 0% -> 0% of each run, Pallas kernels for 12% -> 11%
where the time goes in v4:
time: 113 us; the launch traced here: 112 us
  starting transfers between devices  77.6 us (69%)
  Pallas kernels  12.8 us (11%)
  blocking collectives  12.4 us (11%)
  waiting for transfers between devices  3.97 us (4%)
  local copies, waits for them, and re-layouts  2.07 us (2%)
  other arithmetic  2.05 us (2%)
    ppermute x3, starting transfers between devices, per_device(): lax.ppermute(s, Z, far_shift(d + 1))  14.1 us
    ppermute x3, starting transfers between devices, per_device(): lax.ppermute(s, Z + ('core',), column_shift(by))  12.9 us
    all_gather x1, blocking collectives, per_device(): lax.all_gather(local, PLANE, axis=0, tiled=True, axis_index_groups=first_...  12.4 us
    ppermute x2, starting transfers between devices, per_device(): near = [inputs] + [lax.ppermute(inputs, Z, far_shift(-d)) for d in (1, 2)]  12.3 us
    ppermute x1, starting transfers between devices, per_device(): w_sib = lax.ppermute(weight_then, 'core', swap)  9.74 us
    ppermute x3, starting transfers between devices, per_device(): lax.ppermute(near, Z + ('core',), column_shift(by))  8.41 us
    ppermute x1, starting transfers between devices, per_device(): last = lax.ppermute(inputs, Z, far_shift(-3))  7.26 us
    pallas_call x1, Pallas kernels, partial_sums(): pl.pallas_call(partial_kernel, out_shape=[jax.ShapeDtypeStruct(shape, jnp...  6.33 us
  transfers between devices with their start and end apart: 16, of which 3 were waited for; matrix products, arithmetic and copies ran while one was open for 0% of the time, Pallas kernels for 11%

profile of v4, /device:TPU:1, one launch (start us, length us, event | category | flops | bytes accessed | tf_op | source)
XLA Modules:
  0.0 111.7 jit_solution(4222346044719517172)
XLA Ops:
  0.6 1.3 %fusion.7 = bf16[32,3072]{1,0:T(8,128)(2,1)S(1)} fusion(bf16[32,3072]{1,0:T(8,128)(2,1)} %param.7, bf16[32,3072]{1,0:T(8,128)(2,1)} %param.6), kind=kLoop, calls=%fused_computation.14 | loop fusion | flops 2064384 | bytes 589824 | tf_op jit(solution)/shard_map/convert_element_type | solution.py:226
  1.9 12.4 %all_gather.3 = bf16[128,3072]{1,0:T(8,128)(2,1)S(1)} all-gather(bf16[32,3072]{1,0:T(8,128)(2,1)S(1)} %fusion.7), channel_id=1, replica_groups={{0,128,256,384},{2,130,258,386},{64,192,320,448},{66,194,322,450},{1,3,..., dimensions={0}, use_global_device_ids=true | all-gather | bytes 983040 | tf_op jit(solution)/shard_map/all_gather | solution.py:227
  14.3 2.1 %broadcast_in_dim.2 = bf16[4,4,32,3072]{3,2,1,0:T(8,128)(2,1)} broadcast(bf16[4,32,3072]{2,1,0:T(8,128)(2,1)S(1)} %bitcast.9), dimensions={1,2,3} | broadcast | bytes 3932160 | tf_op jit(solution)/shard_map/broadcast_in_dim | solution.py:233
  16.4 0.0 copy-start
  16.4 0.0 copy-start.1
  16.4 4.8 %all-to-all-start = ((bf16[4,4,32,3072]{3,2,1,0:T(8,128)(2,1)}), bf16[4,4,32,3072]{3,2,1,0:T(8,128)(2,1)}, u32[]{:S(2)}, u32[]{:S(2)}) async-start(bf16[4,4,32,3072]{3,2,1,0:T(8,128)(2,1)} %broadcast_in_dim.2), calls=%async_computation | async-start | bytes 6291456 | tf_op jit(solution)/shard_map/all_to_all | solution.py:232
  21.1 0.0 copy-done
  21.2 9.7 %collective-permute-start.2 = (bf16[384,3072]{1,0:T(8,128)(2,1)S(1)}, bf16[384,3072]{1,0:T(8,128)(2,1)}, u32[]{:S(2)}, u32[]{:S(2)}) collective-permute-start(bf16[384,3072]{1,0:T(8,128)(2,1)S(1)} %copy-done), channel_id=1, source_target_pairs={{0,1},{1,0},{2,3},{3,2},{4,5},{5,4},{6,7},{7,6},{8,9},{9,8},{10,11... | collective-permute-start | bytes 7077896 | tf_op jit(solution)/shard_map/ppermute | solution.py:231
  30.9 0.0 copy-done.1
  30.9 7.4 %collective-permute-start = (bf16[64,384]{1,0:T(8,128)(2,1)S(1)}, bf16[64,384]{1,0:T(8,128)(2,1)S(1)}, u32[]{:S(2)}, u32[]{:S(2)}) collective-permute-start(bf16[64,384]{1,0:T(8,128)(2,1)S(1)} %copy-done.1), channel_id=1, source_target_pairs={{0,48},{4,52},{8,56},{12,60},{16,0},{20,4},{24,8},{28,12},{32,16},... | collective-permute-start | bytes 147464 | tf_op jit(solution)/shard_map/ppermute | solution.py:240
  38.4 4.9 %collective-permute-start.1 = (bf16[64,384]{1,0:T(8,128)(2,1)S(1)}, bf16[64,384]{1,0:T(8,128)(2,1)S(1)}, u32[]{:S(2)}, u32[]{:S(2)}) collective-permute-start(bf16[64,384]{1,0:T(8,128)(2,1)S(1)} %copy-done.1), channel_id=1, source_target_pairs={{0,32},{4,36},{8,40},{12,44},{16,48},{20,52},{24,56},{28,60},{32,0... | collective-permute-start | bytes 147464 | tf_op jit(solution)/shard_map/ppermute | solution.py:240
  43.3 0.1 pad_add_fusion.info_ref
  43.4 0.0 collective-permute-done
  43.4 7.3 %collective-permute-start.3 = (bf16[64,384]{1,0:T(8,128)(2,1)S(1)}, bf16[64,384]{1,0:T(8,128)(2,1)S(1)}, u32[]{:S(2)}, u32[]{:S(2)}) collective-permute-start(bf16[64,384]{1,0:T(8,128)(2,1)S(1)} %copy-done.1), channel_id=1, source_target_pairs={{0,16},{4,20},{8,24},{12,28},{16,32},{20,36},{24,40},{28,44},{32,4... | collective-permute-start | bytes 147464 | tf_op jit(solution)/shard_map/ppermute | solution.py:242
  50.6 1.6 %collective-permute-done.1 = bf16[64,384]{1,0:T(8,128)(2,1)S(1)} collective-permute-done((bf16[64,384]{1,0:T(8,128)(2,1)S(1)}, bf16[64,384]{1,0:T(8,128)(2,1)S(1)}, u32[]{:S(2)}, u32[]{:S(2)}) %collective-permute-start.1) | collective-permute-done | bytes 49184 | tf_op jit(solution)/shard_map/ppermute | solution.py:240
  52.2 0.0 all-to-all-done.lines_ref
  52.2 0.0 collective-permute-done.2.w_sib_ref
  52.2 6.3 %partial_sums.1 = (f32[4,32,768]{2,1,0:T(8,128)S(1)}, bf16[4,32,768]{2,1,0:T(8,128)(2,1)S(1)}, bf16[4,32,768]{2,1,0:T(8,128)(2,1)S(1)}, bf16[4,32,768]{2,1,0:T(8,128)(2,1)S(1)}, bf16[512,3072]{1,0:T(8,128)(2,1)S(1)}) custom-call(s32[4]{0:T(128)S(1)} %pad_add_fusion.info_ref, bf16[4,4,32,3072]{3,2,1,0:T(8,128)(2,1)} %all-to-all-done.lines_ref, ...), custom_call_target="tpu_custom_call" | custom-call | flops 2415919104 | bytes 8388608 | tf_op jit(solution)/shard_map/partial_sums/pallas_call | solution.py:74
  58.6 0.0 collective-permute-done.3
  58.6 3.3 %collective-permute-start.10 = (bf16[512,3072]{1,0:T(8,128)(2,1)S(1)}, bf16[512,3072]{1,0:T(8,128)(2,1)S(1)}, u32[]{:S(2)}, u32[]{:S(2)}) collective-permute-start(bf16[512,3072]{1,0:T(8,128)(2,1)S(1)} %get-tuple-element.54.own_ref), channel_id=1, source_target_pairs={{0,1},{1,0},{2,3},{3,2},{4,5},{5,4},{6,7},{7,6},{8,9},{9,8},{10,11... | collective-permute-start | bytes 9437192 | tf_op jit(solution)/shard_map/ppermute | solution.py:254
  62.0 4.3 %collective-permute-start.4 = (bf16[4,32,768]{2,1,0:T(8,128)(2,1)S(1)}, bf16[4,32,768]{2,1,0:T(8,128)(2,1)S(1)}, u32[]{:S(2)}, u32[]{:S(2)}) collective-permute-start(bf16[4,32,768]{2,1,0:T(8,128)(2,1)S(1)} %get-tuple-element.44), channel_id=1, source_target_pairs={{0,4},{1,5},{4,8},{5,9},{8,12},{9,13},{12,16},{13,17},{16,20},{17,... | collective-permute-start | bytes 589832 | tf_op jit(solution)/shard_map/ppermute | solution.py:252
  66.2 5.3 %collective-permute-start.5 = (bf16[4,32,768]{2,1,0:T(8,128)(2,1)S(1)}, bf16[4,32,768]{2,1,0:T(8,128)(2,1)S(1)}, u32[]{:S(2)}, u32[]{:S(2)}) collective-permute-start(bf16[4,32,768]{2,1,0:T(8,128)(2,1)S(1)} %get-tuple-element.45), channel_id=1, source_target_pairs={{0,8},{1,57},{4,12},{5,61},{8,16},{9,1},{12,20},{13,5},{16,24},{17... | collective-permute-start | bytes 589832 | tf_op jit(solution)/shard_map/ppermute | solution.py:252
  71.5 3.4 %collective-permute-start.6 = (bf16[4,32,768]{2,1,0:T(8,128)(2,1)S(1)}, bf16[4,32,768]{2,1,0:T(8,128)(2,1)S(1)}, u32[]{:S(2)}, u32[]{:S(2)}) collective-permute-start(bf16[4,32,768]{2,1,0:T(8,128)(2,1)S(1)} %get-tuple-element.46), channel_id=1, source_target_pairs={{0,60},{1,61},{4,0},{5,1},{8,4},{9,5},{12,8},{13,9},{16,12},{17,13... | collective-permute-start | bytes 589832 | tf_op jit(solution)/shard_map/ppermute | solution.py:252
  74.9 1.9 %collective-permute-start.7 = (bf16[4,64,384]{2,1,0:T(8,128)(2,1)S(1)}, bf16[4,64,384]{2,1,0:T(8,128)(2,1)S(1)}, u32[]{:S(2)}, u32[]{:S(2)}) collective-permute-start(bf16[4,64,384]{2,1,0:T(8,128)(2,1)S(1)} %pad_maximum_fusion.n0_ref), channel_id=1, source_target_pairs={{0,4},{1,5},{4,8},{5,9},{8,12},{9,13},{12,16},{13,17},{16,20},{17,... | collective-permute-start | bytes 589832 | tf_op jit(solution)/shard_map/ppermute | solution.py:250
  76.8 0.0 collective-permute-done.4.r1_ref
  76.8 3.3 %collective-permute-start.8 = (bf16[4,64,384]{2,1,0:T(8,128)(2,1)S(1)}, bf16[4,64,384]{2,1,0:T(8,128)(2,1)S(1)}, u32[]{:S(2)}, u32[]{:S(2)}) collective-permute-start(bf16[4,64,384]{2,1,0:T(8,128)(2,1)S(1)} %pad_maximum_fusion.n0_ref), channel_id=1, source_target_pairs={{0,8},{1,57},{4,12},{5,61},{8,16},{9,1},{12,20},{13,5},{16,24},{17... | collective-permute-start | bytes 589832 | tf_op jit(solution)/shard_map/ppermute | solution.py:250
  80.1 0.0 collective-permute-done.5.r2_ref
  80.1 3.2 %collective-permute-start.9 = (bf16[4,64,384]{2,1,0:T(8,128)(2,1)S(1)}, bf16[4,64,384]{2,1,0:T(8,128)(2,1)S(1)}, u32[]{:S(2)}, u32[]{:S(2)}) collective-permute-start(bf16[4,64,384]{2,1,0:T(8,128)(2,1)S(1)} %pad_maximum_fusion.n0_ref), channel_id=1, source_target_pairs={{0,60},{1,61},{4,0},{5,1},{8,4},{9,5},{12,8},{13,9},{16,12},{17,13... | collective-permute-start | bytes 589832 | tf_op jit(solution)/shard_map/ppermute | solution.py:250
  83.4 0.0 collective-permute-done.6.r3_ref
  83.4 0.6 stage_sums.1
  84.0 3.7 %collective-permute-start.11 = (bf16[32,768]{1,0:T(8,128)(2,1)S(1)}, bf16[32,768]{1,0:T(8,128)(2,1)S(1)}, u32[]{:S(2)}, u32[]{:S(2)}) collective-permute-start(bf16[32,768]{1,0:T(8,128)(2,1)S(1)} %get-tuple-element.55), channel_id=1, source_target_pairs={{0,16},{4,20},{8,24},{12,28},{16,32},{20,36},{24,40},{28,44},{32,4... | collective-permute-start | bytes 147464 | tf_op jit(solution)/shard_map/ppermute | solution.py:257
  87.8 0.0 collective-permute-done.7.n1_ref
  87.8 6.0 %collective-permute-start.12 = (bf16[32,768]{1,0:T(8,128)(2,1)S(1)}, bf16[32,768]{1,0:T(8,128)(2,1)S(1)}, u32[]{:S(2)}, u32[]{:S(2)}) collective-permute-start(bf16[32,768]{1,0:T(8,128)(2,1)S(1)} %get-tuple-element.56), channel_id=1, source_target_pairs={{0,32},{4,36},{8,40},{12,44},{16,48},{20,52},{24,56},{28,60},{32,0... | collective-permute-start | bytes 147464 | tf_op jit(solution)/shard_map/ppermute | solution.py:257
  93.8 0.0 collective-permute-done.8.n2_ref
  93.8 4.3 %collective-permute-start.13 = (bf16[32,768]{1,0:T(8,128)(2,1)S(1)}, bf16[32,768]{1,0:T(8,128)(2,1)S(1)}, u32[]{:S(2)}, u32[]{:S(2)}) collective-permute-start(bf16[32,768]{1,0:T(8,128)(2,1)S(1)} %get-tuple-element.57), channel_id=1, source_target_pairs={{0,48},{4,52},{8,56},{12,60},{16,0},{20,4},{24,8},{28,12},{32,16},... | collective-permute-start | bytes 147464 | tf_op jit(solution)/shard_map/ppermute | solution.py:257
  98.1 0.0 collective-permute-done.9.n3_ref
  98.2 0.0 collective-permute-done.10.sib_ref
  98.2 5.8 %weight_sums.1 = bf16[384,3072]{1,0:T(8,128)(2,1)} custom-call(s32[4]{0:T(128)S(1)} %pad_add_fusion.info_ref, bf16[4,64,384]{2,1,0:T(8,128)(2,1)S(1)} %pad_maximum_fusion.n0_ref, bf16[4,64,384]{2,1,0:T(8,128)(2,1)S(1)} %collective-permute-done.7.n1_ref, bf16[4,64,384]{2,1,0:T(8,128)(2,1)S(1)} %collective-permute-done.8.n2_ref, ...), custom_call_target="tpu_custom_call" | custom-call | flops 2415919104 | bytes 10485760 | tf_op jit(solution)/shard_map/weight_sums/pallas_call | solution.py:160
  104.0 0.0 collective-permute-done.11.r1_ref
  104.0 0.0 collective-permute-done.12.r2_ref
  104.0 1.5 %collective-permute-done.13.r3_ref = bf16[32,768]{1,0:T(8,128)(2,1)S(1)} collective-permute-done((bf16[32,768]{1,0:T(8,128)(2,1)S(1)}, bf16[32,768]{1,0:T(8,128)(2,1)S(1)}, u32[]{:S(2)}, u32[]{:S(2)}) %collective-permute-start.13) | collective-permute-done | bytes 49184 | tf_op jit(solution)/shard_map/ppermute | solution.py:257
  105.5 4.7 %collective-permute-start.14 = (bf16[32,384]{1,0:T(8,128)(2,1)S(1)}, bf16[32,384]{1,0:T(8,128)(2,1)S(1)}, u32[]{:S(2)}, u32[]{:S(2)}) collective-permute-start(bf16[32,384]{1,0:T(8,128)(2,1)S(1)} %get-tuple-element.62), channel_id=1, source_target_pairs={{0,1},{1,0},{2,3},{3,2},{4,5},{5,4},{6,7},{7,6},{8,9},{9,8},{10,11... | collective-permute-start | bytes 73736 | tf_op jit(solution)/shard_map/ppermute | solution.py:263
  110.2 0.8 collective-permute-done.14
  111.1 0.6 pad_maximum_fusion.1
  (3 shorter events, 0.1 us)
Async XLA Ops:
  16.4 4.8 %copy-start = (bf16[384,3072]{1,0:T(8,128)(2,1)S(1)}, bf16[384,3072]{1,0:T(8,128)(2,1)}, u32[]{:S(2)}) copy-start(bf16[384,3072]{1,0:T(8,128)(2,1)} %w_own_ref.1) | copy-start | bytes 7077892
  16.4 14.6 %copy-start.1 = (bf16[64,384]{1,0:T(8,128)(2,1)S(1)}, bf16[64,384]{1,0:T(8,128)(2,1)}, u32[]{:S(2)}) copy-start(bf16[64,384]{1,0:T(8,128)(2,1)} %param.4) | copy-start | bytes 147460
  16.4 35.9 %all-to-all-start = ((bf16[4,4,32,3072]{3,2,1,0:T(8,128)(2,1)}), bf16[4,4,32,3072]{3,2,1,0:T(8,128)(2,1)}, u32[]{:S(2)}, u32[]{:S(2)}) async-start(bf16[4,4,32,3072]{3,2,1,0:T(8,128)(2,1)} %broadcast_in_dim.2), calls=%async_computation | async-start | bytes 6291456 | tf_op jit(solution)/shard_map/all_to_all | solution.py:232
  21.2 31.1 %collective-permute-start.2 = (bf16[384,3072]{1,0:T(8,128)(2,1)S(1)}, bf16[384,3072]{1,0:T(8,128)(2,1)}, u32[]{:S(2)}, u32[]{:S(2)}) collective-permute-start(bf16[384,3072]{1,0:T(8,128)(2,1)S(1)} %copy-done), channel_id=1, source_target_pairs={{0,1},{1,0},{2,3},{3,2},{4,5},{5,4},{6,7},{7,6},{8,9},{9,8},{10,11... | collective-permute-start | bytes 7077896 | tf_op jit(solution)/shard_map/ppermute | solution.py:231
  30.9 12.5 %collective-permute-start = (bf16[64,384]{1,0:T(8,128)(2,1)S(1)}, bf16[64,384]{1,0:T(8,128)(2,1)S(1)}, u32[]{:S(2)}, u32[]{:S(2)}) collective-permute-start(bf16[64,384]{1,0:T(8,128)(2,1)S(1)} %copy-done.1), channel_id=1, source_target_pairs={{0,48},{4,52},{8,56},{12,60},{16,0},{20,4},{24,8},{28,12},{32,16},... | collective-permute-start | bytes 147464 | tf_op jit(solution)/shard_map/ppermute | solution.py:240
  38.4 13.9 %collective-permute-start.1 = (bf16[64,384]{1,0:T(8,128)(2,1)S(1)}, bf16[64,384]{1,0:T(8,128)(2,1)S(1)}, u32[]{:S(2)}, u32[]{:S(2)}) collective-permute-start(bf16[64,384]{1,0:T(8,128)(2,1)S(1)} %copy-done.1), channel_id=1, source_target_pairs={{0,32},{4,36},{8,40},{12,44},{16,48},{20,52},{24,56},{28,60},{32,0... | collective-permute-start | bytes 147464 | tf_op jit(solution)/shard_map/ppermute | solution.py:240
  43.4 15.2 %collective-permute-start.3 = (bf16[64,384]{1,0:T(8,128)(2,1)S(1)}, bf16[64,384]{1,0:T(8,128)(2,1)S(1)}, u32[]{:S(2)}, u32[]{:S(2)}) collective-permute-start(bf16[64,384]{1,0:T(8,128)(2,1)S(1)} %copy-done.1), channel_id=1, source_target_pairs={{0,16},{4,20},{8,24},{12,28},{16,32},{20,36},{24,40},{28,44},{32,4... | collective-permute-start | bytes 147464 | tf_op jit(solution)/shard_map/ppermute | solution.py:242
  58.6 39.5 %collective-permute-start.10 = (bf16[512,3072]{1,0:T(8,128)(2,1)S(1)}, bf16[512,3072]{1,0:T(8,128)(2,1)S(1)}, u32[]{:S(2)}, u32[]{:S(2)}) collective-permute-start(bf16[512,3072]{1,0:T(8,128)(2,1)S(1)} %get-tuple-element.54.own_ref), channel_id=1, source_target_pairs={{0,1},{1,0},{2,3},{3,2},{4,5},{5,4},{6,7},{7,6},{8,9},{9,8},{10,11... | collective-permute-start | bytes 9437192 | tf_op jit(solution)/shard_map/ppermute | solution.py:254
  62.0 14.9 %collective-permute-start.4 = (bf16[4,32,768]{2,1,0:T(8,128)(2,1)S(1)}, bf16[4,32,768]{2,1,0:T(8,128)(2,1)S(1)}, u32[]{:S(2)}, u32[]{:S(2)}) collective-permute-start(bf16[4,32,768]{2,1,0:T(8,128)(2,1)S(1)} %get-tuple-element.44), channel_id=1, source_target_pairs={{0,4},{1,5},{4,8},{5,9},{8,12},{9,13},{12,16},{13,17},{16,20},{17,... | collective-permute-start | bytes 589832 | tf_op jit(solution)/shard_map/ppermute | solution.py:252
  66.2 13.9 %collective-permute-start.5 = (bf16[4,32,768]{2,1,0:T(8,128)(2,1)S(1)}, bf16[4,32,768]{2,1,0:T(8,128)(2,1)S(1)}, u32[]{:S(2)}, u32[]{:S(2)}) collective-permute-start(bf16[4,32,768]{2,1,0:T(8,128)(2,1)S(1)} %get-tuple-element.45), channel_id=1, source_target_pairs={{0,8},{1,57},{4,12},{5,61},{8,16},{9,1},{12,20},{13,5},{16,24},{17... | collective-permute-start | bytes 589832 | tf_op jit(solution)/shard_map/ppermute | solution.py:252
  71.5 11.8 %collective-permute-start.6 = (bf16[4,32,768]{2,1,0:T(8,128)(2,1)S(1)}, bf16[4,32,768]{2,1,0:T(8,128)(2,1)S(1)}, u32[]{:S(2)}, u32[]{:S(2)}) collective-permute-start(bf16[4,32,768]{2,1,0:T(8,128)(2,1)S(1)} %get-tuple-element.46), channel_id=1, source_target_pairs={{0,60},{1,61},{4,0},{5,1},{8,4},{9,5},{12,8},{13,9},{16,12},{17,13... | collective-permute-start | bytes 589832 | tf_op jit(solution)/shard_map/ppermute | solution.py:252
  74.9 12.8 %collective-permute-start.7 = (bf16[4,64,384]{2,1,0:T(8,128)(2,1)S(1)}, bf16[4,64,384]{2,1,0:T(8,128)(2,1)S(1)}, u32[]{:S(2)}, u32[]{:S(2)}) collective-permute-start(bf16[4,64,384]{2,1,0:T(8,128)(2,1)S(1)} %pad_maximum_fusion.n0_ref), channel_id=1, source_target_pairs={{0,4},{1,5},{4,8},{5,9},{8,12},{9,13},{12,16},{13,17},{16,20},{17,... | collective-permute-start | bytes 589832 | tf_op jit(solution)/shard_map/ppermute | solution.py:250
  76.8 17.0 %collective-permute-start.8 = (bf16[4,64,384]{2,1,0:T(8,128)(2,1)S(1)}, bf16[4,64,384]{2,1,0:T(8,128)(2,1)S(1)}, u32[]{:S(2)}, u32[]{:S(2)}) collective-permute-start(bf16[4,64,384]{2,1,0:T(8,128)(2,1)S(1)} %pad_maximum_fusion.n0_ref), channel_id=1, source_target_pairs={{0,8},{1,57},{4,12},{5,61},{8,16},{9,1},{12,20},{13,5},{16,24},{17... | collective-permute-start | bytes 589832 | tf_op jit(solution)/shard_map/ppermute | solution.py:250
  80.1 18.0 %collective-permute-start.9 = (bf16[4,64,384]{2,1,0:T(8,128)(2,1)S(1)}, bf16[4,64,384]{2,1,0:T(8,128)(2,1)S(1)}, u32[]{:S(2)}, u32[]{:S(2)}) collective-permute-start(bf16[4,64,384]{2,1,0:T(8,128)(2,1)S(1)} %pad_maximum_fusion.n0_ref), channel_id=1, source_target_pairs={{0,60},{1,61},{4,0},{5,1},{8,4},{9,5},{12,8},{13,9},{16,12},{17,13... | collective-permute-start | bytes 589832 | tf_op jit(solution)/shard_map/ppermute | solution.py:250
  84.0 19.9 %collective-permute-start.11 = (bf16[32,768]{1,0:T(8,128)(2,1)S(1)}, bf16[32,768]{1,0:T(8,128)(2,1)S(1)}, u32[]{:S(2)}, u32[]{:S(2)}) collective-permute-start(bf16[32,768]{1,0:T(8,128)(2,1)S(1)} %get-tuple-element.55), channel_id=1, source_target_pairs={{0,16},{4,20},{8,24},{12,28},{16,32},{20,36},{24,40},{28,44},{32,4... | collective-permute-start | bytes 147464 | tf_op jit(solution)/shard_map/ppermute | solution.py:257
  87.8 16.2 %collective-permute-start.12 = (bf16[32,768]{1,0:T(8,128)(2,1)S(1)}, bf16[32,768]{1,0:T(8,128)(2,1)S(1)}, u32[]{:S(2)}, u32[]{:S(2)}) collective-permute-start(bf16[32,768]{1,0:T(8,128)(2,1)S(1)} %get-tuple-element.56), channel_id=1, source_target_pairs={{0,32},{4,36},{8,40},{12,44},{16,48},{20,52},{24,56},{28,60},{32,0... | collective-permute-start | bytes 147464 | tf_op jit(solution)/shard_map/ppermute | solution.py:257
  93.8 11.7 %collective-permute-start.13 = (bf16[32,768]{1,0:T(8,128)(2,1)S(1)}, bf16[32,768]{1,0:T(8,128)(2,1)S(1)}, u32[]{:S(2)}, u32[]{:S(2)}) collective-permute-start(bf16[32,768]{1,0:T(8,128)(2,1)S(1)} %get-tuple-element.57), channel_id=1, source_target_pairs={{0,48},{4,52},{8,56},{12,60},{16,0},{20,4},{24,8},{28,12},{32,16},... | collective-permute-start | bytes 147464 | tf_op jit(solution)/shard_map/ppermute | solution.py:257
  105.5 5.6 %collective-permute-start.14 = (bf16[32,384]{1,0:T(8,128)(2,1)S(1)}, bf16[32,384]{1,0:T(8,128)(2,1)S(1)}, u32[]{:S(2)}, u32[]{:S(2)}) collective-permute-start(bf16[32,384]{1,0:T(8,128)(2,1)S(1)} %get-tuple-element.62), channel_id=1, source_target_pairs={{0,1},{1,0},{2,3},{3,2},{4,5},{5,4},{6,7},{7,6},{8,9},{9,8},{10,11... | collective-permute-start | bytes 73736 | tf_op jit(solution)/shard_map/ppermute | solution.py:263

commit v5 on v3

--- a/solution.py
+++ b/solution.py
@@ -42,14 +42,13 @@
     return pl.ds(pl.multiple_of(k * 32, 32), 32)
 
 
-def partial_kernel(info_ref, l0_ref, l1_ref, l2_ref, l3_ref, w_own_ref, w_sib_ref, own_ref, s1_ref, s2_ref, s3_ref, plane_ref, plane, w, acc, sems):
-    second = info_ref[2]
+def partial_kernel(info_ref, lines_ref, w_own_ref, w_sib_ref, own_ref, send_ref, plane_ref, w, acc, sems):
     copies = []
-    for d, ref in enumerate((l0_ref, l1_ref, l2_ref, l3_ref)):
+    for j in range(4):
         for i in range(4):
-            k = chip_number(info_ref, i, lax.rem(second + d, 4))
+            rows = block_rows(chip_number(info_ref, i, j))
             copies.append(
-                pltpu.make_async_copy(ref.at[i], plane.at[block_rows(k), :], sems.at[d * 4 + i])
+                pltpu.make_async_copy(lines_ref.at[j, i], plane_ref.at[rows, :], sems.at[j * 4 + i])
             )
     weights = [
         pltpu.make_async_copy(ref, w.at[n], sems.at[16 + n])
@@ -59,36 +58,34 @@
         copy.start()
     for copy in copies:
         copy.wait()
-    result = pltpu.make_async_copy(plane, plane_ref, sems.at[18])
-    result.start()
     for n, copy in enumerate(weights):
         copy.wait()
         acc[:, n * 384 : (n + 1) * 384] = lax.dot_general(
-            plane[...], w[n], ROWS_BY_ROWS, preferred_element_type=jnp.float32
+            plane_ref[...], w[n], ROWS_BY_ROWS, preferred_element_type=jnp.float32
         )
-    result.wait()
-    for d, out in enumerate((own_ref, s1_ref, s2_ref, s3_ref)):
-        residue = lax.rem(info_ref[0] + d, 4)
-        for x in range(4):
-            out[x] = acc[block_rows(x * 4 + residue), :].astype(out.dtype)
+    residue = lax.rem(info_ref[0], 4)
+    for x in range(4):
+        own_ref[x] = acc[block_rows(x * 4 + residue), :]
+        for r in range(4):
+            send_ref[r, x] = acc[(x * 4 + r) * 32 : (x * 4 + r + 1) * 32, :].astype(jnp.bfloat16)
 
 
 def partial_sums(info, lines, w_own, w_sib):
-    shape = (4, 32, 768)
     return pl.pallas_call(
         partial_kernel,
-        out_shape=[jax.ShapeDtypeStruct(shape, jnp.float32)]
-        + [jax.ShapeDtypeStruct(shape, jnp.bfloat16)] * 3
-        + [jax.ShapeDtypeStruct((512, 3072), jnp.bfloat16)],
-        in_specs=[smem()] + [pl.BlockSpec(memory_space=pl.ANY)] * 6,
-        out_specs=[vmem()] * 4 + [pl.BlockSpec(memory_space=pl.ANY)],
+        out_shape=[
+            jax.ShapeDtypeStruct((4, 32, 768), jnp.float32),
+            jax.ShapeDtypeStruct((4, 4, 32, 768), jnp.bfloat16),
+            jax.ShapeDtypeStruct((512, 3072), jnp.bfloat16),
+        ],
+        in_specs=[smem()] + [pl.BlockSpec(memory_space=pl.ANY)] * 3,
+        out_specs=[vmem()] * 3,
         scratch_shapes=[
-            pltpu.VMEM((512, 3072), jnp.bfloat16),
             pltpu.VMEM((2, 384, 3072), jnp.bfloat16),
             pltpu.VMEM((512, 768), jnp.float32),
-            pltpu.SemaphoreType.DMA((19,)),
+            pltpu.SemaphoreType.DMA((18,)),
         ],
-        compiler_params=pltpu.CompilerParams(vmem_limit_bytes=52 * MIB),
+        compiler_params=pltpu.CompilerParams(vmem_limit_bytes=44 * MIB),
         cost_estimate=pl.CostEstimate(
             flops=2 * 512 * 3072 * 768, bytes_accessed=8 * MIB, transcendentals=0
         ),
@@ -96,12 +93,12 @@
     )(info, *lines, w_own, w_sib)
 
 
-def stage_kernel(info_ref, own_ref, r1_ref, r2_ref, r3_ref, out_ref):
-    core = info_ref[3]
+def stage_kernel(info_ref, own_ref, r_ref, out_ref):
+    residue, core = lax.rem(info_ref[0], 4), info_ref[3]
     for i in range(4):
         total = own_ref[i]
-        for r in (r1_ref, r2_ref, r3_ref):
-            total = total + r[i].astype(jnp.float32)
+        for d in range(1, 4):
+            total = total + r_ref[lax.rem(residue + d, 4), i].astype(jnp.float32)
         total = total.astype(jnp.bfloat16)
         out_ref[i, core] = total[:, :384]
         out_ref[i, 1 - core] = total[:, 384:]
@@ -111,12 +108,12 @@
     return pl.pallas_call(
         stage_kernel,
         out_shape=jax.ShapeDtypeStruct((4, 2, 32, 384), jnp.bfloat16),
-        in_specs=[smem()] + [vmem()] * 4,
+        in_specs=[smem()] + [vmem()] * 2,
         out_specs=vmem(),
         compiler_params=pltpu.CompilerParams(vmem_limit_bytes=8 * MIB),
         cost_estimate=pl.CostEstimate(flops=400000, bytes_accessed=MIB, transcendentals=0),
         name="stage_sums",
-    )(info, own, *received)
+    )(info, own, received)
 
 
 def weight_kernel(info_ref, n0_ref, n1_ref, n2_ref, n3_ref, own_ref, sib_ref, out_ref, tokens, left):
@@ -124,9 +121,9 @@
     @pl.when(pl.program_id(0) == 0)
     def _():
         z, core = info_ref[0], info_ref[3]
-        for d, ref in enumerate((n0_ref, n1_ref, n2_ref, n3_ref)):
+        for ref, far in ((n0_ref, 0), (n1_ref, -1), (n2_ref, 4 * core - 2), (n3_ref, 1)):
             for e in range(4):
-                k = 4 * e + lax.rem(z + 4 - d, 4)
+                k = lax.rem(z + far + 4 * e + 16, 16)
                 for which in range(2):
                     half = core if which == 0 else 1 - core
                     rows = pl.ds(pl.multiple_of(which * 512 + k * 32, 32), 32)
@@ -154,7 +151,7 @@
                 pltpu.VMEM((384, 1024), jnp.bfloat16),
             ],
         ),
-        compiler_params=pltpu.CompilerParams(vmem_limit_bytes=53 * MIB),
+        compiler_params=pltpu.CompilerParams(vmem_limit_bytes=24 * MIB),
         cost_estimate=pl.CostEstimate(
             flops=2 * 1024 * 3072 * 384, bytes_accessed=10 * MIB, transcendentals=0
         ),
@@ -173,8 +170,27 @@
     return pairs
 
 
+def near_groups():
+    groups = []
+    for start in range(0, 16, 4):
+        groups.append([(start + i) * 2 for i in range(4)])
+        groups.append([(start + i) % 16 * 2 + 1 for i in (4, 5, 2, 3)])
+    return groups
+
+
+def far_shift(by):
+    return [(z, (z + 4 * by) % 16) for z in range(16)]
+
+
 def column_shift(by):
     return [(z * 2 + c, (z + by[c]) % 16 * 2 + c) for z in range(16) for c in range(2)]
+
+
+def second_axis_groups():
+    place = [[[(x * 4 + y) * 2 + c for c in range(2)] for y in range(4)] for x in range(4)]
+    along_y = [[place[j][i][0] for i in range(4)] for j in range(4)]
+    along_x = [[place[i][j][1] for i in range(4)] for j in range(4)]
+    return along_y + along_x
 
 
 def first_axis_groups():
@@ -199,23 +215,33 @@
     line = lax.all_gather(
         local, PLANE, axis=0, tiled=True, axis_index_groups=first_axis_groups()
     ).reshape(4, 32, 3072)
-    weight_then, line = lax.optimization_barrier((weight, line))
+    weight_then, inputs, line = lax.optimization_barrier((weight, inputs, line))
     w_sib = lax.ppermute(weight_then, "core", swap)
-    inputs, w_sib = lax.optimization_barrier((inputs, w_sib))
-    lines = [line] + [lax.ppermute(line, PLANE, plane_shift(False, -d)) for d in (1, 2, 3)]
-    near = lax.all_to_all(
-        jnp.broadcast_to(inputs[None], (4, 64, 384)), "zh", split_axis=0, concat_axis=0, tiled=True
-    )
-    lines, near = lax.optimization_barrier((lines, near))
-
-    own, *sends, hg_own = partial_sums(info, lines, weight, w_sib)
+    lines = lax.all_to_all(
+        jnp.broadcast_to(line[None], (4, 4, 32, 3072)),
+        PLANE,
+        split_axis=0,
+        concat_axis=0,
+        tiled=True,
+        axis_index_groups=second_axis_groups(),
+    )
+    near = [inputs] + [lax.ppermute(inputs, Z, far_shift(-d)) for d in (1, 2, 3)]
+
+    own, send, hg_own = partial_sums(info, [lines], weight, w_sib)
+    received = lax.all_to_all(
+        send,
+        Z + ("core",),
+        split_axis=0,
+        concat_axis=0,
+        tiled=True,
+        axis_index_groups=near_groups(),
+    )
     own, near = lax.optimization_barrier((own, near))
-    received = [
-        lax.ppermute(s, Z + ("core",), column_shift(by)) for s, by in zip(sends, NEAR)
-    ]
+    near, hg_own = lax.optimization_barrier((jnp.stack(near), hg_own))
     nears = [near] + [lax.ppermute(near, Z + ("core",), column_shift(by)) for by in NEAR]
     hg_sib = lax.ppermute(hg_own, "core", swap)
     summed = stage_sums(info, own, received).reshape(8, 32, 384)
+    summed, nears = lax.optimization_barrier((summed, nears))
     summed = lax.all_to_all(summed, ("zh", "core"), split_axis=0, concat_axis=0, tiled=True)
     weight_total = weight_sums(info, nears, hg_own, hg_sib)
     weight_total, summed = lax.optimization_barrier((weight_total, summed))

time: 126 us -> 119 us (0.944)
  the two profiles are of different devices: /device:TPU:1 before, /device:TPU:32 now
where the time goes in v5:
time: 119 us; the launch traced here: 118 us
  starting transfers between devices  57.5 us (48%)
  waiting for transfers between devices  23.4 us (20%)
  Pallas kernels  18.3 us (15%)
  blocking collectives  13.7 us (12%)
  other arithmetic  2.08 us (2%)
  local copies, waits for them, and re-layouts  2.07 us (2%)
    ppermute x3, starting transfers between devices, per_device(): lax.ppermute(inputs, Z, far_shift(-d))  24.6 us
    all_gather x1, blocking collectives, per_device(): lax.all_gather(local, PLANE, axis=0, tiled=True, axis_index_groups=first_...  13.7 us
    all_to_all x1, waiting for transfers between devices, per_device(): lax.all_to_all(send, Z + ('core',), split_axis=0, concat_axis=0, tiled=Tr...  11.8 us
    all_to_all x1, waiting for transfers between devices, per_device(): lax.all_to_all(summed, ('zh', 'core'), split_axis=0, concat_axis=0, tiled...  11.5 us
    ppermute x3, starting transfers between devices, per_device(): lax.ppermute(near, Z + ('core',), column_shift(by))  10.1 us
    all_to_all x1, starting transfers between devices, per_device(): lax.all_to_all(summed, ('zh', 'core'), split_axis=0, concat_axis=0, tiled...  9.71 us
    pallas_call x1, Pallas kernels, partial_sums(): pl.pallas_call(partial_kernel, out_shape=[jax.ShapeDtypeStruct((4, 32, 76...  8.96 us
    pallas_call x1, Pallas kernels, weight_sums(): pl.pallas_call(weight_kernel, out_shape=jax.ShapeDtypeStruct((384, 3072),...  8.04 us
  transfers between devices with their start and end apart: 11, of which 2 were waited for; matrix products, arithmetic and copies ran while one was open for 0% of the time, Pallas kernels for 16%

profile of v5, /device:TPU:32, one launch (start us, length us, event | category | flops | bytes accessed | tf_op | source)
XLA Modules:
  0.0 117.8 jit_solution(4243475804471776337)
XLA Ops:
  0.6 1.3 %fusion.7 = bf16[32,3072]{1,0:T(8,128)(2,1)S(1)} fusion(bf16[32,3072]{1,0:T(8,128)(2,1)} %param.7, bf16[32,3072]{1,0:T(8,128)(2,1)} %param.6), kind=kLoop, calls=%fused_computation.14 | loop fusion | flops 2064384 | bytes 589824 | tf_op jit(solution)/shard_map/convert_element_type | solution.py:214
  1.9 13.7 %all_gather.3 = bf16[128,3072]{1,0:T(8,128)(2,1)S(1)} all-gather(bf16[32,3072]{1,0:T(8,128)(2,1)S(1)} %fusion.7), channel_id=1, replica_groups={{0,128,256,384},{2,130,258,386},{64,192,320,448},{66,194,322,450},{1,3,..., dimensions={0}, use_global_device_ids=true | all-gather | bytes 983040 | tf_op jit(solution)/shard_map/all_gather | solution.py:215
  15.6 2.1 %broadcast_in_dim.2 = bf16[4,4,32,3072]{3,2,1,0:T(8,128)(2,1)} broadcast(bf16[4,32,3072]{2,1,0:T(8,128)(2,1)S(1)} %bitcast.11), dimensions={1,2,3} | broadcast | bytes 3932160 | tf_op jit(solution)/shard_map/broadcast_in_dim | solution.py:221
  17.7 0.0 copy-start
  17.7 4.8 %all-to-all-start = ((bf16[4,4,32,3072]{3,2,1,0:T(8,128)(2,1)}), bf16[4,4,32,3072]{3,2,1,0:T(8,128)(2,1)}, u32[]{:S(2)}, u32[]{:S(2)}) async-start(bf16[4,4,32,3072]{3,2,1,0:T(8,128)(2,1)} %broadcast_in_dim.2), calls=%async_computation | async-start | bytes 6291456 | tf_op jit(solution)/shard_map/all_to_all | solution.py:220
  22.5 1.9 %collective-permute-start = (bf16[384,3072]{1,0:T(8,128)(2,1)}, bf16[384,3072]{1,0:T(8,128)(2,1)}, u32[]{:S(2)}, u32[]{:S(2)}) collective-permute-start(bf16[384,3072]{1,0:T(8,128)(2,1)} %w_own_ref.1), channel_id=1, source_target_pairs={{0,1},{1,0},{2,3},{3,2},{4,5},{5,4},{6,7},{7,6},{8,9},{9,8},{10,11... | collective-permute-start | bytes 7077896 | tf_op jit(solution)/shard_map/ppermute | solution.py:219
  24.4 0.0 copy-done
  24.4 11.8 %collective-permute-start.1 = (bf16[64,384]{1,0:T(8,128)(2,1)S(1)}, bf16[64,384]{1,0:T(8,128)(2,1)S(1)}, u32[]{:S(2)}, u32[]{:S(2)}) collective-permute-start(bf16[64,384]{1,0:T(8,128)(2,1)S(1)} %copy-done), channel_id=1, source_target_pairs={{0,48},{4,52},{8,56},{12,60},{16,0},{20,4},{24,8},{28,12},{32,16},... | collective-permute-start | bytes 147464 | tf_op jit(solution)/shard_map/ppermute | solution.py:228
  36.2 4.9 %collective-permute-start.2 = (bf16[64,384]{1,0:T(8,128)(2,1)S(1)}, bf16[64,384]{1,0:T(8,128)(2,1)S(1)}, u32[]{:S(2)}, u32[]{:S(2)}) collective-permute-start(bf16[64,384]{1,0:T(8,128)(2,1)S(1)} %copy-done), channel_id=1, source_target_pairs={{0,32},{4,36},{8,40},{12,44},{16,48},{20,52},{24,56},{28,60},{32,0... | collective-permute-start | bytes 147464 | tf_op jit(solution)/shard_map/ppermute | solution.py:228
  41.2 7.8 %collective-permute-start.3 = (bf16[64,384]{1,0:T(8,128)(2,1)S(1)}, bf16[64,384]{1,0:T(8,128)(2,1)S(1)}, u32[]{:S(2)}, u32[]{:S(2)}) collective-permute-start(bf16[64,384]{1,0:T(8,128)(2,1)S(1)} %copy-done), channel_id=1, source_target_pairs={{0,16},{4,20},{8,24},{12,28},{16,32},{20,36},{24,40},{28,44},{32,4... | collective-permute-start | bytes 147464 | tf_op jit(solution)/shard_map/ppermute | solution.py:228
  49.0 0.1 pad_add_fusion.info_ref
  49.1 0.0 all-to-all-done.lines_ref
  49.1 0.0 collective-permute-done.w_sib_ref
  49.1 9.0 %partial_sums.1 = (f32[4,32,768]{2,1,0:T(8,128)S(1)}, bf16[4,4,32,768]{3,2,1,0:T(8,128)(2,1)}, bf16[512,3072]{1,0:T(8,128)(2,1)}) custom-call(s32[4]{0:T(128)S(1)} %pad_add_fusion.info_ref, bf16[4,4,32,3072]{3,2,1,0:T(8,128)(2,1)} %all-to-all-done.lines_ref, bf16[384,3072]{1,0:T(8,128)(2,1)} %w_own_ref.1, bf16[384,3072]{1,0:T(8,128)(2,1)} %collective-permute-done.w_sib_ref), custom_call_target="tpu_custom_call" | custom-call | flops 2415919104 | bytes 8388608 | tf_op jit(solution)/shard_map/partial_sums/pallas_call | solution.py:74
  58.1 0.0 collective-permute-done.1
  58.1 0.0 collective-permute-done.2
  58.1 0.0 collective-permute-done.3
  58.1 1.9 %collective-permute-start.7 = (bf16[512,3072]{1,0:T(8,128)(2,1)}, bf16[512,3072]{1,0:T(8,128)(2,1)}, u32[]{:S(2)}, u32[]{:S(2)}) collective-permute-start(bf16[512,3072]{1,0:T(8,128)(2,1)} %get-tuple-element.38.own_ref), channel_id=1, source_target_pairs={{0,1},{1,0},{2,3},{3,2},{4,5},{5,4},{6,7},{7,6},{8,9},{9,8},{10,11... | collective-permute-start | bytes 9437192 | tf_op jit(solution)/shard_map/ppermute | solution.py:242
  60.1 4.5 %all-to-all-start.1 = ((bf16[4,4,32,768]{3,2,1,0:T(8,128)(2,1)}), bf16[4,4,32,768]{3,2,1,0:T(8,128)(2,1)S(1)}, u32[]{:S(2)}, u32[]{:S(2)}) async-start(bf16[4,4,32,768]{3,2,1,0:T(8,128)(2,1)} %get-tuple-element.27), calls=%async_computation.1 | async-start | bytes 1572864 | tf_op jit(solution)/shard_map/all_to_all | solution.py:231
  64.6 3.4 %collective-permute-start.4 = (bf16[4,64,384]{2,1,0:T(8,128)(2,1)S(1)}, bf16[4,64,384]{2,1,0:T(8,128)(2,1)S(1)}, u32[]{:S(2)}, u32[]{:S(2)}) collective-permute-start(bf16[4,64,384]{2,1,0:T(8,128)(2,1)S(1)} %pad_maximum_fusion.n0_ref), channel_id=1, source_target_pairs={{0,4},{1,5},{4,8},{5,9},{8,12},{9,13},{12,16},{13,17},{16,20},{17,... | collective-permute-start | bytes 589832 | tf_op jit(solution)/shard_map/ppermute | solution.py:241
  67.9 3.8 %collective-permute-start.5 = (bf16[4,64,384]{2,1,0:T(8,128)(2,1)S(1)}, bf16[4,64,384]{2,1,0:T(8,128)(2,1)S(1)}, u32[]{:S(2)}, u32[]{:S(2)}) collective-permute-start(bf16[4,64,384]{2,1,0:T(8,128)(2,1)S(1)} %pad_maximum_fusion.n0_ref), channel_id=1, source_target_pairs={{0,8},{1,57},{4,12},{5,61},{8,16},{9,1},{12,20},{13,5},{16,24},{17... | collective-permute-start | bytes 589832 | tf_op jit(solution)/shard_map/ppermute | solution.py:241
  71.8 2.9 %collective-permute-start.6 = (bf16[4,64,384]{2,1,0:T(8,128)(2,1)S(1)}, bf16[4,64,384]{2,1,0:T(8,128)(2,1)S(1)}, u32[]{:S(2)}, u32[]{:S(2)}) collective-permute-start(bf16[4,64,384]{2,1,0:T(8,128)(2,1)S(1)} %pad_maximum_fusion.n0_ref), channel_id=1, source_target_pairs={{0,60},{1,61},{4,0},{5,1},{8,4},{9,5},{12,8},{13,9},{16,12},{17,13... | collective-permute-start | bytes 589832 | tf_op jit(solution)/shard_map/ppermute | solution.py:241
  74.7 11.8 %all-to-all-done.1.r_ref = bf16[4,4,32,768]{3,2,1,0:T(8,128)(2,1)S(1)} async-done(((bf16[4,4,32,768]{3,2,1,0:T(8,128)(2,1)}), bf16[4,4,32,768]{3,2,1,0:T(8,128)(2,1)S(1)}, u32[]{:S(2)}, u32[]{:S(2)}) %all-to-all-start.1) | async-done | bytes 786464 | tf_op jit(solution)/shard_map/all_to_all | solution.py:231
  86.5 1.3 %stage_sums.1 = bf16[4,2,32,384]{3,2,1,0:T(8,128)(2,1)} custom-call(s32[4]{0:T(128)S(1)} %pad_add_fusion.info_ref, f32[4,32,768]{2,1,0:T(8,128)S(1)} %get-tuple-element.26.own_ref, bf16[4,4,32,768]{3,2,1,0:T(8,128)(2,1)S(1)} %all-to-all-done.1.r_ref), custom_call_target="tpu_custom_call" | custom-call | flops 400000 | bytes 1048576 | tf_op jit(solution)/shard_map/stage_sums/pallas_call | solution.py:108
  87.8 0.0 collective-permute-done.4.n1_ref
  87.8 0.0 collective-permute-done.5.n2_ref
  87.8 0.0 collective-permute-done.6.n3_ref
  87.8 9.7 %all-to-all-start.2 = ((bf16[8,32,384]{2,1,0:T(8,128)(2,1)}), bf16[8,32,384]{2,1,0:T(8,128)(2,1)S(1)}, u32[]{:S(2)}, u32[]{:S(2)}) async-start(bf16[8,32,384]{2,1,0:T(8,128)(2,1)} %bitcast.5), calls=%async_computation.2 | async-start | bytes 393216 | tf_op jit(solution)/shard_map/all_to_all | solution.py:245
  97.5 0.0 collective-permute-done.7.sib_ref
  97.5 8.0 %weight_sums.1 = bf16[384,3072]{1,0:T(8,128)(2,1)} custom-call(s32[4]{0:T(128)S(1)} %pad_add_fusion.info_ref, bf16[4,64,384]{2,1,0:T(8,128)(2,1)S(1)} %pad_maximum_fusion.n0_ref, bf16[4,64,384]{2,1,0:T(8,128)(2,1)S(1)} %collective-permute-done.4.n1_ref, bf16[4,64,384]{2,1,0:T(8,128)(2,1)S(1)} %collective-permute-done.5.n2_ref, ...), custom_call_target="tpu_custom_call" | custom-call | flops 2415919104 | bytes 10485760 | tf_op jit(solution)/shard_map/weight_sums/pallas_call | solution.py:140
  105.6 11.5 %all-to-all-done.2 = bf16[8,32,384]{2,1,0:T(8,128)(2,1)S(1)} async-done(((bf16[8,32,384]{2,1,0:T(8,128)(2,1)}), bf16[8,32,384]{2,1,0:T(8,128)(2,1)S(1)}, u32[]{:S(2)}, u32[]{:S(2)}) %all-to-all-start.2) | async-done | bytes 196640 | tf_op jit(solution)/shard_map/all_to_all | solution.py:245
  117.1 0.6 fusion.9
  (2 shorter events, 0.1 us)
Async XLA Ops:
  17.7 6.7 %copy-start = (bf16[64,384]{1,0:T(8,128)(2,1)S(1)}, bf16[64,384]{1,0:T(8,128)(2,1)}, u32[]{:S(2)}) copy-start(bf16[64,384]{1,0:T(8,128)(2,1)} %param.4) | copy-start | bytes 147460
  17.7 31.4 %all-to-all-start = ((bf16[4,4,32,3072]{3,2,1,0:T(8,128)(2,1)}), bf16[4,4,32,3072]{3,2,1,0:T(8,128)(2,1)}, u32[]{:S(2)}, u32[]{:S(2)}) async-start(bf16[4,4,32,3072]{3,2,1,0:T(8,128)(2,1)} %broadcast_in_dim.2), calls=%async_computation | async-start | bytes 6291456 | tf_op jit(solution)/shard_map/all_to_all | solution.py:220
  22.5 26.6 %collective-permute-start = (bf16[384,3072]{1,0:T(8,128)(2,1)}, bf16[384,3072]{1,0:T(8,128)(2,1)}, u32[]{:S(2)}, u32[]{:S(2)}) collective-permute-start(bf16[384,3072]{1,0:T(8,128)(2,1)} %w_own_ref.1), channel_id=1, source_target_pairs={{0,1},{1,0},{2,3},{3,2},{4,5},{5,4},{6,7},{7,6},{8,9},{9,8},{10,11... | collective-permute-start | bytes 7077896 | tf_op jit(solution)/shard_map/ppermute | solution.py:219
  24.4 33.7 %collective-permute-start.1 = (bf16[64,384]{1,0:T(8,128)(2,1)S(1)}, bf16[64,384]{1,0:T(8,128)(2,1)S(1)}, u32[]{:S(2)}, u32[]{:S(2)}) collective-permute-start(bf16[64,384]{1,0:T(8,128)(2,1)S(1)} %copy-done), channel_id=1, source_target_pairs={{0,48},{4,52},{8,56},{12,60},{16,0},{20,4},{24,8},{28,12},{32,16},... | collective-permute-start | bytes 147464 | tf_op jit(solution)/shard_map/ppermute | solution.py:228
  36.2 21.8 %collective-permute-start.2 = (bf16[64,384]{1,0:T(8,128)(2,1)S(1)}, bf16[64,384]{1,0:T(8,128)(2,1)S(1)}, u32[]{:S(2)}, u32[]{:S(2)}) collective-permute-start(bf16[64,384]{1,0:T(8,128)(2,1)S(1)} %copy-done), channel_id=1, source_target_pairs={{0,32},{4,36},{8,40},{12,44},{16,48},{20,52},{24,56},{28,60},{32,0... | collective-permute-start | bytes 147464 | tf_op jit(solution)/shard_map/ppermute | solution.py:228
  41.2 16.9 %collective-permute-start.3 = (bf16[64,384]{1,0:T(8,128)(2,1)S(1)}, bf16[64,384]{1,0:T(8,128)(2,1)S(1)}, u32[]{:S(2)}, u32[]{:S(2)}) collective-permute-start(bf16[64,384]{1,0:T(8,128)(2,1)S(1)} %copy-done), channel_id=1, source_target_pairs={{0,16},{4,20},{8,24},{12,28},{16,32},{20,36},{24,40},{28,44},{32,4... | collective-permute-start | bytes 147464 | tf_op jit(solution)/shard_map/ppermute | solution.py:228
  58.1 39.4 %collective-permute-start.7 = (bf16[512,3072]{1,0:T(8,128)(2,1)}, bf16[512,3072]{1,0:T(8,128)(2,1)}, u32[]{:S(2)}, u32[]{:S(2)}) collective-permute-start(bf16[512,3072]{1,0:T(8,128)(2,1)} %get-tuple-element.38.own_ref), channel_id=1, source_target_pairs={{0,1},{1,0},{2,3},{3,2},{4,5},{5,4},{6,7},{7,6},{8,9},{9,8},{10,11... | collective-permute-start | bytes 9437192 | tf_op jit(solution)/shard_map/ppermute | solution.py:242
  60.1 26.4 %all-to-all-start.1 = ((bf16[4,4,32,768]{3,2,1,0:T(8,128)(2,1)}), bf16[4,4,32,768]{3,2,1,0:T(8,128)(2,1)S(1)}, u32[]{:S(2)}, u32[]{:S(2)}) async-start(bf16[4,4,32,768]{3,2,1,0:T(8,128)(2,1)} %get-tuple-element.27), calls=%async_computation.1 | async-start | bytes 1572864 | tf_op jit(solution)/shard_map/all_to_all | solution.py:231
  64.6 23.3 %collective-permute-start.4 = (bf16[4,64,384]{2,1,0:T(8,128)(2,1)S(1)}, bf16[4,64,384]{2,1,0:T(8,128)(2,1)S(1)}, u32[]{:S(2)}, u32[]{:S(2)}) collective-permute-start(bf16[4,64,384]{2,1,0:T(8,128)(2,1)S(1)} %pad_maximum_fusion.n0_ref), channel_id=1, source_target_pairs={{0,4},{1,5},{4,8},{5,9},{8,12},{9,13},{12,16},{13,17},{16,20},{17,... | collective-permute-start | bytes 589832 | tf_op jit(solution)/shard_map/ppermute | solution.py:241
  67.9 19.9 %collective-permute-start.5 = (bf16[4,64,384]{2,1,0:T(8,128)(2,1)S(1)}, bf16[4,64,384]{2,1,0:T(8,128)(2,1)S(1)}, u32[]{:S(2)}, u32[]{:S(2)}) collective-permute-start(bf16[4,64,384]{2,1,0:T(8,128)(2,1)S(1)} %pad_maximum_fusion.n0_ref), channel_id=1, source_target_pairs={{0,8},{1,57},{4,12},{5,61},{8,16},{9,1},{12,20},{13,5},{16,24},{17... | collective-permute-start | bytes 589832 | tf_op jit(solution)/shard_map/ppermute | solution.py:241
  71.8 16.1 %collective-permute-start.6 = (bf16[4,64,384]{2,1,0:T(8,128)(2,1)S(1)}, bf16[4,64,384]{2,1,0:T(8,128)(2,1)S(1)}, u32[]{:S(2)}, u32[]{:S(2)}) collective-permute-start(bf16[4,64,384]{2,1,0:T(8,128)(2,1)S(1)} %pad_maximum_fusion.n0_ref), channel_id=1, source_target_pairs={{0,60},{1,61},{4,0},{5,1},{8,4},{9,5},{12,8},{13,9},{16,12},{17,13... | collective-permute-start | bytes 589832 | tf_op jit(solution)/shard_map/ppermute | solution.py:241
  87.8 29.3 %all-to-all-start.2 = ((bf16[8,32,384]{2,1,0:T(8,128)(2,1)}), bf16[8,32,384]{2,1,0:T(8,128)(2,1)S(1)}, u32[]{:S(2)}, u32[]{:S(2)}) async-start(bf16[8,32,384]{2,1,0:T(8,128)(2,1)} %bitcast.5), calls=%async_computation.2 | async-start | bytes 393216 | tf_op jit(solution)/shard_map/all_to_all | solution.py:245

commit v6 on v2

--- a/solution.py
+++ b/solution.py
@@ -33,67 +33,36 @@
     return pl.BlockSpec(memory_space=pltpu.SMEM)
 
 
-def chip_number(info_ref, first, second):
-    core = info_ref[3]
-    return first * (4 - 3 * core) + second * (1 + 3 * core)
-
-
 def block_rows(k):
     return pl.ds(pl.multiple_of(k * 32, 32), 32)
 
 
-def partial_kernel(info_ref, l0_ref, l1_ref, l2_ref, l3_ref, w_own_ref, w_sib_ref, own_ref, s1_ref, s2_ref, s3_ref, plane_ref, plane, w, acc, sems):
-    second = info_ref[2]
-    copies = []
-    for d, ref in enumerate((l0_ref, l1_ref, l2_ref, l3_ref)):
-        for i in range(4):
-            k = chip_number(info_ref, i, lax.rem(second + d, 4))
-            copies.append(
-                pltpu.make_async_copy(ref.at[i], plane.at[block_rows(k), :], sems.at[d * 4 + i])
-            )
-    weights = [
-        pltpu.make_async_copy(ref, w.at[n], sems.at[16 + n])
-        for n, ref in enumerate((w_own_ref, w_sib_ref))
-    ]
-    for copy in copies + weights:
-        copy.start()
-    for copy in copies:
-        copy.wait()
-    result = pltpu.make_async_copy(plane, plane_ref, sems.at[18])
-    result.start()
-    for n, copy in enumerate(weights):
-        copy.wait()
+def partial_kernel(info_ref, plane_ref, w_own_ref, w_sib_ref, own_ref, s1_ref, s2_ref, s3_ref, acc):
+    for n, w_ref in enumerate((w_own_ref, w_sib_ref)):
         acc[:, n * 384 : (n + 1) * 384] = lax.dot_general(
-            plane[...], w[n], ROWS_BY_ROWS, preferred_element_type=jnp.float32
+            plane_ref[...], w_ref[...], ROWS_BY_ROWS, preferred_element_type=jnp.float32
         )
-    result.wait()
     for d, out in enumerate((own_ref, s1_ref, s2_ref, s3_ref)):
         residue = lax.rem(info_ref[0] + d, 4)
         for x in range(4):
             out[x] = acc[block_rows(x * 4 + residue), :].astype(out.dtype)
 
 
-def partial_sums(info, lines, w_own, w_sib):
+def partial_sums(info, plane, w_own, w_sib):
     shape = (4, 32, 768)
     return pl.pallas_call(
         partial_kernel,
         out_shape=[jax.ShapeDtypeStruct(shape, jnp.float32)]
-        + [jax.ShapeDtypeStruct(shape, jnp.bfloat16)] * 3
-        + [jax.ShapeDtypeStruct((512, 3072), jnp.bfloat16)],
-        in_specs=[smem()] + [pl.BlockSpec(memory_space=pl.ANY)] * 6,
-        out_specs=[vmem()] * 4 + [pl.BlockSpec(memory_space=pl.ANY)],
-        scratch_shapes=[
-            pltpu.VMEM((512, 3072), jnp.bfloat16),
-            pltpu.VMEM((2, 384, 3072), jnp.bfloat16),
-            pltpu.VMEM((512, 768), jnp.float32),
-            pltpu.SemaphoreType.DMA((19,)),
-        ],
-        compiler_params=pltpu.CompilerParams(vmem_limit_bytes=52 * MIB),
+        + [jax.ShapeDtypeStruct(shape, jnp.bfloat16)] * 3,
+        in_specs=[smem()] + [vmem()] * 3,
+        out_specs=[vmem()] * 4,
+        scratch_shapes=[pltpu.VMEM((512, 768), jnp.float32)],
+        compiler_params=pltpu.CompilerParams(vmem_limit_bytes=20 * MIB),
         cost_estimate=pl.CostEstimate(
             flops=2 * 512 * 3072 * 768, bytes_accessed=8 * MIB, transcendentals=0
         ),
         name="partial_sums",
-    )(info, *lines, w_own, w_sib)
+    )(info, plane, w_own, w_sib)
 
 
 def stage_kernel(info_ref, own_ref, r1_ref, r2_ref, r3_ref, o_ref, s1_ref, s2_ref, s3_ref):
@@ -145,7 +114,7 @@
 
     @pl.when(pl.program_id(0) == 0)
     def _():
-        z, core = info_ref[0], info_ref[3]
+        z, core = info_ref[0], info_ref[1]
         for ref, far in ((n0_ref, 0), (n1_ref, -1), (n2_ref, 4 * core - 2), (n3_ref, 1)):
             for e in range(4):
                 k = lax.rem(z + far + 4 * e + 16, 16)
@@ -184,17 +153,6 @@
     )(info, *near, hg_own, hg_sib)
 
 
-def plane_shift(first, by):
-    pairs = []
-    for x in range(4):
-        for y in range(4):
-            for core in range(2):
-                along_x = (core == 0) == first
-                to = ((x + by) % 4, y) if along_x else (x, (y + by) % 4)
-                pairs.append(((x * 4 + y) * 2 + core, (to[0] * 4 + to[1]) * 2 + core))
-    return pairs
-
-
 def far_shift(by):
     return [(z, (z + 4 * by) % 16) for z in range(16)]
 
@@ -203,42 +161,32 @@
     return [(z * 2 + c, (z + by[c]) % 16 * 2 + c) for z in range(16) for c in range(2)]
 
 
-def first_axis_groups():
-    place = [[[(x * 4 + y) * 2 + c for c in range(2)] for y in range(4)] for x in range(4)]
-    along_x = [[place[i][j][0] for i in range(4)] for j in range(4)]
-    along_y = [[place[j][i][1] for i in range(4)] for j in range(4)]
-    return along_x + along_y
-
-
 NEAR = ((1, 1), (2, -2), (-1, -1))
 
 
 def per_device(inputs, weight, upstream, preactivation):
     core = lax.axis_index("core")
-    x, y, z = lax.axis_index("x"), lax.axis_index(("yh", "yl")), lax.axis_index(Z)
-    first, second = jnp.where(core == 0, x, y), jnp.where(core == 0, y, x)
-    info = jnp.stack([z, first, second, core]).astype(jnp.int32)
+    info = jnp.stack([lax.axis_index(Z), core]).astype(jnp.int32)
     swap = [(0, 1), (1, 0)]
 
     slope = gelu_slope(preactivation.astype(jnp.float32))
     local = (upstream.astype(jnp.float32) * slope).astype(jnp.bfloat16)
-    line = lax.all_gather(
-        local, PLANE, axis=0, tiled=True, axis_index_groups=first_axis_groups()
-    ).reshape(4, 32, 3072)
-    weight_then, line = lax.optimization_barrier((weight, line))
+    hg_own = lax.all_to_all(
+        jnp.broadcast_to(local[None], (16, 32, 3072)),
+        ("x", "yh", "yl"),
+        split_axis=0,
+        concat_axis=0,
+        tiled=True,
+    ).reshape(512, 3072)
+    weight_then, inputs, local = lax.optimization_barrier((weight, inputs, local))
     w_sib = lax.ppermute(weight_then, "core", swap)
-    inputs, w_sib = lax.optimization_barrier((inputs, w_sib))
-    lines = [line] + [lax.ppermute(line, PLANE, plane_shift(False, -d)) for d in (1, 2, 3)]
-    near = [inputs] + [lax.ppermute(inputs, Z, far_shift(-d)) for d in (1, 2)]
-    inputs, near[1] = lax.optimization_barrier((inputs, near[1]))
-    last = lax.ppermute(inputs, Z, far_shift(-3))
-    lines, near = lax.optimization_barrier((lines, near))
-    near = near + [last]
-
-    own, *sends, hg_own = partial_sums(info, lines, weight, w_sib)
-    own, near = lax.optimization_barrier((own, near))
-    near, hg_own = lax.optimization_barrier((jnp.stack(near), hg_own))
+    near = [inputs] + [lax.ppermute(inputs, Z, far_shift(-d)) for d in (1, 2, 3)]
+    near, w_sib = lax.optimization_barrier((near, w_sib))
+    near = jnp.stack(near)
     nears = [near] + [lax.ppermute(near, Z + ("core",), column_shift(by)) for by in NEAR]
+    hg_own, nears = lax.optimization_barrier((hg_own, nears))
+
+    own, *sends = partial_sums(info, hg_own, weight, w_sib)
     received = [
         lax.ppermute(s, Z + ("core",), column_shift(by)) for s, by in zip(sends, NEAR)
     ]

time: 122 us -> 123 us (level)
  blocking collectives: 12.4 us -> 0 us
  waiting for transfers between devices: 10.1 us -> 20.1 us
  local copies, waits for them, and re-layouts: 1.89 us -> 8.1 us
  Pallas kernels: 14.5 us -> 12.3 us
    all_gather x1 -> x0, blocking collectives: 12.4 us -> none  [per_device(): lax.all_gather(local, PLANE, axis=0, tiled=True, axis_index_groups=first_...]
    ppermute x3, waiting for transfers between devices: 0.01 us -> 7.75 us  [per_device(): lax.ppermute(s, Z + ('core',), column_shift(by))]
    all_to_all x0 -> x1, starting transfers between devices: none -> 7.72 us  [per_device(): lax.all_to_all(jnp.broadcast_to(local[None], (16, 32, 3072)), ('x', 'yh',...]
    ppermute x3, waiting for transfers between devices: 0.01 us -> 7.3 us  [per_device(): lax.ppermute(near, Z + ('core',), column_shift(by))]
    ppermute x1, starting transfers between devices: 9.73 us -> 4.95 us  [per_device(): w_sib = lax.ppermute(weight_then, 'core', swap)]
    unnamed x6 -> x16, local copies, waits for them, and re-layouts: 1.89 us -> 6.08 us
    pallas_call x1, Pallas kernels: 8.03 us -> 4.1 us  [partial_sums(): pl.pallas_call(partial_kernel, out_shape=[jax.ShapeDtypeStruct(shape, jnp...]
    ppermute x6 -> x3, starting transfers between devices: 26.3 us -> 22.6 us  [per_device(): lax.ppermute(inputs, Z, far_shift(-d))]
  transfers between devices with their start and end apart: 18 -> 16, of which waited for: 3 -> 7; matrix products, arithmetic and copies ran while one was open for 0% -> 0% of each run, Pallas kernels for 12% -> 10%
where the time goes in v6:
time: 123 us; the launch traced here: 122 us
  starting transfers between devices  79 us (64%)
  waiting for transfers between devices  20.1 us (16%)
  Pallas kernels  12.3 us (10%)
  local copies, waits for them, and re-layouts  8.1 us (7%)
  other arithmetic  2.05 us (2%)
    ppermute x3, starting transfers between devices, per_device(): lax.ppermute(inputs, Z, far_shift(-d))  22.6 us
    ppermute x3, starting transfers between devices, per_device(): lax.ppermute(s, Z, far_shift(d + 1))  17.7 us
    ppermute x3, starting transfers between devices, per_device(): lax.ppermute(near, Z + ('core',), column_shift(by))  9.54 us
    ppermute x3, starting transfers between devices, per_device(): lax.ppermute(s, Z + ('core',), column_shift(by))  8.58 us
    ppermute x3, waiting for transfers between devices, per_device(): lax.ppermute(s, Z + ('core',), column_shift(by))  7.75 us
    all_to_all x1, starting transfers between devices, per_device(): lax.all_to_all(jnp.broadcast_to(local[None], (16, 32, 3072)), ('x', 'yh',...  7.72 us
    pallas_call x1, Pallas kernels, weight_sums(): pl.pallas_call(weight_kernel, out_shape=jax.ShapeDtypeStruct((384, 3072),...  7.55 us
    ppermute x3, waiting for transfers between devices, per_device(): lax.ppermute(near, Z + ('core',), column_shift(by))  7.3 us
  transfers between devices with their start and end apart: 16, of which 7 were waited for; matrix products, arithmetic and copies ran while one was open for 0% of the time, Pallas kernels for 10%

profile of v6, /device:TPU:1, one launch (start us, length us, event | category | flops | bytes accessed | tf_op | source)
XLA Modules:
  0.0 122.5 jit_solution(10416178162639251363)
XLA Ops:
  0.6 1.3 %fusion.7 = bf16[32,3072]{1,0:T(8,128)(2,1)S(1)} fusion(bf16[32,3072]{1,0:T(8,128)(2,1)} %param.7, bf16[32,3072]{1,0:T(8,128)(2,1)} %param.6), kind=kLoop, calls=%fused_computation.14 | loop fusion | flops 2064384 | bytes 589824 | tf_op jit(solution)/shard_map/convert_element_type | solution.py:173
  1.9 2.0 %broadcast_in_dim.2 = bf16[16,32,3072]{2,1,0:T(8,128)(2,1)} broadcast(bf16[32,3072]{1,0:T(8,128)(2,1)S(1)} %fusion.7), dimensions={1,2} | broadcast | bytes 3342336 | tf_op jit(solution)/shard_map/broadcast_in_dim | solution.py:175
  3.9 0.0 copy-start.7
  4.0 7.7 %all-to-all-start = ((bf16[16,32,3072]{2,1,0:T(8,128)(2,1)}), bf16[16,32,3072]{2,1,0:T(8,128)(2,1)S(1)}, u32[]{:S(2)}, u32[]{:S(2)}) async-start(bf16[16,32,3072]{2,1,0:T(8,128)(2,1)} %broadcast_in_dim.2), calls=%async_computation | async-start | bytes 6291456 | tf_op jit(solution)/shard_map/all_to_all | solution.py:174
  11.7 4.9 %collective-permute-start.3 = (bf16[384,3072]{1,0:T(8,128)(2,1)}, bf16[384,3072]{1,0:T(8,128)(2,1)S(1)}, u32[]{:S(2)}, u32[]{:S(2)}) collective-permute-start(bf16[384,3072]{1,0:T(8,128)(2,1)} %w_own_ref.1), channel_id=1, source_target_pairs={{0,1},{1,0},{2,3},{3,2},{4,5},{5,4},{6,7},{7,6},{8,9},{9,8},{10,11... | collective-permute-start | bytes 7077896 | tf_op jit(solution)/shard_map/ppermute | solution.py:182
  16.6 0.0 copy-done.7
  16.6 6.7 %collective-permute-start.2 = (bf16[64,384]{1,0:T(8,128)(2,1)S(1)}, bf16[64,384]{1,0:T(8,128)(2,1)S(1)}, u32[]{:S(2)}, u32[]{:S(2)}) collective-permute-start(bf16[64,384]{1,0:T(8,128)(2,1)S(1)} %copy-done.7), channel_id=1, source_target_pairs={{0,16},{4,20},{8,24},{12,28},{16,32},{20,36},{24,40},{28,44},{32,4... | collective-permute-start | bytes 147464 | tf_op jit(solution)/shard_map/ppermute | solution.py:183
  23.4 10.6 %collective-permute-start.1 = (bf16[64,384]{1,0:T(8,128)(2,1)S(1)}, bf16[64,384]{1,0:T(8,128)(2,1)S(1)}, u32[]{:S(2)}, u32[]{:S(2)}) collective-permute-start(bf16[64,384]{1,0:T(8,128)(2,1)S(1)} %copy-done.7), channel_id=1, source_target_pairs={{0,32},{4,36},{8,40},{12,44},{16,48},{20,52},{24,56},{28,60},{32,0... | collective-permute-start | bytes 147464 | tf_op jit(solution)/shard_map/ppermute | solution.py:183
  34.0 5.2 %collective-permute-start = (bf16[64,384]{1,0:T(8,128)(2,1)S(1)}, bf16[64,384]{1,0:T(8,128)(2,1)S(1)}, u32[]{:S(2)}, u32[]{:S(2)}) collective-permute-start(bf16[64,384]{1,0:T(8,128)(2,1)S(1)} %copy-done.7), channel_id=1, source_target_pairs={{0,48},{4,52},{8,56},{12,60},{16,0},{20,4},{24,8},{28,12},{32,16},... | collective-permute-start | bytes 147464 | tf_op jit(solution)/shard_map/ppermute | solution.py:183
  39.2 0.0 collective-permute-done.2
  39.2 0.0 collective-permute-done.1
  39.2 3.8 %collective-permute-done = bf16[64,384]{1,0:T(8,128)(2,1)S(1)} collective-permute-done((bf16[64,384]{1,0:T(8,128)(2,1)S(1)}, bf16[64,384]{1,0:T(8,128)(2,1)S(1)}, u32[]{:S(2)}, u32[]{:S(2)}) %collective-permute-start) | collective-permute-done | bytes 49184 | tf_op jit(solution)/shard_map/ppermute | solution.py:183
  43.1 0.0 collective-permute-done.3.w_sib_ref
  43.1 1.4 %copy-done.5 = bf16[384,3072]{1,0:T(8,128)(2,1)} copy-done((bf16[384,3072]{1,0:T(8,128)(2,1)}, bf16[384,3072]{1,0:T(8,128)(2,1)S(1)}, u32[]{:S(2)}) %copy-start.5) | copy-done | bytes 2359320
  44.5 3.8 %collective-permute-start.6 = (bf16[4,64,384]{2,1,0:T(8,128)(2,1)S(1)}, bf16[4,64,384]{2,1,0:T(8,128)(2,1)S(1)}, u32[]{:S(2)}, u32[]{:S(2)}) collective-permute-start(bf16[4,64,384]{2,1,0:T(8,128)(2,1)S(1)} %pad_maximum_fusion.n0_ref), channel_id=1, source_target_pairs={{0,60},{1,61},{4,0},{5,1},{8,4},{9,5},{12,8},{13,9},{16,12},{17,13... | collective-permute-start | bytes 589832 | tf_op jit(solution)/shard_map/ppermute | solution.py:186
  48.3 3.0 %collective-permute-start.5 = (bf16[4,64,384]{2,1,0:T(8,128)(2,1)S(1)}, bf16[4,64,384]{2,1,0:T(8,128)(2,1)S(1)}, u32[]{:S(2)}, u32[]{:S(2)}) collective-permute-start(bf16[4,64,384]{2,1,0:T(8,128)(2,1)S(1)} %pad_maximum_fusion.n0_ref), channel_id=1, source_target_pairs={{0,8},{1,57},{4,12},{5,61},{8,16},{9,1},{12,20},{13,5},{16,24},{17... | collective-permute-start | bytes 589832 | tf_op jit(solution)/shard_map/ppermute | solution.py:186
  51.3 2.7 %collective-permute-start.4 = (bf16[4,64,384]{2,1,0:T(8,128)(2,1)S(1)}, bf16[4,64,384]{2,1,0:T(8,128)(2,1)S(1)}, u32[]{:S(2)}, u32[]{:S(2)}) collective-permute-start(bf16[4,64,384]{2,1,0:T(8,128)(2,1)S(1)} %pad_maximum_fusion.n0_ref), channel_id=1, source_target_pairs={{0,4},{1,5},{4,8},{5,9},{8,12},{9,13},{12,16},{13,17},{16,20},{17,... | collective-permute-start | bytes 589832 | tf_op jit(solution)/shard_map/ppermute | solution.py:186
  54.1 0.0 collective-permute-done.6.n3_ref
  54.1 5.1 %collective-permute-done.5.n2_ref = bf16[4,64,384]{2,1,0:T(8,128)(2,1)S(1)} collective-permute-done((bf16[4,64,384]{2,1,0:T(8,128)(2,1)S(1)}, bf16[4,64,384]{2,1,0:T(8,128)(2,1)S(1)}, u32[]{:S(2)}, u32[]{:S(2)}) %collective-permute-start.5) | collective-permute-done | bytes 196640 | tf_op jit(solution)/shard_map/ppermute | solution.py:186
  59.2 0.7 copy-done
  59.8 2.2 %collective-permute-done.4.n1_ref = bf16[4,64,384]{2,1,0:T(8,128)(2,1)S(1)} collective-permute-done((bf16[4,64,384]{2,1,0:T(8,128)(2,1)S(1)}, bf16[4,64,384]{2,1,0:T(8,128)(2,1)S(1)}, u32[]{:S(2)}, u32[]{:S(2)}) %collective-permute-start.4) | collective-permute-done | bytes 196640 | tf_op jit(solution)/shard_map/ppermute | solution.py:186
  62.1 0.7 copy-done.2
  62.7 0.0 all-to-all-done
  62.7 6.1 %collective-permute-start.10 = (bf16[512,3072]{1,0:T(8,128)(2,1)S(1)}, bf16[512,3072]{1,0:T(8,128)(2,1)}, u32[]{:S(2)}, u32[]{:S(2)}) collective-permute-start(bf16[512,3072]{1,0:T(8,128)(2,1)S(1)} %bitcast.7), channel_id=1, source_target_pairs={{0,1},{1,0},{2,3},{3,2},{4,5},{5,4},{6,7},{7,6},{8,9},{9,8},{10,11... | collective-permute-start | bytes 9437192 | tf_op jit(solution)/shard_map/ppermute | solution.py:193
  68.9 0.1 pad_add_fusion.info_ref
  69.0 1.7 %copy-done.4 = bf16[384,3072]{1,0:T(8,128)(2,1)S(1)} copy-done((bf16[384,3072]{1,0:T(8,128)(2,1)S(1)}, bf16[384,3072]{1,0:T(8,128)(2,1)}, u32[]{:S(2)}) %copy-start.4) | copy-done | bytes 2359320
  70.6 1.7 %copy-done.6 = bf16[384,3072]{1,0:T(8,128)(2,1)S(1)} copy-done((bf16[384,3072]{1,0:T(8,128)(2,1)S(1)}, bf16[384,3072]{1,0:T(8,128)(2,1)}, u32[]{:S(2)}) %copy-start.6) | copy-done | bytes 2359320
  72.3 4.1 %partial_sums.1 = (f32[4,32,768]{2,1,0:T(8,128)S(1)}, bf16[4,32,768]{2,1,0:T(8,128)(2,1)S(1)}, bf16[4,32,768]{2,1,0:T(8,128)(2,1)S(1)}, bf16[4,32,768]{2,1,0:T(8,128)(2,1)S(1)}) custom-call(s32[2]{0:T(128)S(1)} %pad_add_fusion.info_ref, bf16[512,3072]{1,0:T(8,128)(2,1)S(1)} %bitcast.8, bf16[384,3072]{1,0:T(8,128)(2,1)S(1)} %copy-done.4, ...), custom_call_target="tpu_custom_call" | custom-call | flops 2415919104 | bytes 8388608 | tf_op jit(solution)/shard_map/partial_sums/pallas_call | solution.py:53
  76.4 1.9 %collective-permute-start.7 = (bf16[4,32,768]{2,1,0:T(8,128)(2,1)S(1)}, bf16[4,32,768]{2,1,0:T(8,128)(2,1)S(1)}, u32[]{:S(2)}, u32[]{:S(2)}) collective-permute-start(bf16[4,32,768]{2,1,0:T(8,128)(2,1)S(1)} %get-tuple-element.37), channel_id=1, source_target_pairs={{0,4},{1,5},{4,8},{5,9},{8,12},{9,13},{12,16},{13,17},{16,20},{17,... | collective-permute-start | bytes 589832 | tf_op jit(solution)/shard_map/ppermute | solution.py:191
  78.3 4.7 %collective-permute-start.8 = (bf16[4,32,768]{2,1,0:T(8,128)(2,1)S(1)}, bf16[4,32,768]{2,1,0:T(8,128)(2,1)S(1)}, u32[]{:S(2)}, u32[]{:S(2)}) collective-permute-start(bf16[4,32,768]{2,1,0:T(8,128)(2,1)S(1)} %get-tuple-element.38), channel_id=1, source_target_pairs={{0,8},{1,57},{4,12},{5,61},{8,16},{9,1},{12,20},{13,5},{16,24},{17... | collective-permute-start | bytes 589832 | tf_op jit(solution)/shard_map/ppermute | solution.py:191
  83.0 2.0 %collective-permute-start.9 = (bf16[4,32,768]{2,1,0:T(8,128)(2,1)S(1)}, bf16[4,32,768]{2,1,0:T(8,128)(2,1)S(1)}, u32[]{:S(2)}, u32[]{:S(2)}) collective-permute-start(bf16[4,32,768]{2,1,0:T(8,128)(2,1)S(1)} %get-tuple-element.39), channel_id=1, source_target_pairs={{0,60},{1,61},{4,0},{5,1},{8,4},{9,5},{12,8},{13,9},{16,12},{17,13... | collective-permute-start | bytes 589832 | tf_op jit(solution)/shard_map/ppermute | solution.py:191
  85.0 1.0 collective-permute-done.7.r1_ref
  86.0 0.7 collective-permute-done.8.r2_ref
  86.7 6.0 %collective-permute-done.9.r3_ref = bf16[4,32,768]{2,1,0:T(8,128)(2,1)S(1)} collective-permute-done((bf16[4,32,768]{2,1,0:T(8,128)(2,1)S(1)}, bf16[4,32,768]{2,1,0:T(8,128)(2,1)S(1)}, u32[]{:S(2)}, u32[]{:S(2)}) %collective-permute-start.9) | collective-permute-done | bytes 196640 | tf_op jit(solution)/shard_map/ppermute | solution.py:191
  92.8 0.6 stage_sums.1
  93.4 2.2 %collective-permute-start.11 = (bf16[32,768]{1,0:T(8,128)(2,1)S(1)}, bf16[32,768]{1,0:T(8,128)(2,1)S(1)}, u32[]{:S(2)}, u32[]{:S(2)}) collective-permute-start(bf16[32,768]{1,0:T(8,128)(2,1)S(1)} %get-tuple-element.45), channel_id=1, source_target_pairs={{0,16},{4,20},{8,24},{12,28},{16,32},{20,36},{24,40},{28,44},{32,4... | collective-permute-start | bytes 147464 | tf_op jit(solution)/shard_map/ppermute | solution.py:196
  95.7 10.8 %collective-permute-start.12 = (bf16[32,768]{1,0:T(8,128)(2,1)S(1)}, bf16[32,768]{1,0:T(8,128)(2,1)S(1)}, u32[]{:S(2)}, u32[]{:S(2)}) collective-permute-start(bf16[32,768]{1,0:T(8,128)(2,1)S(1)} %get-tuple-element.46), channel_id=1, source_target_pairs={{0,32},{4,36},{8,40},{12,44},{16,48},{20,52},{24,56},{28,60},{32,0... | collective-permute-start | bytes 147464 | tf_op jit(solution)/shard_map/ppermute | solution.py:196
  106.5 4.6 %collective-permute-start.13 = (bf16[32,768]{1,0:T(8,128)(2,1)S(1)}, bf16[32,768]{1,0:T(8,128)(2,1)S(1)}, u32[]{:S(2)}, u32[]{:S(2)}) collective-permute-start(bf16[32,768]{1,0:T(8,128)(2,1)S(1)} %get-tuple-element.47), channel_id=1, source_target_pairs={{0,48},{4,52},{8,56},{12,60},{16,0},{20,4},{24,8},{28,12},{32,16},... | collective-permute-start | bytes 147464 | tf_op jit(solution)/shard_map/ppermute | solution.py:196
  111.1 0.0 collective-permute-done.10.sib_ref
  111.1 0.0 copy-done.1
  111.1 0.0 copy-done.3
  111.1 7.6 %weight_sums.1 = bf16[384,3072]{1,0:T(8,128)(2,1)} custom-call(s32[2]{0:T(128)S(1)} %pad_add_fusion.info_ref, bf16[4,64,384]{2,1,0:T(8,128)(2,1)S(1)} %pad_maximum_fusion.n0_ref, bf16[4,64,384]{2,1,0:T(8,128)(2,1)S(1)} %copy-done.3, bf16[4,64,384]{2,1,0:T(8,128)(2,1)S(1)} %copy-done.1, bf16[4,64,384]{2,1,0:T(8,128)(2,1)S(1)} %collective-permute-done.6.n3_ref, ...), custom_call_target="tpu_custom_call" | custom-call | flops 2415919104 | bytes 10485760 | tf_op jit(solution)/shard_map/weight_sums/pallas_call | solution.py:134
  118.7 0.0 collective-permute-done.11.r1_ref
  118.7 0.0 collective-permute-done.12.r2_ref
  118.7 0.0 collective-permute-done.13.r3_ref
  118.7 1.9 %collective-permute-start.14 = (bf16[32,384]{1,0:T(8,128)(2,1)S(1)}, bf16[32,384]{1,0:T(8,128)(2,1)S(1)}, u32[]{:S(2)}, u32[]{:S(2)}) collective-permute-start(bf16[32,384]{1,0:T(8,128)(2,1)S(1)} %get-tuple-element.52), channel_id=1, source_target_pairs={{0,1},{1,0},{2,3},{3,2},{4,5},{5,4},{6,7},{7,6},{8,9},{9,8},{10,11... | collective-permute-start | bytes 73736 | tf_op jit(solution)/shard_map/ppermute | solution.py:202
  120.7 1.2 collective-permute-done.14
  121.8 0.6 pad_maximum_fusion.1
  (10 shorter events, 0.1 us)
Async XLA Ops:
  3.9 12.7 %copy-start.7 = (bf16[64,384]{1,0:T(8,128)(2,1)S(1)}, bf16[64,384]{1,0:T(8,128)(2,1)}, u32[]{:S(2)}) copy-start(bf16[64,384]{1,0:T(8,128)(2,1)} %param.4) | copy-start | bytes 147460
  4.0 58.8 %all-to-all-start = ((bf16[16,32,3072]{2,1,0:T(8,128)(2,1)}), bf16[16,32,3072]{2,1,0:T(8,128)(2,1)S(1)}, u32[]{:S(2)}, u32[]{:S(2)}) async-start(bf16[16,32,3072]{2,1,0:T(8,128)(2,1)} %broadcast_in_dim.2), calls=%async_computation | async-start | bytes 6291456 | tf_op jit(solution)/shard_map/all_to_all | solution.py:174
  11.7 31.4 %collective-permute-start.3 = (bf16[384,3072]{1,0:T(8,128)(2,1)}, bf16[384,3072]{1,0:T(8,128)(2,1)S(1)}, u32[]{:S(2)}, u32[]{:S(2)}) collective-permute-start(bf16[384,3072]{1,0:T(8,128)(2,1)} %w_own_ref.1), channel_id=1, source_target_pairs={{0,1},{1,0},{2,3},{3,2},{4,5},{5,4},{6,7},{7,6},{8,9},{9,8},{10,11... | collective-permute-start | bytes 7077896 | tf_op jit(solution)/shard_map/ppermute | solution.py:182
  16.6 22.6 %collective-permute-start.2 = (bf16[64,384]{1,0:T(8,128)(2,1)S(1)}, bf16[64,384]{1,0:T(8,128)(2,1)S(1)}, u32[]{:S(2)}, u32[]{:S(2)}) collective-permute-start(bf16[64,384]{1,0:T(8,128)(2,1)S(1)} %copy-done.7), channel_id=1, source_target_pairs={{0,16},{4,20},{8,24},{12,28},{16,32},{20,36},{24,40},{28,44},{32,4... | collective-permute-start | bytes 147464 | tf_op jit(solution)/shard_map/ppermute | solution.py:183
  23.4 15.8 %collective-permute-start.1 = (bf16[64,384]{1,0:T(8,128)(2,1)S(1)}, bf16[64,384]{1,0:T(8,128)(2,1)S(1)}, u32[]{:S(2)}, u32[]{:S(2)}) collective-permute-start(bf16[64,384]{1,0:T(8,128)(2,1)S(1)} %copy-done.7), channel_id=1, source_target_pairs={{0,32},{4,36},{8,40},{12,44},{16,48},{20,52},{24,56},{28,60},{32,0... | collective-permute-start | bytes 147464 | tf_op jit(solution)/shard_map/ppermute | solution.py:183
  34.0 9.0 %collective-permute-start = (bf16[64,384]{1,0:T(8,128)(2,1)S(1)}, bf16[64,384]{1,0:T(8,128)(2,1)S(1)}, u32[]{:S(2)}, u32[]{:S(2)}) collective-permute-start(bf16[64,384]{1,0:T(8,128)(2,1)S(1)} %copy-done.7), channel_id=1, source_target_pairs={{0,48},{4,52},{8,56},{12,60},{16,0},{20,4},{24,8},{28,12},{32,16},... | collective-permute-start | bytes 147464 | tf_op jit(solution)/shard_map/ppermute | solution.py:183
  43.1 1.4 %copy-start.5 = (bf16[384,3072]{1,0:T(8,128)(2,1)}, bf16[384,3072]{1,0:T(8,128)(2,1)S(1)}, u32[]{:S(2)}) copy-start(bf16[384,3072]{1,0:T(8,128)(2,1)S(1)} %collective-permute-done.3.w_sib_ref) | copy-start | bytes 7077892
  44.5 9.6 %collective-permute-start.6 = (bf16[4,64,384]{2,1,0:T(8,128)(2,1)S(1)}, bf16[4,64,384]{2,1,0:T(8,128)(2,1)S(1)}, u32[]{:S(2)}, u32[]{:S(2)}) collective-permute-start(bf16[4,64,384]{2,1,0:T(8,128)(2,1)S(1)} %pad_maximum_fusion.n0_ref), channel_id=1, source_target_pairs={{0,60},{1,61},{4,0},{5,1},{8,4},{9,5},{12,8},{13,9},{16,12},{17,13... | collective-permute-start | bytes 589832 | tf_op jit(solution)/shard_map/ppermute | solution.py:186
  48.3 10.8 %collective-permute-start.5 = (bf16[4,64,384]{2,1,0:T(8,128)(2,1)S(1)}, bf16[4,64,384]{2,1,0:T(8,128)(2,1)S(1)}, u32[]{:S(2)}, u32[]{:S(2)}) collective-permute-start(bf16[4,64,384]{2,1,0:T(8,128)(2,1)S(1)} %pad_maximum_fusion.n0_ref), channel_id=1, source_target_pairs={{0,8},{1,57},{4,12},{5,61},{8,16},{9,1},{12,20},{13,5},{16,24},{17... | collective-permute-start | bytes 589832 | tf_op jit(solution)/shard_map/ppermute | solution.py:186
  51.3 10.7 %collective-permute-start.4 = (bf16[4,64,384]{2,1,0:T(8,128)(2,1)S(1)}, bf16[4,64,384]{2,1,0:T(8,128)(2,1)S(1)}, u32[]{:S(2)}, u32[]{:S(2)}) collective-permute-start(bf16[4,64,384]{2,1,0:T(8,128)(2,1)S(1)} %pad_maximum_fusion.n0_ref), channel_id=1, source_target_pairs={{0,4},{1,5},{4,8},{5,9},{8,12},{9,13},{12,16},{13,17},{16,20},{17,... | collective-permute-start | bytes 589832 | tf_op jit(solution)/shard_map/ppermute | solution.py:186
  59.2 0.7 copy-start
  62.1 0.7 copy-start.2
  62.7 48.4 %collective-permute-start.10 = (bf16[512,3072]{1,0:T(8,128)(2,1)S(1)}, bf16[512,3072]{1,0:T(8,128)(2,1)}, u32[]{:S(2)}, u32[]{:S(2)}) collective-permute-start(bf16[512,3072]{1,0:T(8,128)(2,1)S(1)} %bitcast.7), channel_id=1, source_target_pairs={{0,1},{1,0},{2,3},{3,2},{4,5},{5,4},{6,7},{7,6},{8,9},{9,8},{10,11... | collective-permute-start | bytes 9437192 | tf_op jit(solution)/shard_map/ppermute | solution.py:193
  69.0 1.7 %copy-start.4 = (bf16[384,3072]{1,0:T(8,128)(2,1)S(1)}, bf16[384,3072]{1,0:T(8,128)(2,1)}, u32[]{:S(2)}) copy-start(bf16[384,3072]{1,0:T(8,128)(2,1)} %w_own_ref.1) | copy-start | bytes 7077892
  70.6 1.7 %copy-start.6 = (bf16[384,3072]{1,0:T(8,128)(2,1)S(1)}, bf16[384,3072]{1,0:T(8,128)(2,1)}, u32[]{:S(2)}) copy-start(bf16[384,3072]{1,0:T(8,128)(2,1)} %copy-done.5) | copy-start | bytes 7077892
  72.3 38.8 %copy-start.1 = (bf16[4,64,384]{2,1,0:T(8,128)(2,1)S(1)}, bf16[4,64,384]{2,1,0:T(8,128)(2,1)}, u32[]{:S(2)}) copy-start(bf16[4,64,384]{2,1,0:T(8,128)(2,1)} %copy-done) | copy-start | bytes 589828
  72.3 38.8 %copy-start.3 = (bf16[4,64,384]{2,1,0:T(8,128)(2,1)S(1)}, bf16[4,64,384]{2,1,0:T(8,128)(2,1)}, u32[]{:S(2)}) copy-start(bf16[4,64,384]{2,1,0:T(8,128)(2,1)} %copy-done.2) | copy-start | bytes 589828
  76.4 9.6 %collective-permute-start.7 = (bf16[4,32,768]{2,1,0:T(8,128)(2,1)S(1)}, bf16[4,32,768]{2,1,0:T(8,128)(2,1)S(1)}, u32[]{:S(2)}, u32[]{:S(2)}) collective-permute-start(bf16[4,32,768]{2,1,0:T(8,128)(2,1)S(1)} %get-tuple-element.37), channel_id=1, source_target_pairs={{0,4},{1,5},{4,8},{5,9},{8,12},{9,13},{12,16},{13,17},{16,20},{17,... | collective-permute-start | bytes 589832 | tf_op jit(solution)/shard_map/ppermute | solution.py:191
  78.3 8.4 %collective-permute-start.8 = (bf16[4,32,768]{2,1,0:T(8,128)(2,1)S(1)}, bf16[4,32,768]{2,1,0:T(8,128)(2,1)S(1)}, u32[]{:S(2)}, u32[]{:S(2)}) collective-permute-start(bf16[4,32,768]{2,1,0:T(8,128)(2,1)S(1)} %get-tuple-element.38), channel_id=1, source_target_pairs={{0,8},{1,57},{4,12},{5,61},{8,16},{9,1},{12,20},{13,5},{16,24},{17... | collective-permute-start | bytes 589832 | tf_op jit(solution)/shard_map/ppermute | solution.py:191
  83.0 9.7 %collective-permute-start.9 = (bf16[4,32,768]{2,1,0:T(8,128)(2,1)S(1)}, bf16[4,32,768]{2,1,0:T(8,128)(2,1)S(1)}, u32[]{:S(2)}, u32[]{:S(2)}) collective-permute-start(bf16[4,32,768]{2,1,0:T(8,128)(2,1)S(1)} %get-tuple-element.39), channel_id=1, source_target_pairs={{0,60},{1,61},{4,0},{5,1},{8,4},{9,5},{12,8},{13,9},{16,12},{17,13... | collective-permute-start | bytes 589832 | tf_op jit(solution)/shard_map/ppermute | solution.py:191
  93.4 25.3 %collective-permute-start.11 = (bf16[32,768]{1,0:T(8,128)(2,1)S(1)}, bf16[32,768]{1,0:T(8,128)(2,1)S(1)}, u32[]{:S(2)}, u32[]{:S(2)}) collective-permute-start(bf16[32,768]{1,0:T(8,128)(2,1)S(1)} %get-tuple-element.45), channel_id=1, source_target_pairs={{0,16},{4,20},{8,24},{12,28},{16,32},{20,36},{24,40},{28,44},{32,4... | collective-permute-start | bytes 147464 | tf_op jit(solution)/shard_map/ppermute | solution.py:196
  95.7 23.0 %collective-permute-start.12 = (bf16[32,768]{1,0:T(8,128)(2,1)S(1)}, bf16[32,768]{1,0:T(8,128)(2,1)S(1)}, u32[]{:S(2)}, u32[]{:S(2)}) collective-permute-start(bf16[32,768]{1,0:T(8,128)(2,1)S(1)} %get-tuple-element.46), channel_id=1, source_target_pairs={{0,32},{4,36},{8,40},{12,44},{16,48},{20,52},{24,56},{28,60},{32,0... | collective-permute-start | bytes 147464 | tf_op jit(solution)/shard_map/ppermute | solution.py:196
  106.5 12.2 %collective-permute-start.13 = (bf16[32,768]{1,0:T(8,128)(2,1)S(1)}, bf16[32,768]{1,0:T(8,128)(2,1)S(1)}, u32[]{:S(2)}, u32[]{:S(2)}) collective-permute-start(bf16[32,768]{1,0:T(8,128)(2,1)S(1)} %get-tuple-element.47), channel_id=1, source_target_pairs={{0,48},{4,52},{8,56},{12,60},{16,0},{20,4},{24,8},{28,12},{32,16},... | collective-permute-start | bytes 147464 | tf_op jit(solution)/shard_map/ppermute | solution.py:196
  118.7 3.1 %collective-permute-start.14 = (bf16[32,384]{1,0:T(8,128)(2,1)S(1)}, bf16[32,384]{1,0:T(8,128)(2,1)S(1)}, u32[]{:S(2)}, u32[]{:S(2)}) collective-permute-start(bf16[32,384]{1,0:T(8,128)(2,1)S(1)} %get-tuple-element.52), channel_id=1, source_target_pairs={{0,1},{1,0},{2,3},{3,2},{4,5},{5,4},{6,7},{7,6},{8,9},{9,8},{10,11... | collective-permute-start | bytes 73736 | tf_op jit(solution)/shard_map/ppermute | solution.py:202

commit v7 on v4

--- a/solution.py
+++ b/solution.py
@@ -42,7 +42,7 @@
     return pl.ds(pl.multiple_of(k * 32, 32), 32)
 
 
-def partial_kernel(info_ref, lines_ref, w_own_ref, w_sib_ref, own_ref, s1_ref, s2_ref, s3_ref, plane_ref, w_sib, acc, sems):
+def partial_kernel(info_ref, lines_ref, w_own_ref, w_sib_ref, own_ref, send_ref, plane_ref, w_sib, acc, sems):
     copies = []
     for j in range(4):
         for i in range(4):
@@ -63,21 +63,26 @@
     acc[:, 384:] = lax.dot_general(
         plane_ref[...], w_sib[...], ROWS_BY_ROWS, preferred_element_type=jnp.float32
     )
-    for d, out in enumerate((own_ref, s1_ref, s2_ref, s3_ref)):
-        residue = lax.rem(info_ref[0] + d, 4)
+    z, by = info_ref[0], 1 + 2 * info_ref[3]
+    for j in range(2):
         for x in range(4):
-            out[x] = acc[block_rows(x * 4 + residue), :].astype(out.dtype)
+            k = x * 4 + lax.rem(z + 2 * j, 4)
+            own_ref[j, x] = acc[block_rows(k), :]
+            k = x * 4 + lax.rem(z + by + 2 * j, 4)
+            send_ref[j, x] = acc[block_rows(k), :].astype(jnp.bfloat16)
 
 
 def partial_sums(info, lines, w_own, w_sib):
-    shape = (4, 32, 768)
+    shape = (2, 4, 32, 768)
     return pl.pallas_call(
         partial_kernel,
-        out_shape=[jax.ShapeDtypeStruct(shape, jnp.float32)]
-        + [jax.ShapeDtypeStruct(shape, jnp.bfloat16)] * 3
-        + [jax.ShapeDtypeStruct((512, 3072), jnp.bfloat16)],
+        out_shape=[
+            jax.ShapeDtypeStruct(shape, jnp.float32),
+            jax.ShapeDtypeStruct(shape, jnp.bfloat16),
+            jax.ShapeDtypeStruct((512, 3072), jnp.bfloat16),
+        ],
         in_specs=[smem(), pl.BlockSpec(memory_space=pl.ANY), vmem(), pl.BlockSpec(memory_space=pl.ANY)],
-        out_specs=[vmem()] * 5,
+        out_specs=[vmem()] * 3,
         scratch_shapes=[
             pltpu.VMEM((384, 3072), jnp.bfloat16),
             pltpu.VMEM((512, 768), jnp.float32),
@@ -91,14 +96,32 @@
     )(info, *lines, w_own, w_sib)
 
 
-def stage_kernel(info_ref, own_ref, r1_ref, r2_ref, r3_ref, o_ref, s1_ref, s2_ref, s3_ref):
+def pair_kernel(own_ref, r_ref, keep_ref, send_ref):
+    keep_ref[...] = own_ref[0] + r_ref[0].astype(jnp.float32)
+    send_ref[...] = (own_ref[1] + r_ref[1].astype(jnp.float32)).astype(jnp.bfloat16)
+
+
+def pair_sums(own, received):
+    shape = (4, 32, 768)
+    return pl.pallas_call(
+        pair_kernel,
+        out_shape=[
+            jax.ShapeDtypeStruct(shape, jnp.float32),
+            jax.ShapeDtypeStruct(shape, jnp.bfloat16),
+        ],
+        in_specs=[vmem()] * 2,
+        out_specs=[vmem()] * 2,
+        compiler_params=pltpu.CompilerParams(vmem_limit_bytes=8 * MIB),
+        cost_estimate=pl.CostEstimate(flops=400000, bytes_accessed=2 * MIB, transcendentals=0),
+        name="pair_sums",
+    )(own, received)
+
+
+def stage_kernel(info_ref, own_ref, r_ref, o_ref, s1_ref, s2_ref, s3_ref):
     zh = info_ref[0] // 4
     for d, out in enumerate((o_ref, s1_ref, s2_ref, s3_ref)):
         i = lax.rem(zh + d, 4)
-        total = own_ref[i]
-        for r in (r1_ref, r2_ref, r3_ref):
-            total = total + r[i].astype(jnp.float32)
-        out[...] = total.astype(out.dtype)
+        out[...] = (own_ref[i] + r_ref[i].astype(jnp.float32)).astype(out.dtype)
 
 
 def stage_sums(info, own, received):
@@ -107,12 +130,12 @@
         stage_kernel,
         out_shape=[jax.ShapeDtypeStruct(shape, jnp.float32)]
         + [jax.ShapeDtypeStruct(shape, jnp.bfloat16)] * 3,
-        in_specs=[smem()] + [vmem()] * 4,
+        in_specs=[smem()] + [vmem()] * 2,
         out_specs=[vmem()] * 4,
-        compiler_params=pltpu.CompilerParams(vmem_limit_bytes=16 * MIB),
-        cost_estimate=pl.CostEstimate(flops=400000, bytes_accessed=2 * MIB, transcendentals=0),
+        compiler_params=pltpu.CompilerParams(vmem_limit_bytes=8 * MIB),
+        cost_estimate=pl.CostEstimate(flops=400000, bytes_accessed=MIB, transcendentals=0),
         name="stage_sums",
-    )(info, own, *received)
+    )(info, own, received)
 
 
 def final_kernel(own_ref, r1_ref, r2_ref, r3_ref, o_ref, s_ref):
@@ -141,7 +164,12 @@
     @pl.when(pl.program_id(0) == 0)
     def _():
         z, core = info_ref[0], info_ref[3]
-        for ref, far in ((n0_ref, 0), (n1_ref, -1), (n2_ref, 4 * core - 2), (n3_ref, 1)):
+        for ref, far in (
+            (n0_ref, 0),
+            (n1_ref, 1 - 2 * core),
+            (n2_ref, 2 - 4 * core),
+            (n3_ref, 2 * core - 1),
+        ):
             for e in range(4):
                 k = lax.rem(z + far + 4 * e + 16, 16)
                 for which in range(2):
@@ -212,7 +240,7 @@
     return along_x + along_y
 
 
-NEAR = ((1, 1), (2, -2), (-1, -1))
+NEAR = ((-1, 1), (-2, 2), (1, -1))
 
 
 def per_device(inputs, weight, upstream, preactivation):
@@ -244,13 +272,14 @@
     lines = [lines]
     near = near + [last]
 
-    own, *sends, hg_own = partial_sums(info, lines, weight, w_sib)
+    own, send, hg_own = partial_sums(info, lines, weight, w_sib)
     own, near = lax.optimization_barrier((own, near))
     near, hg_own = lax.optimization_barrier((jnp.stack(near), hg_own))
     nears = [near] + [lax.ppermute(near, Z + ("core",), column_shift(by)) for by in NEAR]
-    received = [
-        lax.ppermute(s, Z + ("core",), column_shift(by)) for s, by in zip(sends, NEAR)
-    ]
+    received = lax.ppermute(send, Z + ("core",), column_shift((1, -1)))
+    received, nears[1] = lax.optimization_barrier((received, nears[1]))
+    own, send = pair_sums(own, received)
+    received = lax.ppermute(send, Z + ("core",), column_shift((2, -2)))
     hg_sib = lax.ppermute(hg_own, "core", swap)
     own, *sends = stage_sums(info, own, received)
     received = [

time: 113 us -> 120 us (1.062)
  waiting for transfers between devices: 3.97 us -> 12.2 us
    ppermute x3, waiting for transfers between devices: 0.01 us -> 6.71 us  [per_device(): lax.ppermute(near, Z + ('core',), column_shift(by))]
    ppermute x3 -> x2, starting transfers between devices: 12.9 us -> 9.45 us  [the longest x1 5.55 us: per_device(): received = lax.ppermute(send, Z + ('core',), column_shift((2, -2)))]
    ppermute x1, starting transfers between devices: 4.72 us -> 7.7 us  [per_device(): other = lax.ppermute(other, 'core', swap)]
    ppermute x3, waiting for transfers between devices: 1.52 us -> 3.06 us  [per_device(): lax.ppermute(s, Z, far_shift(d + 1))]
  transfers between devices with their start and end apart: 16 -> 15, of which waited for: 3 -> 4; matrix products, arithmetic and copies ran while one was open for 0% -> 0% of each run, Pallas kernels for 11% -> 11%
where the time goes in v7:
time: 120 us; the launch traced here: 119 us
  starting transfers between devices  76.9 us (64%)
  Pallas kernels  12.8 us (11%)
  blocking collectives  12.4 us (10%)
  waiting for transfers between devices  12.2 us (10%)
  local copies, waits for them, and re-layouts  2.07 us (2%)
  other arithmetic  2.05 us (2%)
    ppermute x3, starting transfers between devices, per_device(): lax.ppermute(s, Z, far_shift(d + 1))  13.8 us
    all_gather x1, blocking collectives, per_device(): lax.all_gather(local, PLANE, axis=0, tiled=True, axis_index_groups=first_...  12.4 us
    ppermute x2, starting transfers between devices, per_device(): near = [inputs] + [lax.ppermute(inputs, Z, far_shift(-d)) for d in (1, 2)]  12.3 us
    ppermute x1, starting transfers between devices, per_device(): w_sib = lax.ppermute(weight_then, 'core', swap)  9.74 us
    ppermute x3, starting transfers between devices, per_device(): lax.ppermute(near, Z + ('core',), column_shift(by))  8.52 us
    ppermute x1, starting transfers between devices, per_device(): other = lax.ppermute(other, 'core', swap)  7.7 us
    ppermute x1, starting transfers between devices, per_device(): last = lax.ppermute(inputs, Z, far_shift(-3))  7.26 us
    ppermute x3, waiting for transfers between devices, per_device(): lax.ppermute(near, Z + ('core',), column_shift(by))  6.71 us
  transfers between devices with their start and end apart: 15, of which 4 were waited for; matrix products, arithmetic and copies ran while one was open for 0% of the time, Pallas kernels for 11%

profile of v7, /device:TPU:1, one launch (start us, length us, event | category | flops | bytes accessed | tf_op | source)
XLA Modules:
  0.0 119.3 jit_solution(12702137214466892742)
XLA Ops:
  0.6 1.3 %fusion.7 = bf16[32,3072]{1,0:T(8,128)(2,1)S(1)} fusion(bf16[32,3072]{1,0:T(8,128)(2,1)} %param.7, bf16[32,3072]{1,0:T(8,128)(2,1)} %param.6), kind=kLoop, calls=%fused_computation.14 | loop fusion | flops 2064384 | bytes 589824 | tf_op jit(solution)/shard_map/convert_element_type | solution.py:254
  1.9 12.4 %all_gather.3 = bf16[128,3072]{1,0:T(8,128)(2,1)S(1)} all-gather(bf16[32,3072]{1,0:T(8,128)(2,1)S(1)} %fusion.7), channel_id=1, replica_groups={{0,128,256,384},{2,130,258,386},{64,192,320,448},{66,194,322,450},{1,3,..., dimensions={0}, use_global_device_ids=true | all-gather | bytes 983040 | tf_op jit(solution)/shard_map/all_gather | solution.py:255
  14.3 2.1 %broadcast_in_dim.2 = bf16[4,4,32,3072]{3,2,1,0:T(8,128)(2,1)} broadcast(bf16[4,32,3072]{2,1,0:T(8,128)(2,1)S(1)} %bitcast.9), dimensions={1,2,3} | broadcast | bytes 3932160 | tf_op jit(solution)/shard_map/broadcast_in_dim | solution.py:261
  16.4 0.0 copy-start
  16.4 0.0 copy-start.1
  16.4 4.8 %all-to-all-start = ((bf16[4,4,32,3072]{3,2,1,0:T(8,128)(2,1)}), bf16[4,4,32,3072]{3,2,1,0:T(8,128)(2,1)}, u32[]{:S(2)}, u32[]{:S(2)}) async-start(bf16[4,4,32,3072]{3,2,1,0:T(8,128)(2,1)} %broadcast_in_dim.2), calls=%async_computation | async-start | bytes 6291456 | tf_op jit(solution)/shard_map/all_to_all | solution.py:260
  21.1 0.0 copy-done
  21.2 9.7 %collective-permute-start.2 = (bf16[384,3072]{1,0:T(8,128)(2,1)S(1)}, bf16[384,3072]{1,0:T(8,128)(2,1)}, u32[]{:S(2)}, u32[]{:S(2)}) collective-permute-start(bf16[384,3072]{1,0:T(8,128)(2,1)S(1)} %copy-done), channel_id=1, source_target_pairs={{0,1},{1,0},{2,3},{3,2},{4,5},{5,4},{6,7},{7,6},{8,9},{9,8},{10,11... | collective-permute-start | bytes 7077896 | tf_op jit(solution)/shard_map/ppermute | solution.py:259
  30.9 0.0 copy-done.1
  30.9 7.4 %collective-permute-start = (bf16[64,384]{1,0:T(8,128)(2,1)S(1)}, bf16[64,384]{1,0:T(8,128)(2,1)S(1)}, u32[]{:S(2)}, u32[]{:S(2)}) collective-permute-start(bf16[64,384]{1,0:T(8,128)(2,1)S(1)} %copy-done.1), channel_id=1, source_target_pairs={{0,48},{4,52},{8,56},{12,60},{16,0},{20,4},{24,8},{28,12},{32,16},... | collective-permute-start | bytes 147464 | tf_op jit(solution)/shard_map/ppermute | solution.py:268
  38.4 4.9 %collective-permute-start.1 = (bf16[64,384]{1,0:T(8,128)(2,1)S(1)}, bf16[64,384]{1,0:T(8,128)(2,1)S(1)}, u32[]{:S(2)}, u32[]{:S(2)}) collective-permute-start(bf16[64,384]{1,0:T(8,128)(2,1)S(1)} %copy-done.1), channel_id=1, source_target_pairs={{0,32},{4,36},{8,40},{12,44},{16,48},{20,52},{24,56},{28,60},{32,0... | collective-permute-start | bytes 147464 | tf_op jit(solution)/shard_map/ppermute | solution.py:268
  43.3 0.1 pad_add_fusion.info_ref
  43.4 0.0 collective-permute-done
  43.4 7.3 %collective-permute-start.3 = (bf16[64,384]{1,0:T(8,128)(2,1)S(1)}, bf16[64,384]{1,0:T(8,128)(2,1)S(1)}, u32[]{:S(2)}, u32[]{:S(2)}) collective-permute-start(bf16[64,384]{1,0:T(8,128)(2,1)S(1)} %copy-done.1), channel_id=1, source_target_pairs={{0,16},{4,20},{8,24},{12,28},{16,32},{20,36},{24,40},{28,44},{32,4... | collective-permute-start | bytes 147464 | tf_op jit(solution)/shard_map/ppermute | solution.py:270
  50.6 1.6 %collective-permute-done.1 = bf16[64,384]{1,0:T(8,128)(2,1)S(1)} collective-permute-done((bf16[64,384]{1,0:T(8,128)(2,1)S(1)}, bf16[64,384]{1,0:T(8,128)(2,1)S(1)}, u32[]{:S(2)}, u32[]{:S(2)}) %collective-permute-start.1) | collective-permute-done | bytes 49184 | tf_op jit(solution)/shard_map/ppermute | solution.py:268
  52.2 0.0 all-to-all-done.lines_ref
  52.2 0.0 collective-permute-done.2.w_sib_ref
  52.2 6.3 %partial_sums.1 = (f32[2,4,32,768]{3,2,1,0:T(8,128)S(1)}, bf16[2,4,32,768]{3,2,1,0:T(8,128)(2,1)S(1)}, bf16[512,3072]{1,0:T(8,128)(2,1)S(1)}) custom-call(s32[4]{0:T(128)S(1)} %pad_add_fusion.info_ref, bf16[4,4,32,3072]{3,2,1,0:T(8,128)(2,1)} %all-to-all-done.lines_ref, bf16[384,3072]{1,0:T(8,128)(2,1)S(1)} %copy-done, ...), custom_call_target="tpu_custom_call" | custom-call | flops 2415919104 | bytes 8388608 | tf_op jit(solution)/shard_map/partial_sums/pallas_call | solution.py:77
  58.6 0.0 collective-permute-done.3
  58.6 3.3 %collective-permute-start.9 = (bf16[512,3072]{1,0:T(8,128)(2,1)S(1)}, bf16[512,3072]{1,0:T(8,128)(2,1)S(1)}, u32[]{:S(2)}, u32[]{:S(2)}) collective-permute-start(bf16[512,3072]{1,0:T(8,128)(2,1)S(1)} %get-tuple-element.58.own_ref), channel_id=1, source_target_pairs={{0,1},{1,0},{2,3},{3,2},{4,5},{5,4},{6,7},{7,6},{8,9},{9,8},{10,11... | collective-permute-start | bytes 9437192 | tf_op jit(solution)/shard_map/ppermute | solution.py:283
  62.0 3.9 %collective-permute-start.4 = (bf16[2,4,32,768]{3,2,1,0:T(8,128)(2,1)S(1)}, bf16[2,4,32,768]{3,2,1,0:T(8,128)(2,1)S(1)}, u32[]{:S(2)}, u32[]{:S(2)}) collective-permute-start(bf16[2,4,32,768]{3,2,1,0:T(8,128)(2,1)S(1)} %get-tuple-element.46), channel_id=1, source_target_pairs={{0,4},{1,61},{4,8},{5,1},{8,12},{9,5},{12,16},{13,9},{16,20},{17,1... | collective-permute-start | bytes 1179656 | tf_op jit(solution)/shard_map/ppermute | solution.py:279
  65.9 2.3 %collective-permute-start.5 = (bf16[4,64,384]{2,1,0:T(8,128)(2,1)S(1)}, bf16[4,64,384]{2,1,0:T(8,128)(2,1)S(1)}, u32[]{:S(2)}, u32[]{:S(2)}) collective-permute-start(bf16[4,64,384]{2,1,0:T(8,128)(2,1)S(1)} %pad_maximum_fusion.n0_ref), channel_id=1, source_target_pairs={{0,60},{1,5},{4,0},{5,9},{8,4},{9,13},{12,8},{13,17},{16,12},{17,2... | collective-permute-start | bytes 589832 | tf_op jit(solution)/shard_map/ppermute | solution.py:278
  68.2 6.7 %collective-permute-done.5.n1_ref = bf16[4,64,384]{2,1,0:T(8,128)(2,1)S(1)} collective-permute-done((bf16[4,64,384]{2,1,0:T(8,128)(2,1)S(1)}, bf16[4,64,384]{2,1,0:T(8,128)(2,1)S(1)}, u32[]{:S(2)}, u32[]{:S(2)}) %collective-permute-start.5) | collective-permute-done | bytes 196640 | tf_op jit(solution)/shard_map/ppermute | solution.py:278
  74.9 0.0 collective-permute-done.4.r_ref
  74.9 0.1 pair_sums.1
  74.9 5.6 %collective-permute-start.6 = (bf16[4,32,768]{2,1,0:T(8,128)(2,1)S(1)}, bf16[4,32,768]{2,1,0:T(8,128)(2,1)S(1)}, u32[]{:S(2)}, u32[]{:S(2)}) collective-permute-start(bf16[4,32,768]{2,1,0:T(8,128)(2,1)S(1)} %get-tuple-element.55), channel_id=1, source_target_pairs={{0,8},{1,57},{4,12},{5,61},{8,16},{9,1},{12,20},{13,5},{16,24},{17... | collective-permute-start | bytes 589832 | tf_op jit(solution)/shard_map/ppermute | solution.py:282
  80.5 1.9 %collective-permute-start.7 = (bf16[4,64,384]{2,1,0:T(8,128)(2,1)S(1)}, bf16[4,64,384]{2,1,0:T(8,128)(2,1)S(1)}, u32[]{:S(2)}, u32[]{:S(2)}) collective-permute-start(bf16[4,64,384]{2,1,0:T(8,128)(2,1)S(1)} %pad_maximum_fusion.n0_ref), channel_id=1, source_target_pairs={{0,56},{1,9},{4,60},{5,13},{8,0},{9,17},{12,4},{13,21},{16,8},{17,... | collective-permute-start | bytes 589832 | tf_op jit(solution)/shard_map/ppermute | solution.py:278
  82.4 4.3 %collective-permute-start.8 = (bf16[4,64,384]{2,1,0:T(8,128)(2,1)S(1)}, bf16[4,64,384]{2,1,0:T(8,128)(2,1)S(1)}, u32[]{:S(2)}, u32[]{:S(2)}) collective-permute-start(bf16[4,64,384]{2,1,0:T(8,128)(2,1)S(1)} %pad_maximum_fusion.n0_ref), channel_id=1, source_target_pairs={{0,4},{1,61},{4,8},{5,1},{8,12},{9,5},{12,16},{13,9},{16,20},{17,1... | collective-permute-start | bytes 589832 | tf_op jit(solution)/shard_map/ppermute | solution.py:278
  86.8 0.0 collective-permute-done.6.r_ref
  86.8 0.6 stage_sums.1
  87.4 4.3 %collective-permute-start.10 = (bf16[32,768]{1,0:T(8,128)(2,1)S(1)}, bf16[32,768]{1,0:T(8,128)(2,1)S(1)}, u32[]{:S(2)}, u32[]{:S(2)}) collective-permute-start(bf16[32,768]{1,0:T(8,128)(2,1)S(1)} %get-tuple-element.59), channel_id=1, source_target_pairs={{0,16},{4,20},{8,24},{12,28},{16,32},{20,36},{24,40},{28,44},{32,4... | collective-permute-start | bytes 147464 | tf_op jit(solution)/shard_map/ppermute | solution.py:286
  91.6 6.1 %collective-permute-start.11 = (bf16[32,768]{1,0:T(8,128)(2,1)S(1)}, bf16[32,768]{1,0:T(8,128)(2,1)S(1)}, u32[]{:S(2)}, u32[]{:S(2)}) collective-permute-start(bf16[32,768]{1,0:T(8,128)(2,1)S(1)} %get-tuple-element.60), channel_id=1, source_target_pairs={{0,32},{4,36},{8,40},{12,44},{16,48},{20,52},{24,56},{28,60},{32,0... | collective-permute-start | bytes 147464 | tf_op jit(solution)/shard_map/ppermute | solution.py:286
  97.7 0.0 collective-permute-done.7.n2_ref
  97.7 3.5 %collective-permute-start.12 = (bf16[32,768]{1,0:T(8,128)(2,1)S(1)}, bf16[32,768]{1,0:T(8,128)(2,1)S(1)}, u32[]{:S(2)}, u32[]{:S(2)}) collective-permute-start(bf16[32,768]{1,0:T(8,128)(2,1)S(1)} %get-tuple-element.61), channel_id=1, source_target_pairs={{0,48},{4,52},{8,56},{12,60},{16,0},{20,4},{24,8},{28,12},{32,16},... | collective-permute-start | bytes 147464 | tf_op jit(solution)/shard_map/ppermute | solution.py:286
  101.2 0.0 collective-permute-done.8.n3_ref
  101.2 0.0 collective-permute-done.9.sib_ref
  101.2 5.8 %weight_sums.1 = bf16[384,3072]{1,0:T(8,128)(2,1)} custom-call(s32[4]{0:T(128)S(1)} %pad_add_fusion.info_ref, bf16[4,64,384]{2,1,0:T(8,128)(2,1)S(1)} %pad_maximum_fusion.n0_ref, bf16[4,64,384]{2,1,0:T(8,128)(2,1)S(1)} %collective-permute-done.5.n1_ref, bf16[4,64,384]{2,1,0:T(8,128)(2,1)S(1)} %collective-permute-done.7.n2_ref, ...), custom_call_target="tpu_custom_call" | custom-call | flops 2415919104 | bytes 10485760 | tf_op jit(solution)/shard_map/weight_sums/pallas_call | solution.py:188
  107.0 0.0 collective-permute-done.10.r1_ref
  107.1 0.0 collective-permute-done.11.r2_ref
  107.1 3.1 %collective-permute-done.12.r3_ref = bf16[32,768]{1,0:T(8,128)(2,1)S(1)} collective-permute-done((bf16[32,768]{1,0:T(8,128)(2,1)S(1)}, bf16[32,768]{1,0:T(8,128)(2,1)S(1)}, u32[]{:S(2)}, u32[]{:S(2)}) %collective-permute-start.12) | collective-permute-done | bytes 49184 | tf_op jit(solution)/shard_map/ppermute | solution.py:286
  110.1 7.7 %collective-permute-start.13 = (bf16[32,384]{1,0:T(8,128)(2,1)S(1)}, bf16[32,384]{1,0:T(8,128)(2,1)S(1)}, u32[]{:S(2)}, u32[]{:S(2)}) collective-permute-start(bf16[32,384]{1,0:T(8,128)(2,1)S(1)} %get-tuple-element.66), channel_id=1, source_target_pairs={{0,1},{1,0},{2,3},{3,2},{4,5},{5,4},{6,7},{7,6},{8,9},{9,8},{10,11... | collective-permute-start | bytes 73736 | tf_op jit(solution)/shard_map/ppermute | solution.py:292
  117.8 0.8 collective-permute-done.13
  118.7 0.6 pad_maximum_fusion.1
  (3 shorter events, 0.1 us)
Async XLA Ops:
  16.4 4.8 %copy-start = (bf16[384,3072]{1,0:T(8,128)(2,1)S(1)}, bf16[384,3072]{1,0:T(8,128)(2,1)}, u32[]{:S(2)}) copy-start(bf16[384,3072]{1,0:T(8,128)(2,1)} %w_own_ref.1) | copy-start | bytes 7077892
  16.4 14.6 %copy-start.1 = (bf16[64,384]{1,0:T(8,128)(2,1)S(1)}, bf16[64,384]{1,0:T(8,128)(2,1)}, u32[]{:S(2)}) copy-start(bf16[64,384]{1,0:T(8,128)(2,1)} %param.4) | copy-start | bytes 147460
  16.4 35.9 %all-to-all-start = ((bf16[4,4,32,3072]{3,2,1,0:T(8,128)(2,1)}), bf16[4,4,32,3072]{3,2,1,0:T(8,128)(2,1)}, u32[]{:S(2)}, u32[]{:S(2)}) async-start(bf16[4,4,32,3072]{3,2,1,0:T(8,128)(2,1)} %broadcast_in_dim.2), calls=%async_computation | async-start | bytes 6291456 | tf_op jit(solution)/shard_map/all_to_all | solution.py:260
  21.2 31.1 %collective-permute-start.2 = (bf16[384,3072]{1,0:T(8,128)(2,1)S(1)}, bf16[384,3072]{1,0:T(8,128)(2,1)}, u32[]{:S(2)}, u32[]{:S(2)}) collective-permute-start(bf16[384,3072]{1,0:T(8,128)(2,1)S(1)} %copy-done), channel_id=1, source_target_pairs={{0,1},{1,0},{2,3},{3,2},{4,5},{5,4},{6,7},{7,6},{8,9},{9,8},{10,11... | collective-permute-start | bytes 7077896 | tf_op jit(solution)/shard_map/ppermute | solution.py:259
  30.9 12.5 %collective-permute-start = (bf16[64,384]{1,0:T(8,128)(2,1)S(1)}, bf16[64,384]{1,0:T(8,128)(2,1)S(1)}, u32[]{:S(2)}, u32[]{:S(2)}) collective-permute-start(bf16[64,384]{1,0:T(8,128)(2,1)S(1)} %copy-done.1), channel_id=1, source_target_pairs={{0,48},{4,52},{8,56},{12,60},{16,0},{20,4},{24,8},{28,12},{32,16},... | collective-permute-start | bytes 147464 | tf_op jit(solution)/shard_map/ppermute | solution.py:268
  38.4 13.9 %collective-permute-start.1 = (bf16[64,384]{1,0:T(8,128)(2,1)S(1)}, bf16[64,384]{1,0:T(8,128)(2,1)S(1)}, u32[]{:S(2)}, u32[]{:S(2)}) collective-permute-start(bf16[64,384]{1,0:T(8,128)(2,1)S(1)} %copy-done.1), channel_id=1, source_target_pairs={{0,32},{4,36},{8,40},{12,44},{16,48},{20,52},{24,56},{28,60},{32,0... | collective-permute-start | bytes 147464 | tf_op jit(solution)/shard_map/ppermute | solution.py:268
  43.4 15.2 %collective-permute-start.3 = (bf16[64,384]{1,0:T(8,128)(2,1)S(1)}, bf16[64,384]{1,0:T(8,128)(2,1)S(1)}, u32[]{:S(2)}, u32[]{:S(2)}) collective-permute-start(bf16[64,384]{1,0:T(8,128)(2,1)S(1)} %copy-done.1), channel_id=1, source_target_pairs={{0,16},{4,20},{8,24},{12,28},{16,32},{20,36},{24,40},{28,44},{32,4... | collective-permute-start | bytes 147464 | tf_op jit(solution)/shard_map/ppermute | solution.py:270
  58.6 42.6 %collective-permute-start.9 = (bf16[512,3072]{1,0:T(8,128)(2,1)S(1)}, bf16[512,3072]{1,0:T(8,128)(2,1)S(1)}, u32[]{:S(2)}, u32[]{:S(2)}) collective-permute-start(bf16[512,3072]{1,0:T(8,128)(2,1)S(1)} %get-tuple-element.58.own_ref), channel_id=1, source_target_pairs={{0,1},{1,0},{2,3},{3,2},{4,5},{5,4},{6,7},{7,6},{8,9},{9,8},{10,11... | collective-permute-start | bytes 9437192 | tf_op jit(solution)/shard_map/ppermute | solution.py:283
  62.0 12.9 %collective-permute-start.4 = (bf16[2,4,32,768]{3,2,1,0:T(8,128)(2,1)S(1)}, bf16[2,4,32,768]{3,2,1,0:T(8,128)(2,1)S(1)}, u32[]{:S(2)}, u32[]{:S(2)}) collective-permute-start(bf16[2,4,32,768]{3,2,1,0:T(8,128)(2,1)S(1)} %get-tuple-element.46), channel_id=1, source_target_pairs={{0,4},{1,61},{4,8},{5,1},{8,12},{9,5},{12,16},{13,9},{16,20},{17,1... | collective-permute-start | bytes 1179656 | tf_op jit(solution)/shard_map/ppermute | solution.py:279
  65.9 9.0 %collective-permute-start.5 = (bf16[4,64,384]{2,1,0:T(8,128)(2,1)S(1)}, bf16[4,64,384]{2,1,0:T(8,128)(2,1)S(1)}, u32[]{:S(2)}, u32[]{:S(2)}) collective-permute-start(bf16[4,64,384]{2,1,0:T(8,128)(2,1)S(1)} %pad_maximum_fusion.n0_ref), channel_id=1, source_target_pairs={{0,60},{1,5},{4,0},{5,9},{8,4},{9,13},{12,8},{13,17},{16,12},{17,2... | collective-permute-start | bytes 589832 | tf_op jit(solution)/shard_map/ppermute | solution.py:278
  74.9 11.8 %collective-permute-start.6 = (bf16[4,32,768]{2,1,0:T(8,128)(2,1)S(1)}, bf16[4,32,768]{2,1,0:T(8,128)(2,1)S(1)}, u32[]{:S(2)}, u32[]{:S(2)}) collective-permute-start(bf16[4,32,768]{2,1,0:T(8,128)(2,1)S(1)} %get-tuple-element.55), channel_id=1, source_target_pairs={{0,8},{1,57},{4,12},{5,61},{8,16},{9,1},{12,20},{13,5},{16,24},{17... | collective-permute-start | bytes 589832 | tf_op jit(solution)/shard_map/ppermute | solution.py:282
  80.5 17.2 %collective-permute-start.7 = (bf16[4,64,384]{2,1,0:T(8,128)(2,1)S(1)}, bf16[4,64,384]{2,1,0:T(8,128)(2,1)S(1)}, u32[]{:S(2)}, u32[]{:S(2)}) collective-permute-start(bf16[4,64,384]{2,1,0:T(8,128)(2,1)S(1)} %pad_maximum_fusion.n0_ref), channel_id=1, source_target_pairs={{0,56},{1,9},{4,60},{5,13},{8,0},{9,17},{12,4},{13,21},{16,8},{17,... | collective-permute-start | bytes 589832 | tf_op jit(solution)/shard_map/ppermute | solution.py:278
  82.4 18.8 %collective-permute-start.8 = (bf16[4,64,384]{2,1,0:T(8,128)(2,1)S(1)}, bf16[4,64,384]{2,1,0:T(8,128)(2,1)S(1)}, u32[]{:S(2)}, u32[]{:S(2)}) collective-permute-start(bf16[4,64,384]{2,1,0:T(8,128)(2,1)S(1)} %pad_maximum_fusion.n0_ref), channel_id=1, source_target_pairs={{0,4},{1,61},{4,8},{5,1},{8,12},{9,5},{12,16},{13,9},{16,20},{17,1... | collective-permute-start | bytes 589832 | tf_op jit(solution)/shard_map/ppermute | solution.py:278
  87.4 19.7 %collective-permute-start.10 = (bf16[32,768]{1,0:T(8,128)(2,1)S(1)}, bf16[32,768]{1,0:T(8,128)(2,1)S(1)}, u32[]{:S(2)}, u32[]{:S(2)}) collective-permute-start(bf16[32,768]{1,0:T(8,128)(2,1)S(1)} %get-tuple-element.59), channel_id=1, source_target_pairs={{0,16},{4,20},{8,24},{12,28},{16,32},{20,36},{24,40},{28,44},{32,4... | collective-permute-start | bytes 147464 | tf_op jit(solution)/shard_map/ppermute | solution.py:286
  91.6 15.4 %collective-permute-start.11 = (bf16[32,768]{1,0:T(8,128)(2,1)S(1)}, bf16[32,768]{1,0:T(8,128)(2,1)S(1)}, u32[]{:S(2)}, u32[]{:S(2)}) collective-permute-start(bf16[32,768]{1,0:T(8,128)(2,1)S(1)} %get-tuple-element.60), channel_id=1, source_target_pairs={{0,32},{4,36},{8,40},{12,44},{16,48},{20,52},{24,56},{28,60},{32,0... | collective-permute-start | bytes 147464 | tf_op jit(solution)/shard_map/ppermute | solution.py:286
  97.7 12.4 %collective-permute-start.12 = (bf16[32,768]{1,0:T(8,128)(2,1)S(1)}, bf16[32,768]{1,0:T(8,128)(2,1)S(1)}, u32[]{:S(2)}, u32[]{:S(2)}) collective-permute-start(bf16[32,768]{1,0:T(8,128)(2,1)S(1)} %get-tuple-element.61), channel_id=1, source_target_pairs={{0,48},{4,52},{8,56},{12,60},{16,0},{20,4},{24,8},{28,12},{32,16},... | collective-permute-start | bytes 147464 | tf_op jit(solution)/shard_map/ppermute | solution.py:286
  110.1 8.5 %collective-permute-start.13 = (bf16[32,384]{1,0:T(8,128)(2,1)S(1)}, bf16[32,384]{1,0:T(8,128)(2,1)S(1)}, u32[]{:S(2)}, u32[]{:S(2)}) collective-permute-start(bf16[32,384]{1,0:T(8,128)(2,1)S(1)} %get-tuple-element.66), channel_id=1, source_target_pairs={{0,1},{1,0},{2,3},{3,2},{4,5},{5,4},{6,7},{7,6},{8,9},{9,8},{10,11... | collective-permute-start | bytes 73736 | tf_op jit(solution)/shard_map/ppermute | solution.py:292

commit v8 on v6

--- a/solution.py
+++ b/solution.py
@@ -37,32 +37,59 @@
     return pl.ds(pl.multiple_of(k * 32, 32), 32)
 
 
-def partial_kernel(info_ref, plane_ref, w_own_ref, w_sib_ref, own_ref, s1_ref, s2_ref, s3_ref, acc):
-    for n, w_ref in enumerate((w_own_ref, w_sib_ref)):
-        acc[:, n * 384 : (n + 1) * 384] = lax.dot_general(
-            plane_ref[...], w_ref[...], ROWS_BY_ROWS, preferred_element_type=jnp.float32
-        )
+def place(core, x, y):
+    return x * (1 + 3 * core) + y * (4 - 3 * core)
+
+
+def own_kernel(lines_ref, w_ref, out_ref):
+    out_ref[...] = lax.dot_general(
+        lines_ref[...], w_ref[...], ROWS_BY_ROWS, preferred_element_type=jnp.float32
+    )
+
+
+def own_sums(lines, w):
+    return pl.pallas_call(
+        own_kernel,
+        out_shape=jax.ShapeDtypeStruct((512, 384), jnp.float32),
+        in_specs=[vmem()] * 2,
+        out_specs=vmem(),
+        compiler_params=pltpu.CompilerParams(vmem_limit_bytes=16 * MIB),
+        cost_estimate=pl.CostEstimate(
+            flops=2 * 512 * 3072 * 384, bytes_accessed=6 * MIB, transcendentals=0
+        ),
+        name="own_sums",
+    )(lines, w)
+
+
+def sib_kernel(info_ref, sums_ref, lines_ref, w_ref, own_ref, s1_ref, s2_ref, s3_ref, acc):
+    acc[...] = lax.dot_general(
+        lines_ref[...], w_ref[...], ROWS_BY_ROWS, preferred_element_type=jnp.float32
+    )
+    core = info_ref[1]
     for d, out in enumerate((own_ref, s1_ref, s2_ref, s3_ref)):
         residue = lax.rem(info_ref[0] + d, 4)
         for x in range(4):
-            out[x] = acc[block_rows(x * 4 + residue), :].astype(out.dtype)
-
-
-def partial_sums(info, plane, w_own, w_sib):
-    shape = (4, 32, 768)
-    return pl.pallas_call(
-        partial_kernel,
+            mine = sums_ref[block_rows(place(core, x, residue)), :]
+            theirs = acc[block_rows(place(1 - core, x, residue)), :]
+            out[x, block_rows(core), :] = mine.astype(out.dtype)
+            out[x, block_rows(1 - core), :] = theirs.astype(out.dtype)
+
+
+def sib_sums(info, sums, lines, w):
+    shape = (4, 64, 384)
+    return pl.pallas_call(
+        sib_kernel,
         out_shape=[jax.ShapeDtypeStruct(shape, jnp.float32)]
         + [jax.ShapeDtypeStruct(shape, jnp.bfloat16)] * 3,
         in_specs=[smem()] + [vmem()] * 3,
         out_specs=[vmem()] * 4,
-        scratch_shapes=[pltpu.VMEM((512, 768), jnp.float32)],
-        compiler_params=pltpu.CompilerParams(vmem_limit_bytes=20 * MIB),
+        scratch_shapes=[pltpu.VMEM((512, 384), jnp.float32)],
+        compiler_params=pltpu.CompilerParams(vmem_limit_bytes=16 * MIB),
         cost_estimate=pl.CostEstimate(
-            flops=2 * 512 * 3072 * 768, bytes_accessed=8 * MIB, transcendentals=0
-        ),
-        name="partial_sums",
-    )(info, plane, w_own, w_sib)
+            flops=2 * 512 * 3072 * 384, bytes_accessed=8 * MIB, transcendentals=0
+        ),
+        name="sib_sums",
+    )(info, sums, lines, w)
 
 
 def stage_kernel(info_ref, own_ref, r1_ref, r2_ref, r3_ref, o_ref, s1_ref, s2_ref, s3_ref):
@@ -76,7 +103,7 @@
 
 
 def stage_sums(info, own, received):
-    shape = (32, 768)
+    shape = (64, 384)
     return pl.pallas_call(
         stage_kernel,
         out_shape=[jax.ShapeDtypeStruct(shape, jnp.float32)]
@@ -89,21 +116,19 @@
     )(info, own, *received)
 
 
-def final_kernel(own_ref, r1_ref, r2_ref, r3_ref, o_ref, s_ref):
+def final_kernel(own_ref, r1_ref, r2_ref, r3_ref, out_ref):
     total = own_ref[...]
     for r in (r1_ref, r2_ref, r3_ref):
         total = total + r[...].astype(jnp.float32)
-    o_ref[...] = total[:, :384].astype(jnp.bfloat16)
-    s_ref[...] = total[:, 384:].astype(jnp.bfloat16)
+    out_ref[...] = total.astype(jnp.bfloat16)
 
 
 def final_sums(own, received):
-    shape = jax.ShapeDtypeStruct((32, 384), jnp.bfloat16)
     return pl.pallas_call(
         final_kernel,
-        out_shape=[shape, shape],
+        out_shape=jax.ShapeDtypeStruct((64, 384), jnp.bfloat16),
         in_specs=[vmem()] * 4,
-        out_specs=[vmem()] * 2,
+        out_specs=vmem(),
         compiler_params=pltpu.CompilerParams(vmem_limit_bytes=4 * MIB),
         cost_estimate=pl.CostEstimate(flops=100000, bytes_accessed=MIB // 4, transcendentals=0),
         name="final_sums",
@@ -120,7 +145,8 @@
                 k = lax.rem(z + far + 4 * e + 16, 16)
                 for which in range(2):
                     half = core if which == 0 else 1 - core
-                    rows = pl.ds(pl.multiple_of(which * 512 + k * 32, 32), 32)
+                    at = place(half, k // 4, lax.rem(k, 4))
+                    rows = pl.ds(pl.multiple_of(which * 512 + at * 32, 32), 32)
                     tokens[rows, :] = ref[e, pl.ds(pl.multiple_of(half * 32, 32), 32), :]
         left[...] = tokens[...].T
 
@@ -153,12 +179,37 @@
     )(info, *near, hg_own, hg_sib)
 
 
+def plane_shift(first, by):
+    pairs = []
+    for x in range(4):
+        for y in range(4):
+            for core in range(2):
+                along_x = (core == 0) == first
+                to = ((x + by) % 4, y) if along_x else (x, (y + by) % 4)
+                pairs.append(((x * 4 + y) * 2 + core, (to[0] * 4 + to[1]) * 2 + core))
+    return pairs
+
+
 def far_shift(by):
     return [(z, (z + 4 * by) % 16) for z in range(16)]
 
 
 def column_shift(by):
     return [(z * 2 + c, (z + by[c]) % 16 * 2 + c) for z in range(16) for c in range(2)]
+
+
+def second_axis_groups():
+    place = [[[(x * 4 + y) * 2 + c for c in range(2)] for y in range(4)] for x in range(4)]
+    along_y = [[place[j][i][0] for i in range(4)] for j in range(4)]
+    along_x = [[place[i][j][1] for i in range(4)] for j in range(4)]
+    return along_y + along_x
+
+
+def first_axis_groups():
+    place = [[[(x * 4 + y) * 2 + c for c in range(2)] for y in range(4)] for x in range(4)]
+    along_x = [[place[i][j][0] for i in range(4)] for j in range(4)]
+    along_y = [[place[j][i][1] for i in range(4)] for j in range(4)]
+    return along_x + along_y
 
 
 NEAR = ((1, 1), (2, -2), (-1, -1))
@@ -171,39 +222,36 @@
 
     slope = gelu_slope(preactivation.astype(jnp.float32))
     local = (upstream.astype(jnp.float32) * slope).astype(jnp.bfloat16)
-    hg_own = lax.all_to_all(
-        jnp.broadcast_to(local[None], (16, 32, 3072)),
-        ("x", "yh", "yl"),
+    line = lax.all_gather(
+        local, PLANE, axis=0, tiled=True, axis_index_groups=first_axis_groups()
+    ).reshape(4, 32, 3072)
+    inputs, line = lax.optimization_barrier((inputs, line))
+    lines = lax.all_to_all(
+        jnp.broadcast_to(line[None], (4, 4, 32, 3072)),
+        PLANE,
         split_axis=0,
         concat_axis=0,
         tiled=True,
-    ).reshape(512, 3072)
-    weight_then, inputs, local = lax.optimization_barrier((weight, inputs, local))
-    w_sib = lax.ppermute(weight_then, "core", swap)
+        axis_index_groups=second_axis_groups(),
+    )
     near = [inputs] + [lax.ppermute(inputs, Z, far_shift(-d)) for d in (1, 2, 3)]
-    near, w_sib = lax.optimization_barrier((near, w_sib))
+    lines, near = lax.optimization_barrier((lines, near))
+    hg_own = lines.reshape(512, 3072)
+
+    hg_sib = lax.ppermute(hg_own, "core", swap)
+    sums = own_sums(hg_own, weight)
+    own, *sends = sib_sums(info, sums, hg_sib, weight)
+    own, near = lax.optimization_barrier((own, near))
     near = jnp.stack(near)
     nears = [near] + [lax.ppermute(near, Z + ("core",), column_shift(by)) for by in NEAR]
-    hg_own, nears = lax.optimization_barrier((hg_own, nears))
-
-    own, *sends = partial_sums(info, hg_own, weight, w_sib)
     received = [
         lax.ppermute(s, Z + ("core",), column_shift(by)) for s, by in zip(sends, NEAR)
     ]
-    hg_sib = lax.ppermute(hg_own, "core", swap)
     own, *sends = stage_sums(info, own, received)
-    received = [
-        lax.ppermute(s, Z, far_shift(d + 1))
-        for d, s in enumerate(sends)
-    ]
+    far = [lax.ppermute(s, Z, far_shift(d + 1)) for d, s in enumerate(sends)]
     weight_total = weight_sums(info, nears, hg_own, hg_sib)
-    weight_total, *received = lax.optimization_barrier((weight_total, *received))
-    mine, other = final_sums(own, received)
-    other = lax.ppermute(other, "core", swap)
-    input_gradient = jnp.concatenate(
-        [jnp.where(core == 0, mine, other), jnp.where(core == 0, other, mine)], axis=0
-    )
-    return (input_gradient, weight_total)
+    weight_total, *far = lax.optimization_barrier((weight_total, *far))
+    return (final_sums(own, far), weight_total)
 
 
 def solution(mesh):

time: 123 us -> 111 us (0.902)
  waiting for transfers between devices: 20.1 us -> 6.17 us
  blocking collectives: 0 us -> 12.4 us
  starting transfers between devices: 79 us -> 71.3 us
  local copies, waits for them, and re-layouts: 8.1 us -> 3.72 us
  Pallas kernels: 12.3 us -> 14.5 us
    all_gather x0 -> x1, blocking collectives: none -> 12.4 us  [per_device(): lax.all_gather(local, PLANE, axis=0, tiled=True, axis_index_groups=first_...]
    ppermute x3, waiting for transfers between devices: 7.75 us -> 0.01 us  [per_device(): lax.ppermute(s, Z + ('core',), column_shift(by))]
    ppermute x3, waiting for transfers between devices: 7.3 us -> 0.01 us  [per_device(): lax.ppermute(near, Z + ('core',), column_shift(by))]
    ppermute x5 -> x3, starting transfers between devices: 24.5 us -> 17.4 us  [per_device(): far = [lax.ppermute(s, Z, far_shift(d + 1)) for d, s in enumerate(sends)]]
    unnamed x16 -> x4, local copies, waits for them, and re-layouts: 6.08 us -> 1.67 us
    all_to_all x1, starting transfers between devices: 7.72 us -> 3.83 us  [per_device(): lax.all_to_all(jnp.broadcast_to(line[None], (4, 4, 32, 3072)), PLANE, spl...]
    ppermute x3, starting transfers between devices: 8.58 us -> 10.7 us  [per_device(): lax.ppermute(s, Z + ('core',), column_shift(by))]
    pallas_call x2 -> x3, Pallas kernels: 4.13 us -> 6.23 us  [the longest x1 3.78 us: sib_sums(): pl.pallas_call(sib_kernel, out_shape=[jax.ShapeDtypeStruct(shape, jnp.flo...]
  transfers between devices with their start and end apart: 16 -> 14, of which waited for: 7 -> 3; matrix products, arithmetic and copies ran while one was open for 0% -> 0% of each run, Pallas kernels for 10% -> 9%
where the time goes in v8:
time: 111 us; the launch traced here: 110 us
  starting transfers between devices  71.3 us (64%)
  Pallas kernels  14.5 us (13%)
  blocking collectives  12.4 us (11%)
  waiting for transfers between devices  6.17 us (6%)
  local copies, waits for them, and re-layouts  3.72 us (3%)
  other arithmetic  1.41 us (1%)
    ppermute x3, starting transfers between devices, per_device(): lax.ppermute(inputs, Z, far_shift(-d))  24.4 us
    ppermute x3, starting transfers between devices, per_device(): far = [lax.ppermute(s, Z, far_shift(d + 1)) for d, s in enumerate(sends)]  17.4 us
    all_gather x1, blocking collectives, per_device(): lax.all_gather(local, PLANE, axis=0, tiled=True, axis_index_groups=first_...  12.4 us
    ppermute x3, starting transfers between devices, per_device(): lax.ppermute(s, Z + ('core',), column_shift(by))  10.7 us
    ppermute x3, starting transfers between devices, per_device(): lax.ppermute(near, Z + ('core',), column_shift(by))  9.09 us
    pallas_call x1, Pallas kernels, weight_sums(): pl.pallas_call(weight_kernel, out_shape=jax.ShapeDtypeStruct((384, 3072),...  7.64 us
    ppermute x1, starting transfers between devices, per_device(): hg_sib = lax.ppermute(hg_own, 'core', swap)  5.8 us
    ppermute x3, waiting for transfers between devices, per_device(): lax.ppermute(inputs, Z, far_shift(-d))  4.3 us
  transfers between devices with their start and end apart: 14, of which 3 were waited for; matrix products, arithmetic and copies ran while one was open for 0% of the time, Pallas kernels for 9%

profile of v8, /device:TPU:1, one launch (start us, length us, event | category | flops | bytes accessed | tf_op | source)
XLA Modules:
  0.0 110.3 jit_solution(12347125033441309158)
XLA Ops:
  0.6 1.3 %fusion.7 = bf16[32,3072]{1,0:T(8,128)(2,1)S(1)} fusion(bf16[32,3072]{1,0:T(8,128)(2,1)} %param.7, bf16[32,3072]{1,0:T(8,128)(2,1)} %param.6), kind=kLoop, calls=%fused_computation.14 | loop fusion | flops 2064384 | bytes 589824 | tf_op jit(solution)/shard_map/convert_element_type | solution.py:224
  1.9 12.4 %all_gather.3 = bf16[128,3072]{1,0:T(8,128)(2,1)S(1)} all-gather(bf16[32,3072]{1,0:T(8,128)(2,1)S(1)} %fusion.7), channel_id=1, replica_groups={{0,128,256,384},{2,130,258,386},{64,192,320,448},{66,194,322,450},{1,3,..., dimensions={0}, use_global_device_ids=true | all-gather | bytes 983040 | tf_op jit(solution)/shard_map/all_gather | solution.py:225
  14.3 2.1 %broadcast_in_dim.2 = bf16[4,4,32,3072]{3,2,1,0:T(8,128)(2,1)} broadcast(bf16[4,32,3072]{2,1,0:T(8,128)(2,1)S(1)} %bitcast.11), dimensions={1,2,3} | broadcast | bytes 3932160 | tf_op jit(solution)/shard_map/broadcast_in_dim | solution.py:230
  16.3 0.0 copy-start.1
  16.4 3.8 %all-to-all-start = ((bf16[4,4,32,3072]{3,2,1,0:T(8,128)(2,1)}), bf16[4,4,32,3072]{3,2,1,0:T(8,128)(2,1)S(1)}, u32[]{:S(2)}, u32[]{:S(2)}) async-start(bf16[4,4,32,3072]{3,2,1,0:T(8,128)(2,1)} %broadcast_in_dim.2), calls=%async_computation | async-start | bytes 6291456 | tf_op jit(solution)/shard_map/all_to_all | solution.py:229
  20.2 0.0 copy-done.1
  20.2 12.2 %collective-permute-start = (bf16[64,384]{1,0:T(8,128)(2,1)S(1)}, bf16[64,384]{1,0:T(8,128)(2,1)S(1)}, u32[]{:S(2)}, u32[]{:S(2)}) collective-permute-start(bf16[64,384]{1,0:T(8,128)(2,1)S(1)} %copy-done.1), channel_id=1, source_target_pairs={{0,48},{4,52},{8,56},{12,60},{16,0},{20,4},{24,8},{28,12},{32,16},... | collective-permute-start | bytes 147464 | tf_op jit(solution)/shard_map/ppermute | solution.py:237
  32.4 4.9 %collective-permute-start.1 = (bf16[64,384]{1,0:T(8,128)(2,1)S(1)}, bf16[64,384]{1,0:T(8,128)(2,1)S(1)}, u32[]{:S(2)}, u32[]{:S(2)}) collective-permute-start(bf16[64,384]{1,0:T(8,128)(2,1)S(1)} %copy-done.1), channel_id=1, source_target_pairs={{0,32},{4,36},{8,40},{12,44},{16,48},{20,52},{24,56},{28,60},{32,0... | collective-permute-start | bytes 147464 | tf_op jit(solution)/shard_map/ppermute | solution.py:237
  37.4 7.3 %collective-permute-start.2 = (bf16[64,384]{1,0:T(8,128)(2,1)S(1)}, bf16[64,384]{1,0:T(8,128)(2,1)S(1)}, u32[]{:S(2)}, u32[]{:S(2)}) collective-permute-start(bf16[64,384]{1,0:T(8,128)(2,1)S(1)} %copy-done.1), channel_id=1, source_target_pairs={{0,16},{4,20},{8,24},{12,28},{16,32},{20,36},{24,40},{28,44},{32,4... | collective-permute-start | bytes 147464 | tf_op jit(solution)/shard_map/ppermute | solution.py:237
  44.6 0.0 collective-permute-done
  44.6 1.7 %collective-permute-done.1 = bf16[64,384]{1,0:T(8,128)(2,1)S(1)} collective-permute-done((bf16[64,384]{1,0:T(8,128)(2,1)S(1)}, bf16[64,384]{1,0:T(8,128)(2,1)S(1)}, u32[]{:S(2)}, u32[]{:S(2)}) %collective-permute-start.1) | collective-permute-done | bytes 49184 | tf_op jit(solution)/shard_map/ppermute | solution.py:237
  46.3 2.6 %collective-permute-done.2 = bf16[64,384]{1,0:T(8,128)(2,1)S(1)} collective-permute-done((bf16[64,384]{1,0:T(8,128)(2,1)S(1)}, bf16[64,384]{1,0:T(8,128)(2,1)S(1)}, u32[]{:S(2)}, u32[]{:S(2)}) %collective-permute-start.2) | collective-permute-done | bytes 49184 | tf_op jit(solution)/shard_map/ppermute | solution.py:237
  48.9 0.0 all-to-all-done
  48.9 5.8 %collective-permute-start.3 = (bf16[512,3072]{1,0:T(8,128)(2,1)S(1)}, bf16[512,3072]{1,0:T(8,128)(2,1)}, u32[]{:S(2)}, u32[]{:S(2)}) collective-permute-start(bf16[512,3072]{1,0:T(8,128)(2,1)S(1)} %bitcast.8), channel_id=1, source_target_pairs={{0,1},{1,0},{2,3},{3,2},{4,5},{5,4},{6,7},{7,6},{8,9},{9,8},{10,11... | collective-permute-start | bytes 9437192 | tf_op jit(solution)/shard_map/ppermute | solution.py:241
  54.8 0.1 pad_add_fusion.info_ref
  54.8 0.0 copy-start
  54.8 1.7 %copy-done = bf16[384,3072]{1,0:T(8,128)(2,1)S(1)} copy-done((bf16[384,3072]{1,0:T(8,128)(2,1)S(1)}, bf16[384,3072]{1,0:T(8,128)(2,1)}, u32[]{:S(2)}) %copy-start) | copy-done | bytes 2359320
  56.5 1.8 %own_sums.1.sums_ref = f32[512,384]{1,0:T(8,128)S(1)} custom-call(bf16[512,3072]{1,0:T(8,128)(2,1)S(1)} %bitcast.9, bf16[384,3072]{1,0:T(8,128)(2,1)S(1)} %copy-done), custom_call_target="tpu_custom_call" | custom-call | flops 1207959552 | bytes 6291456 | tf_op jit(solution)/shard_map/own_sums/pallas_call | solution.py:51
  58.3 1.8 %collective-permute-done.3.lines_ref.sib_ref = bf16[512,3072]{1,0:T(8,128)(2,1)} collective-permute-done((bf16[512,3072]{1,0:T(8,128)(2,1)S(1)}, bf16[512,3072]{1,0:T(8,128)(2,1)}, u32[]{:S(2)}, u32[]{:S(2)}) %collective-permute-start.3) | collective-permute-done | bytes 3145760 | tf_op jit(solution)/shard_map/ppermute | solution.py:241
  60.2 3.8 %sib_sums.1 = (f32[4,64,384]{2,1,0:T(8,128)S(1)}, bf16[4,64,384]{2,1,0:T(8,128)(2,1)S(1)}, bf16[4,64,384]{2,1,0:T(8,128)(2,1)S(1)}, bf16[4,64,384]{2,1,0:T(8,128)(2,1)S(1)}) custom-call(s32[2]{0:T(128)S(1)} %pad_add_fusion.info_ref, f32[512,384]{1,0:T(8,128)S(1)} %own_sums.1.sums_ref, bf16[512,3072]{1,0:T(8,128)(2,1)} %collective-permute-done.3.lines_ref.sib_ref, ...), custom_call_target="tpu_custom_call" | custom-call | flops 1207959552 | bytes 8388608 | tf_op jit(solution)/shard_map/sib_sums/pallas_call | solution.py:80
  63.9 3.6 %collective-permute-start.4 = (bf16[4,64,384]{2,1,0:T(8,128)(2,1)S(1)}, bf16[4,64,384]{2,1,0:T(8,128)(2,1)S(1)}, u32[]{:S(2)}, u32[]{:S(2)}) collective-permute-start(bf16[4,64,384]{2,1,0:T(8,128)(2,1)S(1)} %get-tuple-element.35), channel_id=1, source_target_pairs={{0,4},{1,5},{4,8},{5,9},{8,12},{9,13},{12,16},{13,17},{16,20},{17,... | collective-permute-start | bytes 589832 | tf_op jit(solution)/shard_map/ppermute | solution.py:248
  67.5 3.8 %collective-permute-start.5 = (bf16[4,64,384]{2,1,0:T(8,128)(2,1)S(1)}, bf16[4,64,384]{2,1,0:T(8,128)(2,1)S(1)}, u32[]{:S(2)}, u32[]{:S(2)}) collective-permute-start(bf16[4,64,384]{2,1,0:T(8,128)(2,1)S(1)} %get-tuple-element.36), channel_id=1, source_target_pairs={{0,8},{1,57},{4,12},{5,61},{8,16},{9,1},{12,20},{13,5},{16,24},{17... | collective-permute-start | bytes 589832 | tf_op jit(solution)/shard_map/ppermute | solution.py:248
  71.3 3.4 %collective-permute-start.6 = (bf16[4,64,384]{2,1,0:T(8,128)(2,1)S(1)}, bf16[4,64,384]{2,1,0:T(8,128)(2,1)S(1)}, u32[]{:S(2)}, u32[]{:S(2)}) collective-permute-start(bf16[4,64,384]{2,1,0:T(8,128)(2,1)S(1)} %get-tuple-element.37), channel_id=1, source_target_pairs={{0,60},{1,61},{4,0},{5,1},{8,4},{9,5},{12,8},{13,9},{16,12},{17,13... | collective-permute-start | bytes 589832 | tf_op jit(solution)/shard_map/ppermute | solution.py:248
  74.7 1.9 %collective-permute-start.7 = (bf16[4,64,384]{2,1,0:T(8,128)(2,1)S(1)}, bf16[4,64,384]{2,1,0:T(8,128)(2,1)S(1)}, u32[]{:S(2)}, u32[]{:S(2)}) collective-permute-start(bf16[4,64,384]{2,1,0:T(8,128)(2,1)S(1)} %pad_maximum_fusion.n0_ref), channel_id=1, source_target_pairs={{0,4},{1,5},{4,8},{5,9},{8,12},{9,13},{12,16},{13,17},{16,20},{17,... | collective-permute-start | bytes 589832 | tf_op jit(solution)/shard_map/ppermute | solution.py:246
  76.7 3.8 %collective-permute-start.8 = (bf16[4,64,384]{2,1,0:T(8,128)(2,1)S(1)}, bf16[4,64,384]{2,1,0:T(8,128)(2,1)S(1)}, u32[]{:S(2)}, u32[]{:S(2)}) collective-permute-start(bf16[4,64,384]{2,1,0:T(8,128)(2,1)S(1)} %pad_maximum_fusion.n0_ref), channel_id=1, source_target_pairs={{0,8},{1,57},{4,12},{5,61},{8,16},{9,1},{12,20},{13,5},{16,24},{17... | collective-permute-start | bytes 589832 | tf_op jit(solution)/shard_map/ppermute | solution.py:246
  80.5 0.0 collective-permute-done.4.r1_ref
  80.5 3.4 %collective-permute-start.9 = (bf16[4,64,384]{2,1,0:T(8,128)(2,1)S(1)}, bf16[4,64,384]{2,1,0:T(8,128)(2,1)S(1)}, u32[]{:S(2)}, u32[]{:S(2)}) collective-permute-start(bf16[4,64,384]{2,1,0:T(8,128)(2,1)S(1)} %pad_maximum_fusion.n0_ref), channel_id=1, source_target_pairs={{0,60},{1,61},{4,0},{5,1},{8,4},{9,5},{12,8},{13,9},{16,12},{17,13... | collective-permute-start | bytes 589832 | tf_op jit(solution)/shard_map/ppermute | solution.py:246
  83.8 0.0 collective-permute-done.5.r2_ref
  83.9 0.0 collective-permute-done.6.r3_ref
  83.9 0.6 stage_sums.1
  84.5 5.7 %collective-permute-start.10 = (bf16[64,384]{1,0:T(8,128)(2,1)S(1)}, bf16[64,384]{1,0:T(8,128)(2,1)S(1)}, u32[]{:S(2)}, u32[]{:S(2)}) collective-permute-start(bf16[64,384]{1,0:T(8,128)(2,1)S(1)} %get-tuple-element.43), channel_id=1, source_target_pairs={{0,16},{4,20},{8,24},{12,28},{16,32},{20,36},{24,40},{28,44},{32,4... | collective-permute-start | bytes 147464 | tf_op jit(solution)/shard_map/ppermute | solution.py:251
  90.2 6.1 %collective-permute-start.11 = (bf16[64,384]{1,0:T(8,128)(2,1)S(1)}, bf16[64,384]{1,0:T(8,128)(2,1)S(1)}, u32[]{:S(2)}, u32[]{:S(2)}) collective-permute-start(bf16[64,384]{1,0:T(8,128)(2,1)S(1)} %get-tuple-element.44), channel_id=1, source_target_pairs={{0,32},{4,36},{8,40},{12,44},{16,48},{20,52},{24,56},{28,60},{32,0... | collective-permute-start | bytes 147464 | tf_op jit(solution)/shard_map/ppermute | solution.py:251
  96.4 0.0 collective-permute-done.7.n1_ref
  96.4 5.6 %collective-permute-start.12 = (bf16[64,384]{1,0:T(8,128)(2,1)S(1)}, bf16[64,384]{1,0:T(8,128)(2,1)S(1)}, u32[]{:S(2)}, u32[]{:S(2)}) collective-permute-start(bf16[64,384]{1,0:T(8,128)(2,1)S(1)} %get-tuple-element.45), channel_id=1, source_target_pairs={{0,48},{4,52},{8,56},{12,60},{16,0},{20,4},{24,8},{28,12},{32,16},... | collective-permute-start | bytes 147464 | tf_op jit(solution)/shard_map/ppermute | solution.py:251
  102.0 0.0 collective-permute-done.8.n2_ref
  102.0 0.0 collective-permute-done.9.n3_ref
  102.0 7.6 %weight_sums.1 = bf16[384,3072]{1,0:T(8,128)(2,1)} custom-call(s32[2]{0:T(128)S(1)} %pad_add_fusion.info_ref, bf16[4,64,384]{2,1,0:T(8,128)(2,1)S(1)} %pad_maximum_fusion.n0_ref, bf16[4,64,384]{2,1,0:T(8,128)(2,1)S(1)} %collective-permute-done.7.n1_ref, bf16[4,64,384]{2,1,0:T(8,128)(2,1)S(1)} %collective-permute-done.8.n2_ref, ...), custom_call_target="tpu_custom_call" | custom-call | flops 2415919104 | bytes 10485760 | tf_op jit(solution)/shard_map/weight_sums/pallas_call | solution.py:160
  109.7 0.0 collective-permute-done.10.r1_ref
  109.7 0.0 collective-permute-done.11.r2_ref
  109.7 0.0 collective-permute-done.12.r3_ref
  109.7 0.6 final_sums.1
  (1 shorter events, 0.0 us)
Async XLA Ops:
  16.3 3.8 %copy-start.1 = (bf16[64,384]{1,0:T(8,128)(2,1)S(1)}, bf16[64,384]{1,0:T(8,128)(2,1)}, u32[]{:S(2)}) copy-start(bf16[64,384]{1,0:T(8,128)(2,1)} %param.4) | copy-start | bytes 147460
  16.4 32.6 %all-to-all-start = ((bf16[4,4,32,3072]{3,2,1,0:T(8,128)(2,1)}), bf16[4,4,32,3072]{3,2,1,0:T(8,128)(2,1)S(1)}, u32[]{:S(2)}, u32[]{:S(2)}) async-start(bf16[4,4,32,3072]{3,2,1,0:T(8,128)(2,1)} %broadcast_in_dim.2), calls=%async_computation | async-start | bytes 6291456 | tf_op jit(solution)/shard_map/all_to_all | solution.py:229
  20.2 24.4 %collective-permute-start = (bf16[64,384]{1,0:T(8,128)(2,1)S(1)}, bf16[64,384]{1,0:T(8,128)(2,1)S(1)}, u32[]{:S(2)}, u32[]{:S(2)}) collective-permute-start(bf16[64,384]{1,0:T(8,128)(2,1)S(1)} %copy-done.1), channel_id=1, source_target_pairs={{0,48},{4,52},{8,56},{12,60},{16,0},{20,4},{24,8},{28,12},{32,16},... | collective-permute-start | bytes 147464 | tf_op jit(solution)/shard_map/ppermute | solution.py:237
  32.4 13.9 %collective-permute-start.1 = (bf16[64,384]{1,0:T(8,128)(2,1)S(1)}, bf16[64,384]{1,0:T(8,128)(2,1)S(1)}, u32[]{:S(2)}, u32[]{:S(2)}) collective-permute-start(bf16[64,384]{1,0:T(8,128)(2,1)S(1)} %copy-done.1), channel_id=1, source_target_pairs={{0,32},{4,36},{8,40},{12,44},{16,48},{20,52},{24,56},{28,60},{32,0... | collective-permute-start | bytes 147464 | tf_op jit(solution)/shard_map/ppermute | solution.py:237
  37.4 11.6 %collective-permute-start.2 = (bf16[64,384]{1,0:T(8,128)(2,1)S(1)}, bf16[64,384]{1,0:T(8,128)(2,1)S(1)}, u32[]{:S(2)}, u32[]{:S(2)}) collective-permute-start(bf16[64,384]{1,0:T(8,128)(2,1)S(1)} %copy-done.1), channel_id=1, source_target_pairs={{0,16},{4,20},{8,24},{12,28},{16,32},{20,36},{24,40},{28,44},{32,4... | collective-permute-start | bytes 147464 | tf_op jit(solution)/shard_map/ppermute | solution.py:237
  48.9 11.2 %collective-permute-start.3 = (bf16[512,3072]{1,0:T(8,128)(2,1)S(1)}, bf16[512,3072]{1,0:T(8,128)(2,1)}, u32[]{:S(2)}, u32[]{:S(2)}) collective-permute-start(bf16[512,3072]{1,0:T(8,128)(2,1)S(1)} %bitcast.8), channel_id=1, source_target_pairs={{0,1},{1,0},{2,3},{3,2},{4,5},{5,4},{6,7},{7,6},{8,9},{9,8},{10,11... | collective-permute-start | bytes 9437192 | tf_op jit(solution)/shard_map/ppermute | solution.py:241
  54.8 1.7 %copy-start = (bf16[384,3072]{1,0:T(8,128)(2,1)S(1)}, bf16[384,3072]{1,0:T(8,128)(2,1)}, u32[]{:S(2)}) copy-start(bf16[384,3072]{1,0:T(8,128)(2,1)} %w_ref.3) | copy-start | bytes 7077892
  63.9 16.5 %collective-permute-start.4 = (bf16[4,64,384]{2,1,0:T(8,128)(2,1)S(1)}, bf16[4,64,384]{2,1,0:T(8,128)(2,1)S(1)}, u32[]{:S(2)}, u32[]{:S(2)}) collective-permute-start(bf16[4,64,384]{2,1,0:T(8,128)(2,1)S(1)} %get-tuple-element.35), channel_id=1, source_target_pairs={{0,4},{1,5},{4,8},{5,9},{8,12},{9,13},{12,16},{13,17},{16,20},{17,... | collective-permute-start | bytes 589832 | tf_op jit(solution)/shard_map/ppermute | solution.py:248
  67.5 16.3 %collective-permute-start.5 = (bf16[4,64,384]{2,1,0:T(8,128)(2,1)S(1)}, bf16[4,64,384]{2,1,0:T(8,128)(2,1)S(1)}, u32[]{:S(2)}, u32[]{:S(2)}) collective-permute-start(bf16[4,64,384]{2,1,0:T(8,128)(2,1)S(1)} %get-tuple-element.36), channel_id=1, source_target_pairs={{0,8},{1,57},{4,12},{5,61},{8,16},{9,1},{12,20},{13,5},{16,24},{17... | collective-permute-start | bytes 589832 | tf_op jit(solution)/shard_map/ppermute | solution.py:248
  71.3 12.5 %collective-permute-start.6 = (bf16[4,64,384]{2,1,0:T(8,128)(2,1)S(1)}, bf16[4,64,384]{2,1,0:T(8,128)(2,1)S(1)}, u32[]{:S(2)}, u32[]{:S(2)}) collective-permute-start(bf16[4,64,384]{2,1,0:T(8,128)(2,1)S(1)} %get-tuple-element.37), channel_id=1, source_target_pairs={{0,60},{1,61},{4,0},{5,1},{8,4},{9,5},{12,8},{13,9},{16,12},{17,13... | collective-permute-start | bytes 589832 | tf_op jit(solution)/shard_map/ppermute | solution.py:248
  74.7 21.6 %collective-permute-start.7 = (bf16[4,64,384]{2,1,0:T(8,128)(2,1)S(1)}, bf16[4,64,384]{2,1,0:T(8,128)(2,1)S(1)}, u32[]{:S(2)}, u32[]{:S(2)}) collective-permute-start(bf16[4,64,384]{2,1,0:T(8,128)(2,1)S(1)} %pad_maximum_fusion.n0_ref), channel_id=1, source_target_pairs={{0,4},{1,5},{4,8},{5,9},{8,12},{9,13},{12,16},{13,17},{16,20},{17,... | collective-permute-start | bytes 589832 | tf_op jit(solution)/shard_map/ppermute | solution.py:246
  76.7 25.3 %collective-permute-start.8 = (bf16[4,64,384]{2,1,0:T(8,128)(2,1)S(1)}, bf16[4,64,384]{2,1,0:T(8,128)(2,1)S(1)}, u32[]{:S(2)}, u32[]{:S(2)}) collective-permute-start(bf16[4,64,384]{2,1,0:T(8,128)(2,1)S(1)} %pad_maximum_fusion.n0_ref), channel_id=1, source_target_pairs={{0,8},{1,57},{4,12},{5,61},{8,16},{9,1},{12,20},{13,5},{16,24},{17... | collective-permute-start | bytes 589832 | tf_op jit(solution)/shard_map/ppermute | solution.py:246
  80.5 21.5 %collective-permute-start.9 = (bf16[4,64,384]{2,1,0:T(8,128)(2,1)S(1)}, bf16[4,64,384]{2,1,0:T(8,128)(2,1)S(1)}, u32[]{:S(2)}, u32[]{:S(2)}) collective-permute-start(bf16[4,64,384]{2,1,0:T(8,128)(2,1)S(1)} %pad_maximum_fusion.n0_ref), channel_id=1, source_target_pairs={{0,60},{1,61},{4,0},{5,1},{8,4},{9,5},{12,8},{13,9},{16,12},{17,13... | collective-permute-start | bytes 589832 | tf_op jit(solution)/shard_map/ppermute | solution.py:246
  84.5 25.1 %collective-permute-start.10 = (bf16[64,384]{1,0:T(8,128)(2,1)S(1)}, bf16[64,384]{1,0:T(8,128)(2,1)S(1)}, u32[]{:S(2)}, u32[]{:S(2)}) collective-permute-start(bf16[64,384]{1,0:T(8,128)(2,1)S(1)} %get-tuple-element.43), channel_id=1, source_target_pairs={{0,16},{4,20},{8,24},{12,28},{16,32},{20,36},{24,40},{28,44},{32,4... | collective-permute-start | bytes 147464 | tf_op jit(solution)/shard_map/ppermute | solution.py:251
  90.2 19.4 %collective-permute-start.11 = (bf16[64,384]{1,0:T(8,128)(2,1)S(1)}, bf16[64,384]{1,0:T(8,128)(2,1)S(1)}, u32[]{:S(2)}, u32[]{:S(2)}) collective-permute-start(bf16[64,384]{1,0:T(8,128)(2,1)S(1)} %get-tuple-element.44), channel_id=1, source_target_pairs={{0,32},{4,36},{8,40},{12,44},{16,48},{20,52},{24,56},{28,60},{32,0... | collective-permute-start | bytes 147464 | tf_op jit(solution)/shard_map/ppermute | solution.py:251
  96.4 13.3 %collective-permute-start.12 = (bf16[64,384]{1,0:T(8,128)(2,1)S(1)}, bf16[64,384]{1,0:T(8,128)(2,1)S(1)}, u32[]{:S(2)}, u32[]{:S(2)}) collective-permute-start(bf16[64,384]{1,0:T(8,128)(2,1)S(1)} %get-tuple-element.45), channel_id=1, source_target_pairs={{0,48},{4,52},{8,56},{12,60},{16,0},{20,4},{24,8},{28,12},{32,16},... | collective-permute-start | bytes 147464 | tf_op jit(solution)/shard_map/ppermute | solution.py:251

commit v9 on v8

--- a/solution.py
+++ b/solution.py
@@ -61,10 +61,22 @@
     )(lines, w)
 
 
-def sib_kernel(info_ref, sums_ref, lines_ref, w_ref, own_ref, s1_ref, s2_ref, s3_ref, acc):
-    acc[...] = lax.dot_general(
-        lines_ref[...], w_ref[...], ROWS_BY_ROWS, preferred_element_type=jnp.float32
-    )
+def sib_kernel(info_ref, sums_ref, lines_ref, w_ref, own_ref, s1_ref, s2_ref, s3_ref, acc, chunks, sems):
+    copies = [
+        pltpu.make_async_copy(lines_ref.at[:, pl.ds(c * 768, 768)], chunks.at[c], sems.at[c])
+        for c in range(4)
+    ]
+    for copy in copies:
+        copy.start()
+    for c, copy in enumerate(copies):
+        copy.wait()
+        part = lax.dot_general(
+            chunks[c],
+            w_ref[:, c * 768 : (c + 1) * 768],
+            ROWS_BY_ROWS,
+            preferred_element_type=jnp.float32,
+        )
+        acc[...] = part if c == 0 else acc[...] + part
     core = info_ref[1]
     for d, out in enumerate((own_ref, s1_ref, s2_ref, s3_ref)):
         residue = lax.rem(info_ref[0] + d, 4)
@@ -81,9 +93,13 @@
         sib_kernel,
         out_shape=[jax.ShapeDtypeStruct(shape, jnp.float32)]
         + [jax.ShapeDtypeStruct(shape, jnp.bfloat16)] * 3,
-        in_specs=[smem()] + [vmem()] * 3,
+        in_specs=[smem(), vmem(), pl.BlockSpec(memory_space=pl.ANY), vmem()],
         out_specs=[vmem()] * 4,
-        scratch_shapes=[pltpu.VMEM((512, 384), jnp.float32)],
+        scratch_shapes=[
+            pltpu.VMEM((512, 384), jnp.float32),
+            pltpu.VMEM((4, 512, 768), jnp.bfloat16),
+            pltpu.SemaphoreType.DMA((4,)),
+        ],
         compiler_params=pltpu.CompilerParams(vmem_limit_bytes=16 * MIB),
         cost_estimate=pl.CostEstimate(
             flops=2 * 512 * 3072 * 384, bytes_accessed=8 * MIB, transcendentals=0
@@ -239,11 +255,14 @@
     hg_own = lines.reshape(512, 3072)
 
     hg_sib = lax.ppermute(hg_own, "core", swap)
+    near = jnp.stack(near)
+    first = lax.ppermute(near, Z + ("core",), column_shift(NEAR[0]))
     sums = own_sums(hg_own, weight)
+    sums, first = lax.optimization_barrier((sums, first))
     own, *sends = sib_sums(info, sums, hg_sib, weight)
     own, near = lax.optimization_barrier((own, near))
-    near = jnp.stack(near)
-    nears = [near] + [lax.ppermute(near, Z + ("core",), column_shift(by)) for by in NEAR]
+    nears = [near, first]
+    nears += [lax.ppermute(near, Z + ("core",), column_shift(by)) for by in NEAR[1:]]
     received = [
         lax.ppermute(s, Z + ("core",), column_shift(by)) for s, by in zip(sends, NEAR)
     ]

time: 111 us -> 114 us (1.027)
  waiting for transfers between devices: 6.17 us -> 7.77 us
  starting transfers between devices: 71.3 us -> 72.6 us
    ppermute x0 -> x1, starting transfers between devices: none -> 3.57 us  [per_device(): first = lax.ppermute(near, Z + ('core',), column_shift(NEAR[0]))]
    ppermute x0 -> x1, waiting for transfers between devices: none -> 2.5 us  [per_device(): first = lax.ppermute(near, Z + ('core',), column_shift(NEAR[0]))]
    ppermute x3 -> x2, starting transfers between devices: 9.09 us -> 7 us  [per_device(): lax.ppermute(near, Z + ('core',), column_shift(by))]
    ppermute x1, waiting for transfers between devices: 1.84 us -> 0.01 us  [per_device(): hg_sib = lax.ppermute(hg_own, 'core', swap)]
    ppermute x3, starting transfers between devices: 10.7 us -> 9.51 us  [per_device(): lax.ppermute(s, Z + ('core',), column_shift(by))]
  transfers between devices with their start and end apart: 14 -> 14, of which waited for: 3 -> 4; matrix products, arithmetic and copies ran while one was open for 0% -> 0% of each run, Pallas kernels for 9% -> 9%
where the time goes in v9:
time: 114 us; the launch traced here: 113 us
  starting transfers between devices  72.6 us (64%)
  Pallas kernels  14.5 us (13%)
  blocking collectives  12.4 us (11%)
  waiting for transfers between devices  7.77 us (7%)
  local copies, waits for them, and re-layouts  3.7 us (3%)
  other arithmetic  1.41 us (1%)
    ppermute x3, starting transfers between devices, per_device(): lax.ppermute(inputs, Z, far_shift(-d))  24.4 us
    ppermute x3, starting transfers between devices, per_device(): far = [lax.ppermute(s, Z, far_shift(d + 1)) for d, s in enumerate(sends)]  18.5 us
    all_gather x1, blocking collectives, per_device(): lax.all_gather(local, PLANE, axis=0, tiled=True, axis_index_groups=first_...  12.4 us
    ppermute x3, starting transfers between devices, per_device(): lax.ppermute(s, Z + ('core',), column_shift(by))  9.51 us
    pallas_call x1, Pallas kernels, weight_sums(): pl.pallas_call(weight_kernel, out_shape=jax.ShapeDtypeStruct((384, 3072),...  7.64 us
    ppermute x2, starting transfers between devices, per_device(): lax.ppermute(near, Z + ('core',), column_shift(by))  7 us
    ppermute x1, starting transfers between devices, per_device(): hg_sib = lax.ppermute(hg_own, 'core', swap)  5.8 us
    ppermute x3, waiting for transfers between devices, per_device(): lax.ppermute(inputs, Z, far_shift(-d))  4.3 us
  transfers between devices with their start and end apart: 14, of which 4 were waited for; matrix products, arithmetic and copies ran while one was open for 0% of the time, Pallas kernels for 9%

profile of v9, /device:TPU:1, one launch (start us, length us, event | category | flops | bytes accessed | tf_op | source)
XLA Modules:
  0.0 113.3 jit_solution(12697598723740341569)
XLA Ops:
  0.6 1.3 %fusion.7 = bf16[32,3072]{1,0:T(8,128)(2,1)S(1)} fusion(bf16[32,3072]{1,0:T(8,128)(2,1)} %param.7, bf16[32,3072]{1,0:T(8,128)(2,1)} %param.6), kind=kLoop, calls=%fused_computation.14 | loop fusion | flops 2064384 | bytes 589824 | tf_op jit(solution)/shard_map/convert_element_type | solution.py:240
  1.9 12.4 %all_gather.3 = bf16[128,3072]{1,0:T(8,128)(2,1)S(1)} all-gather(bf16[32,3072]{1,0:T(8,128)(2,1)S(1)} %fusion.7), channel_id=1, replica_groups={{0,128,256,384},{2,130,258,386},{64,192,320,448},{66,194,322,450},{1,3,..., dimensions={0}, use_global_device_ids=true | all-gather | bytes 983040 | tf_op jit(solution)/shard_map/all_gather | solution.py:241
  14.3 2.0 %broadcast_in_dim.2 = bf16[4,4,32,3072]{3,2,1,0:T(8,128)(2,1)} broadcast(bf16[4,32,3072]{2,1,0:T(8,128)(2,1)S(1)} %bitcast.11), dimensions={1,2,3} | broadcast | bytes 3932160 | tf_op jit(solution)/shard_map/broadcast_in_dim | solution.py:246
  16.3 0.0 copy-start.1
  16.3 3.8 %all-to-all-start = ((bf16[4,4,32,3072]{3,2,1,0:T(8,128)(2,1)}), bf16[4,4,32,3072]{3,2,1,0:T(8,128)(2,1)S(1)}, u32[]{:S(2)}, u32[]{:S(2)}) async-start(bf16[4,4,32,3072]{3,2,1,0:T(8,128)(2,1)} %broadcast_in_dim.2), calls=%async_computation | async-start | bytes 6291456 | tf_op jit(solution)/shard_map/all_to_all | solution.py:245
  20.2 0.0 copy-done.1
  20.2 12.2 %collective-permute-start = (bf16[64,384]{1,0:T(8,128)(2,1)S(1)}, bf16[64,384]{1,0:T(8,128)(2,1)S(1)}, u32[]{:S(2)}, u32[]{:S(2)}) collective-permute-start(bf16[64,384]{1,0:T(8,128)(2,1)S(1)} %copy-done.1), channel_id=1, source_target_pairs={{0,48},{4,52},{8,56},{12,60},{16,0},{20,4},{24,8},{28,12},{32,16},... | collective-permute-start | bytes 147464 | tf_op jit(solution)/shard_map/ppermute | solution.py:253
  32.4 4.9 %collective-permute-start.1 = (bf16[64,384]{1,0:T(8,128)(2,1)S(1)}, bf16[64,384]{1,0:T(8,128)(2,1)S(1)}, u32[]{:S(2)}, u32[]{:S(2)}) collective-permute-start(bf16[64,384]{1,0:T(8,128)(2,1)S(1)} %copy-done.1), channel_id=1, source_target_pairs={{0,32},{4,36},{8,40},{12,44},{16,48},{20,52},{24,56},{28,60},{32,0... | collective-permute-start | bytes 147464 | tf_op jit(solution)/shard_map/ppermute | solution.py:253
  37.3 7.3 %collective-permute-start.2 = (bf16[64,384]{1,0:T(8,128)(2,1)S(1)}, bf16[64,384]{1,0:T(8,128)(2,1)S(1)}, u32[]{:S(2)}, u32[]{:S(2)}) collective-permute-start(bf16[64,384]{1,0:T(8,128)(2,1)S(1)} %copy-done.1), channel_id=1, source_target_pairs={{0,16},{4,20},{8,24},{12,28},{16,32},{20,36},{24,40},{28,44},{32,4... | collective-permute-start | bytes 147464 | tf_op jit(solution)/shard_map/ppermute | solution.py:253
  44.6 0.0 collective-permute-done
  44.6 1.7 %collective-permute-done.1 = bf16[64,384]{1,0:T(8,128)(2,1)S(1)} collective-permute-done((bf16[64,384]{1,0:T(8,128)(2,1)S(1)}, bf16[64,384]{1,0:T(8,128)(2,1)S(1)}, u32[]{:S(2)}, u32[]{:S(2)}) %collective-permute-start.1) | collective-permute-done | bytes 49184 | tf_op jit(solution)/shard_map/ppermute | solution.py:253
  46.3 2.6 %collective-permute-done.2 = bf16[64,384]{1,0:T(8,128)(2,1)S(1)} collective-permute-done((bf16[64,384]{1,0:T(8,128)(2,1)S(1)}, bf16[64,384]{1,0:T(8,128)(2,1)S(1)}, u32[]{:S(2)}, u32[]{:S(2)}) %collective-permute-start.2) | collective-permute-done | bytes 49184 | tf_op jit(solution)/shard_map/ppermute | solution.py:253
  48.9 0.0 all-to-all-done
  48.9 5.8 %collective-permute-start.4 = (bf16[512,3072]{1,0:T(8,128)(2,1)S(1)}, bf16[512,3072]{1,0:T(8,128)(2,1)}, u32[]{:S(2)}, u32[]{:S(2)}) collective-permute-start(bf16[512,3072]{1,0:T(8,128)(2,1)S(1)} %bitcast.8), channel_id=1, source_target_pairs={{0,1},{1,0},{2,3},{3,2},{4,5},{5,4},{6,7},{7,6},{8,9},{9,8},{10,11... | collective-permute-start | bytes 9437192 | tf_op jit(solution)/shard_map/ppermute | solution.py:257
  54.8 3.6 %collective-permute-start.3 = (bf16[4,64,384]{2,1,0:T(8,128)(2,1)S(1)}, bf16[4,64,384]{2,1,0:T(8,128)(2,1)S(1)}, u32[]{:S(2)}, u32[]{:S(2)}) collective-permute-start(bf16[4,64,384]{2,1,0:T(8,128)(2,1)S(1)} %pad_maximum_fusion.n0_ref), channel_id=1, source_target_pairs={{0,4},{1,5},{4,8},{5,9},{8,12},{9,13},{12,16},{13,17},{16,20},{17,... | collective-permute-start | bytes 589832 | tf_op jit(solution)/shard_map/ppermute | solution.py:259
  58.4 0.1 pad_add_fusion.info_ref
  58.4 0.0 copy-start
  58.4 1.7 %copy-done = bf16[384,3072]{1,0:T(8,128)(2,1)S(1)} copy-done((bf16[384,3072]{1,0:T(8,128)(2,1)S(1)}, bf16[384,3072]{1,0:T(8,128)(2,1)}, u32[]{:S(2)}) %copy-start) | copy-done | bytes 2359320
  60.1 1.8 %own_sums.1.sums_ref = f32[512,384]{1,0:T(8,128)S(1)} custom-call(bf16[512,3072]{1,0:T(8,128)(2,1)S(1)} %bitcast.9, bf16[384,3072]{1,0:T(8,128)(2,1)S(1)} %copy-done), custom_call_target="tpu_custom_call" | custom-call | flops 1207959552 | bytes 6291456 | tf_op jit(solution)/shard_map/own_sums/pallas_call | solution.py:51
  61.9 2.5 %collective-permute-done.3.n1_ref = bf16[4,64,384]{2,1,0:T(8,128)(2,1)S(1)} collective-permute-done((bf16[4,64,384]{2,1,0:T(8,128)(2,1)S(1)}, bf16[4,64,384]{2,1,0:T(8,128)(2,1)S(1)}, u32[]{:S(2)}, u32[]{:S(2)}) %collective-permute-start.3) | collective-permute-done | bytes 196640 | tf_op jit(solution)/shard_map/ppermute | solution.py:259
  64.4 0.0 collective-permute-done.4.lines_ref.sib_ref
  64.4 3.8 %sib_sums.1 = (f32[4,64,384]{2,1,0:T(8,128)S(1)}, bf16[4,64,384]{2,1,0:T(8,128)(2,1)S(1)}, bf16[4,64,384]{2,1,0:T(8,128)(2,1)S(1)}, bf16[4,64,384]{2,1,0:T(8,128)(2,1)S(1)}) custom-call(s32[2]{0:T(128)S(1)} %pad_add_fusion.info_ref, f32[512,384]{1,0:T(8,128)S(1)} %own_sums.1.sums_ref, bf16[512,3072]{1,0:T(8,128)(2,1)} %collective-permute-done.4.lines_ref.sib_ref, ...), custom_call_target="tpu_custom_call" | custom-call | flops 1207959552 | bytes 8388608 | tf_op jit(solution)/shard_map/sib_sums/pallas_call | solution.py:92
  68.2 2.4 %collective-permute-start.5 = (bf16[4,64,384]{2,1,0:T(8,128)(2,1)S(1)}, bf16[4,64,384]{2,1,0:T(8,128)(2,1)S(1)}, u32[]{:S(2)}, u32[]{:S(2)}) collective-permute-start(bf16[4,64,384]{2,1,0:T(8,128)(2,1)S(1)} %get-tuple-element.35), channel_id=1, source_target_pairs={{0,4},{1,5},{4,8},{5,9},{8,12},{9,13},{12,16},{13,17},{16,20},{17,... | collective-permute-start | bytes 589832 | tf_op jit(solution)/shard_map/ppermute | solution.py:267
  70.6 3.9 %collective-permute-start.6 = (bf16[4,64,384]{2,1,0:T(8,128)(2,1)S(1)}, bf16[4,64,384]{2,1,0:T(8,128)(2,1)S(1)}, u32[]{:S(2)}, u32[]{:S(2)}) collective-permute-start(bf16[4,64,384]{2,1,0:T(8,128)(2,1)S(1)} %get-tuple-element.36), channel_id=1, source_target_pairs={{0,8},{1,57},{4,12},{5,61},{8,16},{9,1},{12,20},{13,5},{16,24},{17... | collective-permute-start | bytes 589832 | tf_op jit(solution)/shard_map/ppermute | solution.py:267
  74.5 3.2 %collective-permute-start.7 = (bf16[4,64,384]{2,1,0:T(8,128)(2,1)S(1)}, bf16[4,64,384]{2,1,0:T(8,128)(2,1)S(1)}, u32[]{:S(2)}, u32[]{:S(2)}) collective-permute-start(bf16[4,64,384]{2,1,0:T(8,128)(2,1)S(1)} %get-tuple-element.37), channel_id=1, source_target_pairs={{0,60},{1,61},{4,0},{5,1},{8,4},{9,5},{12,8},{13,9},{16,12},{17,13... | collective-permute-start | bytes 589832 | tf_op jit(solution)/shard_map/ppermute | solution.py:267
  77.8 5.0 %collective-permute-start.8 = (bf16[4,64,384]{2,1,0:T(8,128)(2,1)S(1)}, bf16[4,64,384]{2,1,0:T(8,128)(2,1)S(1)}, u32[]{:S(2)}, u32[]{:S(2)}) collective-permute-start(bf16[4,64,384]{2,1,0:T(8,128)(2,1)S(1)} %pad_maximum_fusion.n0_ref), channel_id=1, source_target_pairs={{0,8},{1,57},{4,12},{5,61},{8,16},{9,1},{12,20},{13,5},{16,24},{17... | collective-permute-start | bytes 589832 | tf_op jit(solution)/shard_map/ppermute | solution.py:265
  82.8 2.0 %collective-permute-start.9 = (bf16[4,64,384]{2,1,0:T(8,128)(2,1)S(1)}, bf16[4,64,384]{2,1,0:T(8,128)(2,1)S(1)}, u32[]{:S(2)}, u32[]{:S(2)}) collective-permute-start(bf16[4,64,384]{2,1,0:T(8,128)(2,1)S(1)} %pad_maximum_fusion.n0_ref), channel_id=1, source_target_pairs={{0,60},{1,61},{4,0},{5,1},{8,4},{9,5},{12,8},{13,9},{16,12},{17,13... | collective-permute-start | bytes 589832 | tf_op jit(solution)/shard_map/ppermute | solution.py:265
  84.8 0.0 collective-permute-done.5.r1_ref
  84.8 0.0 collective-permute-done.6.r2_ref
  84.8 0.0 collective-permute-done.7.r3_ref
  84.8 0.6 stage_sums.1
  85.5 7.0 %collective-permute-start.10 = (bf16[64,384]{1,0:T(8,128)(2,1)S(1)}, bf16[64,384]{1,0:T(8,128)(2,1)S(1)}, u32[]{:S(2)}, u32[]{:S(2)}) collective-permute-start(bf16[64,384]{1,0:T(8,128)(2,1)S(1)} %get-tuple-element.41), channel_id=1, source_target_pairs={{0,16},{4,20},{8,24},{12,28},{16,32},{20,36},{24,40},{28,44},{32,4... | collective-permute-start | bytes 147464 | tf_op jit(solution)/shard_map/ppermute | solution.py:270
  92.5 5.8 %collective-permute-start.11 = (bf16[64,384]{1,0:T(8,128)(2,1)S(1)}, bf16[64,384]{1,0:T(8,128)(2,1)S(1)}, u32[]{:S(2)}, u32[]{:S(2)}) collective-permute-start(bf16[64,384]{1,0:T(8,128)(2,1)S(1)} %get-tuple-element.42), channel_id=1, source_target_pairs={{0,32},{4,36},{8,40},{12,44},{16,48},{20,52},{24,56},{28,60},{32,0... | collective-permute-start | bytes 147464 | tf_op jit(solution)/shard_map/ppermute | solution.py:270
  98.3 5.7 %collective-permute-start.12 = (bf16[64,384]{1,0:T(8,128)(2,1)S(1)}, bf16[64,384]{1,0:T(8,128)(2,1)S(1)}, u32[]{:S(2)}, u32[]{:S(2)}) collective-permute-start(bf16[64,384]{1,0:T(8,128)(2,1)S(1)} %get-tuple-element.43), channel_id=1, source_target_pairs={{0,48},{4,52},{8,56},{12,60},{16,0},{20,4},{24,8},{28,12},{32,16},... | collective-permute-start | bytes 147464 | tf_op jit(solution)/shard_map/ppermute | solution.py:270
  104.0 0.0 collective-permute-done.8.n2_ref
  104.0 0.0 collective-permute-done.9.n3_ref
  104.0 7.6 %weight_sums.1 = bf16[384,3072]{1,0:T(8,128)(2,1)} custom-call(s32[2]{0:T(128)S(1)} %pad_add_fusion.info_ref, bf16[4,64,384]{2,1,0:T(8,128)(2,1)S(1)} %pad_maximum_fusion.n0_ref, bf16[4,64,384]{2,1,0:T(8,128)(2,1)S(1)} %collective-permute-done.3.n1_ref, bf16[4,64,384]{2,1,0:T(8,128)(2,1)S(1)} %collective-permute-done.8.n2_ref, ...), custom_call_target="tpu_custom_call" | custom-call | flops 2415919104 | bytes 10485760 | tf_op jit(solution)/shard_map/weight_sums/pallas_call | solution.py:176
  111.7 0.0 collective-permute-done.10.r1_ref
  111.7 0.0 collective-permute-done.11.r2_ref
  111.7 0.9 collective-permute-done.12.r3_ref
  112.6 0.6 final_sums.1
  (1 shorter events, 0.0 us)
Async XLA Ops:
  16.3 3.8 %copy-start.1 = (bf16[64,384]{1,0:T(8,128)(2,1)S(1)}, bf16[64,384]{1,0:T(8,128)(2,1)}, u32[]{:S(2)}) copy-start(bf16[64,384]{1,0:T(8,128)(2,1)} %param.4) | copy-start | bytes 147460
  16.3 32.6 %all-to-all-start = ((bf16[4,4,32,3072]{3,2,1,0:T(8,128)(2,1)}), bf16[4,4,32,3072]{3,2,1,0:T(8,128)(2,1)S(1)}, u32[]{:S(2)}, u32[]{:S(2)}) async-start(bf16[4,4,32,3072]{3,2,1,0:T(8,128)(2,1)} %broadcast_in_dim.2), calls=%async_computation | async-start | bytes 6291456 | tf_op jit(solution)/shard_map/all_to_all | solution.py:245
  20.2 24.4 %collective-permute-start = (bf16[64,384]{1,0:T(8,128)(2,1)S(1)}, bf16[64,384]{1,0:T(8,128)(2,1)S(1)}, u32[]{:S(2)}, u32[]{:S(2)}) collective-permute-start(bf16[64,384]{1,0:T(8,128)(2,1)S(1)} %copy-done.1), channel_id=1, source_target_pairs={{0,48},{4,52},{8,56},{12,60},{16,0},{20,4},{24,8},{28,12},{32,16},... | collective-permute-start | bytes 147464 | tf_op jit(solution)/shard_map/ppermute | solution.py:253
  32.4 13.9 %collective-permute-start.1 = (bf16[64,384]{1,0:T(8,128)(2,1)S(1)}, bf16[64,384]{1,0:T(8,128)(2,1)S(1)}, u32[]{:S(2)}, u32[]{:S(2)}) collective-permute-start(bf16[64,384]{1,0:T(8,128)(2,1)S(1)} %copy-done.1), channel_id=1, source_target_pairs={{0,32},{4,36},{8,40},{12,44},{16,48},{20,52},{24,56},{28,60},{32,0... | collective-permute-start | bytes 147464 | tf_op jit(solution)/shard_map/ppermute | solution.py:253
  37.3 11.6 %collective-permute-start.2 = (bf16[64,384]{1,0:T(8,128)(2,1)S(1)}, bf16[64,384]{1,0:T(8,128)(2,1)S(1)}, u32[]{:S(2)}, u32[]{:S(2)}) collective-permute-start(bf16[64,384]{1,0:T(8,128)(2,1)S(1)} %copy-done.1), channel_id=1, source_target_pairs={{0,16},{4,20},{8,24},{12,28},{16,32},{20,36},{24,40},{28,44},{32,4... | collective-permute-start | bytes 147464 | tf_op jit(solution)/shard_map/ppermute | solution.py:253
  48.9 15.5 %collective-permute-start.4 = (bf16[512,3072]{1,0:T(8,128)(2,1)S(1)}, bf16[512,3072]{1,0:T(8,128)(2,1)}, u32[]{:S(2)}, u32[]{:S(2)}) collective-permute-start(bf16[512,3072]{1,0:T(8,128)(2,1)S(1)} %bitcast.8), channel_id=1, source_target_pairs={{0,1},{1,0},{2,3},{3,2},{4,5},{5,4},{6,7},{7,6},{8,9},{9,8},{10,11... | collective-permute-start | bytes 9437192 | tf_op jit(solution)/shard_map/ppermute | solution.py:257
  54.8 9.6 %collective-permute-start.3 = (bf16[4,64,384]{2,1,0:T(8,128)(2,1)S(1)}, bf16[4,64,384]{2,1,0:T(8,128)(2,1)S(1)}, u32[]{:S(2)}, u32[]{:S(2)}) collective-permute-start(bf16[4,64,384]{2,1,0:T(8,128)(2,1)S(1)} %pad_maximum_fusion.n0_ref), channel_id=1, source_target_pairs={{0,4},{1,5},{4,8},{5,9},{8,12},{9,13},{12,16},{13,17},{16,20},{17,... | collective-permute-start | bytes 589832 | tf_op jit(solution)/shard_map/ppermute | solution.py:259
  58.4 1.7 %copy-start = (bf16[384,3072]{1,0:T(8,128)(2,1)S(1)}, bf16[384,3072]{1,0:T(8,128)(2,1)}, u32[]{:S(2)}) copy-start(bf16[384,3072]{1,0:T(8,128)(2,1)} %w_ref.3) | copy-start | bytes 7077892
  68.2 16.6 %collective-permute-start.5 = (bf16[4,64,384]{2,1,0:T(8,128)(2,1)S(1)}, bf16[4,64,384]{2,1,0:T(8,128)(2,1)S(1)}, u32[]{:S(2)}, u32[]{:S(2)}) collective-permute-start(bf16[4,64,384]{2,1,0:T(8,128)(2,1)S(1)} %get-tuple-element.35), channel_id=1, source_target_pairs={{0,4},{1,5},{4,8},{5,9},{8,12},{9,13},{12,16},{13,17},{16,20},{17,... | collective-permute-start | bytes 589832 | tf_op jit(solution)/shard_map/ppermute | solution.py:267
  70.6 14.2 %collective-permute-start.6 = (bf16[4,64,384]{2,1,0:T(8,128)(2,1)S(1)}, bf16[4,64,384]{2,1,0:T(8,128)(2,1)S(1)}, u32[]{:S(2)}, u32[]{:S(2)}) collective-permute-start(bf16[4,64,384]{2,1,0:T(8,128)(2,1)S(1)} %get-tuple-element.36), channel_id=1, source_target_pairs={{0,8},{1,57},{4,12},{5,61},{8,16},{9,1},{12,20},{13,5},{16,24},{17... | collective-permute-start | bytes 589832 | tf_op jit(solution)/shard_map/ppermute | solution.py:267
  74.5 10.3 %collective-permute-start.7 = (bf16[4,64,384]{2,1,0:T(8,128)(2,1)S(1)}, bf16[4,64,384]{2,1,0:T(8,128)(2,1)S(1)}, u32[]{:S(2)}, u32[]{:S(2)}) collective-permute-start(bf16[4,64,384]{2,1,0:T(8,128)(2,1)S(1)} %get-tuple-element.37), channel_id=1, source_target_pairs={{0,60},{1,61},{4,0},{5,1},{8,4},{9,5},{12,8},{13,9},{16,12},{17,13... | collective-permute-start | bytes 589832 | tf_op jit(solution)/shard_map/ppermute | solution.py:267
  77.8 26.2 %collective-permute-start.8 = (bf16[4,64,384]{2,1,0:T(8,128)(2,1)S(1)}, bf16[4,64,384]{2,1,0:T(8,128)(2,1)S(1)}, u32[]{:S(2)}, u32[]{:S(2)}) collective-permute-start(bf16[4,64,384]{2,1,0:T(8,128)(2,1)S(1)} %pad_maximum_fusion.n0_ref), channel_id=1, source_target_pairs={{0,8},{1,57},{4,12},{5,61},{8,16},{9,1},{12,20},{13,5},{16,24},{17... | collective-permute-start | bytes 589832 | tf_op jit(solution)/shard_map/ppermute | solution.py:265
  82.8 21.2 %collective-permute-start.9 = (bf16[4,64,384]{2,1,0:T(8,128)(2,1)S(1)}, bf16[4,64,384]{2,1,0:T(8,128)(2,1)S(1)}, u32[]{:S(2)}, u32[]{:S(2)}) collective-permute-start(bf16[4,64,384]{2,1,0:T(8,128)(2,1)S(1)} %pad_maximum_fusion.n0_ref), channel_id=1, source_target_pairs={{0,60},{1,61},{4,0},{5,1},{8,4},{9,5},{12,8},{13,9},{16,12},{17,13... | collective-permute-start | bytes 589832 | tf_op jit(solution)/shard_map/ppermute | solution.py:265
  85.5 26.2 %collective-permute-start.10 = (bf16[64,384]{1,0:T(8,128)(2,1)S(1)}, bf16[64,384]{1,0:T(8,128)(2,1)S(1)}, u32[]{:S(2)}, u32[]{:S(2)}) collective-permute-start(bf16[64,384]{1,0:T(8,128)(2,1)S(1)} %get-tuple-element.41), channel_id=1, source_target_pairs={{0,16},{4,20},{8,24},{12,28},{16,32},{20,36},{24,40},{28,44},{32,4... | collective-permute-start | bytes 147464 | tf_op jit(solution)/shard_map/ppermute | solution.py:270
  92.5 19.2 %collective-permute-start.11 = (bf16[64,384]{1,0:T(8,128)(2,1)S(1)}, bf16[64,384]{1,0:T(8,128)(2,1)S(1)}, u32[]{:S(2)}, u32[]{:S(2)}) collective-permute-start(bf16[64,384]{1,0:T(8,128)(2,1)S(1)} %get-tuple-element.42), channel_id=1, source_target_pairs={{0,32},{4,36},{8,40},{12,44},{16,48},{20,52},{24,56},{28,60},{32,0... | collective-permute-start | bytes 147464 | tf_op jit(solution)/shard_map/ppermute | solution.py:270
  98.3 14.3 %collective-permute-start.12 = (bf16[64,384]{1,0:T(8,128)(2,1)S(1)}, bf16[64,384]{1,0:T(8,128)(2,1)S(1)}, u32[]{:S(2)}, u32[]{:S(2)}) collective-permute-start(bf16[64,384]{1,0:T(8,128)(2,1)S(1)} %get-tuple-element.43), channel_id=1, source_target_pairs={{0,48},{4,52},{8,56},{12,60},{16,0},{20,4},{24,8},{28,12},{32,16},... | collective-permute-start | bytes 147464 | tf_op jit(solution)/shard_map/ppermute | solution.py:270

commit v10 on v8

--- a/solution.py
+++ b/solution.py
@@ -222,9 +222,14 @@
 
     slope = gelu_slope(preactivation.astype(jnp.float32))
     local = (upstream.astype(jnp.float32) * slope).astype(jnp.bfloat16)
-    line = lax.all_gather(
-        local, PLANE, axis=0, tiled=True, axis_index_groups=first_axis_groups()
-    ).reshape(4, 32, 3072)
+    line = lax.all_to_all(
+        jnp.broadcast_to(local[None], (4, 32, 3072)),
+        PLANE,
+        split_axis=0,
+        concat_axis=0,
+        tiled=True,
+        axis_index_groups=first_axis_groups(),
+    )
     inputs, line = lax.optimization_barrier((inputs, line))
     lines = lax.all_to_all(
         jnp.broadcast_to(line[None], (4, 4, 32, 3072)),

time: 111 us -> 112 us (level)
  starting transfers between devices: 71.3 us -> 69.1 us
  waiting for transfers between devices: 6.17 us -> 7.93 us
    all_to_all x0 -> x1, blocking collectives: none -> 13.2 us  [per_device(): lax.all_to_all(jnp.broadcast_to(local[None], (4, 32, 3072)), PLANE, split...]
    all_gather x1 -> x0, blocking collectives: 12.4 us -> none  [per_device(): lax.all_gather(local, PLANE, axis=0, tiled=True, axis_index_groups=first_...]
    ppermute x1, starting transfers between devices: 5.8 us -> 3.38 us  [per_device(): hg_sib = lax.ppermute(hg_own, 'core', swap)]
    ppermute x3, waiting for transfers between devices: 0.01 us -> 1.25 us  [per_device(): far = [lax.ppermute(s, Z, far_shift(d + 1)) for d, s in enumerate(sends)]]
  transfers between devices with their start and end apart: 14 -> 14, of which waited for: 3 -> 4; matrix products, arithmetic and copies ran while one was open for 0% -> 0% of each run, Pallas kernels for 9% -> 9%
where the time goes in v10:
time: 112 us; the launch traced here: 111 us
  starting transfers between devices  69.1 us (62%)
  Pallas kernels  14.5 us (13%)
  blocking collectives  13.2 us (12%)
  waiting for transfers between devices  7.93 us (7%)
  local copies, waits for them, and re-layouts  3.79 us (3%)
  other arithmetic  1.41 us (1%)
    ppermute x3, starting transfers between devices, per_device(): lax.ppermute(inputs, Z, far_shift(-d))  24.6 us
    ppermute x3, starting transfers between devices, per_device(): far = [lax.ppermute(s, Z, far_shift(d + 1)) for d, s in enumerate(sends)]  16.5 us
    all_to_all x1, blocking collectives, per_device(): lax.all_to_all(jnp.broadcast_to(local[None], (4, 32, 3072)), PLANE, split...  13.2 us
    ppermute x3, starting transfers between devices, per_device(): lax.ppermute(s, Z + ('core',), column_shift(by))  11.3 us
    ppermute x3, starting transfers between devices, per_device(): lax.ppermute(near, Z + ('core',), column_shift(by))  9.22 us
    pallas_call x1, Pallas kernels, weight_sums(): pl.pallas_call(weight_kernel, out_shape=jax.ShapeDtypeStruct((384, 3072),...  7.64 us
    ppermute x3, waiting for transfers between devices, per_device(): lax.ppermute(inputs, Z, far_shift(-d))  4.83 us
    all_to_all x1, starting transfers between devices, per_device(): lax.all_to_all(jnp.broadcast_to(line[None], (4, 4, 32, 3072)), PLANE, spl...  4.14 us
  transfers between devices with their start and end apart: 14, of which 4 were waited for; matrix products, arithmetic and copies ran while one was open for 0% of the time, Pallas kernels for 9%

profile of v10, /device:TPU:1, one launch (start us, length us, event | category | flops | bytes accessed | tf_op | source)
XLA Modules:
  0.0 110.8 jit_solution(12024946406688091680)
XLA Ops:
  0.6 1.3 %fusion.7 = bf16[32,3072]{1,0:T(8,128)(2,1)S(1)} fusion(bf16[32,3072]{1,0:T(8,128)(2,1)} %param.7, bf16[32,3072]{1,0:T(8,128)(2,1)} %param.6), kind=kLoop, calls=%fused_computation.14 | loop fusion | flops 2064384 | bytes 589824 | tf_op jit(solution)/shard_map/convert_element_type | solution.py:224
  1.9 0.1 broadcast_in_dim.4
  2.0 13.2 %all_to_all.10 = bf16[4,32,3072]{2,1,0:T(8,128)(2,1)S(1)} all-to-all(bf16[4,32,3072]{2,1,0:T(8,128)(2,1)S(1)} %broadcast_in_dim.4), channel_id=1, replica_groups={{0,128,256,384},{2,130,258,386},{64,192,320,448},{66,194,322,450},{1,3,..., dimensions={0} | all-to-all | bytes 1572864 | tf_op jit(solution)/shard_map/all_to_all | solution.py:225
  15.2 2.1 %broadcast_in_dim.5 = bf16[4,4,32,3072]{3,2,1,0:T(8,128)(2,1)} broadcast(bf16[4,32,3072]{2,1,0:T(8,128)(2,1)S(1)} %all_to_all.10), dimensions={1,2,3} | broadcast | bytes 3932160 | tf_op jit(solution)/shard_map/broadcast_in_dim | solution.py:235
  17.2 0.0 copy-start.1
  17.2 4.1 %all-to-all-start.1 = ((bf16[4,4,32,3072]{3,2,1,0:T(8,128)(2,1)}), bf16[4,4,32,3072]{3,2,1,0:T(8,128)(2,1)S(1)}, u32[]{:S(2)}, u32[]{:S(2)}) async-start(bf16[4,4,32,3072]{3,2,1,0:T(8,128)(2,1)} %broadcast_in_dim.5), calls=%async_computation.1 | async-start | bytes 6291456 | tf_op jit(solution)/shard_map/all_to_all | solution.py:234
  21.4 0.0 copy-done.1
  21.4 12.4 %collective-permute-start = (bf16[64,384]{1,0:T(8,128)(2,1)S(1)}, bf16[64,384]{1,0:T(8,128)(2,1)S(1)}, u32[]{:S(2)}, u32[]{:S(2)}) collective-permute-start(bf16[64,384]{1,0:T(8,128)(2,1)S(1)} %copy-done.1), channel_id=1, source_target_pairs={{0,48},{4,52},{8,56},{12,60},{16,0},{20,4},{24,8},{28,12},{32,16},... | collective-permute-start | bytes 147464 | tf_op jit(solution)/shard_map/ppermute | solution.py:242
  33.8 4.9 %collective-permute-start.1 = (bf16[64,384]{1,0:T(8,128)(2,1)S(1)}, bf16[64,384]{1,0:T(8,128)(2,1)S(1)}, u32[]{:S(2)}, u32[]{:S(2)}) collective-permute-start(bf16[64,384]{1,0:T(8,128)(2,1)S(1)} %copy-done.1), channel_id=1, source_target_pairs={{0,32},{4,36},{8,40},{12,44},{16,48},{20,52},{24,56},{28,60},{32,0... | collective-permute-start | bytes 147464 | tf_op jit(solution)/shard_map/ppermute | solution.py:242
  38.7 7.3 %collective-permute-start.2 = (bf16[64,384]{1,0:T(8,128)(2,1)S(1)}, bf16[64,384]{1,0:T(8,128)(2,1)S(1)}, u32[]{:S(2)}, u32[]{:S(2)}) collective-permute-start(bf16[64,384]{1,0:T(8,128)(2,1)S(1)} %copy-done.1), channel_id=1, source_target_pairs={{0,16},{4,20},{8,24},{12,28},{16,32},{20,36},{24,40},{28,44},{32,4... | collective-permute-start | bytes 147464 | tf_op jit(solution)/shard_map/ppermute | solution.py:242
  46.0 0.0 collective-permute-done
  46.0 1.7 %collective-permute-done.1 = bf16[64,384]{1,0:T(8,128)(2,1)S(1)} collective-permute-done((bf16[64,384]{1,0:T(8,128)(2,1)S(1)}, bf16[64,384]{1,0:T(8,128)(2,1)S(1)}, u32[]{:S(2)}, u32[]{:S(2)}) %collective-permute-start.1) | collective-permute-done | bytes 49184 | tf_op jit(solution)/shard_map/ppermute | solution.py:242
  47.7 3.2 %collective-permute-done.2 = bf16[64,384]{1,0:T(8,128)(2,1)S(1)} collective-permute-done((bf16[64,384]{1,0:T(8,128)(2,1)S(1)}, bf16[64,384]{1,0:T(8,128)(2,1)S(1)}, u32[]{:S(2)}, u32[]{:S(2)}) %collective-permute-start.2) | collective-permute-done | bytes 49184 | tf_op jit(solution)/shard_map/ppermute | solution.py:242
  50.8 0.0 all-to-all-done.1
  50.8 3.4 %collective-permute-start.3 = (bf16[512,3072]{1,0:T(8,128)(2,1)S(1)}, bf16[512,3072]{1,0:T(8,128)(2,1)}, u32[]{:S(2)}, u32[]{:S(2)}) collective-permute-start(bf16[512,3072]{1,0:T(8,128)(2,1)S(1)} %bitcast.7), channel_id=1, source_target_pairs={{0,1},{1,0},{2,3},{3,2},{4,5},{5,4},{6,7},{7,6},{8,9},{9,8},{10,11... | collective-permute-start | bytes 9437192 | tf_op jit(solution)/shard_map/ppermute | solution.py:246
  54.2 0.1 pad_add_fusion.info_ref
  54.3 0.0 copy-start
  54.3 1.7 %copy-done = bf16[384,3072]{1,0:T(8,128)(2,1)S(1)} copy-done((bf16[384,3072]{1,0:T(8,128)(2,1)S(1)}, bf16[384,3072]{1,0:T(8,128)(2,1)}, u32[]{:S(2)}) %copy-start) | copy-done | bytes 2359320
  56.0 1.8 %own_sums.1.sums_ref = f32[512,384]{1,0:T(8,128)S(1)} custom-call(bf16[512,3072]{1,0:T(8,128)(2,1)S(1)} %bitcast.8, bf16[384,3072]{1,0:T(8,128)(2,1)S(1)} %copy-done), custom_call_target="tpu_custom_call" | custom-call | flops 1207959552 | bytes 6291456 | tf_op jit(solution)/shard_map/own_sums/pallas_call | solution.py:51
  57.8 1.8 %collective-permute-done.3.lines_ref.sib_ref = bf16[512,3072]{1,0:T(8,128)(2,1)} collective-permute-done((bf16[512,3072]{1,0:T(8,128)(2,1)S(1)}, bf16[512,3072]{1,0:T(8,128)(2,1)}, u32[]{:S(2)}, u32[]{:S(2)}) %collective-permute-start.3) | collective-permute-done | bytes 3145760 | tf_op jit(solution)/shard_map/ppermute | solution.py:246
  59.6 3.8 %sib_sums.1 = (f32[4,64,384]{2,1,0:T(8,128)S(1)}, bf16[4,64,384]{2,1,0:T(8,128)(2,1)S(1)}, bf16[4,64,384]{2,1,0:T(8,128)(2,1)S(1)}, bf16[4,64,384]{2,1,0:T(8,128)(2,1)S(1)}) custom-call(s32[2]{0:T(128)S(1)} %pad_add_fusion.info_ref, f32[512,384]{1,0:T(8,128)S(1)} %own_sums.1.sums_ref, bf16[512,3072]{1,0:T(8,128)(2,1)} %collective-permute-done.3.lines_ref.sib_ref, ...), custom_call_target="tpu_custom_call" | custom-call | flops 1207959552 | bytes 8388608 | tf_op jit(solution)/shard_map/sib_sums/pallas_call | solution.py:80
  63.4 3.5 %collective-permute-start.4 = (bf16[4,64,384]{2,1,0:T(8,128)(2,1)S(1)}, bf16[4,64,384]{2,1,0:T(8,128)(2,1)S(1)}, u32[]{:S(2)}, u32[]{:S(2)}) collective-permute-start(bf16[4,64,384]{2,1,0:T(8,128)(2,1)S(1)} %get-tuple-element.35), channel_id=1, source_target_pairs={{0,4},{1,5},{4,8},{5,9},{8,12},{9,13},{12,16},{13,17},{16,20},{17,... | collective-permute-start | bytes 589832 | tf_op jit(solution)/shard_map/ppermute | solution.py:253
  66.9 4.8 %collective-permute-start.5 = (bf16[4,64,384]{2,1,0:T(8,128)(2,1)S(1)}, bf16[4,64,384]{2,1,0:T(8,128)(2,1)S(1)}, u32[]{:S(2)}, u32[]{:S(2)}) collective-permute-start(bf16[4,64,384]{2,1,0:T(8,128)(2,1)S(1)} %get-tuple-element.36), channel_id=1, source_target_pairs={{0,8},{1,57},{4,12},{5,61},{8,16},{9,1},{12,20},{13,5},{16,24},{17... | collective-permute-start | bytes 589832 | tf_op jit(solution)/shard_map/ppermute | solution.py:253
  71.8 3.0 %collective-permute-start.6 = (bf16[4,64,384]{2,1,0:T(8,128)(2,1)S(1)}, bf16[4,64,384]{2,1,0:T(8,128)(2,1)S(1)}, u32[]{:S(2)}, u32[]{:S(2)}) collective-permute-start(bf16[4,64,384]{2,1,0:T(8,128)(2,1)S(1)} %get-tuple-element.37), channel_id=1, source_target_pairs={{0,60},{1,61},{4,0},{5,1},{8,4},{9,5},{12,8},{13,9},{16,12},{17,13... | collective-permute-start | bytes 589832 | tf_op jit(solution)/shard_map/ppermute | solution.py:253
  74.8 2.3 %collective-permute-start.7 = (bf16[4,64,384]{2,1,0:T(8,128)(2,1)S(1)}, bf16[4,64,384]{2,1,0:T(8,128)(2,1)S(1)}, u32[]{:S(2)}, u32[]{:S(2)}) collective-permute-start(bf16[4,64,384]{2,1,0:T(8,128)(2,1)S(1)} %pad_maximum_fusion.n0_ref), channel_id=1, source_target_pairs={{0,4},{1,5},{4,8},{5,9},{8,12},{9,13},{12,16},{13,17},{16,20},{17,... | collective-permute-start | bytes 589832 | tf_op jit(solution)/shard_map/ppermute | solution.py:251
  77.1 3.5 %collective-permute-start.8 = (bf16[4,64,384]{2,1,0:T(8,128)(2,1)S(1)}, bf16[4,64,384]{2,1,0:T(8,128)(2,1)S(1)}, u32[]{:S(2)}, u32[]{:S(2)}) collective-permute-start(bf16[4,64,384]{2,1,0:T(8,128)(2,1)S(1)} %pad_maximum_fusion.n0_ref), channel_id=1, source_target_pairs={{0,8},{1,57},{4,12},{5,61},{8,16},{9,1},{12,20},{13,5},{16,24},{17... | collective-permute-start | bytes 589832 | tf_op jit(solution)/shard_map/ppermute | solution.py:251
  80.6 0.0 collective-permute-done.4.r1_ref
  80.6 3.4 %collective-permute-start.9 = (bf16[4,64,384]{2,1,0:T(8,128)(2,1)S(1)}, bf16[4,64,384]{2,1,0:T(8,128)(2,1)S(1)}, u32[]{:S(2)}, u32[]{:S(2)}) collective-permute-start(bf16[4,64,384]{2,1,0:T(8,128)(2,1)S(1)} %pad_maximum_fusion.n0_ref), channel_id=1, source_target_pairs={{0,60},{1,61},{4,0},{5,1},{8,4},{9,5},{12,8},{13,9},{16,12},{17,13... | collective-permute-start | bytes 589832 | tf_op jit(solution)/shard_map/ppermute | solution.py:251
  84.0 0.0 collective-permute-done.5.r2_ref
  84.0 0.0 collective-permute-done.6.r3_ref
  84.0 0.6 stage_sums.1
  84.7 3.5 %collective-permute-start.10 = (bf16[64,384]{1,0:T(8,128)(2,1)S(1)}, bf16[64,384]{1,0:T(8,128)(2,1)S(1)}, u32[]{:S(2)}, u32[]{:S(2)}) collective-permute-start(bf16[64,384]{1,0:T(8,128)(2,1)S(1)} %get-tuple-element.43), channel_id=1, source_target_pairs={{0,16},{4,20},{8,24},{12,28},{16,32},{20,36},{24,40},{28,44},{32,4... | collective-permute-start | bytes 147464 | tf_op jit(solution)/shard_map/ppermute | solution.py:256
  88.2 8.2 %collective-permute-start.11 = (bf16[64,384]{1,0:T(8,128)(2,1)S(1)}, bf16[64,384]{1,0:T(8,128)(2,1)S(1)}, u32[]{:S(2)}, u32[]{:S(2)}) collective-permute-start(bf16[64,384]{1,0:T(8,128)(2,1)S(1)} %get-tuple-element.44), channel_id=1, source_target_pairs={{0,32},{4,36},{8,40},{12,44},{16,48},{20,52},{24,56},{28,60},{32,0... | collective-permute-start | bytes 147464 | tf_op jit(solution)/shard_map/ppermute | solution.py:256
  96.5 0.0 collective-permute-done.7.n1_ref
  96.5 4.7 %collective-permute-start.12 = (bf16[64,384]{1,0:T(8,128)(2,1)S(1)}, bf16[64,384]{1,0:T(8,128)(2,1)S(1)}, u32[]{:S(2)}, u32[]{:S(2)}) collective-permute-start(bf16[64,384]{1,0:T(8,128)(2,1)S(1)} %get-tuple-element.45), channel_id=1, source_target_pairs={{0,48},{4,52},{8,56},{12,60},{16,0},{20,4},{24,8},{28,12},{32,16},... | collective-permute-start | bytes 147464 | tf_op jit(solution)/shard_map/ppermute | solution.py:256
  101.2 0.0 collective-permute-done.8.n2_ref
  101.2 0.0 collective-permute-done.9.n3_ref
  101.2 7.6 %weight_sums.1 = bf16[384,3072]{1,0:T(8,128)(2,1)} custom-call(s32[2]{0:T(128)S(1)} %pad_add_fusion.info_ref, bf16[4,64,384]{2,1,0:T(8,128)(2,1)S(1)} %pad_maximum_fusion.n0_ref, bf16[4,64,384]{2,1,0:T(8,128)(2,1)S(1)} %collective-permute-done.7.n1_ref, bf16[4,64,384]{2,1,0:T(8,128)(2,1)S(1)} %collective-permute-done.8.n2_ref, ...), custom_call_target="tpu_custom_call" | custom-call | flops 2415919104 | bytes 10485760 | tf_op jit(solution)/shard_map/weight_sums/pallas_call | solution.py:160
  108.9 0.0 collective-permute-done.10.r1_ref
  108.9 0.0 collective-permute-done.11.r2_ref
  108.9 1.2 %collective-permute-done.12.r3_ref = bf16[64,384]{1,0:T(8,128)(2,1)S(1)} collective-permute-done((bf16[64,384]{1,0:T(8,128)(2,1)S(1)}, bf16[64,384]{1,0:T(8,128)(2,1)S(1)}, u32[]{:S(2)}, u32[]{:S(2)}) %collective-permute-start.12) | collective-permute-done | bytes 49184 | tf_op jit(solution)/shard_map/ppermute | solution.py:256
  110.1 0.6 final_sums.1
  (1 shorter events, 0.0 us)
Async XLA Ops:
  17.2 4.1 %copy-start.1 = (bf16[64,384]{1,0:T(8,128)(2,1)S(1)}, bf16[64,384]{1,0:T(8,128)(2,1)}, u32[]{:S(2)}) copy-start(bf16[64,384]{1,0:T(8,128)(2,1)} %param.4) | copy-start | bytes 147460
  17.2 33.6 %all-to-all-start.1 = ((bf16[4,4,32,3072]{3,2,1,0:T(8,128)(2,1)}), bf16[4,4,32,3072]{3,2,1,0:T(8,128)(2,1)S(1)}, u32[]{:S(2)}, u32[]{:S(2)}) async-start(bf16[4,4,32,3072]{3,2,1,0:T(8,128)(2,1)} %broadcast_in_dim.5), calls=%async_computation.1 | async-start | bytes 6291456 | tf_op jit(solution)/shard_map/all_to_all | solution.py:234
  21.4 24.6 %collective-permute-start = (bf16[64,384]{1,0:T(8,128)(2,1)S(1)}, bf16[64,384]{1,0:T(8,128)(2,1)S(1)}, u32[]{:S(2)}, u32[]{:S(2)}) collective-permute-start(bf16[64,384]{1,0:T(8,128)(2,1)S(1)} %copy-done.1), channel_id=1, source_target_pairs={{0,48},{4,52},{8,56},{12,60},{16,0},{20,4},{24,8},{28,12},{32,16},... | collective-permute-start | bytes 147464 | tf_op jit(solution)/shard_map/ppermute | solution.py:242
  33.8 13.9 %collective-permute-start.1 = (bf16[64,384]{1,0:T(8,128)(2,1)S(1)}, bf16[64,384]{1,0:T(8,128)(2,1)S(1)}, u32[]{:S(2)}, u32[]{:S(2)}) collective-permute-start(bf16[64,384]{1,0:T(8,128)(2,1)S(1)} %copy-done.1), channel_id=1, source_target_pairs={{0,32},{4,36},{8,40},{12,44},{16,48},{20,52},{24,56},{28,60},{32,0... | collective-permute-start | bytes 147464 | tf_op jit(solution)/shard_map/ppermute | solution.py:242
  38.7 12.1 %collective-permute-start.2 = (bf16[64,384]{1,0:T(8,128)(2,1)S(1)}, bf16[64,384]{1,0:T(8,128)(2,1)S(1)}, u32[]{:S(2)}, u32[]{:S(2)}) collective-permute-start(bf16[64,384]{1,0:T(8,128)(2,1)S(1)} %copy-done.1), channel_id=1, source_target_pairs={{0,16},{4,20},{8,24},{12,28},{16,32},{20,36},{24,40},{28,44},{32,4... | collective-permute-start | bytes 147464 | tf_op jit(solution)/shard_map/ppermute | solution.py:242
  50.8 8.8 %collective-permute-start.3 = (bf16[512,3072]{1,0:T(8,128)(2,1)S(1)}, bf16[512,3072]{1,0:T(8,128)(2,1)}, u32[]{:S(2)}, u32[]{:S(2)}) collective-permute-start(bf16[512,3072]{1,0:T(8,128)(2,1)S(1)} %bitcast.7), channel_id=1, source_target_pairs={{0,1},{1,0},{2,3},{3,2},{4,5},{5,4},{6,7},{7,6},{8,9},{9,8},{10,11... | collective-permute-start | bytes 9437192 | tf_op jit(solution)/shard_map/ppermute | solution.py:246
  54.3 1.7 %copy-start = (bf16[384,3072]{1,0:T(8,128)(2,1)S(1)}, bf16[384,3072]{1,0:T(8,128)(2,1)}, u32[]{:S(2)}) copy-start(bf16[384,3072]{1,0:T(8,128)(2,1)} %w_ref.3) | copy-start | bytes 7077892
  63.4 17.2 %collective-permute-start.4 = (bf16[4,64,384]{2,1,0:T(8,128)(2,1)S(1)}, bf16[4,64,384]{2,1,0:T(8,128)(2,1)S(1)}, u32[]{:S(2)}, u32[]{:S(2)}) collective-permute-start(bf16[4,64,384]{2,1,0:T(8,128)(2,1)S(1)} %get-tuple-element.35), channel_id=1, source_target_pairs={{0,4},{1,5},{4,8},{5,9},{8,12},{9,13},{12,16},{13,17},{16,20},{17,... | collective-permute-start | bytes 589832 | tf_op jit(solution)/shard_map/ppermute | solution.py:253
  66.9 17.1 %collective-permute-start.5 = (bf16[4,64,384]{2,1,0:T(8,128)(2,1)S(1)}, bf16[4,64,384]{2,1,0:T(8,128)(2,1)S(1)}, u32[]{:S(2)}, u32[]{:S(2)}) collective-permute-start(bf16[4,64,384]{2,1,0:T(8,128)(2,1)S(1)} %get-tuple-element.36), channel_id=1, source_target_pairs={{0,8},{1,57},{4,12},{5,61},{8,16},{9,1},{12,20},{13,5},{16,24},{17... | collective-permute-start | bytes 589832 | tf_op jit(solution)/shard_map/ppermute | solution.py:253
  71.8 12.3 %collective-permute-start.6 = (bf16[4,64,384]{2,1,0:T(8,128)(2,1)S(1)}, bf16[4,64,384]{2,1,0:T(8,128)(2,1)S(1)}, u32[]{:S(2)}, u32[]{:S(2)}) collective-permute-start(bf16[4,64,384]{2,1,0:T(8,128)(2,1)S(1)} %get-tuple-element.37), channel_id=1, source_target_pairs={{0,60},{1,61},{4,0},{5,1},{8,4},{9,5},{12,8},{13,9},{16,12},{17,13... | collective-permute-start | bytes 589832 | tf_op jit(solution)/shard_map/ppermute | solution.py:253
  74.8 21.7 %collective-permute-start.7 = (bf16[4,64,384]{2,1,0:T(8,128)(2,1)S(1)}, bf16[4,64,384]{2,1,0:T(8,128)(2,1)S(1)}, u32[]{:S(2)}, u32[]{:S(2)}) collective-permute-start(bf16[4,64,384]{2,1,0:T(8,128)(2,1)S(1)} %pad_maximum_fusion.n0_ref), channel_id=1, source_target_pairs={{0,4},{1,5},{4,8},{5,9},{8,12},{9,13},{12,16},{13,17},{16,20},{17,... | collective-permute-start | bytes 589832 | tf_op jit(solution)/shard_map/ppermute | solution.py:251
  77.1 24.1 %collective-permute-start.8 = (bf16[4,64,384]{2,1,0:T(8,128)(2,1)S(1)}, bf16[4,64,384]{2,1,0:T(8,128)(2,1)S(1)}, u32[]{:S(2)}, u32[]{:S(2)}) collective-permute-start(bf16[4,64,384]{2,1,0:T(8,128)(2,1)S(1)} %pad_maximum_fusion.n0_ref), channel_id=1, source_target_pairs={{0,8},{1,57},{4,12},{5,61},{8,16},{9,1},{12,20},{13,5},{16,24},{17... | collective-permute-start | bytes 589832 | tf_op jit(solution)/shard_map/ppermute | solution.py:251
  80.6 20.6 %collective-permute-start.9 = (bf16[4,64,384]{2,1,0:T(8,128)(2,1)S(1)}, bf16[4,64,384]{2,1,0:T(8,128)(2,1)S(1)}, u32[]{:S(2)}, u32[]{:S(2)}) collective-permute-start(bf16[4,64,384]{2,1,0:T(8,128)(2,1)S(1)} %pad_maximum_fusion.n0_ref), channel_id=1, source_target_pairs={{0,60},{1,61},{4,0},{5,1},{8,4},{9,5},{12,8},{13,9},{16,12},{17,13... | collective-permute-start | bytes 589832 | tf_op jit(solution)/shard_map/ppermute | solution.py:251
  84.7 24.2 %collective-permute-start.10 = (bf16[64,384]{1,0:T(8,128)(2,1)S(1)}, bf16[64,384]{1,0:T(8,128)(2,1)S(1)}, u32[]{:S(2)}, u32[]{:S(2)}) collective-permute-start(bf16[64,384]{1,0:T(8,128)(2,1)S(1)} %get-tuple-element.43), channel_id=1, source_target_pairs={{0,16},{4,20},{8,24},{12,28},{16,32},{20,36},{24,40},{28,44},{32,4... | collective-permute-start | bytes 147464 | tf_op jit(solution)/shard_map/ppermute | solution.py:256
  88.2 20.7 %collective-permute-start.11 = (bf16[64,384]{1,0:T(8,128)(2,1)S(1)}, bf16[64,384]{1,0:T(8,128)(2,1)S(1)}, u32[]{:S(2)}, u32[]{:S(2)}) collective-permute-start(bf16[64,384]{1,0:T(8,128)(2,1)S(1)} %get-tuple-element.44), channel_id=1, source_target_pairs={{0,32},{4,36},{8,40},{12,44},{16,48},{20,52},{24,56},{28,60},{32,0... | collective-permute-start | bytes 147464 | tf_op jit(solution)/shard_map/ppermute | solution.py:256
  96.5 13.7 %collective-permute-start.12 = (bf16[64,384]{1,0:T(8,128)(2,1)S(1)}, bf16[64,384]{1,0:T(8,128)(2,1)S(1)}, u32[]{:S(2)}, u32[]{:S(2)}) collective-permute-start(bf16[64,384]{1,0:T(8,128)(2,1)S(1)} %get-tuple-element.45), channel_id=1, source_target_pairs={{0,48},{4,52},{8,56},{12,60},{16,0},{20,4},{24,8},{28,12},{32,16},... | collective-permute-start | bytes 147464 | tf_op jit(solution)/shard_map/ppermute | solution.py:256

commit v11 on v8

--- a/solution.py
+++ b/solution.py
@@ -156,7 +156,7 @@
 
 
 def weight_sums(info, near, hg_own, hg_sib):
-    tile = 512
+    tile = 1024
     return pl.pallas_call(
         weight_kernel,
         out_shape=jax.ShapeDtypeStruct((384, 3072), jnp.bfloat16),

time: 111 us -> 111 us (level)
  transfers between devices with their start and end apart: 14 -> 14, of which waited for: 3 -> 4; matrix products, arithmetic and copies ran while one was open for 0% -> 0% of each run, Pallas kernels for 9% -> 8%
where the time goes in v11:
time: 111 us; the launch traced here: 110 us
  starting transfers between devices  71.3 us (64%)
  Pallas kernels  13.5 us (12%)
  blocking collectives  12.4 us (11%)
  waiting for transfers between devices  7.16 us (6%)
  local copies, waits for them, and re-layouts  3.72 us (3%)
  other arithmetic  1.41 us (1%)
    ppermute x3, starting transfers between devices, per_device(): lax.ppermute(inputs, Z, far_shift(-d))  24.4 us
    ppermute x3, starting transfers between devices, per_device(): far = [lax.ppermute(s, Z, far_shift(d + 1)) for d, s in enumerate(sends)]  17.4 us
    all_gather x1, blocking collectives, per_device(): lax.all_gather(local, PLANE, axis=0, tiled=True, axis_index_groups=first_...  12.4 us
    ppermute x3, starting transfers between devices, per_device(): lax.ppermute(s, Z + ('core',), column_shift(by))  10.7 us
    ppermute x3, starting transfers between devices, per_device(): lax.ppermute(near, Z + ('core',), column_shift(by))  9.09 us
    pallas_call x1, Pallas kernels, weight_sums(): pl.pallas_call(weight_kernel, out_shape=jax.ShapeDtypeStruct((384, 3072),...  6.65 us
    ppermute x1, starting transfers between devices, per_device(): hg_sib = lax.ppermute(hg_own, 'core', swap)  5.8 us
    ppermute x3, waiting for transfers between devices, per_device(): lax.ppermute(inputs, Z, far_shift(-d))  4.3 us
  transfers between devices with their start and end apart: 14, of which 4 were waited for; matrix products, arithmetic and copies ran while one was open for 0% of the time, Pallas kernels for 8%

profile of v11, /device:TPU:1, one launch (start us, length us, event | category | flops | bytes accessed | tf_op | source)
XLA Modules:
  0.0 110.3 jit_solution(14229417401381577277)
XLA Ops:
  0.6 1.3 %fusion.7 = bf16[32,3072]{1,0:T(8,128)(2,1)S(1)} fusion(bf16[32,3072]{1,0:T(8,128)(2,1)} %param.7, bf16[32,3072]{1,0:T(8,128)(2,1)} %param.6), kind=kLoop, calls=%fused_computation.14 | loop fusion | flops 2064384 | bytes 589824 | tf_op jit(solution)/shard_map/convert_element_type | solution.py:224
  1.9 12.4 %all_gather.3 = bf16[128,3072]{1,0:T(8,128)(2,1)S(1)} all-gather(bf16[32,3072]{1,0:T(8,128)(2,1)S(1)} %fusion.7), channel_id=1, replica_groups={{0,128,256,384},{2,130,258,386},{64,192,320,448},{66,194,322,450},{1,3,..., dimensions={0}, use_global_device_ids=true | all-gather | bytes 983040 | tf_op jit(solution)/shard_map/all_gather | solution.py:225
  14.3 2.1 %broadcast_in_dim.2 = bf16[4,4,32,3072]{3,2,1,0:T(8,128)(2,1)} broadcast(bf16[4,32,3072]{2,1,0:T(8,128)(2,1)S(1)} %bitcast.11), dimensions={1,2,3} | broadcast | bytes 3932160 | tf_op jit(solution)/shard_map/broadcast_in_dim | solution.py:230
  16.3 0.0 copy-start.1
  16.4 3.8 %all-to-all-start = ((bf16[4,4,32,3072]{3,2,1,0:T(8,128)(2,1)}), bf16[4,4,32,3072]{3,2,1,0:T(8,128)(2,1)S(1)}, u32[]{:S(2)}, u32[]{:S(2)}) async-start(bf16[4,4,32,3072]{3,2,1,0:T(8,128)(2,1)} %broadcast_in_dim.2), calls=%async_computation | async-start | bytes 6291456 | tf_op jit(solution)/shard_map/all_to_all | solution.py:229
  20.2 0.0 copy-done.1
  20.2 12.2 %collective-permute-start = (bf16[64,384]{1,0:T(8,128)(2,1)S(1)}, bf16[64,384]{1,0:T(8,128)(2,1)S(1)}, u32[]{:S(2)}, u32[]{:S(2)}) collective-permute-start(bf16[64,384]{1,0:T(8,128)(2,1)S(1)} %copy-done.1), channel_id=1, source_target_pairs={{0,48},{4,52},{8,56},{12,60},{16,0},{20,4},{24,8},{28,12},{32,16},... | collective-permute-start | bytes 147464 | tf_op jit(solution)/shard_map/ppermute | solution.py:237
  32.4 4.9 %collective-permute-start.1 = (bf16[64,384]{1,0:T(8,128)(2,1)S(1)}, bf16[64,384]{1,0:T(8,128)(2,1)S(1)}, u32[]{:S(2)}, u32[]{:S(2)}) collective-permute-start(bf16[64,384]{1,0:T(8,128)(2,1)S(1)} %copy-done.1), channel_id=1, source_target_pairs={{0,32},{4,36},{8,40},{12,44},{16,48},{20,52},{24,56},{28,60},{32,0... | collective-permute-start | bytes 147464 | tf_op jit(solution)/shard_map/ppermute | solution.py:237
  37.4 7.3 %collective-permute-start.2 = (bf16[64,384]{1,0:T(8,128)(2,1)S(1)}, bf16[64,384]{1,0:T(8,128)(2,1)S(1)}, u32[]{:S(2)}, u32[]{:S(2)}) collective-permute-start(bf16[64,384]{1,0:T(8,128)(2,1)S(1)} %copy-done.1), channel_id=1, source_target_pairs={{0,16},{4,20},{8,24},{12,28},{16,32},{20,36},{24,40},{28,44},{32,4... | collective-permute-start | bytes 147464 | tf_op jit(solution)/shard_map/ppermute | solution.py:237
  44.6 0.0 collective-permute-done
  44.6 1.7 %collective-permute-done.1 = bf16[64,384]{1,0:T(8,128)(2,1)S(1)} collective-permute-done((bf16[64,384]{1,0:T(8,128)(2,1)S(1)}, bf16[64,384]{1,0:T(8,128)(2,1)S(1)}, u32[]{:S(2)}, u32[]{:S(2)}) %collective-permute-start.1) | collective-permute-done | bytes 49184 | tf_op jit(solution)/shard_map/ppermute | solution.py:237
  46.3 2.6 %collective-permute-done.2 = bf16[64,384]{1,0:T(8,128)(2,1)S(1)} collective-permute-done((bf16[64,384]{1,0:T(8,128)(2,1)S(1)}, bf16[64,384]{1,0:T(8,128)(2,1)S(1)}, u32[]{:S(2)}, u32[]{:S(2)}) %collective-permute-start.2) | collective-permute-done | bytes 49184 | tf_op jit(solution)/shard_map/ppermute | solution.py:237
  48.9 0.0 all-to-all-done
  48.9 5.8 %collective-permute-start.3 = (bf16[512,3072]{1,0:T(8,128)(2,1)S(1)}, bf16[512,3072]{1,0:T(8,128)(2,1)}, u32[]{:S(2)}, u32[]{:S(2)}) collective-permute-start(bf16[512,3072]{1,0:T(8,128)(2,1)S(1)} %bitcast.8), channel_id=1, source_target_pairs={{0,1},{1,0},{2,3},{3,2},{4,5},{5,4},{6,7},{7,6},{8,9},{9,8},{10,11... | collective-permute-start | bytes 9437192 | tf_op jit(solution)/shard_map/ppermute | solution.py:241
  54.8 0.1 pad_add_fusion.info_ref
  54.8 0.0 copy-start
  54.8 1.7 %copy-done = bf16[384,3072]{1,0:T(8,128)(2,1)S(1)} copy-done((bf16[384,3072]{1,0:T(8,128)(2,1)S(1)}, bf16[384,3072]{1,0:T(8,128)(2,1)}, u32[]{:S(2)}) %copy-start) | copy-done | bytes 2359320
  56.5 1.8 %own_sums.1.sums_ref = f32[512,384]{1,0:T(8,128)S(1)} custom-call(bf16[512,3072]{1,0:T(8,128)(2,1)S(1)} %bitcast.9, bf16[384,3072]{1,0:T(8,128)(2,1)S(1)} %copy-done), custom_call_target="tpu_custom_call" | custom-call | flops 1207959552 | bytes 6291456 | tf_op jit(solution)/shard_map/own_sums/pallas_call | solution.py:51
  58.3 1.8 %collective-permute-done.3.lines_ref.sib_ref = bf16[512,3072]{1,0:T(8,128)(2,1)} collective-permute-done((bf16[512,3072]{1,0:T(8,128)(2,1)S(1)}, bf16[512,3072]{1,0:T(8,128)(2,1)}, u32[]{:S(2)}, u32[]{:S(2)}) %collective-permute-start.3) | collective-permute-done | bytes 3145760 | tf_op jit(solution)/shard_map/ppermute | solution.py:241
  60.2 3.8 %sib_sums.1 = (f32[4,64,384]{2,1,0:T(8,128)S(1)}, bf16[4,64,384]{2,1,0:T(8,128)(2,1)S(1)}, bf16[4,64,384]{2,1,0:T(8,128)(2,1)S(1)}, bf16[4,64,384]{2,1,0:T(8,128)(2,1)S(1)}) custom-call(s32[2]{0:T(128)S(1)} %pad_add_fusion.info_ref, f32[512,384]{1,0:T(8,128)S(1)} %own_sums.1.sums_ref, bf16[512,3072]{1,0:T(8,128)(2,1)} %collective-permute-done.3.lines_ref.sib_ref, ...), custom_call_target="tpu_custom_call" | custom-call | flops 1207959552 | bytes 8388608 | tf_op jit(solution)/shard_map/sib_sums/pallas_call | solution.py:80
  63.9 3.6 %collective-permute-start.4 = (bf16[4,64,384]{2,1,0:T(8,128)(2,1)S(1)}, bf16[4,64,384]{2,1,0:T(8,128)(2,1)S(1)}, u32[]{:S(2)}, u32[]{:S(2)}) collective-permute-start(bf16[4,64,384]{2,1,0:T(8,128)(2,1)S(1)} %get-tuple-element.35), channel_id=1, source_target_pairs={{0,4},{1,5},{4,8},{5,9},{8,12},{9,13},{12,16},{13,17},{16,20},{17,... | collective-permute-start | bytes 589832 | tf_op jit(solution)/shard_map/ppermute | solution.py:248
  67.5 3.8 %collective-permute-start.5 = (bf16[4,64,384]{2,1,0:T(8,128)(2,1)S(1)}, bf16[4,64,384]{2,1,0:T(8,128)(2,1)S(1)}, u32[]{:S(2)}, u32[]{:S(2)}) collective-permute-start(bf16[4,64,384]{2,1,0:T(8,128)(2,1)S(1)} %get-tuple-element.36), channel_id=1, source_target_pairs={{0,8},{1,57},{4,12},{5,61},{8,16},{9,1},{12,20},{13,5},{16,24},{17... | collective-permute-start | bytes 589832 | tf_op jit(solution)/shard_map/ppermute | solution.py:248
  71.3 3.4 %collective-permute-start.6 = (bf16[4,64,384]{2,1,0:T(8,128)(2,1)S(1)}, bf16[4,64,384]{2,1,0:T(8,128)(2,1)S(1)}, u32[]{:S(2)}, u32[]{:S(2)}) collective-permute-start(bf16[4,64,384]{2,1,0:T(8,128)(2,1)S(1)} %get-tuple-element.37), channel_id=1, source_target_pairs={{0,60},{1,61},{4,0},{5,1},{8,4},{9,5},{12,8},{13,9},{16,12},{17,13... | collective-permute-start | bytes 589832 | tf_op jit(solution)/shard_map/ppermute | solution.py:248
  74.7 1.9 %collective-permute-start.7 = (bf16[4,64,384]{2,1,0:T(8,128)(2,1)S(1)}, bf16[4,64,384]{2,1,0:T(8,128)(2,1)S(1)}, u32[]{:S(2)}, u32[]{:S(2)}) collective-permute-start(bf16[4,64,384]{2,1,0:T(8,128)(2,1)S(1)} %pad_maximum_fusion.n0_ref), channel_id=1, source_target_pairs={{0,4},{1,5},{4,8},{5,9},{8,12},{9,13},{12,16},{13,17},{16,20},{17,... | collective-permute-start | bytes 589832 | tf_op jit(solution)/shard_map/ppermute | solution.py:246
  76.7 3.8 %collective-permute-start.8 = (bf16[4,64,384]{2,1,0:T(8,128)(2,1)S(1)}, bf16[4,64,384]{2,1,0:T(8,128)(2,1)S(1)}, u32[]{:S(2)}, u32[]{:S(2)}) collective-permute-start(bf16[4,64,384]{2,1,0:T(8,128)(2,1)S(1)} %pad_maximum_fusion.n0_ref), channel_id=1, source_target_pairs={{0,8},{1,57},{4,12},{5,61},{8,16},{9,1},{12,20},{13,5},{16,24},{17... | collective-permute-start | bytes 589832 | tf_op jit(solution)/shard_map/ppermute | solution.py:246
  80.5 0.0 collective-permute-done.4.r1_ref
  80.5 3.4 %collective-permute-start.9 = (bf16[4,64,384]{2,1,0:T(8,128)(2,1)S(1)}, bf16[4,64,384]{2,1,0:T(8,128)(2,1)S(1)}, u32[]{:S(2)}, u32[]{:S(2)}) collective-permute-start(bf16[4,64,384]{2,1,0:T(8,128)(2,1)S(1)} %pad_maximum_fusion.n0_ref), channel_id=1, source_target_pairs={{0,60},{1,61},{4,0},{5,1},{8,4},{9,5},{12,8},{13,9},{16,12},{17,13... | collective-permute-start | bytes 589832 | tf_op jit(solution)/shard_map/ppermute | solution.py:246
  83.8 0.0 collective-permute-done.5.r2_ref
  83.9 0.0 collective-permute-done.6.r3_ref
  83.9 0.6 stage_sums.1
  84.5 5.7 %collective-permute-start.10 = (bf16[64,384]{1,0:T(8,128)(2,1)S(1)}, bf16[64,384]{1,0:T(8,128)(2,1)S(1)}, u32[]{:S(2)}, u32[]{:S(2)}) collective-permute-start(bf16[64,384]{1,0:T(8,128)(2,1)S(1)} %get-tuple-element.43), channel_id=1, source_target_pairs={{0,16},{4,20},{8,24},{12,28},{16,32},{20,36},{24,40},{28,44},{32,4... | collective-permute-start | bytes 147464 | tf_op jit(solution)/shard_map/ppermute | solution.py:251
  90.2 6.1 %collective-permute-start.11 = (bf16[64,384]{1,0:T(8,128)(2,1)S(1)}, bf16[64,384]{1,0:T(8,128)(2,1)S(1)}, u32[]{:S(2)}, u32[]{:S(2)}) collective-permute-start(bf16[64,384]{1,0:T(8,128)(2,1)S(1)} %get-tuple-element.44), channel_id=1, source_target_pairs={{0,32},{4,36},{8,40},{12,44},{16,48},{20,52},{24,56},{28,60},{32,0... | collective-permute-start | bytes 147464 | tf_op jit(solution)/shard_map/ppermute | solution.py:251
  96.4 0.0 collective-permute-done.7.n1_ref
  96.4 5.6 %collective-permute-start.12 = (bf16[64,384]{1,0:T(8,128)(2,1)S(1)}, bf16[64,384]{1,0:T(8,128)(2,1)S(1)}, u32[]{:S(2)}, u32[]{:S(2)}) collective-permute-start(bf16[64,384]{1,0:T(8,128)(2,1)S(1)} %get-tuple-element.45), channel_id=1, source_target_pairs={{0,48},{4,52},{8,56},{12,60},{16,0},{20,4},{24,8},{28,12},{32,16},... | collective-permute-start | bytes 147464 | tf_op jit(solution)/shard_map/ppermute | solution.py:251
  102.0 0.0 collective-permute-done.8.n2_ref
  102.0 0.0 collective-permute-done.9.n3_ref
  102.0 6.6 %weight_sums.1 = bf16[384,3072]{1,0:T(8,128)(2,1)} custom-call(s32[2]{0:T(128)S(1)} %pad_add_fusion.info_ref, bf16[4,64,384]{2,1,0:T(8,128)(2,1)S(1)} %pad_maximum_fusion.n0_ref, bf16[4,64,384]{2,1,0:T(8,128)(2,1)S(1)} %collective-permute-done.7.n1_ref, bf16[4,64,384]{2,1,0:T(8,128)(2,1)S(1)} %collective-permute-done.8.n2_ref, ...), custom_call_target="tpu_custom_call" | custom-call | flops 2415919104 | bytes 10485760 | tf_op jit(solution)/shard_map/weight_sums/pallas_call | solution.py:160
  108.7 0.0 collective-permute-done.10.r1_ref
  108.7 0.0 collective-permute-done.11.r2_ref
  108.7 1.0 collective-permute-done.12.r3_ref
  109.7 0.6 final_sums.1
  (1 shorter events, 0.0 us)
Async XLA Ops:
  16.3 3.8 %copy-start.1 = (bf16[64,384]{1,0:T(8,128)(2,1)S(1)}, bf16[64,384]{1,0:T(8,128)(2,1)}, u32[]{:S(2)}) copy-start(bf16[64,384]{1,0:T(8,128)(2,1)} %param.4) | copy-start | bytes 147460
  16.4 32.6 %all-to-all-start = ((bf16[4,4,32,3072]{3,2,1,0:T(8,128)(2,1)}), bf16[4,4,32,3072]{3,2,1,0:T(8,128)(2,1)S(1)}, u32[]{:S(2)}, u32[]{:S(2)}) async-start(bf16[4,4,32,3072]{3,2,1,0:T(8,128)(2,1)} %broadcast_in_dim.2), calls=%async_computation | async-start | bytes 6291456 | tf_op jit(solution)/shard_map/all_to_all | solution.py:229
  20.2 24.4 %collective-permute-start = (bf16[64,384]{1,0:T(8,128)(2,1)S(1)}, bf16[64,384]{1,0:T(8,128)(2,1)S(1)}, u32[]{:S(2)}, u32[]{:S(2)}) collective-permute-start(bf16[64,384]{1,0:T(8,128)(2,1)S(1)} %copy-done.1), channel_id=1, source_target_pairs={{0,48},{4,52},{8,56},{12,60},{16,0},{20,4},{24,8},{28,12},{32,16},... | collective-permute-start | bytes 147464 | tf_op jit(solution)/shard_map/ppermute | solution.py:237
  32.4 13.9 %collective-permute-start.1 = (bf16[64,384]{1,0:T(8,128)(2,1)S(1)}, bf16[64,384]{1,0:T(8,128)(2,1)S(1)}, u32[]{:S(2)}, u32[]{:S(2)}) collective-permute-start(bf16[64,384]{1,0:T(8,128)(2,1)S(1)} %copy-done.1), channel_id=1, source_target_pairs={{0,32},{4,36},{8,40},{12,44},{16,48},{20,52},{24,56},{28,60},{32,0... | collective-permute-start | bytes 147464 | tf_op jit(solution)/shard_map/ppermute | solution.py:237
  37.4 11.6 %collective-permute-start.2 = (bf16[64,384]{1,0:T(8,128)(2,1)S(1)}, bf16[64,384]{1,0:T(8,128)(2,1)S(1)}, u32[]{:S(2)}, u32[]{:S(2)}) collective-permute-start(bf16[64,384]{1,0:T(8,128)(2,1)S(1)} %copy-done.1), channel_id=1, source_target_pairs={{0,16},{4,20},{8,24},{12,28},{16,32},{20,36},{24,40},{28,44},{32,4... | collective-permute-start | bytes 147464 | tf_op jit(solution)/shard_map/ppermute | solution.py:237
  48.9 11.2 %collective-permute-start.3 = (bf16[512,3072]{1,0:T(8,128)(2,1)S(1)}, bf16[512,3072]{1,0:T(8,128)(2,1)}, u32[]{:S(2)}, u32[]{:S(2)}) collective-permute-start(bf16[512,3072]{1,0:T(8,128)(2,1)S(1)} %bitcast.8), channel_id=1, source_target_pairs={{0,1},{1,0},{2,3},{3,2},{4,5},{5,4},{6,7},{7,6},{8,9},{9,8},{10,11... | collective-permute-start | bytes 9437192 | tf_op jit(solution)/shard_map/ppermute | solution.py:241
  54.8 1.7 %copy-start = (bf16[384,3072]{1,0:T(8,128)(2,1)S(1)}, bf16[384,3072]{1,0:T(8,128)(2,1)}, u32[]{:S(2)}) copy-start(bf16[384,3072]{1,0:T(8,128)(2,1)} %w_ref.3) | copy-start | bytes 7077892
  63.9 16.5 %collective-permute-start.4 = (bf16[4,64,384]{2,1,0:T(8,128)(2,1)S(1)}, bf16[4,64,384]{2,1,0:T(8,128)(2,1)S(1)}, u32[]{:S(2)}, u32[]{:S(2)}) collective-permute-start(bf16[4,64,384]{2,1,0:T(8,128)(2,1)S(1)} %get-tuple-element.35), channel_id=1, source_target_pairs={{0,4},{1,5},{4,8},{5,9},{8,12},{9,13},{12,16},{13,17},{16,20},{17,... | collective-permute-start | bytes 589832 | tf_op jit(solution)/shard_map/ppermute | solution.py:248
  67.5 16.3 %collective-permute-start.5 = (bf16[4,64,384]{2,1,0:T(8,128)(2,1)S(1)}, bf16[4,64,384]{2,1,0:T(8,128)(2,1)S(1)}, u32[]{:S(2)}, u32[]{:S(2)}) collective-permute-start(bf16[4,64,384]{2,1,0:T(8,128)(2,1)S(1)} %get-tuple-element.36), channel_id=1, source_target_pairs={{0,8},{1,57},{4,12},{5,61},{8,16},{9,1},{12,20},{13,5},{16,24},{17... | collective-permute-start | bytes 589832 | tf_op jit(solution)/shard_map/ppermute | solution.py:248
  71.3 12.5 %collective-permute-start.6 = (bf16[4,64,384]{2,1,0:T(8,128)(2,1)S(1)}, bf16[4,64,384]{2,1,0:T(8,128)(2,1)S(1)}, u32[]{:S(2)}, u32[]{:S(2)}) collective-permute-start(bf16[4,64,384]{2,1,0:T(8,128)(2,1)S(1)} %get-tuple-element.37), channel_id=1, source_target_pairs={{0,60},{1,61},{4,0},{5,1},{8,4},{9,5},{12,8},{13,9},{16,12},{17,13... | collective-permute-start | bytes 589832 | tf_op jit(solution)/shard_map/ppermute | solution.py:248
  74.7 21.6 %collective-permute-start.7 = (bf16[4,64,384]{2,1,0:T(8,128)(2,1)S(1)}, bf16[4,64,384]{2,1,0:T(8,128)(2,1)S(1)}, u32[]{:S(2)}, u32[]{:S(2)}) collective-permute-start(bf16[4,64,384]{2,1,0:T(8,128)(2,1)S(1)} %pad_maximum_fusion.n0_ref), channel_id=1, source_target_pairs={{0,4},{1,5},{4,8},{5,9},{8,12},{9,13},{12,16},{13,17},{16,20},{17,... | collective-permute-start | bytes 589832 | tf_op jit(solution)/shard_map/ppermute | solution.py:246
  76.7 25.3 %collective-permute-start.8 = (bf16[4,64,384]{2,1,0:T(8,128)(2,1)S(1)}, bf16[4,64,384]{2,1,0:T(8,128)(2,1)S(1)}, u32[]{:S(2)}, u32[]{:S(2)}) collective-permute-start(bf16[4,64,384]{2,1,0:T(8,128)(2,1)S(1)} %pad_maximum_fusion.n0_ref), channel_id=1, source_target_pairs={{0,8},{1,57},{4,12},{5,61},{8,16},{9,1},{12,20},{13,5},{16,24},{17... | collective-permute-start | bytes 589832 | tf_op jit(solution)/shard_map/ppermute | solution.py:246
  80.5 21.5 %collective-permute-start.9 = (bf16[4,64,384]{2,1,0:T(8,128)(2,1)S(1)}, bf16[4,64,384]{2,1,0:T(8,128)(2,1)S(1)}, u32[]{:S(2)}, u32[]{:S(2)}) collective-permute-start(bf16[4,64,384]{2,1,0:T(8,128)(2,1)S(1)} %pad_maximum_fusion.n0_ref), channel_id=1, source_target_pairs={{0,60},{1,61},{4,0},{5,1},{8,4},{9,5},{12,8},{13,9},{16,12},{17,13... | collective-permute-start | bytes 589832 | tf_op jit(solution)/shard_map/ppermute | solution.py:246
  84.5 24.1 %collective-permute-start.10 = (bf16[64,384]{1,0:T(8,128)(2,1)S(1)}, bf16[64,384]{1,0:T(8,128)(2,1)S(1)}, u32[]{:S(2)}, u32[]{:S(2)}) collective-permute-start(bf16[64,384]{1,0:T(8,128)(2,1)S(1)} %get-tuple-element.43), channel_id=1, source_target_pairs={{0,16},{4,20},{8,24},{12,28},{16,32},{20,36},{24,40},{28,44},{32,4... | collective-permute-start | bytes 147464 | tf_op jit(solution)/shard_map/ppermute | solution.py:251
  90.2 18.4 %collective-permute-start.11 = (bf16[64,384]{1,0:T(8,128)(2,1)S(1)}, bf16[64,384]{1,0:T(8,128)(2,1)S(1)}, u32[]{:S(2)}, u32[]{:S(2)}) collective-permute-start(bf16[64,384]{1,0:T(8,128)(2,1)S(1)} %get-tuple-element.44), channel_id=1, source_target_pairs={{0,32},{4,36},{8,40},{12,44},{16,48},{20,52},{24,56},{28,60},{32,0... | collective-permute-start | bytes 147464 | tf_op jit(solution)/shard_map/ppermute | solution.py:251
  96.4 13.3 %collective-permute-start.12 = (bf16[64,384]{1,0:T(8,128)(2,1)S(1)}, bf16[64,384]{1,0:T(8,128)(2,1)S(1)}, u32[]{:S(2)}, u32[]{:S(2)}) collective-permute-start(bf16[64,384]{1,0:T(8,128)(2,1)S(1)} %get-tuple-element.45), channel_id=1, source_target_pairs={{0,48},{4,52},{8,56},{12,60},{16,0},{20,4},{24,8},{28,12},{32,16},... | collective-permute-start | bytes 147464 | tf_op jit(solution)/shard_map/ppermute | solution.py:251

commit v12 on v11

--- a/solution.py
+++ b/solution.py
@@ -156,7 +156,7 @@
 
 
 def weight_sums(info, near, hg_own, hg_sib):
-    tile = 1024
+    tile = 1536
     return pl.pallas_call(
         weight_kernel,
         out_shape=jax.ShapeDtypeStruct((384, 3072), jnp.bfloat16),

time: 111 us -> 111 us (level)
  no operation moved by 1% of the time
where the time goes in v12:
time: 111 us; the launch traced here: 110 us
  starting transfers between devices  71.3 us (64%)
  Pallas kernels  13.2 us (12%)
  blocking collectives  12.4 us (11%)
  waiting for transfers between devices  7.49 us (7%)
  local copies, waits for them, and re-layouts  3.72 us (3%)
  other arithmetic  1.41 us (1%)
    ppermute x3, starting transfers between devices, per_device(): lax.ppermute(inputs, Z, far_shift(-d))  24.4 us
    ppermute x3, starting transfers between devices, per_device(): far = [lax.ppermute(s, Z, far_shift(d + 1)) for d, s in enumerate(sends)]  17.4 us
    all_gather x1, blocking collectives, per_device(): lax.all_gather(local, PLANE, axis=0, tiled=True, axis_index_groups=first_...  12.4 us
    ppermute x3, starting transfers between devices, per_device(): lax.ppermute(s, Z + ('core',), column_shift(by))  10.7 us
    ppermute x3, starting transfers between devices, per_device(): lax.ppermute(near, Z + ('core',), column_shift(by))  9.09 us
    pallas_call x1, Pallas kernels, weight_sums(): pl.pallas_call(weight_kernel, out_shape=jax.ShapeDtypeStruct((384, 3072),...  6.32 us
    ppermute x1, starting transfers between devices, per_device(): hg_sib = lax.ppermute(hg_own, 'core', swap)  5.8 us
    ppermute x3, waiting for transfers between devices, per_device(): lax.ppermute(inputs, Z, far_shift(-d))  4.3 us
  transfers between devices with their start and end apart: 14, of which 4 were waited for; matrix products, arithmetic and copies ran while one was open for 0% of the time, Pallas kernels for 8%

profile of v12, /device:TPU:1, one launch (start us, length us, event | category | flops | bytes accessed | tf_op | source)
XLA Modules:
  0.0 110.3 jit_solution(11876836992319906666)
XLA Ops:
  0.6 1.3 %fusion.7 = bf16[32,3072]{1,0:T(8,128)(2,1)S(1)} fusion(bf16[32,3072]{1,0:T(8,128)(2,1)} %param.7, bf16[32,3072]{1,0:T(8,128)(2,1)} %param.6), kind=kLoop, calls=%fused_computation.14 | loop fusion | flops 2064384 | bytes 589824 | tf_op jit(solution)/shard_map/convert_element_type | solution.py:224
  1.9 12.4 %all_gather.3 = bf16[128,3072]{1,0:T(8,128)(2,1)S(1)} all-gather(bf16[32,3072]{1,0:T(8,128)(2,1)S(1)} %fusion.7), channel_id=1, replica_groups={{0,128,256,384},{2,130,258,386},{64,192,320,448},{66,194,322,450},{1,3,..., dimensions={0}, use_global_device_ids=true | all-gather | bytes 983040 | tf_op jit(solution)/shard_map/all_gather | solution.py:225
  14.3 2.1 %broadcast_in_dim.2 = bf16[4,4,32,3072]{3,2,1,0:T(8,128)(2,1)} broadcast(bf16[4,32,3072]{2,1,0:T(8,128)(2,1)S(1)} %bitcast.11), dimensions={1,2,3} | broadcast | bytes 3932160 | tf_op jit(solution)/shard_map/broadcast_in_dim | solution.py:230
  16.3 0.0 copy-start.1
  16.4 3.8 %all-to-all-start = ((bf16[4,4,32,3072]{3,2,1,0:T(8,128)(2,1)}), bf16[4,4,32,3072]{3,2,1,0:T(8,128)(2,1)S(1)}, u32[]{:S(2)}, u32[]{:S(2)}) async-start(bf16[4,4,32,3072]{3,2,1,0:T(8,128)(2,1)} %broadcast_in_dim.2), calls=%async_computation | async-start | bytes 6291456 | tf_op jit(solution)/shard_map/all_to_all | solution.py:229
  20.2 0.0 copy-done.1
  20.2 12.2 %collective-permute-start = (bf16[64,384]{1,0:T(8,128)(2,1)S(1)}, bf16[64,384]{1,0:T(8,128)(2,1)S(1)}, u32[]{:S(2)}, u32[]{:S(2)}) collective-permute-start(bf16[64,384]{1,0:T(8,128)(2,1)S(1)} %copy-done.1), channel_id=1, source_target_pairs={{0,48},{4,52},{8,56},{12,60},{16,0},{20,4},{24,8},{28,12},{32,16},... | collective-permute-start | bytes 147464 | tf_op jit(solution)/shard_map/ppermute | solution.py:237
  32.4 4.9 %collective-permute-start.1 = (bf16[64,384]{1,0:T(8,128)(2,1)S(1)}, bf16[64,384]{1,0:T(8,128)(2,1)S(1)}, u32[]{:S(2)}, u32[]{:S(2)}) collective-permute-start(bf16[64,384]{1,0:T(8,128)(2,1)S(1)} %copy-done.1), channel_id=1, source_target_pairs={{0,32},{4,36},{8,40},{12,44},{16,48},{20,52},{24,56},{28,60},{32,0... | collective-permute-start | bytes 147464 | tf_op jit(solution)/shard_map/ppermute | solution.py:237
  37.4 7.3 %collective-permute-start.2 = (bf16[64,384]{1,0:T(8,128)(2,1)S(1)}, bf16[64,384]{1,0:T(8,128)(2,1)S(1)}, u32[]{:S(2)}, u32[]{:S(2)}) collective-permute-start(bf16[64,384]{1,0:T(8,128)(2,1)S(1)} %copy-done.1), channel_id=1, source_target_pairs={{0,16},{4,20},{8,24},{12,28},{16,32},{20,36},{24,40},{28,44},{32,4... | collective-permute-start | bytes 147464 | tf_op jit(solution)/shard_map/ppermute | solution.py:237
  44.6 0.0 collective-permute-done
  44.6 1.7 %collective-permute-done.1 = bf16[64,384]{1,0:T(8,128)(2,1)S(1)} collective-permute-done((bf16[64,384]{1,0:T(8,128)(2,1)S(1)}, bf16[64,384]{1,0:T(8,128)(2,1)S(1)}, u32[]{:S(2)}, u32[]{:S(2)}) %collective-permute-start.1) | collective-permute-done | bytes 49184 | tf_op jit(solution)/shard_map/ppermute | solution.py:237
  46.3 2.6 %collective-permute-done.2 = bf16[64,384]{1,0:T(8,128)(2,1)S(1)} collective-permute-done((bf16[64,384]{1,0:T(8,128)(2,1)S(1)}, bf16[64,384]{1,0:T(8,128)(2,1)S(1)}, u32[]{:S(2)}, u32[]{:S(2)}) %collective-permute-start.2) | collective-permute-done | bytes 49184 | tf_op jit(solution)/shard_map/ppermute | solution.py:237
  48.9 0.0 all-to-all-done
  48.9 5.8 %collective-permute-start.3 = (bf16[512,3072]{1,0:T(8,128)(2,1)S(1)}, bf16[512,3072]{1,0:T(8,128)(2,1)}, u32[]{:S(2)}, u32[]{:S(2)}) collective-permute-start(bf16[512,3072]{1,0:T(8,128)(2,1)S(1)} %bitcast.8), channel_id=1, source_target_pairs={{0,1},{1,0},{2,3},{3,2},{4,5},{5,4},{6,7},{7,6},{8,9},{9,8},{10,11... | collective-permute-start | bytes 9437192 | tf_op jit(solution)/shard_map/ppermute | solution.py:241
  54.8 0.1 pad_add_fusion.info_ref
  54.8 0.0 copy-start
  54.8 1.7 %copy-done = bf16[384,3072]{1,0:T(8,128)(2,1)S(1)} copy-done((bf16[384,3072]{1,0:T(8,128)(2,1)S(1)}, bf16[384,3072]{1,0:T(8,128)(2,1)}, u32[]{:S(2)}) %copy-start) | copy-done | bytes 2359320
  56.5 1.8 %own_sums.1.sums_ref = f32[512,384]{1,0:T(8,128)S(1)} custom-call(bf16[512,3072]{1,0:T(8,128)(2,1)S(1)} %bitcast.9, bf16[384,3072]{1,0:T(8,128)(2,1)S(1)} %copy-done), custom_call_target="tpu_custom_call" | custom-call | flops 1207959552 | bytes 6291456 | tf_op jit(solution)/shard_map/own_sums/pallas_call | solution.py:51
  58.3 1.8 %collective-permute-done.3.lines_ref.sib_ref = bf16[512,3072]{1,0:T(8,128)(2,1)} collective-permute-done((bf16[512,3072]{1,0:T(8,128)(2,1)S(1)}, bf16[512,3072]{1,0:T(8,128)(2,1)}, u32[]{:S(2)}, u32[]{:S(2)}) %collective-permute-start.3) | collective-permute-done | bytes 3145760 | tf_op jit(solution)/shard_map/ppermute | solution.py:241
  60.2 3.8 %sib_sums.1 = (f32[4,64,384]{2,1,0:T(8,128)S(1)}, bf16[4,64,384]{2,1,0:T(8,128)(2,1)S(1)}, bf16[4,64,384]{2,1,0:T(8,128)(2,1)S(1)}, bf16[4,64,384]{2,1,0:T(8,128)(2,1)S(1)}) custom-call(s32[2]{0:T(128)S(1)} %pad_add_fusion.info_ref, f32[512,384]{1,0:T(8,128)S(1)} %own_sums.1.sums_ref, bf16[512,3072]{1,0:T(8,128)(2,1)} %collective-permute-done.3.lines_ref.sib_ref, ...), custom_call_target="tpu_custom_call" | custom-call | flops 1207959552 | bytes 8388608 | tf_op jit(solution)/shard_map/sib_sums/pallas_call | solution.py:80
  63.9 3.6 %collective-permute-start.4 = (bf16[4,64,384]{2,1,0:T(8,128)(2,1)S(1)}, bf16[4,64,384]{2,1,0:T(8,128)(2,1)S(1)}, u32[]{:S(2)}, u32[]{:S(2)}) collective-permute-start(bf16[4,64,384]{2,1,0:T(8,128)(2,1)S(1)} %get-tuple-element.35), channel_id=1, source_target_pairs={{0,4},{1,5},{4,8},{5,9},{8,12},{9,13},{12,16},{13,17},{16,20},{17,... | collective-permute-start | bytes 589832 | tf_op jit(solution)/shard_map/ppermute | solution.py:248
  67.5 3.8 %collective-permute-start.5 = (bf16[4,64,384]{2,1,0:T(8,128)(2,1)S(1)}, bf16[4,64,384]{2,1,0:T(8,128)(2,1)S(1)}, u32[]{:S(2)}, u32[]{:S(2)}) collective-permute-start(bf16[4,64,384]{2,1,0:T(8,128)(2,1)S(1)} %get-tuple-element.36), channel_id=1, source_target_pairs={{0,8},{1,57},{4,12},{5,61},{8,16},{9,1},{12,20},{13,5},{16,24},{17... | collective-permute-start | bytes 589832 | tf_op jit(solution)/shard_map/ppermute | solution.py:248
  71.3 3.4 %collective-permute-start.6 = (bf16[4,64,384]{2,1,0:T(8,128)(2,1)S(1)}, bf16[4,64,384]{2,1,0:T(8,128)(2,1)S(1)}, u32[]{:S(2)}, u32[]{:S(2)}) collective-permute-start(bf16[4,64,384]{2,1,0:T(8,128)(2,1)S(1)} %get-tuple-element.37), channel_id=1, source_target_pairs={{0,60},{1,61},{4,0},{5,1},{8,4},{9,5},{12,8},{13,9},{16,12},{17,13... | collective-permute-start | bytes 589832 | tf_op jit(solution)/shard_map/ppermute | solution.py:248
  74.7 1.9 %collective-permute-start.7 = (bf16[4,64,384]{2,1,0:T(8,128)(2,1)S(1)}, bf16[4,64,384]{2,1,0:T(8,128)(2,1)S(1)}, u32[]{:S(2)}, u32[]{:S(2)}) collective-permute-start(bf16[4,64,384]{2,1,0:T(8,128)(2,1)S(1)} %pad_maximum_fusion.n0_ref), channel_id=1, source_target_pairs={{0,4},{1,5},{4,8},{5,9},{8,12},{9,13},{12,16},{13,17},{16,20},{17,... | collective-permute-start | bytes 589832 | tf_op jit(solution)/shard_map/ppermute | solution.py:246
  76.7 3.8 %collective-permute-start.8 = (bf16[4,64,384]{2,1,0:T(8,128)(2,1)S(1)}, bf16[4,64,384]{2,1,0:T(8,128)(2,1)S(1)}, u32[]{:S(2)}, u32[]{:S(2)}) collective-permute-start(bf16[4,64,384]{2,1,0:T(8,128)(2,1)S(1)} %pad_maximum_fusion.n0_ref), channel_id=1, source_target_pairs={{0,8},{1,57},{4,12},{5,61},{8,16},{9,1},{12,20},{13,5},{16,24},{17... | collective-permute-start | bytes 589832 | tf_op jit(solution)/shard_map/ppermute | solution.py:246
  80.5 0.0 collective-permute-done.4.r1_ref
  80.5 3.4 %collective-permute-start.9 = (bf16[4,64,384]{2,1,0:T(8,128)(2,1)S(1)}, bf16[4,64,384]{2,1,0:T(8,128)(2,1)S(1)}, u32[]{:S(2)}, u32[]{:S(2)}) collective-permute-start(bf16[4,64,384]{2,1,0:T(8,128)(2,1)S(1)} %pad_maximum_fusion.n0_ref), channel_id=1, source_target_pairs={{0,60},{1,61},{4,0},{5,1},{8,4},{9,5},{12,8},{13,9},{16,12},{17,13... | collective-permute-start | bytes 589832 | tf_op jit(solution)/shard_map/ppermute | solution.py:246
  83.8 0.0 collective-permute-done.5.r2_ref
  83.9 0.0 collective-permute-done.6.r3_ref
  83.9 0.6 stage_sums.1
  84.5 5.7 %collective-permute-start.10 = (bf16[64,384]{1,0:T(8,128)(2,1)S(1)}, bf16[64,384]{1,0:T(8,128)(2,1)S(1)}, u32[]{:S(2)}, u32[]{:S(2)}) collective-permute-start(bf16[64,384]{1,0:T(8,128)(2,1)S(1)} %get-tuple-element.43), channel_id=1, source_target_pairs={{0,16},{4,20},{8,24},{12,28},{16,32},{20,36},{24,40},{28,44},{32,4... | collective-permute-start | bytes 147464 | tf_op jit(solution)/shard_map/ppermute | solution.py:251
  90.2 6.1 %collective-permute-start.11 = (bf16[64,384]{1,0:T(8,128)(2,1)S(1)}, bf16[64,384]{1,0:T(8,128)(2,1)S(1)}, u32[]{:S(2)}, u32[]{:S(2)}) collective-permute-start(bf16[64,384]{1,0:T(8,128)(2,1)S(1)} %get-tuple-element.44), channel_id=1, source_target_pairs={{0,32},{4,36},{8,40},{12,44},{16,48},{20,52},{24,56},{28,60},{32,0... | collective-permute-start | bytes 147464 | tf_op jit(solution)/shard_map/ppermute | solution.py:251
  96.4 0.0 collective-permute-done.7.n1_ref
  96.4 5.6 %collective-permute-start.12 = (bf16[64,384]{1,0:T(8,128)(2,1)S(1)}, bf16[64,384]{1,0:T(8,128)(2,1)S(1)}, u32[]{:S(2)}, u32[]{:S(2)}) collective-permute-start(bf16[64,384]{1,0:T(8,128)(2,1)S(1)} %get-tuple-element.45), channel_id=1, source_target_pairs={{0,48},{4,52},{8,56},{12,60},{16,0},{20,4},{24,8},{28,12},{32,16},... | collective-permute-start | bytes 147464 | tf_op jit(solution)/shard_map/ppermute | solution.py:251
  102.0 0.0 collective-permute-done.8.n2_ref
  102.0 0.0 collective-permute-done.9.n3_ref
  102.0 6.3 %weight_sums.1 = bf16[384,3072]{1,0:T(8,128)(2,1)} custom-call(s32[2]{0:T(128)S(1)} %pad_add_fusion.info_ref, bf16[4,64,384]{2,1,0:T(8,128)(2,1)S(1)} %pad_maximum_fusion.n0_ref, bf16[4,64,384]{2,1,0:T(8,128)(2,1)S(1)} %collective-permute-done.7.n1_ref, bf16[4,64,384]{2,1,0:T(8,128)(2,1)S(1)} %collective-permute-done.8.n2_ref, ...), custom_call_target="tpu_custom_call" | custom-call | flops 2415919104 | bytes 10485760 | tf_op jit(solution)/shard_map/weight_sums/pallas_call | solution.py:160
  108.3 0.0 collective-permute-done.10.r1_ref
  108.3 0.0 collective-permute-done.11.r2_ref
  108.3 1.3 %collective-permute-done.12.r3_ref = bf16[64,384]{1,0:T(8,128)(2,1)S(1)} collective-permute-done((bf16[64,384]{1,0:T(8,128)(2,1)S(1)}, bf16[64,384]{1,0:T(8,128)(2,1)S(1)}, u32[]{:S(2)}, u32[]{:S(2)}) %collective-permute-start.12) | collective-permute-done | bytes 49184 | tf_op jit(solution)/shard_map/ppermute | solution.py:251
  109.7 0.6 final_sums.1
  (1 shorter events, 0.0 us)
Async XLA Ops:
  16.3 3.8 %copy-start.1 = (bf16[64,384]{1,0:T(8,128)(2,1)S(1)}, bf16[64,384]{1,0:T(8,128)(2,1)}, u32[]{:S(2)}) copy-start(bf16[64,384]{1,0:T(8,128)(2,1)} %param.4) | copy-start | bytes 147460
  16.4 32.6 %all-to-all-start = ((bf16[4,4,32,3072]{3,2,1,0:T(8,128)(2,1)}), bf16[4,4,32,3072]{3,2,1,0:T(8,128)(2,1)S(1)}, u32[]{:S(2)}, u32[]{:S(2)}) async-start(bf16[4,4,32,3072]{3,2,1,0:T(8,128)(2,1)} %broadcast_in_dim.2), calls=%async_computation | async-start | bytes 6291456 | tf_op jit(solution)/shard_map/all_to_all | solution.py:229
  20.2 24.4 %collective-permute-start = (bf16[64,384]{1,0:T(8,128)(2,1)S(1)}, bf16[64,384]{1,0:T(8,128)(2,1)S(1)}, u32[]{:S(2)}, u32[]{:S(2)}) collective-permute-start(bf16[64,384]{1,0:T(8,128)(2,1)S(1)} %copy-done.1), channel_id=1, source_target_pairs={{0,48},{4,52},{8,56},{12,60},{16,0},{20,4},{24,8},{28,12},{32,16},... | collective-permute-start | bytes 147464 | tf_op jit(solution)/shard_map/ppermute | solution.py:237
  32.4 13.9 %collective-permute-start.1 = (bf16[64,384]{1,0:T(8,128)(2,1)S(1)}, bf16[64,384]{1,0:T(8,128)(2,1)S(1)}, u32[]{:S(2)}, u32[]{:S(2)}) collective-permute-start(bf16[64,384]{1,0:T(8,128)(2,1)S(1)} %copy-done.1), channel_id=1, source_target_pairs={{0,32},{4,36},{8,40},{12,44},{16,48},{20,52},{24,56},{28,60},{32,0... | collective-permute-start | bytes 147464 | tf_op jit(solution)/shard_map/ppermute | solution.py:237
  37.4 11.6 %collective-permute-start.2 = (bf16[64,384]{1,0:T(8,128)(2,1)S(1)}, bf16[64,384]{1,0:T(8,128)(2,1)S(1)}, u32[]{:S(2)}, u32[]{:S(2)}) collective-permute-start(bf16[64,384]{1,0:T(8,128)(2,1)S(1)} %copy-done.1), channel_id=1, source_target_pairs={{0,16},{4,20},{8,24},{12,28},{16,32},{20,36},{24,40},{28,44},{32,4... | collective-permute-start | bytes 147464 | tf_op jit(solution)/shard_map/ppermute | solution.py:237
  48.9 11.2 %collective-permute-start.3 = (bf16[512,3072]{1,0:T(8,128)(2,1)S(1)}, bf16[512,3072]{1,0:T(8,128)(2,1)}, u32[]{:S(2)}, u32[]{:S(2)}) collective-permute-start(bf16[512,3072]{1,0:T(8,128)(2,1)S(1)} %bitcast.8), channel_id=1, source_target_pairs={{0,1},{1,0},{2,3},{3,2},{4,5},{5,4},{6,7},{7,6},{8,9},{9,8},{10,11... | collective-permute-start | bytes 9437192 | tf_op jit(solution)/shard_map/ppermute | solution.py:241
  54.8 1.7 %copy-start = (bf16[384,3072]{1,0:T(8,128)(2,1)S(1)}, bf16[384,3072]{1,0:T(8,128)(2,1)}, u32[]{:S(2)}) copy-start(bf16[384,3072]{1,0:T(8,128)(2,1)} %w_ref.3) | copy-start | bytes 7077892
  63.9 16.5 %collective-permute-start.4 = (bf16[4,64,384]{2,1,0:T(8,128)(2,1)S(1)}, bf16[4,64,384]{2,1,0:T(8,128)(2,1)S(1)}, u32[]{:S(2)}, u32[]{:S(2)}) collective-permute-start(bf16[4,64,384]{2,1,0:T(8,128)(2,1)S(1)} %get-tuple-element.35), channel_id=1, source_target_pairs={{0,4},{1,5},{4,8},{5,9},{8,12},{9,13},{12,16},{13,17},{16,20},{17,... | collective-permute-start | bytes 589832 | tf_op jit(solution)/shard_map/ppermute | solution.py:248
  67.5 16.3 %collective-permute-start.5 = (bf16[4,64,384]{2,1,0:T(8,128)(2,1)S(1)}, bf16[4,64,384]{2,1,0:T(8,128)(2,1)S(1)}, u32[]{:S(2)}, u32[]{:S(2)}) collective-permute-start(bf16[4,64,384]{2,1,0:T(8,128)(2,1)S(1)} %get-tuple-element.36), channel_id=1, source_target_pairs={{0,8},{1,57},{4,12},{5,61},{8,16},{9,1},{12,20},{13,5},{16,24},{17... | collective-permute-start | bytes 589832 | tf_op jit(solution)/shard_map/ppermute | solution.py:248
  71.3 12.5 %collective-permute-start.6 = (bf16[4,64,384]{2,1,0:T(8,128)(2,1)S(1)}, bf16[4,64,384]{2,1,0:T(8,128)(2,1)S(1)}, u32[]{:S(2)}, u32[]{:S(2)}) collective-permute-start(bf16[4,64,384]{2,1,0:T(8,128)(2,1)S(1)} %get-tuple-element.37), channel_id=1, source_target_pairs={{0,60},{1,61},{4,0},{5,1},{8,4},{9,5},{12,8},{13,9},{16,12},{17,13... | collective-permute-start | bytes 589832 | tf_op jit(solution)/shard_map/ppermute | solution.py:248
  74.7 21.6 %collective-permute-start.7 = (bf16[4,64,384]{2,1,0:T(8,128)(2,1)S(1)}, bf16[4,64,384]{2,1,0:T(8,128)(2,1)S(1)}, u32[]{:S(2)}, u32[]{:S(2)}) collective-permute-start(bf16[4,64,384]{2,1,0:T(8,128)(2,1)S(1)} %pad_maximum_fusion.n0_ref), channel_id=1, source_target_pairs={{0,4},{1,5},{4,8},{5,9},{8,12},{9,13},{12,16},{13,17},{16,20},{17,... | collective-permute-start | bytes 589832 | tf_op jit(solution)/shard_map/ppermute | solution.py:246
  76.7 25.3 %collective-permute-start.8 = (bf16[4,64,384]{2,1,0:T(8,128)(2,1)S(1)}, bf16[4,64,384]{2,1,0:T(8,128)(2,1)S(1)}, u32[]{:S(2)}, u32[]{:S(2)}) collective-permute-start(bf16[4,64,384]{2,1,0:T(8,128)(2,1)S(1)} %pad_maximum_fusion.n0_ref), channel_id=1, source_target_pairs={{0,8},{1,57},{4,12},{5,61},{8,16},{9,1},{12,20},{13,5},{16,24},{17... | collective-permute-start | bytes 589832 | tf_op jit(solution)/shard_map/ppermute | solution.py:246
  80.5 21.5 %collective-permute-start.9 = (bf16[4,64,384]{2,1,0:T(8,128)(2,1)S(1)}, bf16[4,64,384]{2,1,0:T(8,128)(2,1)S(1)}, u32[]{:S(2)}, u32[]{:S(2)}) collective-permute-start(bf16[4,64,384]{2,1,0:T(8,128)(2,1)S(1)} %pad_maximum_fusion.n0_ref), channel_id=1, source_target_pairs={{0,60},{1,61},{4,0},{5,1},{8,4},{9,5},{12,8},{13,9},{16,12},{17,13... | collective-permute-start | bytes 589832 | tf_op jit(solution)/shard_map/ppermute | solution.py:246
  84.5 23.8 %collective-permute-start.10 = (bf16[64,384]{1,0:T(8,128)(2,1)S(1)}, bf16[64,384]{1,0:T(8,128)(2,1)S(1)}, u32[]{:S(2)}, u32[]{:S(2)}) collective-permute-start(bf16[64,384]{1,0:T(8,128)(2,1)S(1)} %get-tuple-element.43), channel_id=1, source_target_pairs={{0,16},{4,20},{8,24},{12,28},{16,32},{20,36},{24,40},{28,44},{32,4... | collective-permute-start | bytes 147464 | tf_op jit(solution)/shard_map/ppermute | solution.py:251
  90.2 18.1 %collective-permute-start.11 = (bf16[64,384]{1,0:T(8,128)(2,1)S(1)}, bf16[64,384]{1,0:T(8,128)(2,1)S(1)}, u32[]{:S(2)}, u32[]{:S(2)}) collective-permute-start(bf16[64,384]{1,0:T(8,128)(2,1)S(1)} %get-tuple-element.44), channel_id=1, source_target_pairs={{0,32},{4,36},{8,40},{12,44},{16,48},{20,52},{24,56},{28,60},{32,0... | collective-permute-start | bytes 147464 | tf_op jit(solution)/shard_map/ppermute | solution.py:251
  96.4 13.3 %collective-permute-start.12 = (bf16[64,384]{1,0:T(8,128)(2,1)S(1)}, bf16[64,384]{1,0:T(8,128)(2,1)S(1)}, u32[]{:S(2)}, u32[]{:S(2)}) collective-permute-start(bf16[64,384]{1,0:T(8,128)(2,1)S(1)} %get-tuple-element.45), channel_id=1, source_target_pairs={{0,48},{4,52},{8,56},{12,60},{16,0},{20,4},{24,8},{28,12},{32,16},... | collective-permute-start | bytes 147464 | tf_op jit(solution)/shard_map/ppermute | solution.py:251
